TPU v7x, 128 devices: a whole 4x4x4 slice. The times are simulated.
128 devices in a mesh: member: 4 (over x_hi, core), cells: 32 (over y, x_lo, z).
Axes of the slice: x: 4 (x_hi: 2, x_lo: 2; x = x_hi * 2 + x_lo), y: 4, z: 4, core: 2. Of those that a mesh axis runs over, the one named last changes fastest.
Arguments:
- latent: bfloat16 [4, 8192, 1024], P('member', 'cells'), may hold values from -6 to 6
- counts: int32 [32], replicated, may hold values from 129 to 256, as said below
- w_qkv: bfloat16 [1024, 3072], replicated
- w_out: bfloat16 [1024, 1024], replicated, may hold values from -0.1875 to 0.1875
- readout_weight: bfloat16 [1024, 128], replicated, may hold values from -0.1875 to 0.1875
- target: float32 [8192, 128], P('cells'), may hold values from -6 to 6
Outputs:
- crps: float32 [8192, 128], P('cells', 'member')
- grads: float32 [1024, 4224], P(('member', 'cells'))
Inputs may be any that keep to these rules, and one draw needn't show every extreme that they name: counts[b] is the number of valid slots among slots b*256 to b*256 + 255, the valid ones first; at least one block is full.
All inputs are finite; a program needn't handle non-finite values.
Results may differ from a plain program's by a relative error of at most 0.018.
Values may be sent and summed in bfloat16 or wider, within the bound.
No kernel may reach another device: no remote copies, remote signals or barrier semaphores. Data moves between devices by JAX's collectives and lax.ppermute only.
A program may use at most 128 MiB of HBM per device.

v0:
```python
import functools

import jax
import jax.numpy as jnp
import numpy as np
from jax import lax
from jax.experimental import pallas as pl
from jax.experimental.pallas import tpu as pltpu
from jax.sharding import PartitionSpec as P

HEADS = 16
WIN = 256
BLOCK = 256
WIDTH = 256
HEAD_WIDTH = 64
PAIR = 128
NEVER = -1e30
VMEM_BYTES = 56 * 1024 * 1024

alpha_fair = 0.95
smooth_width = 0.0625

BF = jnp.bfloat16
F32 = jnp.float32


def smooth_abs(values):
    return jnp.sqrt(values * values + smooth_width)


def smooth_sign(values):
    return values * lax.rsqrt(values * values + smooth_width)


def layer_norm(latent_rows):
    values = latent_rows.astype(F32)
    center = values - jnp.mean(values, axis=-1, keepdims=True)
    spread = jnp.mean(center * center, axis=-1, keepdims=True)
    return (center * lax.rsqrt(spread + 1e-05)).astype(BF)


def dot_nn(left, right):
    return lax.dot_general(left, right, (((1,), (0,)), ((), ())), preferred_element_type=F32)


def dot_nt(left, right):
    return lax.dot_general(left, right, (((1,), (1,)), ((), ())), preferred_element_type=F32)


def dot_tn(left, right):
    return lax.dot_general(left, right, (((0,), (0,)), ((), ())), preferred_element_type=F32)


def iota(shape, axis):
    return lax.broadcasted_iota(jnp.int32, shape, axis)


def head_part(pair_rows, half, gain=None):
    chosen = (iota(pair_rows.shape, 1) // HEAD_WIDTH) == half
    if gain is not None:
        pair_rows = pair_rows * jnp.asarray(gain, pair_rows.dtype)
    return jnp.where(chosen, pair_rows, jnp.zeros_like(pair_rows))


def project_kernel(latent_ref, weight_ref, source_ref, projected_ref, ordered_ref, normed):
    step = pl.program_id(0)

    @pl.when(step == 0)
    def _():
        normed[...] = layer_norm(latent_ref[...])

    @pl.when(step < 6)
    def _():
        projected_ref[...] = dot_nn(normed[...], weight_ref[...]).astype(BF)

    @pl.when(step >= 6)
    def _():
        order = (iota((1024, 512), 0) == source_ref[...]).astype(BF)
        ordered_ref[...] = dot_nn(normed[...], order).astype(BF)


def project(latent_own, w_qkv, source):
    rows, width = latent_own.shape
    return pl.pallas_call(
        project_kernel,
        grid=(8,),
        in_specs=[
            pl.BlockSpec((rows, width), lambda j: (0, 0)),
            pl.BlockSpec((width, 512), lambda j: (0, jnp.minimum(j, 5))),
            pl.BlockSpec((1, 512), lambda j: (0, jnp.maximum(j - 6, 0))),
        ],
        out_specs=[
            pl.BlockSpec((rows, 512), lambda j: (0, jnp.minimum(j, 5))),
            pl.BlockSpec((rows, 512), lambda j: (0, jnp.maximum(j - 6, 0))),
        ],
        out_shape=[
            jax.ShapeDtypeStruct((rows, 3 * width), BF),
            jax.ShapeDtypeStruct((rows, width), BF),
        ],
        scratch_shapes=[pltpu.VMEM((rows, width), BF)],
        compiler_params=pltpu.CompilerParams(vmem_limit_bytes=VMEM_BYTES),
        cost_estimate=pl.CostEstimate(
            flops=2 * rows * width * width * 4, bytes_accessed=8 << 20, transcendentals=0
        ),
    )(latent_own, w_qkv, source)


def forward_bias(counts_ref):
    query = iota((BLOCK, WIN), 0)
    key = iota((BLOCK, WIN), 1)
    left = jnp.where((key >= query) & (key < counts_ref[0]), 0.0, NEVER).astype(F32)
    own = jnp.where(iota((1, BLOCK), 1) < counts_ref[1], 0.0, NEVER).astype(F32)
    right = jnp.where((key <= query) & (key < counts_ref[2]), 0.0, NEVER).astype(F32)
    return left, own, right


def forward_kernel(
    counts_ref,
    left_ref,
    right_ref,
    latent_ref,
    wk_ref,
    wv_ref,
    q_ref,
    k_ref,
    v_ref,
    w_out_ref,
    readout_ref,
    normed_ref,
    khalo_ref,
    vhalo_ref,
    attended_ref,
    stats_ref,
    hidden_ref,
    forecast_ref,
):
    step = pl.program_id(0)

    @pl.when(step == 0)
    def _():
        normed_ref[:WIN] = layer_norm(left_ref[...])
        normed_ref[WIN:] = layer_norm(right_ref[...])
        stats_ref[...] = jnp.zeros_like(stats_ref)

    khalo_ref[...] = dot_nn(normed_ref[...], wk_ref[...]).astype(BF)
    vhalo_ref[...] = dot_nn(normed_ref[...], wv_ref[...]).astype(BF)
    bias_left, bias_own, bias_right = forward_bias(counts_ref)
    lane = iota((BLOCK, 128), 1)
    stats = stats_ref[...]
    for pair in range(2):
        columns = slice(pair * PAIR, (pair + 1) * PAIR)
        q_pair = q_ref[:, columns]
        halves = []
        for half in range(2):
            q_head = head_part(q_pair, half, HEAD_WIDTH ** (-0.5))
            s_left = dot_nt(q_head, khalo_ref[:WIN, columns]) + bias_left
            s_own = dot_nt(q_head, k_ref[:, columns]) + bias_own
            s_right = dot_nt(q_head, khalo_ref[WIN:, columns]) + bias_right
            top = jnp.max(
                jnp.maximum(jnp.maximum(s_left, s_own), s_right), axis=-1, keepdims=True
            )
            e_left = jnp.exp(s_left - top)
            e_own = jnp.exp(s_own - top)
            e_right = jnp.exp(s_right - top)
            total = jnp.sum(e_left + e_own + e_right, axis=-1, keepdims=True)
            mixed = dot_nn(e_left.astype(BF), vhalo_ref[:WIN, columns])
            mixed += dot_nn(e_own.astype(BF), v_ref[:, columns])
            mixed += dot_nn(e_right.astype(BF), vhalo_ref[WIN:, columns])
            halves.append(mixed / total)
            head = step * 4 + pair * 2 + half
            stats = jnp.where(lane == head, top + jnp.log(total), stats)
        both = jnp.where(lane < HEAD_WIDTH, halves[0], halves[1])
        start = pl.multiple_of(step * WIDTH + pair * PAIR, PAIR)
        attended_ref[:, pl.ds(start, PAIR)] = both
    stats_ref[...] = stats

    @pl.when(step == 3)
    def _():
        mixed = dot_nn(attended_ref[...].astype(BF), w_out_ref[...])
        hidden = (latent_ref[...].astype(F32) + mixed).astype(BF)
        hidden_ref[...] = hidden
        forecast_ref[...] = dot_nn(hidden, readout_ref[...])


def forward(counts, left, right, latent_own, w_qkv, projected, w_out, readout_weight):
    whole = lambda *shape: pl.BlockSpec(shape, lambda j: (0, 0))
    part = lambda rows, first: pl.BlockSpec((rows, WIDTH), lambda j: (0, first + j))
    return pl.pallas_call(
        forward_kernel,
        grid=(4,),
        in_specs=[
            pl.BlockSpec(memory_space=pltpu.SMEM),
            whole(WIN, 1024),
            whole(WIN, 1024),
            whole(BLOCK, 1024),
            part(1024, 4),
            part(1024, 8),
            part(BLOCK, 0),
            part(BLOCK, 4),
            part(BLOCK, 8),
            whole(1024, 1024),
            whole(1024, 128),
        ],
        out_specs=[
            whole(2 * WIN, 1024),
            part(2 * WIN, 0),
            part(2 * WIN, 0),
            whole(BLOCK, 1024),
            whole(BLOCK, 128),
            whole(BLOCK, 1024),
            whole(BLOCK, 128),
        ],
        out_shape=[
            jax.ShapeDtypeStruct((2 * WIN, 1024), BF),
            jax.ShapeDtypeStruct((2 * WIN, 1024), BF),
            jax.ShapeDtypeStruct((2 * WIN, 1024), BF),
            jax.ShapeDtypeStruct((BLOCK, 1024), F32),
            jax.ShapeDtypeStruct((BLOCK, 128), F32),
            jax.ShapeDtypeStruct((BLOCK, 1024), BF),
            jax.ShapeDtypeStruct((BLOCK, 128), F32),
        ],
        compiler_params=pltpu.CompilerParams(vmem_limit_bytes=VMEM_BYTES),
        cost_estimate=pl.CostEstimate(
            flops=6 << 30, bytes_accessed=12 << 20, transcendentals=3 << 20
        ),
    )(
        counts,
        left,
        right,
        latent_own,
        w_qkv,
        w_qkv,
        projected,
        projected,
        projected,
        w_out,
        readout_weight,
    )


def score_kernel(
    counts_ref,
    forecasts_ref,
    target_ref,
    attended_ref,
    hidden_ref,
    stats_ref,
    w_out_ref,
    readout_ref,
    crps_ref,
    slope_ref,
    grad_ref,
    stats_out_ref,
    turned_ref,
    small_ref,
):
    members = 4
    fair_eps = (1.0 - alpha_fair) / members
    coefficient = (1.0 - fair_eps) / (members * (members - 1))
    valid = (iota((BLOCK, 1), 0) < counts_ref[1]).astype(F32)
    forecasts = [forecasts_ref[member] for member in range(members)]
    own = forecasts_ref[counts_ref[3]]
    target = target_ref[...]
    error = jnp.zeros_like(target)
    for forecast in forecasts:
        error += smooth_abs(forecast - target)
    spread = jnp.full_like(target, members * smooth_width**0.5)
    for first in range(members):
        for second in range(first + 1, members):
            spread += 2.0 * smooth_abs(forecasts[first] - forecasts[second])
    crps_ref[...] = valid * (error / members - 0.5 * coefficient * spread)
    pull = jnp.zeros_like(target)
    for other in forecasts:
        pull += smooth_sign(own - other)
    slope = (
        valid / 128 * (smooth_sign(own - target) / members - coefficient * pull)
    ).astype(BF)
    slope_ref[...] = slope
    dhidden = dot_nt(slope, readout_ref[...]).astype(BF)
    dattended = dot_nt(dhidden, w_out_ref[...]).astype(BF)
    grad_ref[...] = dattended
    attended = attended_ref[...]
    product = dattended.astype(F32) * attended
    high = product.astype(BF)
    low = (product - high.astype(F32)).astype(BF)
    pick = (iota((1024, 128), 0) // HEAD_WIDTH + HEADS == iota((1024, 128), 1)).astype(BF)
    stats = stats_ref[...] + dot_nn(high, pick) + dot_nn(low, pick)
    stats_out_ref[...] = stats
    turned_ref[...] = stats.T[: 2 * HEADS]
    small_ref[:, :128] = dot_tn(attended.astype(BF), slope).astype(BF)
    small_ref[:, 128:] = dot_tn(hidden_ref[...], slope).astype(BF)


def score(counts, forecasts, target, attended, hidden, stats, w_out, readout_weight):
    vmem = pl.BlockSpec(memory_space=pltpu.VMEM)
    return pl.pallas_call(
        score_kernel,
        in_specs=[pl.BlockSpec(memory_space=pltpu.SMEM)] + [vmem] * 7,
        out_specs=[vmem] * 6,
        out_shape=[
            jax.ShapeDtypeStruct((BLOCK, 128), F32),
            jax.ShapeDtypeStruct((BLOCK, 128), BF),
            jax.ShapeDtypeStruct((BLOCK, 1024), BF),
            jax.ShapeDtypeStruct((BLOCK, 128), F32),
            jax.ShapeDtypeStruct((2 * HEADS, BLOCK), F32),
            jax.ShapeDtypeStruct((1024, 256), BF),
        ],
        compiler_params=pltpu.CompilerParams(vmem_limit_bytes=VMEM_BYTES),
    )(counts, forecasts, target, attended, hidden, stats, w_out, readout_weight)


def query_kernel(
    counts_ref, q_ref, k_ref, v_ref, khalo_ref, vhalo_ref, grad_ref, stats_ref, dq_ref
):
    step = pl.program_id(0)
    bias_left, bias_own, bias_right = forward_bias(counts_ref)
    lane = iota((BLOCK, 128), 1)
    stats = stats_ref[...]
    for pair in range(2):
        columns = slice(pair * PAIR, (pair + 1) * PAIR)
        q_pair = q_ref[:, columns]
        g_pair = grad_ref[:, columns]
        blocks = [
            (khalo_ref[:WIN, columns], vhalo_ref[:WIN, columns], bias_left),
            (k_ref[:, columns], v_ref[:, columns], bias_own),
            (khalo_ref[WIN:, columns], vhalo_ref[WIN:, columns], bias_right),
        ]
        halves = []
        for half in range(2):
            head = step * 4 + pair * 2 + half
            q_head = head_part(q_pair, half, HEAD_WIDTH ** (-0.5))
            g_head = head_part(g_pair, half)
            level = jnp.sum(jnp.where(lane == head, stats, 0.0), axis=-1, keepdims=True)
            delta = jnp.sum(jnp.where(lane == head + HEADS, stats, 0.0), axis=-1, keepdims=True)
            total = jnp.zeros((BLOCK, PAIR), F32)
            for keys, values, bias in blocks:
                probs = jnp.exp(dot_nt(q_head, keys) + bias - level)
                dscore = (probs * (dot_nt(g_head, values) - delta)).astype(BF)
                total += dot_nn(dscore, keys)
            halves.append(total)
        both = jnp.where(lane < HEAD_WIDTH, halves[0], halves[1])
        dq_ref[:, columns] = (both * HEAD_WIDTH ** (-0.5)).astype(BF)


def query_grads(counts, projected, khalo, vhalo, grad, stats):
    part = lambda rows, first: pl.BlockSpec((rows, WIDTH), lambda j: (0, first + j))
    return pl.pallas_call(
        query_kernel,
        grid=(4,),
        in_specs=[
            pl.BlockSpec(memory_space=pltpu.SMEM),
            part(BLOCK, 0),
            part(BLOCK, 4),
            part(BLOCK, 8),
            part(2 * WIN, 0),
            part(2 * WIN, 0),
            part(BLOCK, 0),
            pl.BlockSpec((BLOCK, 128), lambda j: (0, 0)),
        ],
        out_specs=part(BLOCK, 0),
        out_shape=jax.ShapeDtypeStruct((BLOCK, 1024), BF),
        compiler_params=pltpu.CompilerParams(vmem_limit_bytes=VMEM_BYTES),
        cost_estimate=pl.CostEstimate(
            flops=6 << 30, bytes_accessed=5 << 20, transcendentals=3 << 20
        ),
    )(counts, projected, projected, projected, khalo, vhalo, grad, stats)


def key_kernel(
    first_step,
    counts_ref,
    q_ref,
    k_ref,
    v_ref,
    qhalo_ref,
    grad_ref,
    ghalo_ref,
    left_ref,
    own_ref,
    right_ref,
    dk_ref,
    dv_ref,
):
    step = pl.program_id(0) + first_step
    key = iota((BLOCK, WIN), 0)
    query = iota((BLOCK, WIN), 1)
    present = key < counts_ref[1]
    bias_left = jnp.where(present & (query >= key), 0.0, NEVER).astype(F32)
    bias_own = jnp.where(present, 0.0, NEVER).astype(F32)
    bias_right = jnp.where(present & (query <= key), 0.0, NEVER).astype(F32)
    for pair in range(2):
        columns = slice(pair * PAIR, (pair + 1) * PAIR)
        keys = k_ref[:, columns]
        values = v_ref[:, columns]
        blocks = [
            (qhalo_ref[:WIN, columns], ghalo_ref[:WIN, columns], left_ref, bias_left),
            (q_ref[:, columns], grad_ref[:, columns], own_ref, bias_own),
            (qhalo_ref[WIN:, columns], ghalo_ref[WIN:, columns], right_ref, bias_right),
        ]
        dk = jnp.zeros((BLOCK, PAIR), F32)
        dv = jnp.zeros((BLOCK, PAIR), F32)
        for half in range(2):
            head = step * 4 + pair * 2 + half
            for queries, grads, turned_ref, bias in blocks:
                q_head = head_part(queries, half, HEAD_WIDTH ** (-0.5))
                g_head = head_part(grads, half)
                level = turned_ref[pl.ds(head, 1), :]
                delta = turned_ref[pl.ds(head + HEADS, 1), :]
                probs = jnp.exp(dot_nt(keys, q_head) + bias - level)
                dscore = (probs * (dot_nt(values, g_head) - delta)).astype(BF)
                dv += dot_nn(probs.astype(BF), g_head)
                dk += dot_nn(dscore, q_head)
        dk_ref[:, columns] = dk.astype(BF)
        dv_ref[:, columns] = dv.astype(BF)


def key_grads(counts, projected, qhalo, grad, ghalo, turned, first_step, steps):
    part = lambda rows, first: pl.BlockSpec(
        (rows, WIDTH), lambda j: (0, first + first_step + j)
    )
    whole = pl.BlockSpec((2 * HEADS, BLOCK), lambda j: (0, 0))
    out = pl.BlockSpec((BLOCK, WIDTH), lambda j: (0, j))
    return pl.pallas_call(
        functools.partial(key_kernel, first_step),
        grid=(steps,),
        in_specs=[
            pl.BlockSpec(memory_space=pltpu.SMEM),
            part(BLOCK, 0),
            part(BLOCK, 4),
            part(BLOCK, 8),
            part(2 * WIN, 0),
            part(BLOCK, 0),
            part(2 * WIN, 0),
            whole,
            whole,
            whole,
        ],
        out_specs=[out, out],
        out_shape=[jax.ShapeDtypeStruct((BLOCK, WIDTH * steps), BF)] * 2,
        compiler_params=pltpu.CompilerParams(vmem_limit_bytes=VMEM_BYTES),
        cost_estimate=pl.CostEstimate(
            flops=(2 << 30) * steps, bytes_accessed=5 << 20, transcendentals=3 << 20
        ),
    )(counts, projected, projected, projected, qhalo, grad, ghalo, *turned)


AXES = ("x_hi", "core", "y", "x_lo", "z")
MEMBER = ("x_hi", "core")
CELLS = ("y", "x_lo", "z")
CHIPS = ("x_hi", "y", "x_lo", "z")


def row_source(core):
    place = jnp.arange(1024, dtype=jnp.int32)
    other, chip, row = place // 512, (place % 512) // 8, place % 8
    x_hi, block = chip // 32, chip % 32
    return (x_hi * 512 + (other ^ core) * 256 + block * 8 + row)[None]


def swap_core(values):
    return lax.ppermute(values, "core", [(0, 1), (1, 0)])


def scatter_sum(partial):
    columns = partial.shape[1]
    pieces = lax.all_to_all(
        partial.reshape(64, 8, columns), CHIPS, split_axis=0, concat_axis=0
    )
    return jnp.sum(pieces.astype(F32), axis=0)


def per_device(latent, counts, w_qkv, w_out, readout_weight, target):
    latent_own = latent[0]
    cell_count = 32
    cell_index = lax.axis_index(CELLS)
    member_index = lax.axis_index(MEMBER)
    core = lax.axis_index("core")
    up = [(i, i + 1) for i in range(cell_count - 1)]
    down = [(i + 1, i) for i in range(cell_count - 1)]
    from_left = lax.ppermute(latent_own, CELLS, up)
    from_right = lax.ppermute(latent_own, CELLS, down)

    own_count = counts[cell_index]
    left_count = jnp.where(cell_index > 0, counts[jnp.maximum(cell_index - 1, 0)], 0)
    right_count = jnp.where(
        cell_index < cell_count - 1, counts[jnp.minimum(cell_index + 1, cell_count - 1)], 0
    )
    scalars = jnp.stack([left_count, own_count, right_count, member_index.astype(jnp.int32)])

    source = row_source(core)
    projected, ordered = project(latent_own, w_qkv, source)
    normed_pair = jnp.concatenate([ordered[:, :512], swap_core(ordered[:, 512:])], axis=0)
    normed_halo, khalo, vhalo, attended, stats, hidden, forecast = forward(
        scalars, from_left, from_right, latent_own, w_qkv, projected, w_out, readout_weight
    )
    forecasts = lax.all_gather(forecast, MEMBER, axis=0, tiled=False)
    qhalo = dot_nn(normed_halo, w_qkv[:, :1024]).astype(BF)
    crps_whole, slope, grad, stats, turned, small = score(
        scalars, forecasts, target, attended, hidden, stats, w_out, readout_weight
    )
    crps = lax.dynamic_slice_in_dim(crps_whole, member_index * 32, 32, 1)
    packed = jnp.concatenate([slope.astype(F32), turned.reshape(64, 128)], axis=0)
    packed_left = lax.ppermute(packed, CELLS, up)
    packed_right = lax.ppermute(packed, CELLS, down)

    dquery = query_grads(scalars, projected, khalo, vhalo, grad, stats)

    slope_halo = jnp.concatenate([packed_left[:BLOCK], packed_right[:BLOCK]], axis=0).astype(BF)
    dhidden_halo = dot_nt(slope_halo, readout_weight).astype(BF)
    ghalo = dot_nt(dhidden_halo, w_out).astype(BF)
    turned_left = packed_left[BLOCK:].reshape(2 * HEADS, BLOCK)
    turned_right = packed_right[BLOCK:].reshape(2 * HEADS, BLOCK)

    def partial_of(piece):
        paired = jnp.concatenate([piece, swap_core(piece)], axis=0)
        return dot_tn(normed_pair, paired).astype(BF)

    small = dot_tn((jnp.arange(1024)[:, None] == source).astype(BF), small).astype(BF)
    small = (small[:512].astype(F32) + swap_core(small[512:]).astype(F32)).astype(BF)
    first = scatter_sum(jnp.concatenate([partial_of(dquery), small], axis=1))
    dkey, dvalue = key_grads(
        scalars, projected, qhalo, grad, ghalo, (turned_left, turned, turned_right), 0, 4
    )
    second = scatter_sum(partial_of(jnp.concatenate([dkey, dvalue], axis=1)))
    grad_out = lax.dot_general(
        first[:, 1024:1152],
        readout_weight.astype(F32),
        (((1,), (1,)), ((), ())),
        precision=lax.Precision.HIGHEST,
        preferred_element_type=F32,
    )
    grads = jnp.concatenate([first[:, :1024], second, grad_out, first[:, 1152:]], axis=1)
    return (crps, grads)


def solution(mesh):
    fine = jax.sharding.Mesh(mesh.devices.reshape(2, 2, 4, 2, 4), AXES)
    placed = (P(MEMBER, CELLS, None), P(), P(), P(), P(), P(CELLS, None))
    return jax.shard_map(
        per_device,
        mesh=fine,
        in_specs=placed,
        out_specs=(P(CELLS, MEMBER), P(MEMBER + CELLS, None)),
        check_vma=False,
    )
```

profile of v0, /device:TPU:0, one launch (start us, length us, event | category | flops | bytes accessed | tf_op | source)
XLA Modules:
  0.0 175.0 jit_solution(9659012914669649027)
XLA Ops:
  0.6 3.9 %collective-permute-start = (bf16[256,1024]{1,0:T(8,128)(2,1)}, bf16[256,1024]{1,0:T(8,128)(2,1)S(1)}, u32[]{:S(2)}, u32[]{:S(2)}) collective-permute-start(bf16[256,1024]{1,0:T(8,128)(2,1)} %bitcast.17), channel_id=1, source_target_pairs={{0,1},{1,2},{2,3},{3,4},{4,5},{5,6},{6,7},{7,8},{8,9},{9,10},{10,1... | collective-permute-start | bytes 1572872 | tf_op jit(solution)/shard_map/ppermute | solution.py:480
  4.6 1.3 collective-permute-start.1
  6.5 8.5 %shard_map.77 = (bf16[256,3072]{1,0:T(8,128)(2,1)}, bf16[256,1024]{1,0:T(8,128)(2,1)}) custom-call(bf16[256,1024]{1,0:T(8,128)(2,1)} %bitcast.19, bf16[1024,3072]{1,0:T(8,128)(2,1)} %wv_ref.1, s32[1,1024]{1,0:T(1,128)} %fusion.21.source_ref), custom_call_target="tpu_custom_call" | custom-call | flops 2147483648 | bytes 8388608 | tf_op jit(solution)/shard_map/pallas_call | solution.py:84
  15.0 1.9 %fusion.55 = (bf16[256,512]{1,0:T(8,128)(2,1)}, bf16[256,512]{1,0:T(8,128)(2,1)}) fusion(bf16[256,1024]{1,0:T(8,128)(2,1)} %get-tuple-element.25), kind=kLoop, calls=%fused_computation.99 | loop fusion | bytes 1048576 | tf_op jit(solution)/shard_map/slice | solution.py:492
  18.9 1.2 pad_add_fusion.counts_ref
  21.1 16.0 %shard_map.78 = (bf16[512,1024]{1,0:T(8,128)(2,1)}, bf16[512,1024]{1,0:T(8,128)(2,1)}, bf16[512,1024]{1,0:T(8,128)(2,1)}, f32[256,1024]{1,0:T(8,128)}, f32[256,1...) custom-call(s32[4]{0:T(128)} %pad_add_fusion.counts_ref, bf16[256,1024]{1,0:T(8,128)(2,1)} %copy-done.8, ...), custom_call_target="tpu_custom_call" | custom-call | flops 6442450944 | bytes 12582912 | tf_op jit(solution)/shard_map/pallas_call | solution.py:188
  37.1 10.9 %all-gather = f32[1024,128]{1,0:T(8,128)} all-gather(f32[256,128]{1,0:T(8,128)} %get-tuple-element.20), channel_id=2, replica_groups=mesh['x_hi'=2,'core'=2,'y'=4,'x_lo'=2,'z'=4] {'x_hi','core'}, dimensions={0}, use_global_device_ids=true | all-gather | bytes 655360 | tf_op jit(solution)/shard_map/all_gather | solution.py:496
  48.0 5.2 %shard_map.79 = (f32[256,128]{1,0:T(8,128)}, bf16[256,128]{1,0:T(8,128)(2,1)}, bf16[256,1024]{1,0:T(8,128)(2,1)}, f32[256,128]{1,0:T(8,128)}, f32[32,256]{1,0:T(8,128)}, /*index=5*/bf16[1024,256]{1,0:T(8,128)(2,1)}) custom-call(s32[4]{0:T(128)} %pad_add_fusion.counts_ref, f32[4,256,128]{2,1,0:T(8,128)} %bitcast.16, f32[256,128]{1,0:T(8,128)} %target_ref.1, ...), custom_call_target="tpu_custom_call" | custom-call | tf_op jit(solution)/shard_map/pallas_call | solution.py:296
  55.5 1.3 collective-permute-start.6
  56.8 5.2 %collective-permute-start.5 = (f32[320,128]{1,0:T(8,128)}, f32[320,128]{1,0:T(8,128)S(1)}, u32[]{:S(2)}, u32[]{:S(2)}) collective-permute-start(f32[320,128]{1,0:T(8,128)} %pad_maximum_fusion.3), channel_id=1, source_target_pairs={{0,1},{1,2},{2,3},{3,4},{4,5},{5,6},{6,7},{7,8},{8,9},{9,10},{10,1... | collective-permute-start | bytes 491528 | tf_op jit(solution)/shard_map/ppermute | solution.py:503
  61.9 2.3 %fusion.11 = bf16[1024,256]{1,0:T(8,128)(2,1)S(1)} fusion(bf16[1024,256]{1,0:T(8,128)(2,1)} %get-tuple-element.30, s32[1024]{0:T(1024)S(1)} %fusion.26), kind=kOutput, calls=%fused_computation.17 | convolution fusion | flops 538181632 | bytes 1052672 | tf_op jit(solution)/shard_map/dot_general | solution.py:51
  64.4 10.7 %shard_map.80 = bf16[256,1024]{1,0:T(8,128)(2,1)} custom-call(s32[4]{0:T(128)} %pad_add_fusion.counts_ref, bf16[256,3072]{1,0:T(8,128)(2,1)} %get-tuple-element.19.q_ref.k_ref.v_ref, bf16[256,3072]{1,0:T(8,128)(2,1)} %get-tuple-element.19.q_ref.k_ref.v_ref, bf16[256,3072]{1,0:T(8,128)(2,1)} %get-tuple-element.19.q_ref.k_ref.v_ref, ...), custom_call_target="tpu_custom_call" | custom-call | flops 6442450944 | bytes 5242880 | tf_op jit(solution)/shard_map/pallas_call | solution.py:347
  75.6 4.0 %fusion.8.qhalo_ref = bf16[512,1024]{1,0:T(8,128)(2,1)} fusion(bf16[512,1024]{1,0:T(8,128)(2,1)S(1)} %copy-done.11, bf16[1024,3072]{1,0:T(8,128)(2,1)} %wv_ref.1), kind=kOutput, calls=%fused_computation.13 | convolution fusion | flops 1074266112 | bytes 4194304 | tf_op jit(solution)/shard_map/dot_general | solution.py:43
  84.1 2.5 %convolution_convert_fusion.2.ghalo_ref = bf16[512,1024]{1,0:T(8,128)(2,1)} fusion(bf16[1024,1024]{1,0:T(8,128)(2,1)S(1)} %copy-done, bf16[1024,128]{1,0:T(8,128)(2,1)S(1)} %copy-done.1, bf16[256,128]{1,0:T(8,128)(2,1)S(1)} %slice.68, bf16[256,128]{1,0:T(8,128)(2,1)S(1)} %slice.69), kind=kOutput, calls=%fused_computation.14 | convolution fusion | flops 1209270272 | bytes 3538944 | tf_op jit(solution)/shard_map/dot_general | solution.py:47
  86.6 13.0 %shard_map.81 = (bf16[256,1024]{1,0:T(8,128)(2,1)}, bf16[256,1024]{1,0:T(8,128)(2,1)}) custom-call(s32[4]{0:T(128)} %pad_add_fusion.counts_ref, bf16[256,3072]{1,0:T(8,128)(2,1)} %get-tuple-element.19.q_ref.k_ref.v_ref, bf16[256,3072]{1,0:T(8,128)(2,1)} %get-tuple-element.19.q_ref.k_ref.v_ref, bf16[256,3072]{1,0:T(8,128)(2,1)} %get-tuple-element.19.q_ref.k_ref.v_ref, ...), custom_call_target="tpu_custom_call" | custom-call | flops 8589934592 | bytes 5242880 | tf_op jit(solution)/shard_map/pallas_call | solution.py:423
  99.6 1.9 %constant_dynamic-update-slice_fusion.1 = bf16[256,2048]{1,0:T(8,128)(2,1)} fusion(bf16[256,1024]{1,0:T(8,128)(2,1)} %get-tuple-element.34), kind=kLoop, calls=%fused_computation.43 | loop fusion | bytes 1048576
  101.6 1.9 %convolution_convert_fusion.3 = bf16[512,1024]{1,0:T(8,128)(2,1)S(1)} fusion(bf16[256,1024]{1,0:T(8,128)(2,1)} %collective-permute-done.3, bf16[256,1024]{1,0:T(8,128)(2,1)S(1)} %copy-done.10, bf16[256,512]{1,0:T(8,128)(2,1)} %collective-permute-done.2, bf16[256,512]{1,0:T(8,128)(2,1)S(1)} %copy-done.4), kind=kOutput, calls=%fused_computation.15 | convolution fusion | flops 540540928 | bytes 2621440 | tf_op jit(solution)/shard_map/dot_general | solution.py:51
  104.6 13.0 %all-to-all-start = ((bf16[64,8,1280]{2,1,0:T(8,128)(2,1)}), bf16[64,8,1280]{2,1,0:T(8,128)(2,1)S(1)}, u32[]{:S(2)}, u32[]{:S(2)}) async-start(bf16[64,8,1280]{2,1,0:T(8,128)(2,1)} %maximum_bitcast_fusion), calls=%async_computation | async-start | bytes 2621440 | tf_op jit(solution)/shard_map/all_to_all | solution.py:466
  117.8 2.6 %collective-permute-done.7 = bf16[256,2048]{1,0:T(8,128)(2,1)S(1)} collective-permute-done((bf16[256,2048]{1,0:T(8,128)(2,1)S(1)}, bf16[256,2048]{1,0:T(8,128)(2,1)S(1)}, u32[]{:S(2)}, u32[]{:S(2)}) %collective-permute-start.7) | collective-permute-done | bytes 1048608 | tf_op jit(solution)/shard_map/ppermute | solution.py:461
  120.5 3.6 %fusion.1 = bf16[64,8,2048]{2,1,0:T(8,128)(2,1)} fusion(bf16[256,2048]{1,0:T(8,128)(2,1)S(1)} %collective-permute-done.7, bf16[256,2048]{1,0:T(8,128)(2,1)S(1)} %constant_dynamic-update-slice_fusion, bf16[256,512]{1,0:T(8,128)(2,1)} %collective-permute-done.2, bf16[256,512]{1,0:T(8,128)(2,1)S(1)} %copy-done.5), kind=kOutput, calls=%fused_computation.4 | convolution fusion | flops 1080033280 | bytes 4718592 | tf_op jit(solution)/shard_map/dot_general | solution.py:51
  124.0 15.3 %all-to-all-done = bf16[64,8,1280]{2,1,0:T(8,128)(2,1)S(1)} async-done(((bf16[64,8,1280]{2,1,0:T(8,128)(2,1)}), bf16[64,8,1280]{2,1,0:T(8,128)(2,1)S(1)}, u32[]{:S(2)}, u32[]{:S(2)}) %all-to-all-start) | async-done | bytes 1310752 | tf_op jit(solution)/shard_map/all_to_all | solution.py:466
  139.3 5.5 %all-to-all-start.1 = ((bf16[64,8,2048]{2,1,0:T(8,128)(2,1)}), bf16[64,8,2048]{2,1,0:T(8,128)(2,1)S(1)}, u32[]{:S(2)}, u32[]{:S(2)}) async-start(bf16[64,8,2048]{2,1,0:T(8,128)(2,1)} %fusion.1), calls=%async_computation.1 | async-start | bytes 4194304 | tf_op jit(solution)/shard_map/all_to_all | solution.py:466
  146.7 1.3 fusion.36
  148.0 26.0 %all-to-all-done.1 = bf16[64,8,2048]{2,1,0:T(8,128)(2,1)S(1)} async-done(((bf16[64,8,2048]{2,1,0:T(8,128)(2,1)}), bf16[64,8,2048]{2,1,0:T(8,128)(2,1)S(1)}, u32[]{:S(2)}, u32[]{:S(2)}) %all-to-all-start.1) | async-done | bytes 2097184 | tf_op jit(solution)/shard_map/all_to_all | solution.py:466
  (58 shorter events, 13.9 us)
Async XLA Ops:
  0.6 19.5 %collective-permute-start = (bf16[256,1024]{1,0:T(8,128)(2,1)}, bf16[256,1024]{1,0:T(8,128)(2,1)S(1)}, u32[]{:S(2)}, u32[]{:S(2)}) collective-permute-start(bf16[256,1024]{1,0:T(8,128)(2,1)} %bitcast.17), channel_id=1, source_target_pairs={{0,1},{1,2},{2,3},{3,4},{4,5},{5,6},{6,7},{7,8},{8,9},{9,10},{10,1... | collective-permute-start | bytes 1572872 | tf_op jit(solution)/shard_map/ppermute | solution.py:480
  4.6 15.6 %collective-permute-start.1 = (bf16[256,1024]{1,0:T(8,128)(2,1)}, bf16[256,1024]{1,0:T(8,128)(2,1)S(1)}, u32[]{:S(2)}, u32[]{:S(2)}) collective-permute-start(bf16[256,1024]{1,0:T(8,128)(2,1)} %bitcast.18), channel_id=1, source_target_pairs={{1,0},{2,1},{3,2},{4,3},{5,4},{6,5},{7,6},{8,7},{9,8},{10,9},{11,1... | collective-permute-start | bytes 1572872 | tf_op jit(solution)/shard_map/ppermute | solution.py:481
  6.5 10.5 %copy-start.7 = (s32[32]{0:T(128)S(1)}, s32[32]{0:T(128)}, u32[]{:S(2)}) copy-start(s32[32]{0:T(128)} %param.7) | copy-start | bytes 388
  17.0 84.6 %collective-permute-start.2 = (bf16[256,512]{1,0:T(8,128)(2,1)}, bf16[256,512]{1,0:T(8,128)(2,1)}, u32[]{:S(2)}, u32[]{:S(2)}) collective-permute-start(bf16[256,512]{1,0:T(8,128)(2,1)} %get-tuple-element.39), channel_id=1, source_target_pairs={{0,32},{32,0},{1,33},{33,1},{2,34},{34,2},{3,35},{35,3},{4,36},{36... | collective-permute-start | bytes 786440 | tf_op jit(solution)/shard_map/ppermute | solution.py:461
  20.1 0.8 copy-start.8
  20.2 0.9 copy-start.9
  55.5 25.4 %collective-permute-start.6 = (f32[320,128]{1,0:T(8,128)}, f32[320,128]{1,0:T(8,128)}, u32[]{:S(2)}, u32[]{:S(2)}) collective-permute-start(f32[320,128]{1,0:T(8,128)} %pad_maximum_fusion.3), channel_id=1, source_target_pairs={{1,0},{2,1},{3,2},{4,3},{5,4},{6,5},{7,6},{8,7},{9,8},{10,9},{11,1... | collective-permute-start | bytes 491528 | tf_op jit(solution)/shard_map/ppermute | solution.py:504
  56.8 22.8 %collective-permute-start.5 = (f32[320,128]{1,0:T(8,128)}, f32[320,128]{1,0:T(8,128)S(1)}, u32[]{:S(2)}, u32[]{:S(2)}) collective-permute-start(f32[320,128]{1,0:T(8,128)} %pad_maximum_fusion.3), channel_id=1, source_target_pairs={{0,1},{1,2},{2,3},{3,4},{4,5},{5,6},{6,7},{7,8},{8,9},{9,10},{10,1... | collective-permute-start | bytes 491528 | tf_op jit(solution)/shard_map/ppermute | solution.py:503
  64.3 37.2 %collective-permute-start.4 = (bf16[512,256]{1,0:T(8,128)(2,1)S(1)}, bf16[512,256]{1,0:T(8,128)(2,1)S(1)}, u32[]{:S(2)}, u32[]{:S(2)}) collective-permute-start(bf16[512,256]{1,0:T(8,128)(2,1)S(1)} %slice.51), channel_id=1, source_target_pairs={{0,32},{32,0},{1,33},{33,1},{2,34},{34,2},{3,35},{35,3},{4,36},{36... | collective-permute-start | bytes 786440 | tf_op jit(solution)/shard_map/ppermute | solution.py:461
  64.4 11.1 %copy-start.11 = (bf16[512,1024]{1,0:T(8,128)(2,1)S(1)}, bf16[512,1024]{1,0:T(8,128)(2,1)}, u32[]{:S(2)}) copy-start(bf16[512,1024]{1,0:T(8,128)(2,1)} %get-tuple-element.31) | copy-start | bytes 3145732
  75.1 26.4 %collective-permute-start.3 = (bf16[256,1024]{1,0:T(8,128)(2,1)}, bf16[256,1024]{1,0:T(8,128)(2,1)}, u32[]{:S(2)}, u32[]{:S(2)}) collective-permute-start(bf16[256,1024]{1,0:T(8,128)(2,1)} %shard_map.80), channel_id=1, source_target_pairs={{0,32},{32,0},{1,33},{33,1},{2,34},{34,2},{3,35},{35,3},{4,36},{36... | collective-permute-start | bytes 1572872 | tf_op jit(solution)/shard_map/ppermute | solution.py:461
  75.6 8.5 %copy-start = (bf16[1024,1024]{1,0:T(8,128)(2,1)S(1)}, bf16[1024,1024]{1,0:T(8,128)(2,1)}, u32[]{:S(2)}) copy-start(bf16[1024,1024]{1,0:T(8,128)(2,1)} %w_out_ref.3) | copy-start | bytes 6291460
  75.6 8.5 %copy-start.1 = (bf16[1024,128]{1,0:T(8,128)(2,1)S(1)}, bf16[1024,128]{1,0:T(8,128)(2,1)}, u32[]{:S(2)}) copy-start(bf16[1024,128]{1,0:T(8,128)(2,1)} %readout_ref.3) | copy-start | bytes 786436
  79.6 0.7 copy-start.6
  86.6 15.0 %copy-start.4 = (bf16[256,512]{1,0:T(8,128)(2,1)S(1)}, bf16[256,512]{1,0:T(8,128)(2,1)}, u32[]{:S(2)}) copy-start(bf16[256,512]{1,0:T(8,128)(2,1)} %get-tuple-element.38) | copy-start | bytes 786436
  86.6 15.0 %copy-start.10 = (bf16[256,1024]{1,0:T(8,128)(2,1)S(1)}, bf16[256,1024]{1,0:T(8,128)(2,1)}, u32[]{:S(2)}) copy-start(bf16[256,1024]{1,0:T(8,128)(2,1)} %shard_map.80) | copy-start | bytes 1572868
  103.4 14.2 %copy-start.2 = (bf16[256,1024]{1,0:T(8,128)(2,1)S(1)}, bf16[256,1024]{1,0:T(8,128)(2,1)}, u32[]{:S(2)}) copy-start(bf16[256,1024]{1,0:T(8,128)(2,1)} %get-tuple-element.35) | copy-start | bytes 1572868
  103.4 14.2 %copy-start.3 = (bf16[256,2048]{1,0:T(8,128)(2,1)S(1)}, bf16[256,2048]{1,0:T(8,128)(2,1)}, u32[]{:S(2)}) copy-start(bf16[256,2048]{1,0:T(8,128)(2,1)} %constant_dynamic-update-slice_fusion.1) | copy-start | bytes 3145732
  104.6 15.9 %copy-start.5 = (bf16[256,512]{1,0:T(8,128)(2,1)S(1)}, bf16[256,512]{1,0:T(8,128)(2,1)}, u32[]{:S(2)}) copy-start(bf16[256,512]{1,0:T(8,128)(2,1)} %get-tuple-element.38) | copy-start | bytes 786436
  104.6 34.7 %all-to-all-start = ((bf16[64,8,1280]{2,1,0:T(8,128)(2,1)}), bf16[64,8,1280]{2,1,0:T(8,128)(2,1)S(1)}, u32[]{:S(2)}, u32[]{:S(2)}) async-start(bf16[64,8,1280]{2,1,0:T(8,128)(2,1)} %maximum_bitcast_fusion), calls=%async_computation | async-start | bytes 2621440 | tf_op jit(solution)/shard_map/all_to_all | solution.py:466
  117.7 2.7 %collective-permute-start.7 = (bf16[256,2048]{1,0:T(8,128)(2,1)S(1)}, bf16[256,2048]{1,0:T(8,128)(2,1)S(1)}, u32[]{:S(2)}, u32[]{:S(2)}) collective-permute-start(bf16[256,2048]{1,0:T(8,128)(2,1)S(1)} %constant_dynamic-update-slice_fusion), channel_id=1, source_target_pairs={{0,32},{32,0},{1,33},{33,1},{2,34},{34,2},{3,35},{35,3},{4,36},{36... | collective-permute-start | bytes 3145736 | tf_op jit(solution)/shard_map/ppermute | solution.py:461
  139.3 34.7 %all-to-all-start.1 = ((bf16[64,8,2048]{2,1,0:T(8,128)(2,1)}), bf16[64,8,2048]{2,1,0:T(8,128)(2,1)S(1)}, u32[]{:S(2)}, u32[]{:S(2)}) async-start(bf16[64,8,2048]{2,1,0:T(8,128)(2,1)} %fusion.1), calls=%async_computation.1 | async-start | bytes 4194304 | tf_op jit(solution)/shard_map/all_to_all | solution.py:466
where the time goes:
time: 176 us; the launch traced here: 175 us
  Pallas kernels  53.4 us (30%)
  waiting for transfers between devices  44.1 us (25%)
  starting transfers between devices  30.9 us (18%)
  matrix products  15.5 us (9%)
  local copies, waits for them, and re-layouts  12.3 us (7%)
  blocking collectives  10.9 us (6%)
  other arithmetic  5.79 us (3%)
  between operations  2.17 us (1%)
    all_to_all x2, waiting for transfers between devices, scatter_sum(): lax.all_to_all(partial.reshape(64, 8, columns), CHIPS, split_axis=0, conc...  41.3 us
    all_to_all x2, starting transfers between devices, scatter_sum(): lax.all_to_all(partial.reshape(64, 8, columns), CHIPS, split_axis=0, conc...  18.5 us
    pallas_call x1, Pallas kernels, forward(): pl.pallas_call(forward_kernel, grid=(4,), in_specs=[pl.BlockSpec(memory_s...  16 us
    pallas_call x1, Pallas kernels, key_grads(): pl.pallas_call(functools.partial(key_kernel, first_step), grid=(steps,),...  13 us
    all_gather x1, blocking collectives, per_device(): forecasts = lax.all_gather(forecast, MEMBER, axis=0, tiled=False)  10.9 us
    pallas_call x1, Pallas kernels, query_grads(): pl.pallas_call(query_kernel, grid=(4,), in_specs=[pl.BlockSpec(memory_spa...  10.7 us
    pallas_call x1, Pallas kernels, project(): pl.pallas_call(project_kernel, grid=(8,), in_specs=[pl.BlockSpec((rows, w...  8.53 us
    dot_general x3, matrix products, dot_tn(): lax.dot_general(left, right, (((0,), (0,)), ((), ())), preferred_element_...  7.74 us
  transfers between devices with their start and end apart: 10, of which 4 were waited for; matrix products, arithmetic and copies ran while one was open for 16% of the time, Pallas kernels for 30%

commit v1 on v0

v1 whole, which is shorter than its diff:
```python
import functools

import jax
import jax.numpy as jnp
import numpy as np
from jax import lax
from jax.experimental import pallas as pl
from jax.experimental.pallas import tpu as pltpu
from jax.sharding import PartitionSpec as P

HEADS = 16
WIN = 256
BLOCK = 256
WIDTH = 256
HEAD_WIDTH = 64
PAIR = 128
NEVER = -1e30
VMEM_BYTES = 56 * 1024 * 1024

alpha_fair = 0.95
smooth_width = 0.0625

BF = jnp.bfloat16
F32 = jnp.float32


def smooth_abs(values):
    return jnp.sqrt(values * values + smooth_width)


def smooth_sign(values):
    return values * lax.rsqrt(values * values + smooth_width)


def layer_norm(latent_rows):
    values = latent_rows.astype(F32)
    center = values - jnp.mean(values, axis=-1, keepdims=True)
    spread = jnp.mean(center * center, axis=-1, keepdims=True)
    return (center * lax.rsqrt(spread + 1e-05)).astype(BF)


def dot_nn(left, right):
    return lax.dot_general(left, right, (((1,), (0,)), ((), ())), preferred_element_type=F32)


def dot_nt(left, right):
    return lax.dot_general(left, right, (((1,), (1,)), ((), ())), preferred_element_type=F32)


def dot_tn(left, right):
    return lax.dot_general(left, right, (((0,), (0,)), ((), ())), preferred_element_type=F32)


def iota(shape, axis):
    return lax.broadcasted_iota(jnp.int32, shape, axis)


def project_kernel(latent_ref, weight_ref, projected_ref, turned_ref, normed):
    step = pl.program_id(0)

    @pl.when(step == 0)
    def _():
        normed[...] = layer_norm(latent_ref[...])

    projected_ref[...] = dot_nn(normed[...], weight_ref[...]).astype(BF)

    @pl.when(step == 5)
    def _():
        turned_ref[...] = normed[...].T


def project(latent_own, w_qkv):
    rows, width = latent_own.shape
    return pl.pallas_call(
        project_kernel,
        grid=(6,),
        in_specs=[
            pl.BlockSpec((rows, width), lambda j: (0, 0)),
            pl.BlockSpec((width, 512), lambda j: (0, j)),
        ],
        out_specs=[
            pl.BlockSpec((rows, 512), lambda j: (0, j)),
            pl.BlockSpec((width, rows), lambda j: (0, 0)),
        ],
        out_shape=[
            jax.ShapeDtypeStruct((rows, 3 * width), BF),
            jax.ShapeDtypeStruct((width, rows), BF),
        ],
        scratch_shapes=[pltpu.VMEM((rows, width), BF)],
        compiler_params=pltpu.CompilerParams(vmem_limit_bytes=VMEM_BYTES),
        cost_estimate=pl.CostEstimate(
            flops=2 * rows * width * width * 4, bytes_accessed=8 << 20, transcendentals=0
        ),
    )(latent_own, w_qkv)


def spare_lane(shape):
    lane = iota(shape, len(shape) - 1)
    return lane % HEAD_WIDTH


def key_fill(count_pieces):
    fills = []
    for count, rows in count_pieces:
        spare = spare_lane((rows, PAIR))
        bias = jnp.where(iota((rows, PAIR), 0) < count, 0.0, NEVER)
        fills.append(
            jnp.where(spare < 3, 1.0, jnp.where(spare == 3, bias, 0.0)).astype(BF)
        )
    return jnp.concatenate(fills, axis=0)


def stat_spread(step, offset):
    shape = (128, WIDTH)
    lane = iota(shape, 1)
    head = step * 4 + 2 * (lane // PAIR) + jnp.where(lane % PAIR < HEAD_WIDTH, 1, 0)
    term = lane % HEAD_WIDTH
    chosen = (term < 3) & (iota(shape, 0) == term * 32 + offset + head)
    return jnp.where(chosen, -1.0, 0.0).astype(BF)


def keep_band(window, fill):
    shape = (128, 128)
    apart = iota(shape, 0) - iota(shape, 1)
    first = jnp.where(apart >= 0, window[:128], fill)
    last = jnp.where(apart <= 0, window[512:], fill)
    return first, window[128:512], last


def forward_kernel(
    counts_ref,
    left_ref,
    right_ref,
    latent_ref,
    wk_ref,
    wv_ref,
    q_ref,
    k_ref,
    v_ref,
    w_out_ref,
    readout_ref,
    normed_ref,
    kcat_ref,
    vcat_ref,
    attended_ref,
    stats_ref,
    hidden_ref,
    forecast_ref,
    probs,
    stat_rows,
):
    step = pl.program_id(0)

    @pl.when(step == 0)
    def _():
        normed_ref[:WIN] = layer_norm(left_ref[...])
        normed_ref[WIN:] = layer_norm(right_ref[...])
        probs[...] = jnp.zeros_like(probs)

    khalo = dot_nn(normed_ref[...], wk_ref[...]).astype(BF)
    kcat_ref[:WIN] = khalo[:WIN]
    kcat_ref[WIN : WIN + BLOCK] = k_ref[...]
    kcat_ref[WIN + BLOCK :] = khalo[WIN:]
    vhalo = dot_nn(normed_ref[...], wv_ref[...]).astype(BF)
    vcat_ref[:WIN] = vhalo[:WIN]
    vcat_ref[WIN : WIN + BLOCK] = v_ref[...]
    vcat_ref[WIN + BLOCK :] = vhalo[WIN:]
    fill = key_fill([(counts_ref[0], WIN), (counts_ref[1], BLOCK), (counts_ref[2], WIN)])
    low_q = iota((BLOCK, PAIR), 1) < HEAD_WIDTH
    low_k = iota(fill.shape, 1) < HEAD_WIDTH
    query_fill = (spare_lane((BLOCK, PAIR)) == 3).astype(BF)
    for pair in range(2):
        columns = slice(pair * PAIR, (pair + 1) * PAIR)
        q_pair = q_ref[:, columns] * jnp.asarray(HEAD_WIDTH ** (-0.5), BF)
        k_pair = kcat_ref[:, columns]
        v_turned = vcat_ref[:, columns].T
        halves = []
        for half in range(2):
            slot = pair * 2 + half
            if half == 0:
                q_head = jnp.where(low_q, q_pair, query_fill)
                k_head = jnp.where(low_k, k_pair, fill)
            else:
                q_head = jnp.where(low_q, query_fill, q_pair)
                k_head = jnp.where(low_k, fill, k_pair)
            scores = dot_nt(k_head, q_head)
            totals, levels = [], []
            for tile in range(2):
                rows = slice(tile * 128, tile * 128 + 640)
                lanes = slice(tile * 128, tile * 128 + 128)
                first, middle, last = keep_band(scores[rows, lanes], NEVER)
                top = jnp.maximum(
                    jnp.max(middle, axis=0, keepdims=True),
                    jnp.max(jnp.maximum(first, last), axis=0, keepdims=True),
                )
                first = jnp.exp(first - top)
                middle = jnp.exp(middle - top)
                last = jnp.exp(last - top)
                total = jnp.sum(middle, axis=0, keepdims=True) + jnp.sum(
                    first + last, axis=0, keepdims=True
                )
                start = tile * 128
                probs[slot, start : start + 128, lanes] = first.astype(BF)
                probs[slot, start + 128 : start + 512, lanes] = middle.astype(BF)
                probs[slot, start + 512 : start + 640, lanes] = last.astype(BF)
                totals.append(total)
                levels.append(top + jnp.log(total))
            total = jnp.concatenate(totals, axis=1)
            mixed = dot_nn(
                v_turned[half * HEAD_WIDTH : (half + 1) * HEAD_WIDTH], probs[slot]
            )
            halves.append(mixed * (1.0 / total))
            stat_rows[pl.ds(step * 4 + slot, 1), :] = jnp.concatenate(levels, axis=1)
        both = jnp.concatenate(halves, axis=0).T
        start = pl.multiple_of(step * WIDTH + pair * PAIR, PAIR)
        attended_ref[:, pl.ds(start, PAIR)] = both

    @pl.when(step == 3)
    def _():
        mixed = dot_nn(attended_ref[...].astype(BF), w_out_ref[...])
        hidden = (latent_ref[...].astype(F32) + mixed).astype(BF)
        hidden_ref[...] = hidden
        forecast_ref[...] = dot_nn(hidden, readout_ref[...])
        stat_rows[HEADS:] = jnp.zeros((128 - HEADS, BLOCK), F32)
        stats_ref[...] = stat_rows[...].T


def forward(counts, left, right, latent_own, w_qkv, projected, w_out, readout_weight):
    whole = lambda *shape: pl.BlockSpec(shape, lambda j: (0, 0))
    part = lambda rows, first: pl.BlockSpec((rows, WIDTH), lambda j: (0, first + j))
    window = 2 * WIN + BLOCK
    return pl.pallas_call(
        forward_kernel,
        grid=(4,),
        in_specs=[
            pl.BlockSpec(memory_space=pltpu.SMEM),
            whole(WIN, 1024),
            whole(WIN, 1024),
            whole(BLOCK, 1024),
            part(1024, 4),
            part(1024, 8),
            part(BLOCK, 0),
            part(BLOCK, 4),
            part(BLOCK, 8),
            whole(1024, 1024),
            whole(1024, 128),
        ],
        out_specs=[
            whole(2 * WIN, 1024),
            part(window, 0),
            part(window, 0),
            whole(BLOCK, 1024),
            whole(BLOCK, 128),
            whole(BLOCK, 1024),
            whole(BLOCK, 128),
        ],
        out_shape=[
            jax.ShapeDtypeStruct((2 * WIN, 1024), BF),
            jax.ShapeDtypeStruct((window, 1024), BF),
            jax.ShapeDtypeStruct((window, 1024), BF),
            jax.ShapeDtypeStruct((BLOCK, 1024), F32),
            jax.ShapeDtypeStruct((BLOCK, 128), F32),
            jax.ShapeDtypeStruct((BLOCK, 1024), BF),
            jax.ShapeDtypeStruct((BLOCK, 128), F32),
        ],
        scratch_shapes=[pltpu.VMEM((4, window, BLOCK), BF), pltpu.VMEM((128, BLOCK), F32)],
        compiler_params=pltpu.CompilerParams(vmem_limit_bytes=VMEM_BYTES),
        cost_estimate=pl.CostEstimate(
            flops=6 << 30, bytes_accessed=12 << 20, transcendentals=3 << 20
        ),
    )(
        counts,
        left,
        right,
        latent_own,
        w_qkv,
        w_qkv,
        projected,
        projected,
        projected,
        w_out,
        readout_weight,
    )


def score_kernel(
    counts_ref,
    own_ref,
    near_ref,
    others_ref,
    target_ref,
    attended_ref,
    hidden_ref,
    stats_ref,
    w_out_ref,
    readout_ref,
    crps_ref,
    packed_ref,
    grad_ref,
    small_ref,
):
    members = 4
    fair_eps = (1.0 - alpha_fair) / members
    coefficient = (1.0 - fair_eps) / (members * (members - 1))
    valid = (iota((BLOCK, 1), 0) < counts_ref[1]).astype(F32)
    own = own_ref[...]
    forecasts = [own, near_ref[...], others_ref[0], others_ref[1]]
    target = target_ref[...]
    error = jnp.zeros_like(target)
    for forecast in forecasts:
        error += smooth_abs(forecast - target)
    spread = jnp.full_like(target, members * smooth_width**0.5)
    for first in range(members):
        for second in range(first + 1, members):
            spread += 2.0 * smooth_abs(forecasts[first] - forecasts[second])
    crps_ref[...] = valid * (error / members - 0.5 * coefficient * spread)
    pull = jnp.zeros_like(target)
    for other in forecasts[1:]:
        pull += smooth_sign(own - other)
    slope = (
        valid / 128 * (smooth_sign(own - target) / members - coefficient * pull)
    ).astype(BF)
    dhidden = dot_nt(slope, readout_ref[...]).astype(BF)
    dattended = dot_nt(dhidden, w_out_ref[...]).astype(BF)
    grad_ref[...] = dattended
    attended = attended_ref[...]
    product = dattended.astype(F32) * attended
    high = product.astype(BF)
    low = (product - high.astype(F32)).astype(BF)
    pick = (iota((1024, 128), 0) // HEAD_WIDTH + HEADS == iota((1024, 128), 1)).astype(BF)
    stats = stats_ref[...] + dot_nn(high, pick) + dot_nn(low, pick)
    first = stats.astype(BF)
    rest = stats - first.astype(F32)
    second = rest.astype(BF)
    third = (rest - second.astype(F32)).astype(BF)
    terms = jnp.zeros((BLOCK, 128), F32)
    for place, term in enumerate((first, second, third)):
        shift = (iota((128, 128), 0) + 32 * place == iota((128, 128), 1)) & (
            iota((128, 128), 0) < 32
        )
        terms += dot_nn(term, shift.astype(BF))
    packed_ref[:, :128] = slope
    packed_ref[:, 128:] = terms.astype(BF)
    small_ref[:, :128] = dot_tn(attended.astype(BF), slope).astype(BF)
    small_ref[:, 128:] = dot_tn(hidden_ref[...], slope).astype(BF)


def score(counts, own, near, others, target, attended, hidden, stats, w_out, readout_weight):
    vmem = pl.BlockSpec(memory_space=pltpu.VMEM)
    return pl.pallas_call(
        score_kernel,
        in_specs=[pl.BlockSpec(memory_space=pltpu.SMEM)] + [vmem] * 9,
        out_specs=[vmem] * 4,
        out_shape=[
            jax.ShapeDtypeStruct((BLOCK, 128), F32),
            jax.ShapeDtypeStruct((BLOCK, 256), BF),
            jax.ShapeDtypeStruct((BLOCK, 1024), BF),
            jax.ShapeDtypeStruct((1024, 256), BF),
        ],
        compiler_params=pltpu.CompilerParams(vmem_limit_bytes=VMEM_BYTES),
    )(counts, own, near, others, target, attended, hidden, stats, w_out, readout_weight)


def query_kernel(
    counts_ref, q_ref, kcat_ref, vcat_ref, grad_ref, packed_ref, dq_ref, dscores
):
    step = pl.program_id(0)

    @pl.when(step == 0)
    def _():
        dscores[...] = jnp.zeros_like(dscores)

    fill = key_fill([(counts_ref[0], WIN), (counts_ref[1], BLOCK), (counts_ref[2], WIN)])
    value_fill = (spare_lane(fill.shape) < 3).astype(BF)
    low_q = iota((BLOCK, PAIR), 1) < HEAD_WIDTH
    low_k = iota(fill.shape, 1) < HEAD_WIDTH
    terms = packed_ref[:, 128:]
    ones = (spare_lane((BLOCK, WIDTH)) == 3).astype(F32)
    q_fill = (dot_nn(terms, stat_spread(step, 0)) + ones).astype(BF)
    g_fill = dot_nn(terms, stat_spread(step, HEADS)).astype(BF)
    for pair in range(2):
        columns = slice(pair * PAIR, (pair + 1) * PAIR)
        q_pair = q_ref[:, columns] * jnp.asarray(HEAD_WIDTH ** (-0.5), BF)
        g_pair = grad_ref[:, columns]
        k_pair = kcat_ref[:, columns]
        v_pair = vcat_ref[:, columns]
        k_turned = k_pair.T
        for half in range(2):
            slot = pair * 2 + half
            pick_q = low_q if half == 0 else ~low_q
            pick_k = low_k if half == 0 else ~low_k
            q_head = jnp.where(pick_q, q_pair, q_fill[:, columns])
            g_head = jnp.where(pick_q, g_pair, g_fill[:, columns])
            k_head = jnp.where(pick_k, k_pair, fill)
            v_head = jnp.where(pick_k, v_pair, value_fill)
            scores = dot_nt(k_head, q_head)
            change = dot_nt(v_head, g_head)
            for tile in range(2):
                rows = slice(tile * 128, tile * 128 + 640)
                lanes = slice(tile * 128, tile * 128 + 128)
                ends = jnp.exp(scores[rows, lanes]) * change[rows, lanes]
                first, middle, last = keep_band(ends, 0.0)
                start = tile * 128
                dscores[slot, start : start + 128, lanes] = first.astype(BF)
                dscores[slot, start + 128 : start + 512, lanes] = middle.astype(BF)
                dscores[slot, start + 512 : start + 640, lanes] = last.astype(BF)
            turned = dot_nn(
                k_turned[half * HEAD_WIDTH : (half + 1) * HEAD_WIDTH], dscores[slot]
            )
            dq_ref[slot * HEAD_WIDTH : (slot + 1) * HEAD_WIDTH] = (
                turned * HEAD_WIDTH ** (-0.5)
            ).astype(BF)


def query_grads(counts, projected, kcat, vcat, grad, packed):
    part = lambda rows, first: pl.BlockSpec((rows, WIDTH), lambda j: (0, first + j))
    window = 2 * WIN + BLOCK
    return pl.pallas_call(
        query_kernel,
        grid=(4,),
        in_specs=[
            pl.BlockSpec(memory_space=pltpu.SMEM),
            part(BLOCK, 0),
            part(window, 0),
            part(window, 0),
            part(BLOCK, 0),
            pl.BlockSpec((BLOCK, 256), lambda j: (0, 0)),
        ],
        out_specs=pl.BlockSpec((WIDTH, BLOCK), lambda j: (j, 0)),
        out_shape=jax.ShapeDtypeStruct((1024, BLOCK), BF),
        scratch_shapes=[pltpu.VMEM((4, window, BLOCK), BF)],
        compiler_params=pltpu.CompilerParams(vmem_limit_bytes=VMEM_BYTES),
        cost_estimate=pl.CostEstimate(
            flops=6 << 30, bytes_accessed=5 << 20, transcendentals=3 << 20
        ),
    )(counts, projected, kcat, vcat, grad, packed)


def key_kernel(
    counts_ref,
    q_ref,
    k_ref,
    v_ref,
    qhalo_ref,
    grad_ref,
    own_ref,
    left_ref,
    right_ref,
    w_out_ref,
    readout_ref,
    out_ref,
    probs,
    dscores,
    dhidden,
):
    step = pl.program_id(0)

    @pl.when(step == 0)
    def _():
        probs[...] = jnp.zeros_like(probs)
        dscores[...] = jnp.zeros_like(dscores)
        dhidden[:WIN] = dot_nt(left_ref[:, :128], readout_ref[...]).astype(BF)
        dhidden[WIN:] = dot_nt(right_ref[:, :128], readout_ref[...]).astype(BF)

    ghalo = dot_nt(dhidden[...], w_out_ref[...]).astype(BF)
    terms = jnp.concatenate(
        [left_ref[:, 128:], own_ref[:, 128:], right_ref[:, 128:]], axis=0
    )
    window = terms.shape[0]
    fill = key_fill([(counts_ref[1], BLOCK)])
    value_fill = (spare_lane(fill.shape) < 3).astype(BF)
    low_q = iota((window, PAIR), 1) < HEAD_WIDTH
    low_k = iota(fill.shape, 1) < HEAD_WIDTH
    ones = (spare_lane((window, WIDTH)) == 3).astype(F32)
    q_fill = (dot_nn(terms, stat_spread(step, 0)) + ones).astype(BF)
    g_fill = dot_nn(terms, stat_spread(step, HEADS)).astype(BF)
    for pair in range(2):
        columns = slice(pair * PAIR, (pair + 1) * PAIR)
        q_pair = jnp.concatenate(
            [qhalo_ref[:WIN, columns], q_ref[:, columns], qhalo_ref[WIN:, columns]], axis=0
        ) * jnp.asarray(HEAD_WIDTH ** (-0.5), BF)
        g_pair = jnp.concatenate(
            [ghalo[:WIN, columns], grad_ref[:, columns], ghalo[WIN:, columns]], axis=0
        )
        k_pair = k_ref[:, columns]
        v_pair = v_ref[:, columns]
        q_turned = q_pair.T
        g_turned = g_pair.T
        for half in range(2):
            slot = pair * 2 + half
            pick_q = low_q if half == 0 else ~low_q
            pick_k = low_k if half == 0 else ~low_k
            q_head = jnp.where(pick_q, q_pair, q_fill[:, columns])
            g_head = jnp.where(pick_q, g_pair, g_fill[:, columns])
            k_head = jnp.where(pick_k, k_pair, fill)
            v_head = jnp.where(pick_k, v_pair, value_fill)
            scores = dot_nt(q_head, k_head)
            change = dot_nt(g_head, v_head)
            for tile in range(2):
                rows = slice(tile * 128, tile * 128 + 640)
                lanes = slice(tile * 128, tile * 128 + 128)
                weight = keep_band(jnp.exp(scores[rows, lanes]), 0.0)
                moved = change[rows, lanes]
                start = tile * 128
                for piece, (low, high) in zip(weight, ((0, 128), (128, 512), (512, 640))):
                    place = slice(start + low, start + high)
                    probs[slot, place, lanes] = piece.astype(BF)
                    dscores[slot, place, lanes] = (piece * moved[low:high]).astype(BF)
            lanes = slice(half * HEAD_WIDTH, (half + 1) * HEAD_WIDTH)
            place = slice(slot * HEAD_WIDTH, (slot + 1) * HEAD_WIDTH)
            out_ref[0, place] = dot_nn(q_turned[lanes], dscores[slot]).astype(BF)
            out_ref[1, place] = dot_nn(g_turned[lanes], probs[slot]).astype(BF)


def key_grads(counts, projected, qhalo, grad, own, left, right, w_out, readout_weight):
    part = lambda rows, first: pl.BlockSpec((rows, WIDTH), lambda j: (0, first + j))
    whole = lambda *shape: pl.BlockSpec(shape, lambda j: (0, 0))
    window = 2 * WIN + BLOCK
    return pl.pallas_call(
        key_kernel,
        grid=(4,),
        in_specs=[
            pl.BlockSpec(memory_space=pltpu.SMEM),
            part(BLOCK, 0),
            part(BLOCK, 4),
            part(BLOCK, 8),
            part(2 * WIN, 0),
            part(BLOCK, 0),
            whole(BLOCK, 256),
            whole(BLOCK, 256),
            whole(BLOCK, 256),
            pl.BlockSpec((WIDTH, 1024), lambda j: (j, 0)),
            whole(1024, 128),
        ],
        out_specs=pl.BlockSpec((2, WIDTH, BLOCK), lambda j: (0, j, 0)),
        out_shape=jax.ShapeDtypeStruct((2, 1024, BLOCK), BF),
        scratch_shapes=[
            pltpu.VMEM((4, window, BLOCK), BF),
            pltpu.VMEM((4, window, BLOCK), BF),
            pltpu.VMEM((2 * WIN, 1024), BF),
        ],
        compiler_params=pltpu.CompilerParams(vmem_limit_bytes=VMEM_BYTES),
        cost_estimate=pl.CostEstimate(
            flops=9 << 30, bytes_accessed=5 << 20, transcendentals=3 << 20
        ),
    )(
        counts,
        projected,
        projected,
        projected,
        qhalo,
        grad,
        own,
        left,
        right,
        w_out,
        readout_weight,
    )


AXES = ("x_hi", "core", "y", "x_lo", "z")
MEMBER = ("x_hi", "core")
CELLS = ("y", "x_lo", "z")
CHIPS = ("x_hi", "y", "x_lo", "z")
SWAP = [(0, 1), (1, 0)]


def swap_core(values):
    return lax.ppermute(values, "core", SWAP)


def core_rows(values, core):
    rows, columns = values.shape
    chosen = lax.dynamic_slice_in_dim(values.reshape(2, 2, rows // 4, columns), core, 1, 1)
    return chosen.reshape(rows // 2, columns)


def scatter_sum(partial):
    columns = partial.shape[1]
    pieces = lax.all_to_all(
        partial.reshape(64, 8, columns), CHIPS, split_axis=0, concat_axis=0
    )
    return jnp.sum(pieces.astype(F32), axis=0)


def per_device(latent, counts, w_qkv, w_out, readout_weight, target):
    latent_own = latent[0]
    cell_count = 32
    cell_index = lax.axis_index(CELLS)
    member_index = lax.axis_index(MEMBER)
    core = lax.axis_index("core")
    up = [(i, i + 1) for i in range(cell_count - 1)]
    down = [(i + 1, i) for i in range(cell_count - 1)]
    from_left = lax.ppermute(latent_own, CELLS, up)
    from_right = lax.ppermute(latent_own, CELLS, down)

    own_count = counts[cell_index]
    left_count = jnp.where(cell_index > 0, counts[jnp.maximum(cell_index - 1, 0)], 0)
    right_count = jnp.where(
        cell_index < cell_count - 1, counts[jnp.minimum(cell_index + 1, cell_count - 1)], 0
    )
    scalars = jnp.stack([left_count, own_count, right_count])

    projected, turned = project(latent_own, w_qkv)
    turned_own = core_rows(turned, core)
    turned_other = swap_core(core_rows(turned, 1 - core))
    normed_halo, kcat, vcat, attended, stats, hidden, forecast = forward(
        scalars, from_left, from_right, latent_own, w_qkv, projected, w_out, readout_weight
    )
    near = lax.ppermute(forecast, "x_hi", SWAP)
    others = swap_core(jnp.stack([forecast, near]))
    qhalo = dot_nn(normed_halo, w_qkv[:, :1024]).astype(BF)
    crps_whole, packed, grad, small = score(
        scalars, forecast, near, others, target, attended, hidden, stats, w_out, readout_weight
    )
    crps = lax.dynamic_slice_in_dim(crps_whole, member_index * 32, 32, 1)
    packed_left = lax.ppermute(packed, CELLS, up)
    packed_right = lax.ppermute(packed, CELLS, down)

    dquery = query_grads(scalars, projected, kcat, vcat, grad, packed)

    def partial_of(piece):
        return dot_nt(turned_own, piece) + dot_nt(turned_other, swap_core(piece))

    small_sum = core_rows(small, core).astype(F32) + swap_core(
        core_rows(small, 1 - core)
    ).astype(F32)
    first_part = jnp.concatenate([partial_of(dquery), small_sum], axis=1).astype(BF)
    first_part, scalars = lax.optimization_barrier((first_part, scalars))
    first = scatter_sum(first_part)
    pairs = key_grads(
        scalars,
        projected,
        qhalo,
        grad,
        packed,
        packed_left,
        packed_right,
        w_out,
        readout_weight,
    )
    second = scatter_sum(partial_of(pairs.reshape(2048, BLOCK)).astype(BF))
    grad_out = lax.dot_general(
        first[:, 1024:1152],
        readout_weight.astype(F32),
        (((1,), (1,)), ((), ())),
        precision=lax.Precision.HIGHEST,
        preferred_element_type=F32,
    )
    grads = jnp.concatenate([first[:, :1024], second, grad_out, first[:, 1152:]], axis=1)
    return (crps, grads)


def solution(mesh):
    fine = jax.sharding.Mesh(mesh.devices.reshape(2, 2, 4, 2, 4), AXES)
    placed = (P(MEMBER, CELLS, None), P(), P(), P(), P(), P(CELLS, None))
    return jax.shard_map(
        per_device,
        mesh=fine,
        in_specs=placed,
        out_specs=(P(CELLS, MEMBER), P(MEMBER + CELLS, None)),
        check_vma=False,
    )
```

time: 176 us -> 169 us (0.960)
  waiting for transfers between devices: 44.1 us -> 56.1 us
  blocking collectives: 10.9 us -> 0 us
  matrix products: 15.5 us -> 8.9 us
  local copies, waits for them, and re-layouts: 12.3 us -> 6.31 us
  starting transfers between devices: 30.9 us -> 33.9 us
  Pallas kernels: 53.4 us -> 56 us
    all_gather x1 -> x0, blocking collectives: 10.9 us -> none  [per_device(): forecasts = lax.all_gather(forecast, MEMBER, axis=0, tiled=False)]
    dot_general x3 -> x0, matrix products: 7.74 us -> none  [dot_tn(): lax.dot_general(left, right, (((0,), (0,)), ((), ())), preferred_element_...]
    slice x6 -> x0, local copies, waits for them, and re-layouts: 4.52 us -> none  [the longest x1 1.92 us: per_device(): ordered[:, :512]]
    all_to_all x2, waiting for transfers between devices: 41.3 us -> 44.8 us  [scatter_sum(): lax.all_to_all(partial.reshape(64, 8, columns), CHIPS, split_axis=0, conc...]
    ppermute x1, waiting for transfers between devices: 0.01 us -> 3.4 us  [per_device(): packed_right = lax.ppermute(packed, CELLS, down)]
    ppermute x4 -> x6, starting transfers between devices: 0.68 us -> 3.92 us  [the longest x1 3.1 us: per_device(): near = lax.ppermute(forecast, 'x_hi', SWAP)]
    ppermute x1, waiting for transfers between devices: 0.1 us -> 2.67 us  [per_device(): from_right = lax.ppermute(latent_own, CELLS, down)]
    ppermute x4 -> x6, waiting for transfers between devices: 2.65 us -> 5.19 us  [the longest x1 3.66 us: per_device(): near = lax.ppermute(forecast, 'x_hi', SWAP)]
  transfers between devices with their start and end apart: 10 -> 12, of which waited for: 4 -> 6; matrix products, arithmetic and copies ran while one was open for 16% -> 9% of each run, Pallas kernels for 30% -> 5%
where the time goes in v1:
time: 169 us; the launch traced here: 168 us
  waiting for transfers between devices  56.1 us (33%)
  Pallas kernels  56 us (33%)
  starting transfers between devices  33.9 us (20%)
  matrix products  8.9 us (5%)
  local copies, waits for them, and re-layouts  6.31 us (4%)
  other arithmetic  4.71 us (3%)
  between operations  2.15 us (1%)
    all_to_all x2, waiting for transfers between devices, scatter_sum(): lax.all_to_all(partial.reshape(64, 8, columns), CHIPS, split_axis=0, conc...  44.8 us
    all_to_all x2, starting transfers between devices, scatter_sum(): lax.all_to_all(partial.reshape(64, 8, columns), CHIPS, split_axis=0, conc...  19.5 us
    pallas_call x1, Pallas kernels, forward(): pl.pallas_call(forward_kernel, grid=(4,), in_specs=[pl.BlockSpec(memory_s...  18.3 us
    pallas_call x1, Pallas kernels, key_grads(): pl.pallas_call(key_kernel, grid=(4,), in_specs=[pl.BlockSpec(memory_space...  13.7 us
    pallas_call x1, Pallas kernels, query_grads(): pl.pallas_call(query_kernel, grid=(4,), in_specs=[pl.BlockSpec(memory_spa...  11 us
    pallas_call x1, Pallas kernels, project(): pl.pallas_call(project_kernel, grid=(6,), in_specs=[pl.BlockSpec((rows, w...  7.61 us
    pallas_call x1, Pallas kernels, score(): pl.pallas_call(score_kernel, in_specs=[pl.BlockSpec(memory_space=pltpu.SM...  5.43 us
    ppermute x1, starting transfers between devices, per_device(): from_left = lax.ppermute(latent_own, CELLS, up)  3.94 us
  transfers between devices with their start and end apart: 12, of which 6 were waited for; matrix products, arithmetic and copies ran while one was open for 9% of the time, Pallas kernels for 5%

profile of v1, /device:TPU:0, one launch (start us, length us, event | category | flops | bytes accessed | tf_op | source)
XLA Modules:
  0.0 168.0 jit_solution(11958214788134877080)
XLA Ops:
  0.6 3.9 %collective-permute-start = (bf16[256,1024]{1,0:T(8,128)(2,1)}, bf16[256,1024]{1,0:T(8,128)(2,1)S(1)}, u32[]{:S(2)}, u32[]{:S(2)}) collective-permute-start(bf16[256,1024]{1,0:T(8,128)(2,1)} %bitcast.39), channel_id=1, source_target_pairs={{0,1},{1,2},{2,3},{3,4},{4,5},{5,6},{6,7},{7,8},{8,9},{9,10},{10,1... | collective-permute-start | bytes 1572872 | tf_op jit(solution)/shard_map/ppermute | solution.py:594
  4.6 1.3 collective-permute-start.1
  5.9 1.4 fusion.9
  8.6 1.3 pad_add_fusion.counts_ref
  9.9 7.6 %shard_map.77 = (bf16[256,3072]{1,0:T(8,128)(2,1)}, bf16[1024,256]{1,0:T(8,128)(2,1)}) custom-call(bf16[256,1024]{1,0:T(8,128)(2,1)} %bitcast.41, bf16[1024,3072]{1,0:T(8,128)(2,1)} %wv_ref.1), custom_call_target="tpu_custom_call" | custom-call | flops 2147483648 | bytes 8388608 | tf_op jit(solution)/shard_map/pallas_call | solution.py:74
  17.6 2.7 %collective-permute-done.1.right_ref = bf16[256,1024]{1,0:T(8,128)(2,1)S(1)} collective-permute-done((bf16[256,1024]{1,0:T(8,128)(2,1)}, bf16[256,1024]{1,0:T(8,128)(2,1)S(1)}, u32[]{:S(2)}, u32[]{:S(2)}) %collective-permute-start.1) | collective-permute-done | bytes 524320 | tf_op jit(solution)/shard_map/ppermute | solution.py:595
  21.1 18.3 %shard_map.78 = (bf16[512,1024]{1,0:T(8,128)(2,1)}, bf16[768,1024]{1,0:T(8,128)(2,1)}, bf16[768,1024]{1,0:T(8,128)(2,1)}, f32[256,1024]{1,0:T(8,128)}, f32[256,1...) custom-call(s32[3]{0:T(128)} %pad_add_fusion.counts_ref, bf16[256,1024]{1,0:T(8,128)(2,1)} %copy-done.6, ...), custom_call_target="tpu_custom_call" | custom-call | flops 6442450944 | bytes 12582912 | tf_op jit(solution)/shard_map/pallas_call | solution.py:232
  39.4 3.1 %collective-permute-start.2 = (f32[256,128]{1,0:T(8,128)}, f32[256,128]{1,0:T(8,128)S(1)}, u32[]{:S(2)}, u32[]{:S(2)}) collective-permute-start(f32[256,128]{1,0:T(8,128)} %get-tuple-element.18.own_ref), channel_id=1, source_target_pairs={{0,64},{64,0},{1,65},{65,1},{2,66},{66,2},{3,67},{67,3},{4,68},{68... | collective-permute-start | bytes 393224 | tf_op jit(solution)/shard_map/ppermute | solution.py:610
  42.5 3.7 %collective-permute-done.2.near_ref = f32[256,128]{1,0:T(8,128)S(1)} collective-permute-done((f32[256,128]{1,0:T(8,128)}, f32[256,128]{1,0:T(8,128)S(1)}, u32[]{:S(2)}, u32[]{:S(2)}) %collective-permute-start.2) | collective-permute-done | bytes 131104 | tf_op jit(solution)/shard_map/ppermute | solution.py:610
  47.2 1.5 collective-permute-done.3.others_ref
  49.4 5.4 %shard_map.79 = (f32[256,128]{1,0:T(8,128)}, bf16[256,256]{1,0:T(8,128)(2,1)}, bf16[256,1024]{1,0:T(8,128)(2,1)}, bf16[1024,256]{1,0:T(8,128)(2,1)}) custom-call(s32[3]{0:T(128)} %pad_add_fusion.counts_ref, f32[256,128]{1,0:T(8,128)} %get-tuple-element.18.own_ref, f32[256,128]{1,0:T(8,128)} %copy-done.2, f32[2,256,128]{2,1,0:T(8,128)} %copy-done.5, ...), custom_call_target="tpu_custom_call" | custom-call | tf_op jit(solution)/shard_map/pallas_call | solution.py:350
  54.9 11.0 %shard_map.80 = bf16[1024,256]{1,0:T(8,128)(2,1)} custom-call(s32[3]{0:T(128)} %pad_add_fusion.counts_ref, bf16[256,3072]{1,0:T(8,128)(2,1)} %get-tuple-element.17.q_ref.k_ref.v_ref, bf16[768,1024]{1,0:T(8,128)(2,1)} %get-tuple-element.24.kcat_ref, bf16[768,1024]{1,0:T(8,128)(2,1)} %get-tuple-element.25.vcat_ref, ...), custom_call_target="tpu_custom_call" | custom-call | flops 6442450944 | bytes 5242880 | tf_op jit(solution)/shard_map/pallas_call | solution.py:418
  67.1 3.9 %fusion.3.qhalo_ref = bf16[512,1024]{1,0:T(8,128)(2,1)} fusion(bf16[512,1024]{1,0:T(8,128)(2,1)S(1)} %copy-done.11, bf16[1024,3072]{1,0:T(8,128)(2,1)} %wv_ref.1), kind=kOutput, calls=%fused_computation.7 | convolution fusion | flops 1074266112 | bytes 4194304 | tf_op jit(solution)/shard_map/dot_general | solution.py:43
  70.9 3.8 %collective-permute-start.7 = (bf16[256,256]{1,0:T(8,128)(2,1)S(1)}, bf16[256,256]{1,0:T(8,128)(2,1)S(1)}, u32[]{:S(2)}, u32[]{:S(2)}) collective-permute-start(bf16[256,256]{1,0:T(8,128)(2,1)S(1)} %copy-done.8), channel_id=1, source_target_pairs={{0,1},{1,2},{2,3},{3,4},{4,5},{5,6},{6,7},{7,8},{8,9},{9,10},{10,1... | collective-permute-start | bytes 393224 | tf_op jit(solution)/shard_map/ppermute | solution.py:617
  74.7 1.5 collective-permute-start.8
  77.3 1.2 pad_maximum_fusion
  78.5 3.4 %collective-permute-done.8.right_ref = bf16[256,256]{1,0:T(8,128)(2,1)S(1)} collective-permute-done((bf16[256,256]{1,0:T(8,128)(2,1)S(1)}, bf16[256,256]{1,0:T(8,128)(2,1)S(1)}, u32[]{:S(2)}, u32[]{:S(2)}) %collective-permute-start.8) | collective-permute-done | bytes 131104 | tf_op jit(solution)/shard_map/ppermute | solution.py:618
  82.5 13.7 %shard_map.81 = bf16[2,1024,256]{2,1,0:T(8,128)(2,1)} custom-call(s32[3]{0:T(128)} %pad_add_fusion.counts_ref, bf16[256,3072]{1,0:T(8,128)(2,1)} %get-tuple-element.17.q_ref.k_ref.v_ref, bf16[256,3072]{1,0:T(8,128)(2,1)} %get-tuple-element.17.q_ref.k_ref.v_ref, bf16[256,3072]{1,0:T(8,128)(2,1)} %get-tuple-element.17.q_ref.k_ref.v_ref, ...), custom_call_target="tpu_custom_call" | custom-call | flops 9663676416 | bytes 5242880 | tf_op jit(solution)/shard_map/pallas_call | solution.py:519
  96.3 13.9 %all-to-all-start = ((bf16[64,8,1280]{2,1,0:T(8,128)(2,1)}), bf16[64,8,1280]{2,1,0:T(8,128)(2,1)S(1)}, u32[]{:S(2)}, u32[]{:S(2)}) async-start(bf16[64,8,1280]{2,1,0:T(8,128)(2,1)} %bitcast.13), calls=%async_computation | async-start | bytes 2621440 | tf_op jit(solution)/shard_map/all_to_all | solution.py:580
  111.4 2.1 %fusion = bf16[64,8,2048]{2,1,0:T(8,128)(2,1)} fusion(f32[512,2048]{1,0:T(8,128)S(1)} %fusion.11, bf16[512,256]{1,0:T(8,128)(2,1)S(1)} %bitcast.30, bf16[2048,256]{1,0:T(8,128)(2,1)S(1)} %bitcast.32), kind=kOutput, calls=%fused_computation.2 | convolution fusion | flops 538968064 | bytes 7602176 | tf_op jit(solution)/shard_map/dot_general | solution.py:47
  113.5 18.8 %all-to-all-done = bf16[64,8,1280]{2,1,0:T(8,128)(2,1)S(1)} async-done(((bf16[64,8,1280]{2,1,0:T(8,128)(2,1)}), bf16[64,8,1280]{2,1,0:T(8,128)(2,1)S(1)}, u32[]{:S(2)}, u32[]{:S(2)}) %all-to-all-start) | async-done | bytes 1310752 | tf_op jit(solution)/shard_map/all_to_all | solution.py:580
  132.3 5.5 %all-to-all-start.1 = ((bf16[64,8,2048]{2,1,0:T(8,128)(2,1)}), bf16[64,8,2048]{2,1,0:T(8,128)(2,1)S(1)}, u32[]{:S(2)}, u32[]{:S(2)}) async-start(bf16[64,8,2048]{2,1,0:T(8,128)(2,1)} %fusion), calls=%async_computation.1 | async-start | bytes 4194304 | tf_op jit(solution)/shard_map/all_to_all | solution.py:580
  139.8 1.3 fusion.7
  141.0 26.0 %all-to-all-done.1 = bf16[64,8,2048]{2,1,0:T(8,128)(2,1)S(1)} async-done(((bf16[64,8,2048]{2,1,0:T(8,128)(2,1)}), bf16[64,8,2048]{2,1,0:T(8,128)(2,1)S(1)}, u32[]{:S(2)}, u32[]{:S(2)}) %all-to-all-start.1) | async-done | bytes 2097184 | tf_op jit(solution)/shard_map/all_to_all | solution.py:580
  (48 shorter events, 9.6 us)
Async XLA Ops:
  0.6 16.9 %collective-permute-start = (bf16[256,1024]{1,0:T(8,128)(2,1)}, bf16[256,1024]{1,0:T(8,128)(2,1)S(1)}, u32[]{:S(2)}, u32[]{:S(2)}) collective-permute-start(bf16[256,1024]{1,0:T(8,128)(2,1)} %bitcast.39), channel_id=1, source_target_pairs={{0,1},{1,2},{2,3},{3,4},{4,5},{5,6},{6,7},{7,8},{8,9},{9,10},{10,1... | collective-permute-start | bytes 1572872 | tf_op jit(solution)/shard_map/ppermute | solution.py:594
  4.6 15.6 %collective-permute-start.1 = (bf16[256,1024]{1,0:T(8,128)(2,1)}, bf16[256,1024]{1,0:T(8,128)(2,1)S(1)}, u32[]{:S(2)}, u32[]{:S(2)}) collective-permute-start(bf16[256,1024]{1,0:T(8,128)(2,1)} %bitcast.40), channel_id=1, source_target_pairs={{1,0},{2,1},{3,2},{4,3},{5,4},{6,5},{7,6},{8,7},{9,8},{10,9},{11,1... | collective-permute-start | bytes 1572872 | tf_op jit(solution)/shard_map/ppermute | solution.py:595
  17.5 2.7 %copy-start.6 = (bf16[256,1024]{1,0:T(8,128)(2,1)}, bf16[256,1024]{1,0:T(8,128)(2,1)S(1)}, u32[]{:S(2)}) copy-start(bf16[256,1024]{1,0:T(8,128)(2,1)S(1)} %collective-permute-done.left_ref) | copy-start | bytes 1572868
  20.2 0.9 copy-start.7
  39.4 6.8 %collective-permute-start.2 = (f32[256,128]{1,0:T(8,128)}, f32[256,128]{1,0:T(8,128)S(1)}, u32[]{:S(2)}, u32[]{:S(2)}) collective-permute-start(f32[256,128]{1,0:T(8,128)} %get-tuple-element.18.own_ref), channel_id=1, source_target_pairs={{0,64},{64,0},{1,65},{65,1},{2,66},{66,2},{3,67},{67,3},{4,68},{68... | collective-permute-start | bytes 393224 | tf_op jit(solution)/shard_map/ppermute | solution.py:610
  46.1 2.6 %copy-start.2 = (f32[256,128]{1,0:T(8,128)}, f32[256,128]{1,0:T(8,128)S(1)}, u32[]{:S(2)}) copy-start(f32[256,128]{1,0:T(8,128)S(1)} %collective-permute-done.2.near_ref) | copy-start | bytes 393220
  47.1 1.6 collective-permute-start.3
  48.7 0.7 copy-start.5
  54.9 11.1 %copy-start.3 = (bf16[1024,256]{1,0:T(8,128)(2,1)S(1)}, bf16[1024,256]{1,0:T(8,128)(2,1)}, u32[]{:S(2)}) copy-start(bf16[1024,256]{1,0:T(8,128)(2,1)} %get-tuple-element.23) | copy-start | bytes 1572868
  54.9 11.1 %copy-start.4 = (bf16[1024,256]{1,0:T(8,128)(2,1)S(1)}, bf16[1024,256]{1,0:T(8,128)(2,1)}, u32[]{:S(2)}) copy-start(bf16[1024,256]{1,0:T(8,128)(2,1)} %get-tuple-element.28) | copy-start | bytes 1572868
  65.8 1.2 copy-start.11
  65.8 10.5 %collective-permute-start.5 = (bf16[1024,256]{1,0:T(8,128)(2,1)}, bf16[1024,256]{1,0:T(8,128)(2,1)S(1)}, u32[]{:S(2)}, u32[]{:S(2)}) collective-permute-start(bf16[1024,256]{1,0:T(8,128)(2,1)} %shard_map.80), channel_id=1, source_target_pairs={{0,32},{32,0},{1,33},{33,1},{2,34},{34,2},{3,35},{35,3},{4,36},{36... | collective-permute-start | bytes 1572872 | tf_op jit(solution)/shard_map/ppermute | solution.py:569
  66.0 10.3 %collective-permute-start.4 = (bf16[512,256]{1,0:T(8,128)(2,1)S(1)}, bf16[512,256]{1,0:T(8,128)(2,1)S(1)}, u32[]{:S(2)}, u32[]{:S(2)}) collective-permute-start(bf16[512,256]{1,0:T(8,128)(2,1)S(1)} %bitcast.37), channel_id=1, source_target_pairs={{0,32},{32,0},{1,33},{33,1},{2,34},{34,2},{3,35},{35,3},{4,36},{36... | collective-permute-start | bytes 786440 | tf_op jit(solution)/shard_map/ppermute | solution.py:569
  66.5 9.7 %collective-permute-start.6 = (bf16[512,256]{1,0:T(8,128)(2,1)S(1)}, bf16[512,256]{1,0:T(8,128)(2,1)S(1)}, u32[]{:S(2)}, u32[]{:S(2)}) collective-permute-start(bf16[512,256]{1,0:T(8,128)(2,1)S(1)} %bitcast.38), channel_id=1, source_target_pairs={{0,32},{32,0},{1,33},{33,1},{2,34},{34,2},{3,35},{35,3},{4,36},{36... | collective-permute-start | bytes 786440 | tf_op jit(solution)/shard_map/ppermute | solution.py:569
  67.0 3.9 %copy-start.8 = (bf16[256,256]{1,0:T(8,128)(2,1)S(1)}, bf16[256,256]{1,0:T(8,128)(2,1)}, u32[]{:S(2)}) copy-start(bf16[256,256]{1,0:T(8,128)(2,1)} %get-tuple-element.27.packed_ref.own_ref) | copy-start | bytes 393220
  70.9 5.9 %copy-start.1 = (bf16[1024,256]{1,0:T(8,128)(2,1)S(1)}, bf16[1024,256]{1,0:T(8,128)(2,1)}, u32[]{:S(2)}) copy-start(bf16[1024,256]{1,0:T(8,128)(2,1)} %shard_map.80) | copy-start | bytes 1572868
  70.9 7.5 %collective-permute-start.7 = (bf16[256,256]{1,0:T(8,128)(2,1)S(1)}, bf16[256,256]{1,0:T(8,128)(2,1)S(1)}, u32[]{:S(2)}, u32[]{:S(2)}) collective-permute-start(bf16[256,256]{1,0:T(8,128)(2,1)S(1)} %copy-done.8), channel_id=1, source_target_pairs={{0,1},{1,2},{2,3},{3,4},{4,5},{5,6},{6,7},{7,8},{8,9},{9,10},{10,1... | collective-permute-start | bytes 393224 | tf_op jit(solution)/shard_map/ppermute | solution.py:617
  74.7 7.2 %collective-permute-start.8 = (bf16[256,256]{1,0:T(8,128)(2,1)S(1)}, bf16[256,256]{1,0:T(8,128)(2,1)S(1)}, u32[]{:S(2)}, u32[]{:S(2)}) collective-permute-start(bf16[256,256]{1,0:T(8,128)(2,1)S(1)} %copy-done.8), channel_id=1, source_target_pairs={{1,0},{2,1},{3,2},{4,3},{5,4},{6,5},{7,6},{8,7},{9,8},{10,9},{11,1... | collective-permute-start | bytes 393224 | tf_op jit(solution)/shard_map/ppermute | solution.py:618
  78.5 3.4 %copy-start.9 = (bf16[256,256]{1,0:T(8,128)(2,1)}, bf16[256,256]{1,0:T(8,128)(2,1)S(1)}, u32[]{:S(2)}) copy-start(bf16[256,256]{1,0:T(8,128)(2,1)S(1)} %collective-permute-done.7.left_ref) | copy-start | bytes 393220
  81.9 0.6 copy-start.10
  96.2 14.0 %collective-permute-start.9 = (bf16[2048,256]{1,0:T(8,128)(2,1)}, bf16[2048,256]{1,0:T(8,128)(2,1)S(1)}, u32[]{:S(2)}, u32[]{:S(2)}) collective-permute-start(bf16[2048,256]{1,0:T(8,128)(2,1)} %bitcast.31), channel_id=1, source_target_pairs={{0,32},{32,0},{1,33},{33,1},{2,34},{34,2},{3,35},{35,3},{4,36},{36... | collective-permute-start | bytes 3145736 | tf_op jit(solution)/shard_map/ppermute | solution.py:569
  96.3 36.0 %all-to-all-start = ((bf16[64,8,1280]{2,1,0:T(8,128)(2,1)}), bf16[64,8,1280]{2,1,0:T(8,128)(2,1)S(1)}, u32[]{:S(2)}, u32[]{:S(2)}) async-start(bf16[64,8,1280]{2,1,0:T(8,128)(2,1)} %bitcast.13), calls=%async_computation | async-start | bytes 2621440 | tf_op jit(solution)/shard_map/all_to_all | solution.py:580
  110.2 1.2 copy-start
  132.3 34.8 %all-to-all-start.1 = ((bf16[64,8,2048]{2,1,0:T(8,128)(2,1)}), bf16[64,8,2048]{2,1,0:T(8,128)(2,1)S(1)}, u32[]{:S(2)}, u32[]{:S(2)}) async-start(bf16[64,8,2048]{2,1,0:T(8,128)(2,1)} %fusion), calls=%async_computation.1 | async-start | bytes 4194304 | tf_op jit(solution)/shard_map/all_to_all | solution.py:580

commit v2 on v1

--- a/solution.py
+++ b/solution.py
@@ -169,51 +169,53 @@
     low_q = iota((BLOCK, PAIR), 1) < HEAD_WIDTH
     low_k = iota(fill.shape, 1) < HEAD_WIDTH
     query_fill = (spare_lane((BLOCK, PAIR)) == 3).astype(BF)
+    scores, turned = [], []
     for pair in range(2):
         columns = slice(pair * PAIR, (pair + 1) * PAIR)
         q_pair = q_ref[:, columns] * jnp.asarray(HEAD_WIDTH ** (-0.5), BF)
         k_pair = kcat_ref[:, columns]
-        v_turned = vcat_ref[:, columns].T
-        halves = []
+        turned.append(vcat_ref[:, columns].T)
         for half in range(2):
-            slot = pair * 2 + half
             if half == 0:
                 q_head = jnp.where(low_q, q_pair, query_fill)
                 k_head = jnp.where(low_k, k_pair, fill)
             else:
                 q_head = jnp.where(low_q, query_fill, q_pair)
                 k_head = jnp.where(low_k, fill, k_pair)
-            scores = dot_nt(k_head, q_head)
-            totals, levels = [], []
-            for tile in range(2):
-                rows = slice(tile * 128, tile * 128 + 640)
-                lanes = slice(tile * 128, tile * 128 + 128)
-                first, middle, last = keep_band(scores[rows, lanes], NEVER)
-                top = jnp.maximum(
-                    jnp.max(middle, axis=0, keepdims=True),
-                    jnp.max(jnp.maximum(first, last), axis=0, keepdims=True),
-                )
-                first = jnp.exp(first - top)
-                middle = jnp.exp(middle - top)
-                last = jnp.exp(last - top)
-                total = jnp.sum(middle, axis=0, keepdims=True) + jnp.sum(
-                    first + last, axis=0, keepdims=True
-                )
-                start = tile * 128
-                probs[slot, start : start + 128, lanes] = first.astype(BF)
-                probs[slot, start + 128 : start + 512, lanes] = middle.astype(BF)
-                probs[slot, start + 512 : start + 640, lanes] = last.astype(BF)
-                totals.append(total)
-                levels.append(top + jnp.log(total))
-            total = jnp.concatenate(totals, axis=1)
-            mixed = dot_nn(
-                v_turned[half * HEAD_WIDTH : (half + 1) * HEAD_WIDTH], probs[slot]
+            scores.append(dot_nt(k_head, q_head))
+    scales = []
+    for slot in range(4):
+        totals, levels = [], []
+        for tile in range(2):
+            rows = slice(tile * 128, tile * 128 + 640)
+            lanes = slice(tile * 128, tile * 128 + 128)
+            first, middle, last = keep_band(scores[slot][rows, lanes], NEVER)
+            top = jnp.maximum(
+                jnp.max(middle, axis=0, keepdims=True),
+                jnp.max(jnp.maximum(first, last), axis=0, keepdims=True),
             )
-            halves.append(mixed * (1.0 / total))
-            stat_rows[pl.ds(step * 4 + slot, 1), :] = jnp.concatenate(levels, axis=1)
-        both = jnp.concatenate(halves, axis=0).T
+            first = jnp.exp(first - top)
+            middle = jnp.exp(middle - top)
+            last = jnp.exp(last - top)
+            total = jnp.sum(middle, axis=0, keepdims=True) + jnp.sum(
+                first + last, axis=0, keepdims=True
+            )
+            start = tile * 128
+            probs[slot, start : start + 128, lanes] = first.astype(BF)
+            probs[slot, start + 128 : start + 512, lanes] = middle.astype(BF)
+            probs[slot, start + 512 : start + 640, lanes] = last.astype(BF)
+            totals.append(total)
+            levels.append(top + jnp.log(total))
+        scales.append(1.0 / jnp.concatenate(totals, axis=1))
+        stat_rows[pl.ds(step * 4 + slot, 1), :] = jnp.concatenate(levels, axis=1)
+    for pair in range(2):
+        halves = []
+        for half in range(2):
+            slot = pair * 2 + half
+            lanes = slice(half * HEAD_WIDTH, (half + 1) * HEAD_WIDTH)
+            halves.append(dot_nn(turned[pair][lanes], probs[slot]) * scales[slot])
         start = pl.multiple_of(step * WIDTH + pair * PAIR, PAIR)
-        attended_ref[:, pl.ds(start, PAIR)] = both
+        attended_ref[:, pl.ds(start, PAIR)] = jnp.concatenate(halves, axis=0).T
 
     @pl.when(step == 3)
     def _():
@@ -378,6 +380,7 @@
     ones = (spare_lane((BLOCK, WIDTH)) == 3).astype(F32)
     q_fill = (dot_nn(terms, stat_spread(step, 0)) + ones).astype(BF)
     g_fill = dot_nn(terms, stat_spread(step, HEADS)).astype(BF)
+    turned = []
     for pair in range(2):
         columns = slice(pair * PAIR, (pair + 1) * PAIR)
         q_pair = q_ref[:, columns] * jnp.asarray(HEAD_WIDTH ** (-0.5), BF)
@@ -404,12 +407,10 @@
                 dscores[slot, start : start + 128, lanes] = first.astype(BF)
                 dscores[slot, start + 128 : start + 512, lanes] = middle.astype(BF)
                 dscores[slot, start + 512 : start + 640, lanes] = last.astype(BF)
-            turned = dot_nn(
-                k_turned[half * HEAD_WIDTH : (half + 1) * HEAD_WIDTH], dscores[slot]
-            )
-            dq_ref[slot * HEAD_WIDTH : (slot + 1) * HEAD_WIDTH] = (
-                turned * HEAD_WIDTH ** (-0.5)
-            ).astype(BF)
+            turned.append(k_turned[half * HEAD_WIDTH : (half + 1) * HEAD_WIDTH])
+    for slot in range(4):
+        dquery = dot_nn(turned[slot], dscores[slot]) * HEAD_WIDTH ** (-0.5)
+        dq_ref[slot * HEAD_WIDTH : (slot + 1) * HEAD_WIDTH] = dquery.astype(BF)
 
 
 def query_grads(counts, projected, kcat, vcat, grad, packed):
@@ -474,6 +475,7 @@
     ones = (spare_lane((window, WIDTH)) == 3).astype(F32)
     q_fill = (dot_nn(terms, stat_spread(step, 0)) + ones).astype(BF)
     g_fill = dot_nn(terms, stat_spread(step, HEADS)).astype(BF)
+    turned = []
     for pair in range(2):
         columns = slice(pair * PAIR, (pair + 1) * PAIR)
         q_pair = jnp.concatenate(
@@ -507,9 +509,11 @@
                     probs[slot, place, lanes] = piece.astype(BF)
                     dscores[slot, place, lanes] = (piece * moved[low:high]).astype(BF)
             lanes = slice(half * HEAD_WIDTH, (half + 1) * HEAD_WIDTH)
-            place = slice(slot * HEAD_WIDTH, (slot + 1) * HEAD_WIDTH)
-            out_ref[0, place] = dot_nn(q_turned[lanes], dscores[slot]).astype(BF)
-            out_ref[1, place] = dot_nn(g_turned[lanes], probs[slot]).astype(BF)
+            turned.append((q_turned[lanes], g_turned[lanes]))
+    for slot in range(4):
+        place = slice(slot * HEAD_WIDTH, (slot + 1) * HEAD_WIDTH)
+        out_ref[0, place] = dot_nn(turned[slot][0], dscores[slot]).astype(BF)
+        out_ref[1, place] = dot_nn(turned[slot][1], probs[slot]).astype(BF)
 
 
 def key_grads(counts, projected, qhalo, grad, own, left, right, w_out, readout_weight):
@@ -575,11 +579,12 @@
     return chosen.reshape(rows // 2, columns)
 
 
-def scatter_sum(partial):
+def scatter(partial):
     columns = partial.shape[1]
-    pieces = lax.all_to_all(
-        partial.reshape(64, 8, columns), CHIPS, split_axis=0, concat_axis=0
-    )
+    return lax.all_to_all(partial.reshape(64, 8, columns), CHIPS, split_axis=0, concat_axis=0)
+
+
+def add_up(pieces):
     return jnp.sum(pieces.astype(F32), axis=0)
 
 
@@ -610,6 +615,7 @@
     near = lax.ppermute(forecast, "x_hi", SWAP)
     others = swap_core(jnp.stack([forecast, near]))
     qhalo = dot_nn(normed_halo, w_qkv[:, :1024]).astype(BF)
+    others, qhalo = lax.optimization_barrier((others, qhalo))
     crps_whole, packed, grad, small = score(
         scalars, forecast, near, others, target, attended, hidden, stats, w_out, readout_weight
     )
@@ -618,6 +624,9 @@
     packed_right = lax.ppermute(packed, CELLS, down)
 
     dquery = query_grads(scalars, projected, kcat, vcat, grad, packed)
+    dquery, packed_left, packed_right = lax.optimization_barrier(
+        (dquery, packed_left, packed_right)
+    )
 
     def partial_of(piece):
         return dot_nt(turned_own, piece) + dot_nt(turned_other, swap_core(piece))
@@ -627,7 +636,7 @@
     ).astype(F32)
     first_part = jnp.concatenate([partial_of(dquery), small_sum], axis=1).astype(BF)
     first_part, scalars = lax.optimization_barrier((first_part, scalars))
-    first = scatter_sum(first_part)
+    first = scatter(first_part)
     pairs = key_grads(
         scalars,
         projected,
@@ -639,7 +648,9 @@
         w_out,
         readout_weight,
     )
-    second = scatter_sum(partial_of(pairs.reshape(2048, BLOCK)).astype(BF))
+    pairs, first = lax.optimization_barrier((pairs, first))
+    second = add_up(scatter(partial_of(pairs.reshape(2048, BLOCK)).astype(BF)))
+    first = add_up(first)
     grad_out = lax.dot_general(
         first[:, 1024:1152],
         readout_weight.astype(F32),

time: 169 us -> 149 us (0.88)
  waiting for transfers between devices: 56.1 us -> 46.3 us
  Pallas kernels: 56 us -> 47 us
    all_to_all x2, waiting for transfers between devices: 44.8 us -> 37.3 us  [scatter(): lax.all_to_all(partial.reshape(64, 8, columns), CHIPS, split_axis=0, conc...]
    pallas_call x1, Pallas kernels: 18.3 us -> 14.6 us  [forward(): pl.pallas_call(forward_kernel, grid=(4,), in_specs=[pl.BlockSpec(memory_s...]
    ppermute x1, waiting for transfers between devices: 3.4 us -> 0.01 us  [per_device(): packed_right = lax.ppermute(packed, CELLS, down)]
    pallas_call x1, Pallas kernels: 11 us -> 8.15 us  [query_grads(): pl.pallas_call(query_kernel, grid=(4,), in_specs=[pl.BlockSpec(memory_spa...]
    pallas_call x1, Pallas kernels: 13.7 us -> 11.2 us  [key_grads(): pl.pallas_call(key_kernel, grid=(4,), in_specs=[pl.BlockSpec(memory_space...]
    unnamed x25 -> x19, local copies, waits for them, and re-layouts: 3.79 us -> 2.24 us
  transfers between devices with their start and end apart: 12 -> 12, of which waited for: 6 -> 7; matrix products, arithmetic and copies ran while one was open for 9% -> 8% of each run, Pallas kernels for 5% -> 18%
where the time goes in v2:
time: 149 us; the launch traced here: 148 us
  Pallas kernels  47 us (32%)
  waiting for transfers between devices  46.3 us (31%)
  starting transfers between devices  32.9 us (22%)
  matrix products  10.4 us (7%)
  local copies, waits for them, and re-layouts  4.71 us (3%)
  other arithmetic  4.65 us (3%)
  between operations  2.16 us (1%)
    all_to_all x2, waiting for transfers between devices, scatter(): lax.all_to_all(partial.reshape(64, 8, columns), CHIPS, split_axis=0, conc...  37.3 us
    all_to_all x2, starting transfers between devices, scatter(): lax.all_to_all(partial.reshape(64, 8, columns), CHIPS, split_axis=0, conc...  18.7 us
    pallas_call x1, Pallas kernels, forward(): pl.pallas_call(forward_kernel, grid=(4,), in_specs=[pl.BlockSpec(memory_s...  14.6 us
    pallas_call x1, Pallas kernels, key_grads(): pl.pallas_call(key_kernel, grid=(4,), in_specs=[pl.BlockSpec(memory_space...  11.2 us
    pallas_call x1, Pallas kernels, query_grads(): pl.pallas_call(query_kernel, grid=(4,), in_specs=[pl.BlockSpec(memory_spa...  8.15 us
    pallas_call x1, Pallas kernels, project(): pl.pallas_call(project_kernel, grid=(6,), in_specs=[pl.BlockSpec((rows, w...  7.64 us
    pallas_call x1, Pallas kernels, score(): pl.pallas_call(score_kernel, in_specs=[pl.BlockSpec(memory_space=pltpu.SM...  5.37 us
    dot_general x4, matrix products, dot_nt(): lax.dot_general(left, right, (((1,), (1,)), ((), ())), preferred_element_...  5 us
  transfers between devices with their start and end apart: 12, of which 7 were waited for; matrix products, arithmetic and copies ran while one was open for 8% of the time, Pallas kernels for 18%

profile of v2, /device:TPU:0, one launch (start us, length us, event | category | flops | bytes accessed | tf_op | source)
XLA Modules:
  0.0 148.1 jit_solution(16763034666949441432)
XLA Ops:
  0.6 3.9 %collective-permute-start = (bf16[256,1024]{1,0:T(8,128)(2,1)}, bf16[256,1024]{1,0:T(8,128)(2,1)S(1)}, u32[]{:S(2)}, u32[]{:S(2)}) collective-permute-start(bf16[256,1024]{1,0:T(8,128)(2,1)} %bitcast.39), channel_id=1, source_target_pairs={{0,1},{1,2},{2,3},{3,4},{4,5},{5,6},{6,7},{7,8},{8,9},{9,10},{10,1... | collective-permute-start | bytes 1572872 | tf_op jit(solution)/shard_map/ppermute | solution.py:599
  4.6 1.3 collective-permute-start.1
  5.9 1.4 fusion.9
  8.6 1.2 pad_add_fusion.counts_ref
  9.8 7.6 %shard_map.77 = (bf16[256,3072]{1,0:T(8,128)(2,1)}, bf16[1024,256]{1,0:T(8,128)(2,1)}) custom-call(bf16[256,1024]{1,0:T(8,128)(2,1)} %bitcast.41, bf16[1024,3072]{1,0:T(8,128)(2,1)} %wv_ref.1), custom_call_target="tpu_custom_call" | custom-call | flops 2147483648 | bytes 8388608 | tf_op jit(solution)/shard_map/pallas_call | solution.py:74
  17.5 2.7 %collective-permute-done.1.right_ref = bf16[256,1024]{1,0:T(8,128)(2,1)S(1)} collective-permute-done((bf16[256,1024]{1,0:T(8,128)(2,1)}, bf16[256,1024]{1,0:T(8,128)(2,1)S(1)}, u32[]{:S(2)}, u32[]{:S(2)}) %collective-permute-start.1) | collective-permute-done | bytes 524320 | tf_op jit(solution)/shard_map/ppermute | solution.py:600
  21.0 14.6 %shard_map.78 = (bf16[512,1024]{1,0:T(8,128)(2,1)}, bf16[768,1024]{1,0:T(8,128)(2,1)}, bf16[768,1024]{1,0:T(8,128)(2,1)}, f32[256,1024]{1,0:T(8,128)}, f32[256,1...) custom-call(s32[3]{0:T(128)} %pad_add_fusion.counts_ref, bf16[256,1024]{1,0:T(8,128)(2,1)} %copy-done.5, ...), custom_call_target="tpu_custom_call" | custom-call | flops 6442450944 | bytes 12582912 | tf_op jit(solution)/shard_map/pallas_call | solution.py:234
  35.6 3.1 %collective-permute-start.2 = (f32[256,128]{1,0:T(8,128)}, f32[256,128]{1,0:T(8,128)S(1)}, u32[]{:S(2)}, u32[]{:S(2)}) collective-permute-start(f32[256,128]{1,0:T(8,128)} %get-tuple-element.25.own_ref), channel_id=1, source_target_pairs={{0,64},{64,0},{1,65},{65,1},{2,66},{66,2},{3,67},{67,3},{4,68},{68... | collective-permute-start | bytes 393224 | tf_op jit(solution)/shard_map/ppermute | solution.py:615
  38.7 3.7 %collective-permute-done.2.near_ref = f32[256,128]{1,0:T(8,128)S(1)} collective-permute-done((f32[256,128]{1,0:T(8,128)}, f32[256,128]{1,0:T(8,128)S(1)}, u32[]{:S(2)}, u32[]{:S(2)}) %collective-permute-start.2) | collective-permute-done | bytes 131104 | tf_op jit(solution)/shard_map/ppermute | solution.py:615
  43.4 4.2 %fusion.3.qhalo_ref = bf16[512,1024]{1,0:T(8,128)(2,1)} fusion(bf16[512,1024]{1,0:T(8,128)(2,1)} %get-tuple-element.26, bf16[1024,3072]{1,0:T(8,128)(2,1)} %wv_ref.1), kind=kOutput, calls=%fused_computation.7 | convolution fusion | flops 1074266112 | bytes 4194304 | tf_op jit(solution)/shard_map/dot_general | solution.py:43
  48.3 5.4 %shard_map.79 = (f32[256,128]{1,0:T(8,128)}, bf16[256,256]{1,0:T(8,128)(2,1)}, bf16[256,1024]{1,0:T(8,128)(2,1)}, bf16[1024,256]{1,0:T(8,128)(2,1)}) custom-call(s32[3]{0:T(128)} %pad_add_fusion.counts_ref, f32[256,128]{1,0:T(8,128)} %get-tuple-element.25.own_ref, f32[256,128]{1,0:T(8,128)} %copy-done.1, f32[2,256,128]{2,1,0:T(8,128)} %copy-done.4, ...), custom_call_target="tpu_custom_call" | custom-call | tf_op jit(solution)/shard_map/pallas_call | solution.py:352
  53.7 3.6 %collective-permute-start.4 = (bf16[256,256]{1,0:T(8,128)(2,1)}, bf16[256,256]{1,0:T(8,128)(2,1)S(1)}, u32[]{:S(2)}, u32[]{:S(2)}) collective-permute-start(bf16[256,256]{1,0:T(8,128)(2,1)} %get-tuple-element.36.packed_ref.own_ref), channel_id=1, source_target_pairs={{0,1},{1,2},{2,3},{3,4},{4,5},{5,6},{6,7},{7,8},{8,9},{9,10},{10,1... | collective-permute-start | bytes 393224 | tf_op jit(solution)/shard_map/ppermute | solution.py:623
  57.3 1.3 collective-permute-start.5
  58.7 8.1 %shard_map.80 = bf16[1024,256]{1,0:T(8,128)(2,1)} custom-call(s32[3]{0:T(128)} %pad_add_fusion.counts_ref, bf16[256,3072]{1,0:T(8,128)(2,1)} %get-tuple-element.24.q_ref.k_ref.v_ref, bf16[768,1024]{1,0:T(8,128)(2,1)} %get-tuple-element.33.kcat_ref, bf16[768,1024]{1,0:T(8,128)(2,1)} %get-tuple-element.34.vcat_ref, ...), custom_call_target="tpu_custom_call" | custom-call | flops 6442450944 | bytes 5242880 | tf_op jit(solution)/shard_map/pallas_call | solution.py:419
  67.8 1.4 collective-permute-done.8
  70.6 1.2 pad_maximum_fusion
  71.8 13.3 %all-to-all-start = ((bf16[64,8,1280]{2,1,0:T(8,128)(2,1)}), bf16[64,8,1280]{2,1,0:T(8,128)(2,1)S(1)}, u32[]{:S(2)}, u32[]{:S(2)}) async-start(bf16[64,8,1280]{2,1,0:T(8,128)(2,1)} %bitcast.13), calls=%async_computation | async-start | bytes 2621440 | tf_op jit(solution)/shard_map/all_to_all | solution.py:584
  85.0 11.2 %shard_map.81 = bf16[2,1024,256]{2,1,0:T(8,128)(2,1)} custom-call(s32[3]{0:T(128)} %pad_add_fusion.counts_ref, bf16[256,3072]{1,0:T(8,128)(2,1)} %get-tuple-element.24.q_ref.k_ref.v_ref, bf16[256,3072]{1,0:T(8,128)(2,1)} %get-tuple-element.24.q_ref.k_ref.v_ref, bf16[256,3072]{1,0:T(8,128)(2,1)} %get-tuple-element.24.q_ref.k_ref.v_ref, ...), custom_call_target="tpu_custom_call" | custom-call | flops 9663676416 | bytes 5242880 | tf_op jit(solution)/shard_map/pallas_call | solution.py:523
  96.2 10.5 %all-to-all-done = bf16[64,8,1280]{2,1,0:T(8,128)(2,1)S(1)} async-done(((bf16[64,8,1280]{2,1,0:T(8,128)(2,1)}), bf16[64,8,1280]{2,1,0:T(8,128)(2,1)S(1)}, u32[]{:S(2)}, u32[]{:S(2)}) %all-to-all-start) | async-done | bytes 1310752 | tf_op jit(solution)/shard_map/all_to_all | solution.py:584
  106.8 2.0 %fusion.11 = f32[512,2048]{1,0:T(8,128)S(1)} fusion(bf16[512,256]{1,0:T(8,128)(2,1)S(1)} %bitcast.30, bf16[2048,256]{1,0:T(8,128)(2,1)} %bitcast.32), kind=kOutput, calls=%fused_computation.23 | convolution fusion | flops 536870912 | bytes 5505024 | tf_op jit(solution)/shard_map/dot_general | solution.py:47
  109.6 2.1 %fusion = bf16[64,8,2048]{2,1,0:T(8,128)(2,1)} fusion(f32[512,2048]{1,0:T(8,128)S(1)} %fusion.11, bf16[512,256]{1,0:T(8,128)(2,1)S(1)} %collective-permute-done.6, bf16[2048,256]{1,0:T(8,128)(2,1)S(1)} %collective-permute-done.9), kind=kOutput, calls=%fused_computation.2 | convolution fusion | flops 538968064 | bytes 7602176 | tf_op jit(solution)/shard_map/dot_general | solution.py:47
  111.7 5.4 %all-to-all-start.1 = ((bf16[64,8,2048]{2,1,0:T(8,128)(2,1)}), bf16[64,8,2048]{2,1,0:T(8,128)(2,1)S(1)}, u32[]{:S(2)}, u32[]{:S(2)}) async-start(bf16[64,8,2048]{2,1,0:T(8,128)(2,1)} %fusion), calls=%async_computation.1 | async-start | bytes 4194304 | tf_op jit(solution)/shard_map/all_to_all | solution.py:584
  119.1 1.3 fusion.7
  120.3 26.8 %all-to-all-done.1 = bf16[64,8,2048]{2,1,0:T(8,128)(2,1)S(1)} async-done(((bf16[64,8,2048]{2,1,0:T(8,128)(2,1)}), bf16[64,8,2048]{2,1,0:T(8,128)(2,1)S(1)}, u32[]{:S(2)}, u32[]{:S(2)}) %all-to-all-start.1) | async-done | bytes 2097184 | tf_op jit(solution)/shard_map/all_to_all | solution.py:584
  (42 shorter events, 8.7 us)
Async XLA Ops:
  0.6 16.8 %collective-permute-start = (bf16[256,1024]{1,0:T(8,128)(2,1)}, bf16[256,1024]{1,0:T(8,128)(2,1)S(1)}, u32[]{:S(2)}, u32[]{:S(2)}) collective-permute-start(bf16[256,1024]{1,0:T(8,128)(2,1)} %bitcast.39), channel_id=1, source_target_pairs={{0,1},{1,2},{2,3},{3,4},{4,5},{5,6},{6,7},{7,8},{8,9},{9,10},{10,1... | collective-permute-start | bytes 1572872 | tf_op jit(solution)/shard_map/ppermute | solution.py:599
  4.6 15.6 %collective-permute-start.1 = (bf16[256,1024]{1,0:T(8,128)(2,1)}, bf16[256,1024]{1,0:T(8,128)(2,1)S(1)}, u32[]{:S(2)}, u32[]{:S(2)}) collective-permute-start(bf16[256,1024]{1,0:T(8,128)(2,1)} %bitcast.40), channel_id=1, source_target_pairs={{1,0},{2,1},{3,2},{4,3},{5,4},{6,5},{7,6},{8,7},{9,8},{10,9},{11,1... | collective-permute-start | bytes 1572872 | tf_op jit(solution)/shard_map/ppermute | solution.py:600
  17.5 2.8 %copy-start.5 = (bf16[256,1024]{1,0:T(8,128)(2,1)}, bf16[256,1024]{1,0:T(8,128)(2,1)S(1)}, u32[]{:S(2)}) copy-start(bf16[256,1024]{1,0:T(8,128)(2,1)S(1)} %collective-permute-done.left_ref) | copy-start | bytes 1572868
  20.2 0.8 copy-start.6
  35.6 6.8 %collective-permute-start.2 = (f32[256,128]{1,0:T(8,128)}, f32[256,128]{1,0:T(8,128)S(1)}, u32[]{:S(2)}, u32[]{:S(2)}) collective-permute-start(f32[256,128]{1,0:T(8,128)} %get-tuple-element.25.own_ref), channel_id=1, source_target_pairs={{0,64},{64,0},{1,65},{65,1},{2,66},{66,2},{3,67},{67,3},{4,68},{68... | collective-permute-start | bytes 393224 | tf_op jit(solution)/shard_map/ppermute | solution.py:615
  42.4 5.2 %copy-start.1 = (f32[256,128]{1,0:T(8,128)}, f32[256,128]{1,0:T(8,128)S(1)}, u32[]{:S(2)}) copy-start(f32[256,128]{1,0:T(8,128)S(1)} %collective-permute-done.2.near_ref) | copy-start | bytes 393220
  43.3 4.3 %collective-permute-start.3 = (f32[2,256,128]{2,1,0:T(8,128)S(1)}, f32[2,256,128]{2,1,0:T(8,128)S(1)}, u32[]{:S(2)}, u32[]{:S(2)}) collective-permute-start(f32[2,256,128]{2,1,0:T(8,128)S(1)} %pad_maximum_fusion.1), channel_id=1, source_target_pairs={{0,32},{32,0},{1,33},{33,1},{2,34},{34,2},{3,35},{35,3},{4,36},{36... | collective-permute-start | bytes 786440 | tf_op jit(solution)/shard_map/ppermute | solution.py:573
  47.6 0.7 copy-start.4
  53.7 13.1 %collective-permute-start.4 = (bf16[256,256]{1,0:T(8,128)(2,1)}, bf16[256,256]{1,0:T(8,128)(2,1)S(1)}, u32[]{:S(2)}, u32[]{:S(2)}) collective-permute-start(bf16[256,256]{1,0:T(8,128)(2,1)} %get-tuple-element.36.packed_ref.own_ref), channel_id=1, source_target_pairs={{0,1},{1,2},{2,3},{3,4},{4,5},{5,6},{6,7},{7,8},{8,9},{9,10},{10,1... | collective-permute-start | bytes 393224 | tf_op jit(solution)/shard_map/ppermute | solution.py:623
  57.3 9.5 %collective-permute-start.5 = (bf16[256,256]{1,0:T(8,128)(2,1)}, bf16[256,256]{1,0:T(8,128)(2,1)S(1)}, u32[]{:S(2)}, u32[]{:S(2)}) collective-permute-start(bf16[256,256]{1,0:T(8,128)(2,1)} %get-tuple-element.36.packed_ref.own_ref), channel_id=1, source_target_pairs={{1,0},{2,1},{3,2},{4,3},{5,4},{6,5},{7,6},{8,7},{9,8},{10,9},{11,1... | collective-permute-start | bytes 393224 | tf_op jit(solution)/shard_map/ppermute | solution.py:624
  58.6 8.5 %copy-start.2 = (bf16[1024,256]{1,0:T(8,128)(2,1)S(1)}, bf16[1024,256]{1,0:T(8,128)(2,1)}, u32[]{:S(2)}) copy-start(bf16[1024,256]{1,0:T(8,128)(2,1)} %get-tuple-element.32) | copy-start | bytes 1572868
  58.7 8.5 %copy-start.3 = (bf16[1024,256]{1,0:T(8,128)(2,1)S(1)}, bf16[1024,256]{1,0:T(8,128)(2,1)}, u32[]{:S(2)}) copy-start(bf16[1024,256]{1,0:T(8,128)(2,1)} %get-tuple-element.38) | copy-start | bytes 1572868
  66.8 3.2 %copy-start.7 = (bf16[256,256]{1,0:T(8,128)(2,1)}, bf16[256,256]{1,0:T(8,128)(2,1)S(1)}, u32[]{:S(2)}) copy-start(bf16[256,256]{1,0:T(8,128)(2,1)S(1)} %collective-permute-done.4.left_ref) | copy-start | bytes 393220
  66.8 3.2 %copy-start.8 = (bf16[256,256]{1,0:T(8,128)(2,1)}, bf16[256,256]{1,0:T(8,128)(2,1)S(1)}, u32[]{:S(2)}) copy-start(bf16[256,256]{1,0:T(8,128)(2,1)S(1)} %collective-permute-done.5.right_ref) | copy-start | bytes 393220
  66.8 2.7 %collective-permute-start.7 = (bf16[1024,256]{1,0:T(8,128)(2,1)}, bf16[1024,256]{1,0:T(8,128)(2,1)S(1)}, u32[]{:S(2)}, u32[]{:S(2)}) collective-permute-start(bf16[1024,256]{1,0:T(8,128)(2,1)} %shard_map.80), channel_id=1, source_target_pairs={{0,32},{32,0},{1,33},{33,1},{2,34},{34,2},{3,35},{35,3},{4,36},{36... | collective-permute-start | bytes 1572872 | tf_op jit(solution)/shard_map/ppermute | solution.py:573
  67.2 2.9 %copy-start = (bf16[1024,256]{1,0:T(8,128)(2,1)S(1)}, bf16[1024,256]{1,0:T(8,128)(2,1)}, u32[]{:S(2)}) copy-start(bf16[1024,256]{1,0:T(8,128)(2,1)} %shard_map.80) | copy-start | bytes 1572868
  67.2 2.0 %collective-permute-start.8 = (bf16[512,256]{1,0:T(8,128)(2,1)S(1)}, bf16[512,256]{1,0:T(8,128)(2,1)S(1)}, u32[]{:S(2)}, u32[]{:S(2)}) collective-permute-start(bf16[512,256]{1,0:T(8,128)(2,1)S(1)} %bitcast.38), channel_id=1, source_target_pairs={{0,32},{32,0},{1,33},{33,1},{2,34},{34,2},{3,35},{35,3},{4,36},{36... | collective-permute-start | bytes 786440 | tf_op jit(solution)/shard_map/ppermute | solution.py:573
  67.6 2.0 %collective-permute-start.6 = (bf16[512,256]{1,0:T(8,128)(2,1)S(1)}, bf16[512,256]{1,0:T(8,128)(2,1)S(1)}, u32[]{:S(2)}, u32[]{:S(2)}) collective-permute-start(bf16[512,256]{1,0:T(8,128)(2,1)S(1)} %bitcast.37), channel_id=1, source_target_pairs={{0,32},{32,0},{1,33},{33,1},{2,34},{34,2},{3,35},{35,3},{4,36},{36... | collective-permute-start | bytes 786440 | tf_op jit(solution)/shard_map/ppermute | solution.py:573
  71.8 35.0 %all-to-all-start = ((bf16[64,8,1280]{2,1,0:T(8,128)(2,1)}), bf16[64,8,1280]{2,1,0:T(8,128)(2,1)S(1)}, u32[]{:S(2)}, u32[]{:S(2)}) async-start(bf16[64,8,1280]{2,1,0:T(8,128)(2,1)} %bitcast.13), calls=%async_computation | async-start | bytes 2621440 | tf_op jit(solution)/shard_map/all_to_all | solution.py:584
  106.8 2.9 %collective-permute-start.9 = (bf16[2048,256]{1,0:T(8,128)(2,1)}, bf16[2048,256]{1,0:T(8,128)(2,1)S(1)}, u32[]{:S(2)}, u32[]{:S(2)}) collective-permute-start(bf16[2048,256]{1,0:T(8,128)(2,1)} %bitcast.31), channel_id=1, source_target_pairs={{0,32},{32,0},{1,33},{33,1},{2,34},{34,2},{3,35},{35,3},{4,36},{36... | collective-permute-start | bytes 3145736 | tf_op jit(solution)/shard_map/ppermute | solution.py:573
  111.7 35.4 %all-to-all-start.1 = ((bf16[64,8,2048]{2,1,0:T(8,128)(2,1)}), bf16[64,8,2048]{2,1,0:T(8,128)(2,1)S(1)}, u32[]{:S(2)}, u32[]{:S(2)}) async-start(bf16[64,8,2048]{2,1,0:T(8,128)(2,1)} %fusion), calls=%async_computation.1 | async-start | bytes 4194304 | tf_op jit(solution)/shard_map/all_to_all | solution.py:584

commit v3 on v2

--- a/solution.py
+++ b/solution.py
@@ -15,7 +15,6 @@
 HEAD_WIDTH = 64
 PAIR = 128
 NEVER = -1e30
-VMEM_BYTES = 56 * 1024 * 1024
 
 alpha_fair = 0.95
 smooth_width = 0.0625
@@ -87,7 +86,7 @@
             jax.ShapeDtypeStruct((width, rows), BF),
         ],
         scratch_shapes=[pltpu.VMEM((rows, width), BF)],
-        compiler_params=pltpu.CompilerParams(vmem_limit_bytes=VMEM_BYTES),
+        compiler_params=pltpu.CompilerParams(vmem_limit_bytes=10 * 1024 * 1024),
         cost_estimate=pl.CostEstimate(
             flops=2 * rows * width * width * 4, bytes_accessed=8 << 20, transcendentals=0
         ),
@@ -266,7 +265,7 @@
             jax.ShapeDtypeStruct((BLOCK, 128), F32),
         ],
         scratch_shapes=[pltpu.VMEM((4, window, BLOCK), BF), pltpu.VMEM((128, BLOCK), F32)],
-        compiler_params=pltpu.CompilerParams(vmem_limit_bytes=VMEM_BYTES),
+        compiler_params=pltpu.CompilerParams(vmem_limit_bytes=28 * 1024 * 1024),
         cost_estimate=pl.CostEstimate(
             flops=6 << 30, bytes_accessed=12 << 20, transcendentals=3 << 20
         ),
@@ -359,7 +358,7 @@
             jax.ShapeDtypeStruct((BLOCK, 1024), BF),
             jax.ShapeDtypeStruct((1024, 256), BF),
         ],
-        compiler_params=pltpu.CompilerParams(vmem_limit_bytes=VMEM_BYTES),
+        compiler_params=pltpu.CompilerParams(vmem_limit_bytes=12 * 1024 * 1024),
     )(counts, own, near, others, target, attended, hidden, stats, w_out, readout_weight)
 
 
@@ -430,7 +429,7 @@
         out_specs=pl.BlockSpec((WIDTH, BLOCK), lambda j: (j, 0)),
         out_shape=jax.ShapeDtypeStruct((1024, BLOCK), BF),
         scratch_shapes=[pltpu.VMEM((4, window, BLOCK), BF)],
-        compiler_params=pltpu.CompilerParams(vmem_limit_bytes=VMEM_BYTES),
+        compiler_params=pltpu.CompilerParams(vmem_limit_bytes=12 * 1024 * 1024),
         cost_estimate=pl.CostEstimate(
             flops=6 << 30, bytes_accessed=5 << 20, transcendentals=3 << 20
         ),
@@ -543,7 +542,7 @@
             pltpu.VMEM((4, window, BLOCK), BF),
             pltpu.VMEM((2 * WIN, 1024), BF),
         ],
-        compiler_params=pltpu.CompilerParams(vmem_limit_bytes=VMEM_BYTES),
+        compiler_params=pltpu.CompilerParams(vmem_limit_bytes=18 * 1024 * 1024),
         cost_estimate=pl.CostEstimate(
             flops=9 << 30, bytes_accessed=5 << 20, transcendentals=3 << 20
         ),
@@ -613,9 +612,9 @@
         scalars, from_left, from_right, latent_own, w_qkv, projected, w_out, readout_weight
     )
     near = lax.ppermute(forecast, "x_hi", SWAP)
+    qhalo = dot_nn(normed_halo, w_qkv[:, :1024]).astype(BF)
+    near, qhalo = lax.optimization_barrier((near, qhalo))
     others = swap_core(jnp.stack([forecast, near]))
-    qhalo = dot_nn(normed_halo, w_qkv[:, :1024]).astype(BF)
-    others, qhalo = lax.optimization_barrier((others, qhalo))
     crps_whole, packed, grad, small = score(
         scalars, forecast, near, others, target, attended, hidden, stats, w_out, readout_weight
     )
@@ -648,8 +647,9 @@
         w_out,
         readout_weight,
     )
-    pairs, first = lax.optimization_barrier((pairs, first))
-    second = add_up(scatter(partial_of(pairs.reshape(2048, BLOCK)).astype(BF)))
+    second_part = partial_of(pairs.reshape(2048, BLOCK)).astype(BF)
+    second_part, first = lax.optimization_barrier((second_part, first))
+    second = add_up(scatter(second_part))
     first = add_up(first)
     grad_out = lax.dot_general(
         first[:, 1024:1152],

time: 149 us -> 156 us (1.047)
  local copies, waits for them, and re-layouts: 4.71 us -> 19.7 us
  Pallas kernels: 47 us -> 35.6 us
  waiting for transfers between devices: 46.3 us -> 50.7 us
  matrix products: 10.4 us -> 7.58 us
    unnamed x19 -> x63, local copies, waits for them, and re-layouts: 2.24 us -> 18.1 us
    all_to_all x2, waiting for transfers between devices: 37.3 us -> 44.4 us  [scatter(): lax.all_to_all(partial.reshape(64, 8, columns), CHIPS, split_axis=0, conc...]
    pallas_call x1, Pallas kernels: 7.64 us -> 3.78 us  [project(): pl.pallas_call(project_kernel, grid=(6,), in_specs=[pl.BlockSpec((rows, w...]
    pallas_call x1, Pallas kernels: 14.6 us -> 11.9 us  [forward(): pl.pallas_call(forward_kernel, grid=(4,), in_specs=[pl.BlockSpec(memory_s...]
    ppermute x1, waiting for transfers between devices: 3.66 us -> 1.19 us  [per_device(): near = lax.ppermute(forecast, 'x_hi', SWAP)]
    pallas_call x1, Pallas kernels: 5.37 us -> 3.36 us  [score(): pl.pallas_call(score_kernel, in_specs=[pl.BlockSpec(memory_space=pltpu.SM...]
    dot_general x1, matrix products: 4.16 us -> 2.24 us  [dot_nn(): lax.dot_general(left, right, (((1,), (0,)), ((), ())), preferred_element_...]
  transfers between devices with their start and end apart: 12 -> 12, of which waited for: 7 -> 7; matrix products, arithmetic and copies ran while one was open for 8% -> 7% of each run, Pallas kernels for 18% -> 7%
where the time goes in v3:
time: 156 us; the launch traced here: 155 us
  waiting for transfers between devices  50.7 us (32%)
  Pallas kernels  35.6 us (23%)
  starting transfers between devices  33.6 us (22%)
  local copies, waits for them, and re-layouts  19.7 us (13%)
  matrix products  7.58 us (5%)
  other arithmetic  5.22 us (3%)
  between operations  2.29 us (1%)
    all_to_all x2, waiting for transfers between devices, scatter(): lax.all_to_all(partial.reshape(64, 8, columns), CHIPS, split_axis=0, conc...  44.4 us
    all_to_all x2, starting transfers between devices, scatter(): lax.all_to_all(partial.reshape(64, 8, columns), CHIPS, split_axis=0, conc...  19.2 us
    unnamed x63, local copies, waits for them, and re-layouts  18.1 us
    pallas_call x1, Pallas kernels, forward(): pl.pallas_call(forward_kernel, grid=(4,), in_specs=[pl.BlockSpec(memory_s...  11.9 us
    pallas_call x1, Pallas kernels, key_grads(): pl.pallas_call(key_kernel, grid=(4,), in_specs=[pl.BlockSpec(memory_space...  9.66 us
    pallas_call x1, Pallas kernels, query_grads(): pl.pallas_call(query_kernel, grid=(4,), in_specs=[pl.BlockSpec(memory_spa...  6.89 us
    dot_general x4, matrix products, dot_nt(): lax.dot_general(left, right, (((1,), (1,)), ((), ())), preferred_element_...  5.04 us
    ppermute x1, starting transfers between devices, per_device(): from_left = lax.ppermute(latent_own, CELLS, up)  3.94 us
  transfers between devices with their start and end apart: 12, of which 7 were waited for; matrix products, arithmetic and copies ran while one was open for 7% of the time, Pallas kernels for 7%

profile of v3, /device:TPU:0, one launch (start us, length us, event | category | flops | bytes accessed | tf_op | source)
XLA Modules:
  0.0 154.8 jit_solution(12577063609953296979)
XLA Ops:
  0.6 3.9 %collective-permute-start = (bf16[256,1024]{1,0:T(8,128)(2,1)}, bf16[256,1024]{1,0:T(8,128)(2,1)S(1)}, u32[]{:S(2)}, u32[]{:S(2)}) collective-permute-start(bf16[256,1024]{1,0:T(8,128)(2,1)} %bitcast.34), channel_id=1, source_target_pairs={{0,1},{1,2},{2,3},{3,4},{4,5},{5,6},{6,7},{7,8},{8,9},{9,10},{10,1... | collective-permute-start | bytes 1572872 | tf_op jit(solution)/shard_map/ppermute | solution.py:598
  4.6 1.3 collective-permute-start.1
  5.9 1.4 fusion.8
  9.4 2.8 %copy-done.13 = bf16[1024,3072]{1,0:T(8,128)(2,1)S(1)} copy-done((bf16[1024,3072]{1,0:T(8,128)(2,1)S(1)}, bf16[1024,3072]{1,0:T(8,128)(2,1)}, u32[]{:S(2)}) %copy-start.13) | copy-done | bytes 6291480
  13.2 3.8 %shard_map.77 = (bf16[256,3072]{1,0:T(8,128)(2,1)S(1)}, bf16[1024,256]{1,0:T(8,128)(2,1)S(1)}) custom-call(bf16[256,1024]{1,0:T(8,128)(2,1)S(1)} %bitcast.36, bf16[1024,3072]{1,0:T(8,128)(2,1)S(1)} %copy-done.13), custom_call_target="tpu_custom_call" | custom-call | flops 2147483648 | bytes 8388608 | tf_op jit(solution)/shard_map/pallas_call | solution.py:73
  18.6 1.7 %collective-permute-done.1.right_ref = bf16[256,1024]{1,0:T(8,128)(2,1)} collective-permute-done((bf16[256,1024]{1,0:T(8,128)(2,1)}, bf16[256,1024]{1,0:T(8,128)(2,1)}, u32[]{:S(2)}, u32[]{:S(2)}) %collective-permute-start.1) | collective-permute-done | bytes 524320 | tf_op jit(solution)/shard_map/ppermute | solution.py:599
  20.4 2.8 %copy-done.14 = bf16[1024,3072]{1,0:T(8,128)(2,1)S(1)} copy-done((bf16[1024,3072]{1,0:T(8,128)(2,1)S(1)}, bf16[1024,3072]{1,0:T(8,128)(2,1)}, u32[]{:S(2)}) %copy-start.14) | copy-done | bytes 6291480
  24.2 11.9 %shard_map.78 = (bf16[512,1024]{1,0:T(8,128)(2,1)S(1)}, bf16[768,1024]{1,0:T(8,128)(2,1)S(1)}, bf16[768,1024]{1,0:T(8,128)(2,1)S(1)}, f32[256,1024]{1,0:T(8,128)...) custom-call(s32[3]{0:T(128)S(1)} %pad_add_fusion.counts_ref, ...), custom_call_target="tpu_custom_call" | custom-call | flops 6442450944 | bytes 12582912 | tf_op jit(solution)/shard_map/pallas_call | solution.py:233
  37.3 3.1 %collective-permute-start.2 = (f32[256,128]{1,0:T(8,128)S(1)}, f32[256,128]{1,0:T(8,128)S(1)}, u32[]{:S(2)}, u32[]{:S(2)}) collective-permute-start(f32[256,128]{1,0:T(8,128)S(1)} %get-tuple-element.25.own_ref), channel_id=1, source_target_pairs={{0,64},{64,0},{1,65},{65,1},{2,66},{66,2},{3,67},{67,3},{4,68},{68... | collective-permute-start | bytes 393224 | tf_op jit(solution)/shard_map/ppermute | solution.py:614
  40.4 2.2 %fusion.2.qhalo_ref = bf16[512,1024]{1,0:T(8,128)(2,1)} fusion(bf16[512,1024]{1,0:T(8,128)(2,1)S(1)} %get-tuple-element.26, bf16[1024,3072]{1,0:T(8,128)(2,1)S(1)} %copy-done.14), kind=kOutput, calls=%fused_computation.6 | convolution fusion | flops 1074266112 | bytes 4194304 | tf_op jit(solution)/shard_map/dot_general | solution.py:42
  45.2 1.9 %collective-permute-done.3.others_ref = f32[2,256,128]{2,1,0:T(8,128)} collective-permute-done((f32[2,256,128]{2,1,0:T(8,128)}, f32[2,256,128]{2,1,0:T(8,128)}, u32[]{:S(2)}, u32[]{:S(2)}) %collective-permute-start.3) | collective-permute-done | bytes 262176 | tf_op jit(solution)/shard_map/ppermute | solution.py:572
  50.9 3.4 %shard_map.79 = (f32[256,128]{1,0:T(8,128)S(1)}, bf16[256,256]{1,0:T(8,128)(2,1)S(1)}, bf16[256,1024]{1,0:T(8,128)(2,1)S(1)}, bf16[1024,256]{1,0:T(8,128)(2,1)S(1)}) custom-call(s32[3]{0:T(128)S(1)} %pad_add_fusion.counts_ref, f32[256,128]{1,0:T(8,128)S(1)} %get-tuple-element.25.own_ref, f32[256,128]{1,0:T(8,128)S(1)} %copy-done.5, ...), custom_call_target="tpu_custom_call" | custom-call | tf_op jit(solution)/shard_map/pallas_call | solution.py:351
  54.9 3.6 %collective-permute-start.4 = (bf16[256,256]{1,0:T(8,128)(2,1)S(1)}, bf16[256,256]{1,0:T(8,128)(2,1)S(1)}, u32[]{:S(2)}, u32[]{:S(2)}) collective-permute-start(bf16[256,256]{1,0:T(8,128)(2,1)S(1)} %get-tuple-element.36.packed_ref.own_ref), channel_id=1, source_target_pairs={{0,1},{1,2},{2,3},{3,4},{4,5},{5,6},{6,7},{7,8},{8,9},{9,10},{10,1... | collective-permute-start | bytes 393224 | tf_op jit(solution)/shard_map/ppermute | solution.py:622
  58.5 1.3 collective-permute-start.5
  59.9 6.9 %shard_map.80 = bf16[1024,256]{1,0:T(8,128)(2,1)S(1)} custom-call(s32[3]{0:T(128)S(1)} %pad_add_fusion.counts_ref, bf16[256,3072]{1,0:T(8,128)(2,1)S(1)} %copy-done.20, bf16[768,1024]{1,0:T(8,128)(2,1)S(1)} %copy-done.22, bf16[768,1024]{1,0:T(8,128)(2,1)S(1)} %copy-done.24, bf16[256,1024]{1,0:T(8,128)(2,1)S(1)} %get-tuple-element.35.grad_ref, ...), custom_call_target="tpu_custom_call" | custom-call | flops 6442450944 | bytes 5242880 | tf_op jit(solution)/shard_map/pallas_call | solution.py:418
  67.8 1.3 collective-permute-done.8
  72.4 9.7 %shard_map.81 = bf16[2,1024,256]{2,1,0:T(8,128)(2,1)S(1)} custom-call(s32[3]{0:T(128)S(1)} %pad_add_fusion.counts_ref, bf16[256,3072]{1,0:T(8,128)(2,1)S(1)} %copy-done.20, bf16[256,3072]{1,0:T(8,128)(2,1)S(1)} %copy-done.20, bf16[256,3072]{1,0:T(8,128)(2,1)S(1)} %copy-done.20, bf16[512,1024]{1,0:T(8,128)(2,1)S(1)} %copy-done.25, ...), custom_call_target="tpu_custom_call" | custom-call | flops 9663676416 | bytes 5242880 | tf_op jit(solution)/shard_map/pallas_call | solution.py:522
  82.3 13.9 %all-to-all-start = ((bf16[64,8,1280]{2,1,0:T(8,128)(2,1)}), bf16[64,8,1280]{2,1,0:T(8,128)(2,1)S(1)}, u32[]{:S(2)}, u32[]{:S(2)}) async-start(bf16[64,8,1280]{2,1,0:T(8,128)(2,1)} %bitcast.39), calls=%async_computation | async-start | bytes 2621440 | tf_op jit(solution)/shard_map/all_to_all | solution.py:583
  96.2 2.0 %fusion.10 = f32[512,2048]{1,0:T(8,128)S(1)} fusion(bf16[512,256]{1,0:T(8,128)(2,1)S(1)} %copy-done.30, bf16[2048,256]{1,0:T(8,128)(2,1)} %collective-permute-done.9), kind=kOutput, calls=%fused_computation.22 | convolution fusion | flops 536870912 | bytes 5505024 | tf_op jit(solution)/shard_map/dot_general | solution.py:46
  98.3 2.1 %add_convert_fusion = bf16[512,2048]{1,0:T(8,128)(2,1)} fusion(f32[512,2048]{1,0:T(8,128)S(1)} %fusion.10, bf16[512,256]{1,0:T(8,128)(2,1)S(1)} %bitcast.41, bf16[2048,256]{1,0:T(8,128)(2,1)S(1)} %bitcast.29), kind=kOutput, calls=%fused_computation.1 | convolution fusion | flops 538968064 | bytes 7602176 | tf_op jit(solution)/shard_map/dot_general | solution.py:46
  100.4 17.8 %all-to-all-done = bf16[64,8,1280]{2,1,0:T(8,128)(2,1)S(1)} async-done(((bf16[64,8,1280]{2,1,0:T(8,128)(2,1)}), bf16[64,8,1280]{2,1,0:T(8,128)(2,1)S(1)}, u32[]{:S(2)}, u32[]{:S(2)}) %all-to-all-start) | async-done | bytes 1310752 | tf_op jit(solution)/shard_map/all_to_all | solution.py:583
  119.2 5.3 %all-to-all-start.1 = ((bf16[64,8,2048]{2,1,0:T(8,128)(2,1)}), bf16[64,8,2048]{2,1,0:T(8,128)(2,1)S(1)}, u32[]{:S(2)}, u32[]{:S(2)}) async-start(bf16[64,8,2048]{2,1,0:T(8,128)(2,1)} %bitcast.38), calls=%async_computation.1 | async-start | bytes 4194304 | tf_op jit(solution)/shard_map/all_to_all | solution.py:583
  125.4 1.5 convert_reduce_fusion.1
  127.3 26.5 %all-to-all-done.1 = bf16[64,8,2048]{2,1,0:T(8,128)(2,1)S(1)} async-done(((bf16[64,8,2048]{2,1,0:T(8,128)(2,1)}), bf16[64,8,2048]{2,1,0:T(8,128)(2,1)S(1)}, u32[]{:S(2)}, u32[]{:S(2)}) %all-to-all-start.1) | async-done | bytes 2097184 | tf_op jit(solution)/shard_map/all_to_all | solution.py:583
  (86 shorter events, 20.2 us)
Async XLA Ops:
  0.6 17.2 %collective-permute-start = (bf16[256,1024]{1,0:T(8,128)(2,1)}, bf16[256,1024]{1,0:T(8,128)(2,1)S(1)}, u32[]{:S(2)}, u32[]{:S(2)}) collective-permute-start(bf16[256,1024]{1,0:T(8,128)(2,1)} %bitcast.34), channel_id=1, source_target_pairs={{0,1},{1,2},{2,3},{3,4},{4,5},{5,6},{6,7},{7,8},{8,9},{9,10},{10,1... | collective-permute-start | bytes 1572872 | tf_op jit(solution)/shard_map/ppermute | solution.py:598
  4.6 15.8 %collective-permute-start.1 = (bf16[256,1024]{1,0:T(8,128)(2,1)}, bf16[256,1024]{1,0:T(8,128)(2,1)}, u32[]{:S(2)}, u32[]{:S(2)}) collective-permute-start(bf16[256,1024]{1,0:T(8,128)(2,1)} %bitcast.35), channel_id=1, source_target_pairs={{1,0},{2,1},{3,2},{4,3},{5,4},{6,5},{7,6},{8,7},{9,8},{10,9},{11,1... | collective-permute-start | bytes 1572872 | tf_op jit(solution)/shard_map/ppermute | solution.py:599
  13.2 7.1 %copy-start = (bf16[1024,1024]{1,0:T(8,128)(2,1)S(1)}, bf16[1024,1024]{1,0:T(8,128)(2,1)}, u32[]{:S(2)}) copy-start(bf16[1024,1024]{1,0:T(8,128)(2,1)} %w_out_ref.5) | copy-start | bytes 6291460
  13.2 7.1 %copy-start.1 = (bf16[1024,128]{1,0:T(8,128)(2,1)S(1)}, bf16[1024,128]{1,0:T(8,128)(2,1)}, u32[]{:S(2)}) copy-start(bf16[1024,128]{1,0:T(8,128)(2,1)} %readout_ref.5) | copy-start | bytes 786436
  13.2 7.1 %copy-start.16 = (bf16[1,256,1024]{2,1,0:T(8,128)(2,1)S(1)}, bf16[1,256,1024]{2,1,0:T(8,128)(2,1)}, u32[]{:S(2)}) copy-start(bf16[1,256,1024]{2,1,0:T(8,128)(2,1)} %param.6) | copy-start | bytes 1572868
  37.3 5.4 %copy-start.9 = (f32[256,128]{1,0:T(8,128)}, f32[256,128]{1,0:T(8,128)S(1)}, u32[]{:S(2)}) copy-start(f32[256,128]{1,0:T(8,128)S(1)} %get-tuple-element.30.stats_ref) | copy-start | bytes 393220
  37.3 5.4 %copy-start.21 = (bf16[768,1024]{1,0:T(8,128)(2,1)}, bf16[768,1024]{1,0:T(8,128)(2,1)S(1)}, u32[]{:S(2)}) copy-start(bf16[768,1024]{1,0:T(8,128)(2,1)S(1)} %get-tuple-element.33.kcat_ref) | copy-start | bytes 4718596
  37.3 5.4 %copy-start.23 = (bf16[768,1024]{1,0:T(8,128)(2,1)}, bf16[768,1024]{1,0:T(8,128)(2,1)S(1)}, u32[]{:S(2)}) copy-start(bf16[768,1024]{1,0:T(8,128)(2,1)S(1)} %get-tuple-element.34.vcat_ref) | copy-start | bytes 4718596
  37.3 6.6 %collective-permute-start.2 = (f32[256,128]{1,0:T(8,128)S(1)}, f32[256,128]{1,0:T(8,128)S(1)}, u32[]{:S(2)}, u32[]{:S(2)}) collective-permute-start(f32[256,128]{1,0:T(8,128)S(1)} %get-tuple-element.25.own_ref), channel_id=1, source_target_pairs={{0,64},{64,0},{1,65},{65,1},{2,66},{66,2},{3,67},{67,3},{4,68},{68... | collective-permute-start | bytes 393224 | tf_op jit(solution)/shard_map/ppermute | solution.py:614
  45.2 1.9 %collective-permute-start.3 = (f32[2,256,128]{2,1,0:T(8,128)}, f32[2,256,128]{2,1,0:T(8,128)}, u32[]{:S(2)}, u32[]{:S(2)}) collective-permute-start(f32[2,256,128]{2,1,0:T(8,128)} %pad_maximum_fusion.1), channel_id=1, source_target_pairs={{0,32},{32,0},{1,33},{33,1},{2,34},{34,2},{3,35},{35,3},{4,36},{36... | collective-permute-start | bytes 786440 | tf_op jit(solution)/shard_map/ppermute | solution.py:572
  50.9 9.0 %copy-start.20 = (bf16[256,3072]{1,0:T(8,128)(2,1)S(1)}, bf16[256,3072]{1,0:T(8,128)(2,1)}, u32[]{:S(2)}) copy-start(bf16[256,3072]{1,0:T(8,128)(2,1)} %copy-done.19) | copy-start | bytes 4718596
  50.9 9.0 %copy-start.22 = (bf16[768,1024]{1,0:T(8,128)(2,1)S(1)}, bf16[768,1024]{1,0:T(8,128)(2,1)}, u32[]{:S(2)}) copy-start(bf16[768,1024]{1,0:T(8,128)(2,1)} %copy-done.21) | copy-start | bytes 4718596
  50.9 9.0 %copy-start.24 = (bf16[768,1024]{1,0:T(8,128)(2,1)S(1)}, bf16[768,1024]{1,0:T(8,128)(2,1)}, u32[]{:S(2)}) copy-start(bf16[768,1024]{1,0:T(8,128)(2,1)} %copy-done.23) | copy-start | bytes 4718596
  54.9 11.9 %collective-permute-start.4 = (bf16[256,256]{1,0:T(8,128)(2,1)S(1)}, bf16[256,256]{1,0:T(8,128)(2,1)S(1)}, u32[]{:S(2)}, u32[]{:S(2)}) collective-permute-start(bf16[256,256]{1,0:T(8,128)(2,1)S(1)} %get-tuple-element.36.packed_ref.own_ref), channel_id=1, source_target_pairs={{0,1},{1,2},{2,3},{3,4},{4,5},{5,6},{6,7},{7,8},{8,9},{9,10},{10,1... | collective-permute-start | bytes 393224 | tf_op jit(solution)/shard_map/ppermute | solution.py:622
  58.5 8.2 %collective-permute-start.5 = (bf16[256,256]{1,0:T(8,128)(2,1)S(1)}, bf16[256,256]{1,0:T(8,128)(2,1)S(1)}, u32[]{:S(2)}, u32[]{:S(2)}) collective-permute-start(bf16[256,256]{1,0:T(8,128)(2,1)S(1)} %get-tuple-element.36.packed_ref.own_ref), channel_id=1, source_target_pairs={{1,0},{2,1},{3,2},{4,3},{5,4},{6,5},{7,6},{8,7},{9,8},{10,9},{11,1... | collective-permute-start | bytes 393224 | tf_op jit(solution)/shard_map/ppermute | solution.py:623
  59.8 7.0 %copy-start.7 = (bf16[1024,256]{1,0:T(8,128)(2,1)S(1)}, bf16[1024,256]{1,0:T(8,128)(2,1)}, u32[]{:S(2)}) copy-start(bf16[1024,256]{1,0:T(8,128)(2,1)} %copy-done.6) | copy-start | bytes 1572868
  66.8 2.7 %collective-permute-start.7 = (bf16[1024,256]{1,0:T(8,128)(2,1)S(1)}, bf16[1024,256]{1,0:T(8,128)(2,1)S(1)}, u32[]{:S(2)}, u32[]{:S(2)}) collective-permute-start(bf16[1024,256]{1,0:T(8,128)(2,1)S(1)} %shard_map.80), channel_id=1, source_target_pairs={{0,32},{32,0},{1,33},{33,1},{2,34},{34,2},{3,35},{35,3},{4,36},{36... | collective-permute-start | bytes 1572872 | tf_op jit(solution)/shard_map/ppermute | solution.py:572
  67.0 2.2 %collective-permute-start.8 = (bf16[512,256]{1,0:T(8,128)(2,1)S(1)}, bf16[512,256]{1,0:T(8,128)(2,1)S(1)}, u32[]{:S(2)}, u32[]{:S(2)}) collective-permute-start(bf16[512,256]{1,0:T(8,128)(2,1)S(1)} %bitcast.43), channel_id=1, source_target_pairs={{0,32},{32,0},{1,33},{33,1},{2,34},{34,2},{3,35},{35,3},{4,36},{36... | collective-permute-start | bytes 786440 | tf_op jit(solution)/shard_map/ppermute | solution.py:572
  67.5 2.0 %collective-permute-start.6 = (bf16[512,256]{1,0:T(8,128)(2,1)S(1)}, bf16[512,256]{1,0:T(8,128)(2,1)S(1)}, u32[]{:S(2)}, u32[]{:S(2)}) collective-permute-start(bf16[512,256]{1,0:T(8,128)(2,1)S(1)} %bitcast.42), channel_id=1, source_target_pairs={{0,32},{32,0},{1,33},{33,1},{2,34},{34,2},{3,35},{35,3},{4,36},{36... | collective-permute-start | bytes 786440 | tf_op jit(solution)/shard_map/ppermute | solution.py:572
  82.1 14.1 %copy-start.30 = (bf16[512,256]{1,0:T(8,128)(2,1)S(1)}, bf16[512,256]{1,0:T(8,128)(2,1)}, u32[]{:S(2)}) copy-start(bf16[512,256]{1,0:T(8,128)(2,1)} %copy-done.29) | copy-start | bytes 786436
  82.1 14.1 %collective-permute-start.9 = (bf16[2048,256]{1,0:T(8,128)(2,1)S(1)}, bf16[2048,256]{1,0:T(8,128)(2,1)}, u32[]{:S(2)}, u32[]{:S(2)}) collective-permute-start(bf16[2048,256]{1,0:T(8,128)(2,1)S(1)} %bitcast.28), channel_id=1, source_target_pairs={{0,32},{32,0},{1,33},{33,1},{2,34},{34,2},{3,35},{35,3},{4,36},{36... | collective-permute-start | bytes 3145736 | tf_op jit(solution)/shard_map/ppermute | solution.py:572
  82.3 35.9 %all-to-all-start = ((bf16[64,8,1280]{2,1,0:T(8,128)(2,1)}), bf16[64,8,1280]{2,1,0:T(8,128)(2,1)S(1)}, u32[]{:S(2)}, u32[]{:S(2)}) async-start(bf16[64,8,1280]{2,1,0:T(8,128)(2,1)} %bitcast.39), calls=%async_computation | async-start | bytes 2621440 | tf_op jit(solution)/shard_map/all_to_all | solution.py:583
  118.2 6.4 %copy-start.12 = (f32[256,128]{1,0:T(8,128)S(1)}, f32[256,128]{1,0:T(8,128)}, u32[]{:S(2)}) copy-start(f32[256,128]{1,0:T(8,128)} %copy-done.11) | copy-start | bytes 393220
  119.2 34.5 %all-to-all-start.1 = ((bf16[64,8,2048]{2,1,0:T(8,128)(2,1)}), bf16[64,8,2048]{2,1,0:T(8,128)(2,1)S(1)}, u32[]{:S(2)}, u32[]{:S(2)}) async-start(bf16[64,8,2048]{2,1,0:T(8,128)(2,1)} %bitcast.38), calls=%async_computation.1 | async-start | bytes 4194304 | tf_op jit(solution)/shard_map/all_to_all | solution.py:583
  (19 other events, 29.4 us)

commit v4 on v3

--- a/solution.py
+++ b/solution.py
@@ -54,18 +54,40 @@
     return lax.broadcasted_iota(jnp.int32, shape, axis)
 
 
-def project_kernel(latent_ref, weight_ref, projected_ref, turned_ref, normed):
+FREE = pl.CostEstimate(flops=0, bytes_accessed=0, transcendentals=0)
+HBM = pl.BlockSpec(memory_space=pltpu.HBM)
+
+
+def fetches(weight_ref, buffer, arrived, width, first):
+    return [
+        pltpu.make_async_copy(
+            weight_ref.at[:, pl.ds(first + place * width, width)],
+            buffer.at[place],
+            arrived.at[place],
+        )
+        for place in range(buffer.shape[0])
+    ]
+
+
+def fetch_one(weight_ref, buffer, arrived, width, first, place):
+    start = pl.multiple_of(first + place * width, width)
+    return pltpu.make_async_copy(
+        weight_ref.at[:, pl.ds(start, width)], buffer.at[place], arrived.at[place]
+    )
+
+
+def project_kernel(latent_ref, weight_ref, projected_ref, turned_ref, normed, buffer, arrived):
     step = pl.program_id(0)
 
     @pl.when(step == 0)
     def _():
+        for copy in fetches(weight_ref, buffer, arrived, 512, 0):
+            copy.start()
         normed[...] = layer_norm(latent_ref[...])
-
-    projected_ref[...] = dot_nn(normed[...], weight_ref[...]).astype(BF)
-
-    @pl.when(step == 5)
-    def _():
         turned_ref[...] = normed[...].T
+
+    fetch_one(weight_ref, buffer, arrived, 512, 0, step).wait()
+    projected_ref[...] = dot_nn(normed[...], buffer[step]).astype(BF)
 
 
 def project(latent_own, w_qkv):
@@ -73,10 +95,7 @@
     return pl.pallas_call(
         project_kernel,
         grid=(6,),
-        in_specs=[
-            pl.BlockSpec((rows, width), lambda j: (0, 0)),
-            pl.BlockSpec((width, 512), lambda j: (0, j)),
-        ],
+        in_specs=[pl.BlockSpec((rows, width), lambda j: (0, 0)), HBM],
         out_specs=[
             pl.BlockSpec((rows, 512), lambda j: (0, j)),
             pl.BlockSpec((width, rows), lambda j: (0, 0)),
@@ -85,12 +104,92 @@
             jax.ShapeDtypeStruct((rows, 3 * width), BF),
             jax.ShapeDtypeStruct((width, rows), BF),
         ],
-        scratch_shapes=[pltpu.VMEM((rows, width), BF)],
-        compiler_params=pltpu.CompilerParams(vmem_limit_bytes=10 * 1024 * 1024),
+        scratch_shapes=[
+            pltpu.VMEM((rows, width), BF),
+            pltpu.VMEM((6, width, 512), BF),
+            pltpu.SemaphoreType.DMA((6,)),
+        ],
+        compiler_params=pltpu.CompilerParams(vmem_limit_bytes=16 * 1024 * 1024),
         cost_estimate=pl.CostEstimate(
             flops=2 * rows * width * width * 4, bytes_accessed=8 << 20, transcendentals=0
         ),
     )(latent_own, w_qkv)
+
+
+def halo_query_kernel(normed_ref, weight_ref, out_ref, buffer, arrived):
+    step = pl.program_id(0)
+
+    @pl.when(step == 0)
+    def _():
+        for copy in fetches(weight_ref, buffer, arrived, 256, 0):
+            copy.start()
+
+    fetch_one(weight_ref, buffer, arrived, 256, 0, step).wait()
+    out_ref[...] = dot_nn(normed_ref[...], buffer[step]).astype(BF)
+
+
+def halo_queries(normed_halo, w_qkv):
+    rows, width = normed_halo.shape
+    return pl.pallas_call(
+        halo_query_kernel,
+        grid=(4,),
+        in_specs=[pl.BlockSpec((rows, width), lambda j: (0, 0)), HBM],
+        out_specs=pl.BlockSpec((rows, 256), lambda j: (0, j)),
+        out_shape=jax.ShapeDtypeStruct((rows, width), BF),
+        scratch_shapes=[
+            pltpu.VMEM((4, width, 256), BF),
+            pltpu.SemaphoreType.DMA((4,)),
+        ],
+        compiler_params=pltpu.CompilerParams(vmem_limit_bytes=12 * 1024 * 1024),
+        cost_estimate=FREE,
+    )(normed_halo, w_qkv)
+
+
+def partial_kernel(
+    core_ref, normed_ref, normed_other_ref, piece_ref, other_ref, small_ref, small_other_ref,
+    out_ref,
+):
+    core = core_ref[0]
+    for top in range(2):
+        rows = slice(top * 256, (top + 1) * 256)
+        own = normed_ref[top, core]
+        near = normed_other_ref[top, core]
+        for first in range(0, piece_ref.shape[0], 512):
+            columns = slice(first, first + 512)
+            out_ref[rows, columns] = (
+                dot_nt(own, piece_ref[columns]) + dot_nt(near, other_ref[columns])
+            ).astype(BF)
+        if small_ref is not None:
+            out_ref[rows, piece_ref.shape[0] :] = (
+                small_ref[top, core].astype(F32) + small_other_ref[top, core].astype(F32)
+            ).astype(BF)
+
+
+def plain_partial_kernel(core_ref, normed_ref, normed_other_ref, piece_ref, other_ref, out_ref):
+    partial_kernel(
+        core_ref, normed_ref, normed_other_ref, piece_ref, other_ref, None, None, out_ref
+    )
+
+
+def partial_sums(core, turned, turned_other, piece, other, smalls=()):
+    by_core = lambda values: values.reshape(2, 2, 256, 256)
+    vmem = pl.BlockSpec(memory_space=pltpu.VMEM)
+    columns = piece.shape[0] + 256 * (len(smalls) // 2)
+    return pl.pallas_call(
+        partial_kernel if smalls else plain_partial_kernel,
+        in_specs=[pl.BlockSpec(memory_space=pltpu.SMEM)] + [vmem] * (4 + len(smalls)),
+        out_specs=vmem,
+        out_shape=jax.ShapeDtypeStruct((512, columns), BF),
+        compiler_params=pltpu.CompilerParams(vmem_limit_bytes=12 * 1024 * 1024),
+        cost_estimate=FREE,
+    )(
+        core.astype(jnp.int32).reshape(1),
+        by_core(turned),
+        by_core(turned_other),
+        piece,
+        other,
+        *(by_core(small) for small in smalls),
+    )
 
 
 def spare_lane(shape):
@@ -131,8 +230,7 @@
     left_ref,
     right_ref,
     latent_ref,
-    wk_ref,
-    wv_ref,
+    weight_ref,
     q_ref,
     k_ref,
     v_ref,
@@ -147,20 +245,27 @@
     forecast_ref,
     probs,
     stat_rows,
+    buffer,
+    arrived,
 ):
     step = pl.program_id(0)
 
     @pl.when(step == 0)
     def _():
+        copies = fetches(weight_ref, buffer, arrived, WIDTH, 1024)
+        for place in (0, 4, 1, 5, 2, 6, 3, 7):
+            copies[place].start()
         normed_ref[:WIN] = layer_norm(left_ref[...])
         normed_ref[WIN:] = layer_norm(right_ref[...])
         probs[...] = jnp.zeros_like(probs)
 
-    khalo = dot_nn(normed_ref[...], wk_ref[...]).astype(BF)
+    fetch_one(weight_ref, buffer, arrived, WIDTH, 1024, step).wait()
+    fetch_one(weight_ref, buffer, arrived, WIDTH, 1024, step + 4).wait()
+    khalo = dot_nn(normed_ref[...], buffer[step]).astype(BF)
     kcat_ref[:WIN] = khalo[:WIN]
     kcat_ref[WIN : WIN + BLOCK] = k_ref[...]
     kcat_ref[WIN + BLOCK :] = khalo[WIN:]
-    vhalo = dot_nn(normed_ref[...], wv_ref[...]).astype(BF)
+    vhalo = dot_nn(normed_ref[...], buffer[step + 4]).astype(BF)
     vcat_ref[:WIN] = vhalo[:WIN]
     vcat_ref[WIN : WIN + BLOCK] = v_ref[...]
     vcat_ref[WIN + BLOCK :] = vhalo[WIN:]
@@ -238,8 +343,7 @@
             whole(WIN, 1024),
             whole(WIN, 1024),
             whole(BLOCK, 1024),
-            part(1024, 4),
-            part(1024, 8),
+            HBM,
             part(BLOCK, 0),
             part(BLOCK, 4),
             part(BLOCK, 8),
@@ -264,7 +368,12 @@
             jax.ShapeDtypeStruct((BLOCK, 1024), BF),
             jax.ShapeDtypeStruct((BLOCK, 128), F32),
         ],
-        scratch_shapes=[pltpu.VMEM((4, window, BLOCK), BF), pltpu.VMEM((128, BLOCK), F32)],
+        scratch_shapes=[
+            pltpu.VMEM((4, window, BLOCK), BF),
+            pltpu.VMEM((128, BLOCK), F32),
+            pltpu.VMEM((8, 1024, WIDTH), BF),
+            pltpu.SemaphoreType.DMA((8,)),
+        ],
         compiler_params=pltpu.CompilerParams(vmem_limit_bytes=28 * 1024 * 1024),
         cost_estimate=pl.CostEstimate(
             flops=6 << 30, bytes_accessed=12 << 20, transcendentals=3 << 20
@@ -274,7 +383,6 @@
         left,
         right,
         latent_own,
-        w_qkv,
         w_qkv,
         projected,
         projected,
@@ -543,9 +651,7 @@
             pltpu.VMEM((2 * WIN, 1024), BF),
         ],
         compiler_params=pltpu.CompilerParams(vmem_limit_bytes=18 * 1024 * 1024),
-        cost_estimate=pl.CostEstimate(
-            flops=9 << 30, bytes_accessed=5 << 20, transcendentals=3 << 20
-        ),
+        cost_estimate=FREE,
     )(
         counts,
         projected,
@@ -572,12 +678,6 @@
     return lax.ppermute(values, "core", SWAP)
 
 
-def core_rows(values, core):
-    rows, columns = values.shape
-    chosen = lax.dynamic_slice_in_dim(values.reshape(2, 2, rows // 4, columns), core, 1, 1)
-    return chosen.reshape(rows // 2, columns)
-
-
 def scatter(partial):
     columns = partial.shape[1]
     return lax.all_to_all(partial.reshape(64, 8, columns), CHIPS, split_axis=0, concat_axis=0)
@@ -606,13 +706,12 @@
     scalars = jnp.stack([left_count, own_count, right_count])
 
     projected, turned = project(latent_own, w_qkv)
-    turned_own = core_rows(turned, core)
-    turned_other = swap_core(core_rows(turned, 1 - core))
+    turned_other = swap_core(turned)
     normed_halo, kcat, vcat, attended, stats, hidden, forecast = forward(
         scalars, from_left, from_right, latent_own, w_qkv, projected, w_out, readout_weight
     )
     near = lax.ppermute(forecast, "x_hi", SWAP)
-    qhalo = dot_nn(normed_halo, w_qkv[:, :1024]).astype(BF)
+    qhalo = halo_queries(normed_halo, w_qkv)
     near, qhalo = lax.optimization_barrier((near, qhalo))
     others = swap_core(jnp.stack([forecast, near]))
     crps_whole, packed, grad, small = score(
@@ -627,13 +726,9 @@
         (dquery, packed_left, packed_right)
     )
 
-    def partial_of(piece):
-        return dot_nt(turned_own, piece) + dot_nt(turned_other, swap_core(piece))
-
-    small_sum = core_rows(small, core).astype(F32) + swap_core(
-        core_rows(small, 1 - core)
-    ).astype(F32)
-    first_part = jnp.concatenate([partial_of(dquery), small_sum], axis=1).astype(BF)
+    first_part = partial_sums(
+        core, turned, turned_other, dquery, swap_core(dquery), (small, swap_core(small))
+    )
     first_part, scalars = lax.optimization_barrier((first_part, scalars))
     first = scatter(first_part)
     pairs = key_grads(
@@ -647,7 +742,8 @@
         w_out,
         readout_weight,
     )
-    second_part = partial_of(pairs.reshape(2048, BLOCK)).astype(BF)
+    pairs = pairs.reshape(2048, BLOCK)
+    second_part = partial_sums(core, turned, turned_other, pairs, swap_core(pairs))
     second_part, first = lax.optimization_barrier((second_part, first))
     second = add_up(scatter(second_part))
     first = add_up(first)

time: 156 us -> 143 us (0.917)
  waiting for transfers between devices: 50.7 us -> 38.4 us
  Pallas kernels: 35.6 us -> 45.8 us
  matrix products: 7.58 us -> 0.3 us
  local copies, waits for them, and re-layouts: 19.7 us -> 14.6 us
  starting transfers between devices: 33.6 us -> 37.4 us
  other arithmetic: 5.22 us -> 3.28 us
    all_to_all x2, waiting for transfers between devices: 44.4 us -> 28.7 us  [scatter(): lax.all_to_all(partial.reshape(64, 8, columns), CHIPS, split_axis=0, conc...]
    pallas_call x0 -> x3, Pallas kernels: none -> 9.37 us  [the longest x2 7.21 us: partial_sums(): pl.pallas_call(partial_kernel if smalls else plain_partial_kernel, in_spe...]
    dot_general x5 -> x0, matrix products: 7.28 us -> none  [the longest x4 5.04 us: dot_nt(): lax.dot_general(left, right, (((1,), (1,)), ((), ())), preferred_element_...]
    unnamed x63 -> x33, local copies, waits for them, and re-layouts: 18.1 us -> 13.1 us
    all_to_all x2, starting transfers between devices: 19.2 us -> 22.8 us  [scatter(): lax.all_to_all(partial.reshape(64, 8, columns), CHIPS, split_axis=0, conc...]
    ppermute x5, waiting for transfers between devices: 3.49 us -> 5.48 us  [swap_core(): return lax.ppermute(values, 'core', SWAP)]
  transfers between devices with their start and end apart: 12 -> 12, of which waited for: 7 -> 7; matrix products, arithmetic and copies ran while one was open for 7% -> 3% of each run, Pallas kernels for 7% -> 22%
where the time goes in v4:
time: 143 us; the launch traced here: 142 us
  Pallas kernels  45.8 us (32%)
  waiting for transfers between devices  38.4 us (27%)
  starting transfers between devices  37.4 us (26%)
  local copies, waits for them, and re-layouts  14.6 us (10%)
  other arithmetic  3.28 us (2%)
  between operations  2.14 us (1%)
    all_to_all x2, waiting for transfers between devices, scatter(): lax.all_to_all(partial.reshape(64, 8, columns), CHIPS, split_axis=0, conc...  28.7 us
    all_to_all x2, starting transfers between devices, scatter(): lax.all_to_all(partial.reshape(64, 8, columns), CHIPS, split_axis=0, conc...  22.8 us
    unnamed x33, local copies, waits for them, and re-layouts  13.1 us
    pallas_call x1, Pallas kernels, forward(): pl.pallas_call(forward_kernel, grid=(4,), in_specs=[pl.BlockSpec(memory_s...  11.7 us
    pallas_call x1, Pallas kernels, key_grads(): pl.pallas_call(key_kernel, grid=(4,), in_specs=[pl.BlockSpec(memory_space...  9.62 us
    pallas_call x1, Pallas kernels, query_grads(): pl.pallas_call(query_kernel, grid=(4,), in_specs=[pl.BlockSpec(memory_spa...  7.54 us
    pallas_call x2, Pallas kernels, partial_sums(): pl.pallas_call(partial_kernel if smalls else plain_partial_kernel, in_spe...  7.21 us
    ppermute x5, waiting for transfers between devices, swap_core(): return lax.ppermute(values, 'core', SWAP)  5.48 us
  transfers between devices with their start and end apart: 12, of which 7 were waited for; matrix products, arithmetic and copies ran while one was open for 3% of the time, Pallas kernels for 22%

profile of v4, /device:TPU:0, one launch (start us, length us, event | category | flops | bytes accessed | tf_op | source)
XLA Modules:
  0.0 141.9 jit_solution(8683141533194903832)
XLA Ops:
  0.6 3.9 %collective-permute-start = (bf16[256,1024]{1,0:T(8,128)(2,1)}, bf16[256,1024]{1,0:T(8,128)(2,1)S(1)}, u32[]{:S(2)}, u32[]{:S(2)}) collective-permute-start(bf16[256,1024]{1,0:T(8,128)(2,1)} %bitcast.22), channel_id=1, source_target_pairs={{0,1},{1,2},{2,3},{3,4},{4,5},{5,6},{6,7},{7,8},{8,9},{9,10},{10,1... | collective-permute-start | bytes 1572872 | tf_op jit(solution)/shard_map/ppermute | solution.py:698
  4.6 1.3 collective-permute-start.1
  5.9 1.4 %fusion.2 = (s32[1]{0:T(128)}, s32[1]{0:T(128)}, s32[1]{0:T(128)}) fusion(s32[32]{0:T(128)} %param.7, s32[]{:T(128)S(6)} %max.3, s32[]{:T(128)S(6)} %select_n.19, s32[]{:T(128)S(6)} %select_n.18), kind=kLoop, calls=%fused_computation.8 | loop fusion | bytes 36 | tf_op jit(solution)/shard_map/dynamic_slice | solution.py:702
  9.4 2.8 %copy-done.2 = bf16[1024,3072]{1,0:T(8,128)(2,1)S(1)} copy-done((bf16[1024,3072]{1,0:T(8,128)(2,1)S(1)}, bf16[1024,3072]{1,0:T(8,128)(2,1)}, u32[]{:S(2)}) %copy-start.2) | copy-done | bytes 6291480
  13.2 4.1 %shard_map.77 = (bf16[256,3072]{1,0:T(8,128)(2,1)S(1)}, bf16[1024,256]{1,0:T(8,128)(2,1)S(1)}) custom-call(bf16[256,1024]{1,0:T(8,128)(2,1)S(1)} %bitcast.24, bf16[1024,3072]{1,0:T(8,128)(2,1)S(1)} %copy-done.2), custom_call_target="tpu_custom_call" | custom-call | flops 2147483648 | bytes 8388608 | tf_op jit(solution)/shard_map/pallas_call | solution.py:95
  17.3 2.9 %collective-permute-done.1.right_ref = bf16[256,1024]{1,0:T(8,128)(2,1)S(1)} collective-permute-done((bf16[256,1024]{1,0:T(8,128)(2,1)}, bf16[256,1024]{1,0:T(8,128)(2,1)S(1)}, u32[]{:S(2)}, u32[]{:S(2)}) %collective-permute-start.1) | collective-permute-done | bytes 524320 | tf_op jit(solution)/shard_map/ppermute | solution.py:699
  20.2 2.8 %copy-done.3 = bf16[1024,3072]{1,0:T(8,128)(2,1)S(1)} copy-done((bf16[1024,3072]{1,0:T(8,128)(2,1)S(1)}, bf16[1024,3072]{1,0:T(8,128)(2,1)}, u32[]{:S(2)}) %copy-start.3) | copy-done | bytes 6291480
  23.0 11.7 %shard_map.78 = (bf16[512,1024]{1,0:T(8,128)(2,1)S(1)}, bf16[768,1024]{1,0:T(8,128)(2,1)S(1)}, bf16[768,1024]{1,0:T(8,128)(2,1)S(1)}, f32[256,1024]{1,0:T(8,128)...) custom-call(s32[3]{0:T(128)S(1)} %pad_add_fusion.counts_ref, ...), custom_call_target="tpu_custom_call" | custom-call | flops 6442450944 | bytes 12582912 | tf_op jit(solution)/shard_map/pallas_call | solution.py:338
  34.7 3.1 %collective-permute-start.2 = (f32[256,128]{1,0:T(8,128)S(1)}, f32[256,128]{1,0:T(8,128)S(1)}, u32[]{:S(2)}, u32[]{:S(2)}) collective-permute-start(f32[256,128]{1,0:T(8,128)S(1)} %get-tuple-element.25.own_ref), channel_id=1, source_target_pairs={{0,64},{64,0},{1,65},{65,1},{2,66},{66,2},{3,67},{67,3},{4,68},{68... | collective-permute-start | bytes 393224 | tf_op jit(solution)/shard_map/ppermute | solution.py:713
  37.8 2.2 %shard_map.79.qhalo_ref = bf16[512,1024]{1,0:T(8,128)(2,1)S(1)} custom-call(bf16[512,1024]{1,0:T(8,128)(2,1)S(1)} %get-tuple-element.26.normed_ref, bf16[1024,3072]{1,0:T(8,128)(2,1)S(1)} %copy-done.3), custom_call_target="tpu_custom_call" | custom-call | tf_op jit(solution)/shard_map/pallas_call | solution.py:133
  42.9 3.6 %shard_map.80 = (f32[256,128]{1,0:T(8,128)S(1)}, bf16[256,256]{1,0:T(8,128)(2,1)S(1)}, bf16[256,1024]{1,0:T(8,128)(2,1)S(1)}, bf16[1024,256]{1,0:T(8,128)(2,1)}) custom-call(s32[3]{0:T(128)S(1)} %pad_add_fusion.counts_ref, f32[256,128]{1,0:T(8,128)S(1)} %get-tuple-element.25.own_ref, f32[256,128]{1,0:T(8,128)S(1)} %collective-permute-done.2.near_ref, ...), custom_call_target="tpu_custom_call" | custom-call | tf_op jit(solution)/shard_map/pallas_call | solution.py:459
  46.5 3.6 %collective-permute-start.5 = (bf16[256,256]{1,0:T(8,128)(2,1)S(1)}, bf16[256,256]{1,0:T(8,128)(2,1)S(1)}, u32[]{:S(2)}, u32[]{:S(2)}) collective-permute-start(bf16[256,256]{1,0:T(8,128)(2,1)S(1)} %get-tuple-element.36.packed_ref.own_ref), channel_id=1, source_target_pairs={{0,1},{1,2},{2,3},{3,4},{4,5},{5,6},{6,7},{7,8},{8,9},{9,10},{10,1... | collective-permute-start | bytes 393224 | tf_op jit(solution)/shard_map/ppermute | solution.py:721
  51.5 7.5 %shard_map.81.piece_ref = bf16[1024,256]{1,0:T(8,128)(2,1)} custom-call(s32[3]{0:T(128)S(1)} %pad_add_fusion.counts_ref, bf16[256,3072]{1,0:T(8,128)(2,1)S(1)} %get-tuple-element.24.q_ref.k_ref.v_ref, bf16[768,1024]{1,0:T(8,128)(2,1)S(1)} %get-tuple-element.33.kcat_ref, bf16[768,1024]{1,0:T(8,128)(2,1)S(1)} %get-tuple-element.34.vcat_ref, ...), custom_call_target="tpu_custom_call" | custom-call | flops 6442450944 | bytes 5242880 | tf_op jit(solution)/shard_map/pallas_call | solution.py:526
  60.9 1.9 %collective-permute-done.7.other_ref = bf16[1024,256]{1,0:T(8,128)(2,1)} collective-permute-done((bf16[1024,256]{1,0:T(8,128)(2,1)}, bf16[1024,256]{1,0:T(8,128)(2,1)}, u32[]{:S(2)}, u32[]{:S(2)}) %collective-permute-start.7) | collective-permute-done | bytes 524320 | tf_op jit(solution)/shard_map/ppermute | solution.py:678
  62.7 3.5 %shard_map.82 = bf16[512,1280]{1,0:T(8,128)(2,1)} custom-call(s32[1]{0:T(128)} %bitcast.7.core_ref, bf16[2,2,256,256]{3,2,1,0:T(8,128)(2,1)S(1)} %bitcast.18, bf16[2,2,256,256]{3,2,1,0:T(8,128)(2,1)} %bitcast.9.normed_other_ref, bf16[1024,256]{1,0:T(8,128)(2,1)} %shard_map.81.piece_ref, bf16[1024,256]{1,0:T(8,128)(2,1)} %collective-permute-done.7.other_ref, ...), custom_call_target="tpu_custom_call" | custom-call | tf_op jit(solution)/shard_map/pallas_call | solution.py:178
  66.3 13.7 %all-to-all-start = ((bf16[64,8,1280]{2,1,0:T(8,128)(2,1)}), bf16[64,8,1280]{2,1,0:T(8,128)(2,1)}, u32[]{:S(2)}, u32[]{:S(2)}) async-start(bf16[64,8,1280]{2,1,0:T(8,128)(2,1)} %bitcast.13), calls=%async_computation | async-start | bytes 2621440 | tf_op jit(solution)/shard_map/all_to_all | solution.py:683
  80.0 1.6 %copy-done.1 = bf16[1024,1024]{1,0:T(8,128)(2,1)S(1)} copy-done((bf16[1024,1024]{1,0:T(8,128)(2,1)S(1)}, bf16[1024,1024]{1,0:T(8,128)(2,1)}, u32[]{:S(2)}) %copy-start.1) | copy-done | bytes 2097176
  84.4 9.6 %shard_map.83 = bf16[2,1024,256]{2,1,0:T(8,128)(2,1)S(1)} custom-call(s32[3]{0:T(128)S(1)} %pad_add_fusion.counts_ref, bf16[256,3072]{1,0:T(8,128)(2,1)S(1)} %get-tuple-element.24.q_ref.k_ref.v_ref, bf16[256,3072]{1,0:T(8,128)(2,1)S(1)} %get-tuple-element.24.q_ref.k_ref.v_ref, bf16[256,3072]{1,0:T(8,128)(2,1)S(1)} %get-tuple-element.24.q_ref.k_ref.v_ref, ...), custom_call_target="tpu_custom_call" | custom-call | tf_op jit(solution)/shard_map/pallas_call | solution.py:630
  94.2 2.6 %collective-permute-done.9.other_ref = bf16[2048,256]{1,0:T(8,128)(2,1)S(1)} collective-permute-done((bf16[2048,256]{1,0:T(8,128)(2,1)S(1)}, bf16[2048,256]{1,0:T(8,128)(2,1)S(1)}, u32[]{:S(2)}, u32[]{:S(2)}) %collective-permute-start.9) | collective-permute-done | bytes 1048608 | tf_op jit(solution)/shard_map/ppermute | solution.py:678
  96.8 3.7 %shard_map.84 = bf16[512,2048]{1,0:T(8,128)(2,1)} custom-call(s32[1]{0:T(128)} %bitcast.7.core_ref, bf16[2,2,256,256]{3,2,1,0:T(8,128)(2,1)S(1)} %bitcast.19, bf16[2,2,256,256]{3,2,1,0:T(8,128)(2,1)} %bitcast.9.normed_other_ref, bf16[2048,256]{1,0:T(8,128)(2,1)S(1)} %bitcast.17, bf16[2048,256]{1,0:T(8,128)(2,1)S(1)} %collective-permute-done.9.other_ref), custom_call_target="tpu_custom_call" | custom-call | tf_op jit(solution)/shard_map/pallas_call | solution.py:178
  100.4 1.4 all-to-all-done
  101.8 9.1 %all-to-all-start.1 = ((bf16[64,8,2048]{2,1,0:T(8,128)(2,1)}), bf16[64,8,2048]{2,1,0:T(8,128)(2,1)S(1)}, u32[]{:S(2)}, u32[]{:S(2)}) async-start(bf16[64,8,2048]{2,1,0:T(8,128)(2,1)} %bitcast.14), calls=%async_computation.1 | async-start | bytes 4194304 | tf_op jit(solution)/shard_map/all_to_all | solution.py:683
  111.7 1.5 %convert_reduce_fusion.1 = f32[8,1280]{1,0:T(8,128)S(1)} fusion(bf16[64,8,1280]{2,1,0:T(8,128)(2,1)} %all-to-all-done), kind=kLoop, calls=%fused_computation.1 | loop fusion | flops 1300480 | bytes 1351680 | tf_op jit(solution)/shard_map/reduce_sum | solution.py:687
  113.6 27.3 %all-to-all-done.1 = bf16[64,8,2048]{2,1,0:T(8,128)(2,1)S(1)} async-done(((bf16[64,8,2048]{2,1,0:T(8,128)(2,1)}), bf16[64,8,2048]{2,1,0:T(8,128)(2,1)S(1)}, u32[]{:S(2)}, u32[]{:S(2)}) %all-to-all-start.1) | async-done | bytes 2097184 | tf_op jit(solution)/shard_map/all_to_all | solution.py:683
  (51 shorter events, 13.0 us)
Async XLA Ops:
  0.6 16.7 %collective-permute-start = (bf16[256,1024]{1,0:T(8,128)(2,1)}, bf16[256,1024]{1,0:T(8,128)(2,1)S(1)}, u32[]{:S(2)}, u32[]{:S(2)}) collective-permute-start(bf16[256,1024]{1,0:T(8,128)(2,1)} %bitcast.22), channel_id=1, source_target_pairs={{0,1},{1,2},{2,3},{3,4},{4,5},{5,6},{6,7},{7,8},{8,9},{9,10},{10,1... | collective-permute-start | bytes 1572872 | tf_op jit(solution)/shard_map/ppermute | solution.py:698
  4.6 15.6 %collective-permute-start.1 = (bf16[256,1024]{1,0:T(8,128)(2,1)}, bf16[256,1024]{1,0:T(8,128)(2,1)S(1)}, u32[]{:S(2)}, u32[]{:S(2)}) collective-permute-start(bf16[256,1024]{1,0:T(8,128)(2,1)} %bitcast.23), channel_id=1, source_target_pairs={{1,0},{2,1},{3,2},{4,3},{5,4},{6,5},{7,6},{8,7},{9,8},{10,9},{11,1... | collective-permute-start | bytes 1572872 | tf_op jit(solution)/shard_map/ppermute | solution.py:699
  9.4 2.8 %copy-start.2 = (bf16[1024,3072]{1,0:T(8,128)(2,1)S(1)}, bf16[1024,3072]{1,0:T(8,128)(2,1)}, u32[]{:S(2)}) copy-start(bf16[1024,3072]{1,0:T(8,128)(2,1)} %weight_ref.5) | copy-start | bytes 18874372
  12.2 1.0 copy-start.14
  13.2 7.0 %copy-start = (bf16[1024,1024]{1,0:T(8,128)(2,1)S(1)}, bf16[1024,1024]{1,0:T(8,128)(2,1)}, u32[]{:S(2)}) copy-start(bf16[1024,1024]{1,0:T(8,128)(2,1)} %w_out_ref.5) | copy-start | bytes 6291460
  13.2 7.0 %copy-start.4 = (bf16[1024,128]{1,0:T(8,128)(2,1)S(1)}, bf16[1024,128]{1,0:T(8,128)(2,1)}, u32[]{:S(2)}) copy-start(bf16[1024,128]{1,0:T(8,128)(2,1)} %readout_ref.5) | copy-start | bytes 786436
  13.2 7.0 %copy-start.15 = (bf16[1,256,1024]{2,1,0:T(8,128)(2,1)S(1)}, bf16[1,256,1024]{2,1,0:T(8,128)(2,1)}, u32[]{:S(2)}) copy-start(bf16[1,256,1024]{2,1,0:T(8,128)(2,1)} %param.6) | copy-start | bytes 1572868
  20.2 2.8 %copy-start.3 = (bf16[1024,3072]{1,0:T(8,128)(2,1)S(1)}, bf16[1024,3072]{1,0:T(8,128)(2,1)}, u32[]{:S(2)}) copy-start(bf16[1024,3072]{1,0:T(8,128)(2,1)} %weight_ref.5) | copy-start | bytes 18874372
  34.7 6.6 %collective-permute-start.2 = (f32[256,128]{1,0:T(8,128)S(1)}, f32[256,128]{1,0:T(8,128)S(1)}, u32[]{:S(2)}, u32[]{:S(2)}) collective-permute-start(f32[256,128]{1,0:T(8,128)S(1)} %get-tuple-element.25.own_ref), channel_id=1, source_target_pairs={{0,64},{64,0},{1,65},{65,1},{2,66},{66,2},{3,67},{67,3},{4,68},{68... | collective-permute-start | bytes 393224 | tf_op jit(solution)/shard_map/ppermute | solution.py:713
  37.8 5.1 %copy-start.11 = (f32[256,128]{1,0:T(8,128)S(1)}, f32[256,128]{1,0:T(8,128)}, u32[]{:S(2)}) copy-start(f32[256,128]{1,0:T(8,128)} %target_ref.1) | copy-start | bytes 393220
  41.3 1.6 %collective-permute-start.3 = (f32[2,256,128]{2,1,0:T(8,128)S(1)}, f32[2,256,128]{2,1,0:T(8,128)S(1)}, u32[]{:S(2)}, u32[]{:S(2)}) collective-permute-start(f32[2,256,128]{2,1,0:T(8,128)S(1)} %pad_maximum_fusion), channel_id=1, source_target_pairs={{0,32},{32,0},{1,33},{33,1},{2,34},{34,2},{3,35},{35,3},{4,36},{36... | collective-permute-start | bytes 786440 | tf_op jit(solution)/shard_map/ppermute | solution.py:678
  41.4 19.5 %collective-permute-start.4 = (bf16[1024,256]{1,0:T(8,128)(2,1)S(1)}, bf16[1024,256]{1,0:T(8,128)(2,1)}, u32[]{:S(2)}, u32[]{:S(2)}) collective-permute-start(bf16[1024,256]{1,0:T(8,128)(2,1)S(1)} %get-tuple-element.32), channel_id=1, source_target_pairs={{0,32},{32,0},{1,33},{33,1},{2,34},{34,2},{3,35},{35,3},{4,36},{36... | collective-permute-start | bytes 1572872 | tf_op jit(solution)/shard_map/ppermute | solution.py:678
  46.5 12.6 %copy-start.5 = (bf16[256,1024]{1,0:T(8,128)(2,1)}, bf16[256,1024]{1,0:T(8,128)(2,1)S(1)}, u32[]{:S(2)}) copy-start(bf16[256,1024]{1,0:T(8,128)(2,1)S(1)} %get-tuple-element.35.grad_ref) | copy-start | bytes 1572868
  46.5 12.6 %copy-start.12 = (f32[256,128]{1,0:T(8,128)}, f32[256,128]{1,0:T(8,128)S(1)}, u32[]{:S(2)}) copy-start(f32[256,128]{1,0:T(8,128)S(1)} %get-tuple-element.31) | copy-start | bytes 393220
  46.5 12.6 %collective-permute-start.5 = (bf16[256,256]{1,0:T(8,128)(2,1)S(1)}, bf16[256,256]{1,0:T(8,128)(2,1)S(1)}, u32[]{:S(2)}, u32[]{:S(2)}) collective-permute-start(bf16[256,256]{1,0:T(8,128)(2,1)S(1)} %get-tuple-element.36.packed_ref.own_ref), channel_id=1, source_target_pairs={{0,1},{1,2},{2,3},{3,4},{4,5},{5,6},{6,7},{7,8},{8,9},{9,10},{10,1... | collective-permute-start | bytes 393224 | tf_op jit(solution)/shard_map/ppermute | solution.py:721
  50.1 9.6 %collective-permute-start.6 = (bf16[256,256]{1,0:T(8,128)(2,1)S(1)}, bf16[256,256]{1,0:T(8,128)(2,1)S(1)}, u32[]{:S(2)}, u32[]{:S(2)}) collective-permute-start(bf16[256,256]{1,0:T(8,128)(2,1)S(1)} %get-tuple-element.36.packed_ref.own_ref), channel_id=1, source_target_pairs={{1,0},{2,1},{3,2},{4,3},{5,4},{6,5},{7,6},{8,7},{9,8},{10,9},{11,1... | collective-permute-start | bytes 393224 | tf_op jit(solution)/shard_map/ppermute | solution.py:722
  51.4 9.4 %collective-permute-start.8 = (bf16[1024,256]{1,0:T(8,128)(2,1)}, bf16[1024,256]{1,0:T(8,128)(2,1)}, u32[]{:S(2)}, u32[]{:S(2)}) collective-permute-start(bf16[1024,256]{1,0:T(8,128)(2,1)} %get-tuple-element.38), channel_id=1, source_target_pairs={{0,32},{32,0},{1,33},{33,1},{2,34},{34,2},{3,35},{35,3},{4,36},{36... | collective-permute-start | bytes 1572872 | tf_op jit(solution)/shard_map/ppermute | solution.py:678
  60.4 2.4 %collective-permute-start.7 = (bf16[1024,256]{1,0:T(8,128)(2,1)}, bf16[1024,256]{1,0:T(8,128)(2,1)}, u32[]{:S(2)}, u32[]{:S(2)}) collective-permute-start(bf16[1024,256]{1,0:T(8,128)(2,1)} %shard_map.81.piece_ref), channel_id=1, source_target_pairs={{0,32},{32,0},{1,33},{33,1},{2,34},{34,2},{3,35},{35,3},{4,36},{36... | collective-permute-start | bytes 1572872 | tf_op jit(solution)/shard_map/ppermute | solution.py:678
  66.3 35.5 %all-to-all-start = ((bf16[64,8,1280]{2,1,0:T(8,128)(2,1)}), bf16[64,8,1280]{2,1,0:T(8,128)(2,1)}, u32[]{:S(2)}, u32[]{:S(2)}) async-start(bf16[64,8,1280]{2,1,0:T(8,128)(2,1)} %bitcast.13), calls=%async_computation | async-start | bytes 2621440 | tf_op jit(solution)/shard_map/all_to_all | solution.py:683
  79.9 1.6 %copy-start.1 = (bf16[1024,1024]{1,0:T(8,128)(2,1)S(1)}, bf16[1024,1024]{1,0:T(8,128)(2,1)}, u32[]{:S(2)}) copy-start(bf16[1024,1024]{1,0:T(8,128)(2,1)} %w_out_ref.5) | copy-start | bytes 6291460
  81.5 1.0 copy-start.6
  94.0 2.7 %collective-permute-start.9 = (bf16[2048,256]{1,0:T(8,128)(2,1)S(1)}, bf16[2048,256]{1,0:T(8,128)(2,1)S(1)}, u32[]{:S(2)}, u32[]{:S(2)}) collective-permute-start(bf16[2048,256]{1,0:T(8,128)(2,1)S(1)} %bitcast.16), channel_id=1, source_target_pairs={{0,32},{32,0},{1,33},{33,1},{2,34},{34,2},{3,35},{35,3},{4,36},{36... | collective-permute-start | bytes 3145736 | tf_op jit(solution)/shard_map/ppermute | solution.py:678
  101.8 9.1 %copy-start.13 = (f32[256,128]{1,0:T(8,128)S(1)}, f32[256,128]{1,0:T(8,128)}, u32[]{:S(2)}) copy-start(f32[256,128]{1,0:T(8,128)} %copy-done.12) | copy-start | bytes 393220
  101.8 39.1 %all-to-all-start.1 = ((bf16[64,8,2048]{2,1,0:T(8,128)(2,1)}), bf16[64,8,2048]{2,1,0:T(8,128)(2,1)S(1)}, u32[]{:S(2)}, u32[]{:S(2)}) async-start(bf16[64,8,2048]{2,1,0:T(8,128)(2,1)} %bitcast.14), calls=%async_computation.1 | async-start | bytes 4194304 | tf_op jit(solution)/shard_map/all_to_all | solution.py:683
  (4 other events, 3.1 us)

commit v5 on v4

--- a/solution.py
+++ b/solution.py
@@ -109,7 +109,7 @@
             pltpu.VMEM((6, width, 512), BF),
             pltpu.SemaphoreType.DMA((6,)),
         ],
-        compiler_params=pltpu.CompilerParams(vmem_limit_bytes=16 * 1024 * 1024),
+        compiler_params=pltpu.CompilerParams(vmem_limit_bytes=56 * 1024 * 1024),
         cost_estimate=pl.CostEstimate(
             flops=2 * rows * width * width * 4, bytes_accessed=8 << 20, transcendentals=0
         ),
@@ -140,7 +140,7 @@
             pltpu.VMEM((4, width, 256), BF),
             pltpu.SemaphoreType.DMA((4,)),
         ],
-        compiler_params=pltpu.CompilerParams(vmem_limit_bytes=12 * 1024 * 1024),
+        compiler_params=pltpu.CompilerParams(vmem_limit_bytes=52 * 1024 * 1024),
         cost_estimate=FREE,
     )(normed_halo, w_qkv)
 
@@ -374,7 +374,7 @@
             pltpu.VMEM((8, 1024, WIDTH), BF),
             pltpu.SemaphoreType.DMA((8,)),
         ],
-        compiler_params=pltpu.CompilerParams(vmem_limit_bytes=28 * 1024 * 1024),
+        compiler_params=pltpu.CompilerParams(vmem_limit_bytes=48 * 1024 * 1024),
         cost_estimate=pl.CostEstimate(
             flops=6 << 30, bytes_accessed=12 << 20, transcendentals=3 << 20
         ),
@@ -650,7 +650,7 @@
             pltpu.VMEM((4, window, BLOCK), BF),
             pltpu.VMEM((2 * WIN, 1024), BF),
         ],
-        compiler_params=pltpu.CompilerParams(vmem_limit_bytes=18 * 1024 * 1024),
+        compiler_params=pltpu.CompilerParams(vmem_limit_bytes=56 * 1024 * 1024),
         cost_estimate=FREE,
     )(
         counts,

time: 143 us -> 139 us (0.972)
  local copies, waits for them, and re-layouts: 14.6 us -> 5.53 us
  Pallas kernels: 45.8 us -> 52.2 us
  starting transfers between devices: 37.4 us -> 33.6 us
  waiting for transfers between devices: 38.4 us -> 41.3 us
    unnamed x33 -> x41, local copies, waits for them, and re-layouts: 13.1 us -> 4.07 us
    all_to_all x2, starting transfers between devices: 22.8 us -> 19.1 us  [scatter(): lax.all_to_all(partial.reshape(64, 8, columns), CHIPS, split_axis=0, conc...]
    all_to_all x2, waiting for transfers between devices: 28.7 us -> 31.1 us  [scatter(): lax.all_to_all(partial.reshape(64, 8, columns), CHIPS, split_axis=0, conc...]
    pallas_call x1, Pallas kernels: 4.06 us -> 6.37 us  [project(): pl.pallas_call(project_kernel, grid=(6,), in_specs=[pl.BlockSpec((rows, w...]
    pallas_call x1, Pallas kernels: 2.17 us -> 4.31 us  [halo_queries(): pl.pallas_call(halo_query_kernel, grid=(4,), in_specs=[pl.BlockSpec((rows...]
    pallas_call x1, Pallas kernels: 11.7 us -> 13.3 us  [forward(): pl.pallas_call(forward_kernel, grid=(4,), in_specs=[pl.BlockSpec(memory_s...]
    pallas_call x1, Pallas kernels: 9.62 us -> 11.2 us  [key_grads(): pl.pallas_call(key_kernel, grid=(4,), in_specs=[pl.BlockSpec(memory_space...]
  transfers between devices with their start and end apart: 12 -> 12, of which waited for: 7 -> 7; matrix products, arithmetic and copies ran while one was open for 3% -> 3% of each run, Pallas kernels for 22% -> 26%
where the time goes in v5:
time: 139 us; the launch traced here: 138 us
  Pallas kernels  52.2 us (38%)
  waiting for transfers between devices  41.3 us (30%)
  starting transfers between devices  33.6 us (24%)
  local copies, waits for them, and re-layouts  5.53 us (4%)
  other arithmetic  3.16 us (2%)
  between operations  2.23 us (2%)
    all_to_all x2, waiting for transfers between devices, scatter(): lax.all_to_all(partial.reshape(64, 8, columns), CHIPS, split_axis=0, conc...  31.1 us
    all_to_all x2, starting transfers between devices, scatter(): lax.all_to_all(partial.reshape(64, 8, columns), CHIPS, split_axis=0, conc...  19.1 us
    pallas_call x1, Pallas kernels, forward(): pl.pallas_call(forward_kernel, grid=(4,), in_specs=[pl.BlockSpec(memory_s...  13.3 us
    pallas_call x1, Pallas kernels, key_grads(): pl.pallas_call(key_kernel, grid=(4,), in_specs=[pl.BlockSpec(memory_space...  11.2 us
    pallas_call x1, Pallas kernels, query_grads(): pl.pallas_call(query_kernel, grid=(4,), in_specs=[pl.BlockSpec(memory_spa...  7.56 us
    pallas_call x1, Pallas kernels, project(): pl.pallas_call(project_kernel, grid=(6,), in_specs=[pl.BlockSpec((rows, w...  6.37 us
    pallas_call x2, Pallas kernels, partial_sums(): pl.pallas_call(partial_kernel if smalls else plain_partial_kernel, in_spe...  5.86 us
    ppermute x5, waiting for transfers between devices, swap_core(): return lax.ppermute(values, 'core', SWAP)  5.56 us
  transfers between devices with their start and end apart: 12, of which 7 were waited for; matrix products, arithmetic and copies ran while one was open for 3% of the time, Pallas kernels for 26%

profile of v5, /device:TPU:0, one launch (start us, length us, event | category | flops | bytes accessed | tf_op | source)
XLA Modules:
  0.0 138.4 jit_solution(12454382272177643109)
XLA Ops:
  0.6 3.9 %collective-permute-start = (bf16[256,1024]{1,0:T(8,128)(2,1)}, bf16[256,1024]{1,0:T(8,128)(2,1)S(1)}, u32[]{:S(2)}, u32[]{:S(2)}) collective-permute-start(bf16[256,1024]{1,0:T(8,128)(2,1)} %bitcast.24), channel_id=1, source_target_pairs={{0,1},{1,2},{2,3},{3,4},{4,5},{5,6},{6,7},{7,8},{8,9},{9,10},{10,1... | collective-permute-start | bytes 1572872 | tf_op jit(solution)/shard_map/ppermute | solution.py:698
  4.6 1.3 collective-permute-start.1
  5.9 1.4 fusion.2
  9.2 6.4 %shard_map.77 = (bf16[256,3072]{1,0:T(8,128)(2,1)}, bf16[1024,256]{1,0:T(8,128)(2,1)}) custom-call(bf16[256,1024]{1,0:T(8,128)(2,1)} %bitcast.26, bf16[1024,3072]{1,0:T(8,128)(2,1)} %weight_ref.5), custom_call_target="tpu_custom_call" | custom-call | flops 2147483648 | bytes 8388608 | tf_op jit(solution)/shard_map/pallas_call | solution.py:95
  16.0 4.2 %collective-permute-done.1.right_ref = bf16[256,1024]{1,0:T(8,128)(2,1)S(1)} collective-permute-done((bf16[256,1024]{1,0:T(8,128)(2,1)}, bf16[256,1024]{1,0:T(8,128)(2,1)S(1)}, u32[]{:S(2)}, u32[]{:S(2)}) %collective-permute-start.1) | collective-permute-done | bytes 524320 | tf_op jit(solution)/shard_map/ppermute | solution.py:699
  20.2 13.3 %shard_map.78 = (bf16[512,1024]{1,0:T(8,128)(2,1)S(1)}, bf16[768,1024]{1,0:T(8,128)(2,1)}, bf16[768,1024]{1,0:T(8,128)(2,1)}, f32[256,1024]{1,0:T(8,128)S(1)}, f...) custom-call(s32[3]{0:T(128)S(1)} %pad_add_fusion.counts_ref, ...), custom_call_target="tpu_custom_call" | custom-call | flops 6442450944 | bytes 12582912 | tf_op jit(solution)/shard_map/pallas_call | solution.py:338
  34.5 3.0 %collective-permute-start.2 = (f32[256,128]{1,0:T(8,128)S(1)}, f32[256,128]{1,0:T(8,128)S(1)}, u32[]{:S(2)}, u32[]{:S(2)}) collective-permute-start(f32[256,128]{1,0:T(8,128)S(1)} %get-tuple-element.25.own_ref), channel_id=1, source_target_pairs={{0,64},{64,0},{1,65},{65,1},{2,66},{66,2},{3,67},{67,3},{4,68},{68... | collective-permute-start | bytes 393224 | tf_op jit(solution)/shard_map/ppermute | solution.py:713
  37.6 4.3 %shard_map.79.qhalo_ref = bf16[512,1024]{1,0:T(8,128)(2,1)S(1)} custom-call(bf16[512,1024]{1,0:T(8,128)(2,1)} %copy-done.7, bf16[1024,3072]{1,0:T(8,128)(2,1)} %weight_ref.5), custom_call_target="tpu_custom_call" | custom-call | tf_op jit(solution)/shard_map/pallas_call | solution.py:133
  43.6 3.6 %shard_map.80 = (f32[256,128]{1,0:T(8,128)S(1)}, bf16[256,256]{1,0:T(8,128)(2,1)S(1)}, bf16[256,1024]{1,0:T(8,128)(2,1)S(1)}, bf16[1024,256]{1,0:T(8,128)(2,1)}) custom-call(s32[3]{0:T(128)S(1)} %pad_add_fusion.counts_ref, f32[256,128]{1,0:T(8,128)S(1)} %get-tuple-element.25.own_ref, f32[256,128]{1,0:T(8,128)S(1)} %collective-permute-done.2.near_ref, ...), custom_call_target="tpu_custom_call" | custom-call | tf_op jit(solution)/shard_map/pallas_call | solution.py:459
  47.2 3.6 %collective-permute-start.5 = (bf16[256,256]{1,0:T(8,128)(2,1)S(1)}, bf16[256,256]{1,0:T(8,128)(2,1)S(1)}, u32[]{:S(2)}, u32[]{:S(2)}) collective-permute-start(bf16[256,256]{1,0:T(8,128)(2,1)S(1)} %get-tuple-element.36.packed_ref.own_ref), channel_id=1, source_target_pairs={{0,1},{1,2},{2,3},{3,4},{4,5},{5,6},{6,7},{7,8},{8,9},{9,10},{10,1... | collective-permute-start | bytes 393224 | tf_op jit(solution)/shard_map/ppermute | solution.py:721
  50.9 1.3 collective-permute-start.6
  52.3 7.6 %shard_map.81.piece_ref = bf16[1024,256]{1,0:T(8,128)(2,1)} custom-call(s32[3]{0:T(128)S(1)} %pad_add_fusion.counts_ref, bf16[256,3072]{1,0:T(8,128)(2,1)S(1)} %copy-done, bf16[768,1024]{1,0:T(8,128)(2,1)S(1)} %copy-done.15, bf16[768,1024]{1,0:T(8,128)(2,1)S(1)} %copy-done.16, bf16[256,1024]{1,0:T(8,128)(2,1)S(1)} %get-tuple-element.35.grad_ref, ...), custom_call_target="tpu_custom_call" | custom-call | flops 6442450944 | bytes 5242880 | tf_op jit(solution)/shard_map/pallas_call | solution.py:526
  60.5 1.7 %collective-permute-done.7.other_ref = bf16[1024,256]{1,0:T(8,128)(2,1)S(1)} collective-permute-done((bf16[1024,256]{1,0:T(8,128)(2,1)}, bf16[1024,256]{1,0:T(8,128)(2,1)S(1)}, u32[]{:S(2)}, u32[]{:S(2)}) %collective-permute-start.7) | collective-permute-done | bytes 524320 | tf_op jit(solution)/shard_map/ppermute | solution.py:678
  62.2 3.2 %shard_map.82 = bf16[512,1280]{1,0:T(8,128)(2,1)} custom-call(s32[1]{0:T(128)} %bitcast.7.core_ref, bf16[2,2,256,256]{3,2,1,0:T(8,128)(2,1)S(1)} %bitcast.18, bf16[2,2,256,256]{3,2,1,0:T(8,128)(2,1)S(1)} %bitcast.20, bf16[1024,256]{1,0:T(8,128)(2,1)} %shard_map.81.piece_ref, bf16[1024,256]{1,0:T(8,128)(2,1)S(1)} %collective-permute-done.7.other_ref, ...), custom_call_target="tpu_custom_call" | custom-call | tf_op jit(solution)/shard_map/pallas_call | solution.py:178
  65.4 12.5 %all-to-all-start = ((bf16[64,8,1280]{2,1,0:T(8,128)(2,1)}), bf16[64,8,1280]{2,1,0:T(8,128)(2,1)S(1)}, u32[]{:S(2)}, u32[]{:S(2)}) async-start(bf16[64,8,1280]{2,1,0:T(8,128)(2,1)} %bitcast.13), calls=%async_computation | async-start | bytes 2621440 | tf_op jit(solution)/shard_map/all_to_all | solution.py:683
  78.0 11.2 %shard_map.83 = bf16[2,1024,256]{2,1,0:T(8,128)(2,1)} custom-call(s32[3]{0:T(128)} %copy-done.13, bf16[256,3072]{1,0:T(8,128)(2,1)} %get-tuple-element.24.q_ref.k_ref.v_ref, bf16[256,3072]{1,0:T(8,128)(2,1)} %get-tuple-element.24.q_ref.k_ref.v_ref, bf16[256,3072]{1,0:T(8,128)(2,1)} %get-tuple-element.24.q_ref.k_ref.v_ref, bf16[512,1024]{1,0:T(8,128)(2,1)} %copy-done.3, ...), custom_call_target="tpu_custom_call" | custom-call | tf_op jit(solution)/shard_map/pallas_call | solution.py:630
  89.3 2.8 %collective-permute-done.9.other_ref = bf16[2048,256]{1,0:T(8,128)(2,1)S(1)} collective-permute-done((bf16[2048,256]{1,0:T(8,128)(2,1)}, bf16[2048,256]{1,0:T(8,128)(2,1)S(1)}, u32[]{:S(2)}, u32[]{:S(2)}) %collective-permute-start.9) | collective-permute-done | bytes 1048608 | tf_op jit(solution)/shard_map/ppermute | solution.py:678
  92.1 1.2 copy-done.2
  93.3 2.6 %shard_map.84 = bf16[512,2048]{1,0:T(8,128)(2,1)} custom-call(s32[1]{0:T(128)} %bitcast.7.core_ref, bf16[2,2,256,256]{3,2,1,0:T(8,128)(2,1)S(1)} %bitcast.19, bf16[2,2,256,256]{3,2,1,0:T(8,128)(2,1)S(1)} %bitcast.21, bf16[2048,256]{1,0:T(8,128)(2,1)S(1)} %bitcast.17, bf16[2048,256]{1,0:T(8,128)(2,1)S(1)} %collective-permute-done.9.other_ref), custom_call_target="tpu_custom_call" | custom-call | tf_op jit(solution)/shard_map/pallas_call | solution.py:178
  95.9 3.8 %all-to-all-done = bf16[64,8,1280]{2,1,0:T(8,128)(2,1)S(1)} async-done(((bf16[64,8,1280]{2,1,0:T(8,128)(2,1)}), bf16[64,8,1280]{2,1,0:T(8,128)(2,1)S(1)}, u32[]{:S(2)}, u32[]{:S(2)}) %all-to-all-start) | async-done | bytes 1310752 | tf_op jit(solution)/shard_map/all_to_all | solution.py:683
  99.8 1.1 copy-done.17
  100.8 6.5 %all-to-all-start.1 = ((bf16[64,8,2048]{2,1,0:T(8,128)(2,1)}), bf16[64,8,2048]{2,1,0:T(8,128)(2,1)S(1)}, u32[]{:S(2)}, u32[]{:S(2)}) async-start(bf16[64,8,2048]{2,1,0:T(8,128)(2,1)} %bitcast.14), calls=%async_computation.1 | async-start | bytes 4194304 | tf_op jit(solution)/shard_map/all_to_all | solution.py:683
  108.2 1.5 %convert_reduce_fusion.1 = f32[8,1280]{1,0:T(8,128)S(1)} fusion(bf16[64,8,1280]{2,1,0:T(8,128)(2,1)} %copy-done.17), kind=kLoop, calls=%fused_computation.1 | loop fusion | flops 1300480 | bytes 1351680 | tf_op jit(solution)/shard_map/reduce_sum | solution.py:687
  110.1 27.3 %all-to-all-done.1 = bf16[64,8,2048]{2,1,0:T(8,128)(2,1)S(1)} async-done(((bf16[64,8,2048]{2,1,0:T(8,128)(2,1)}), bf16[64,8,2048]{2,1,0:T(8,128)(2,1)S(1)}, u32[]{:S(2)}, u32[]{:S(2)}) %all-to-all-start.1) | async-done | bytes 2097184 | tf_op jit(solution)/shard_map/all_to_all | solution.py:683
  (59 shorter events, 6.6 us)
Async XLA Ops:
  0.6 15.4 %collective-permute-start = (bf16[256,1024]{1,0:T(8,128)(2,1)}, bf16[256,1024]{1,0:T(8,128)(2,1)S(1)}, u32[]{:S(2)}, u32[]{:S(2)}) collective-permute-start(bf16[256,1024]{1,0:T(8,128)(2,1)} %bitcast.24), channel_id=1, source_target_pairs={{0,1},{1,2},{2,3},{3,4},{4,5},{5,6},{6,7},{7,8},{8,9},{9,10},{10,1... | collective-permute-start | bytes 1572872 | tf_op jit(solution)/shard_map/ppermute | solution.py:698
  4.6 15.6 %collective-permute-start.1 = (bf16[256,1024]{1,0:T(8,128)(2,1)}, bf16[256,1024]{1,0:T(8,128)(2,1)S(1)}, u32[]{:S(2)}, u32[]{:S(2)}) collective-permute-start(bf16[256,1024]{1,0:T(8,128)(2,1)} %bitcast.25), channel_id=1, source_target_pairs={{1,0},{2,1},{3,2},{4,3},{5,4},{6,5},{7,6},{8,7},{9,8},{10,9},{11,1... | collective-permute-start | bytes 1572872 | tf_op jit(solution)/shard_map/ppermute | solution.py:699
  9.2 43.1 %copy-start.13 = (s32[3]{0:T(128)}, s32[3]{0:T(128)S(1)}, u32[]{:S(2)}) copy-start(s32[3]{0:T(128)S(1)} %pad_add_fusion.counts_ref) | copy-start | bytes 40
  9.2 11.0 %copy-start.4 = (bf16[1024,128]{1,0:T(8,128)(2,1)S(1)}, bf16[1024,128]{1,0:T(8,128)(2,1)}, u32[]{:S(2)}) copy-start(bf16[1024,128]{1,0:T(8,128)(2,1)} %readout_ref.5) | copy-start | bytes 786436
  9.2 11.0 %copy-start.14 = (bf16[1,256,1024]{2,1,0:T(8,128)(2,1)S(1)}, bf16[1,256,1024]{2,1,0:T(8,128)(2,1)}, u32[]{:S(2)}) copy-start(bf16[1,256,1024]{2,1,0:T(8,128)(2,1)} %param.6) | copy-start | bytes 1572868
  34.5 7.4 %collective-permute-start.2 = (f32[256,128]{1,0:T(8,128)S(1)}, f32[256,128]{1,0:T(8,128)S(1)}, u32[]{:S(2)}, u32[]{:S(2)}) collective-permute-start(f32[256,128]{1,0:T(8,128)S(1)} %get-tuple-element.25.own_ref), channel_id=1, source_target_pairs={{0,64},{64,0},{1,65},{65,1},{2,66},{66,2},{3,67},{67,3},{4,68},{68... | collective-permute-start | bytes 393224 | tf_op jit(solution)/shard_map/ppermute | solution.py:713
  37.6 6.0 %copy-start.10 = (f32[256,128]{1,0:T(8,128)S(1)}, f32[256,128]{1,0:T(8,128)}, u32[]{:S(2)}) copy-start(f32[256,128]{1,0:T(8,128)} %target_ref.1) | copy-start | bytes 393220
  41.9 1.6 %collective-permute-start.3 = (f32[2,256,128]{2,1,0:T(8,128)S(1)}, f32[2,256,128]{2,1,0:T(8,128)S(1)}, u32[]{:S(2)}, u32[]{:S(2)}) collective-permute-start(f32[2,256,128]{2,1,0:T(8,128)S(1)} %pad_maximum_fusion), channel_id=1, source_target_pairs={{0,32},{32,0},{1,33},{33,1},{2,34},{34,2},{3,35},{35,3},{4,36},{36... | collective-permute-start | bytes 786440 | tf_op jit(solution)/shard_map/ppermute | solution.py:678
  42.0 18.4 %collective-permute-start.4 = (bf16[1024,256]{1,0:T(8,128)(2,1)S(1)}, bf16[1024,256]{1,0:T(8,128)(2,1)S(1)}, u32[]{:S(2)}, u32[]{:S(2)}) collective-permute-start(bf16[1024,256]{1,0:T(8,128)(2,1)S(1)} %copy-done.6), channel_id=1, source_target_pairs={{0,32},{32,0},{1,33},{33,1},{2,34},{34,2},{3,35},{35,3},{4,36},{36... | collective-permute-start | bytes 1572872 | tf_op jit(solution)/shard_map/ppermute | solution.py:678
  43.6 8.7 %copy-start = (bf16[256,3072]{1,0:T(8,128)(2,1)S(1)}, bf16[256,3072]{1,0:T(8,128)(2,1)}, u32[]{:S(2)}) copy-start(bf16[256,3072]{1,0:T(8,128)(2,1)} %get-tuple-element.24.q_ref.k_ref.v_ref) | copy-start | bytes 4718596
  43.6 8.7 %copy-start.15 = (bf16[768,1024]{1,0:T(8,128)(2,1)S(1)}, bf16[768,1024]{1,0:T(8,128)(2,1)}, u32[]{:S(2)}) copy-start(bf16[768,1024]{1,0:T(8,128)(2,1)} %get-tuple-element.33.kcat_ref) | copy-start | bytes 4718596
  43.6 8.7 %copy-start.16 = (bf16[768,1024]{1,0:T(8,128)(2,1)S(1)}, bf16[768,1024]{1,0:T(8,128)(2,1)}, u32[]{:S(2)}) copy-start(bf16[768,1024]{1,0:T(8,128)(2,1)} %get-tuple-element.34.vcat_ref) | copy-start | bytes 4718596
  47.2 12.7 %copy-start.8 = (bf16[256,1024]{1,0:T(8,128)(2,1)}, bf16[256,1024]{1,0:T(8,128)(2,1)S(1)}, u32[]{:S(2)}) copy-start(bf16[256,1024]{1,0:T(8,128)(2,1)S(1)} %get-tuple-element.35.grad_ref) | copy-start | bytes 1572868
  47.2 12.7 %copy-start.9 = (bf16[256,256]{1,0:T(8,128)(2,1)}, bf16[256,256]{1,0:T(8,128)(2,1)S(1)}, u32[]{:S(2)}) copy-start(bf16[256,256]{1,0:T(8,128)(2,1)S(1)} %get-tuple-element.36.packed_ref.own_ref) | copy-start | bytes 393220
  47.2 12.7 %copy-start.11 = (f32[256,128]{1,0:T(8,128)}, f32[256,128]{1,0:T(8,128)S(1)}, u32[]{:S(2)}) copy-start(f32[256,128]{1,0:T(8,128)S(1)} %get-tuple-element.31) | copy-start | bytes 393220
  47.2 12.7 %collective-permute-start.5 = (bf16[256,256]{1,0:T(8,128)(2,1)S(1)}, bf16[256,256]{1,0:T(8,128)(2,1)S(1)}, u32[]{:S(2)}, u32[]{:S(2)}) collective-permute-start(bf16[256,256]{1,0:T(8,128)(2,1)S(1)} %get-tuple-element.36.packed_ref.own_ref), channel_id=1, source_target_pairs={{0,1},{1,2},{2,3},{3,4},{4,5},{5,6},{6,7},{7,8},{8,9},{9,10},{10,1... | collective-permute-start | bytes 393224 | tf_op jit(solution)/shard_map/ppermute | solution.py:721
  50.9 9.0 %collective-permute-start.6 = (bf16[256,256]{1,0:T(8,128)(2,1)S(1)}, bf16[256,256]{1,0:T(8,128)(2,1)S(1)}, u32[]{:S(2)}, u32[]{:S(2)}) collective-permute-start(bf16[256,256]{1,0:T(8,128)(2,1)S(1)} %get-tuple-element.36.packed_ref.own_ref), channel_id=1, source_target_pairs={{1,0},{2,1},{3,2},{4,3},{5,4},{6,5},{7,6},{8,7},{9,8},{10,9},{11,1... | collective-permute-start | bytes 393224 | tf_op jit(solution)/shard_map/ppermute | solution.py:722
  52.2 8.3 %collective-permute-start.8 = (bf16[1024,256]{1,0:T(8,128)(2,1)}, bf16[1024,256]{1,0:T(8,128)(2,1)}, u32[]{:S(2)}, u32[]{:S(2)}) collective-permute-start(bf16[1024,256]{1,0:T(8,128)(2,1)} %get-tuple-element.38), channel_id=1, source_target_pairs={{0,32},{32,0},{1,33},{33,1},{2,34},{34,2},{3,35},{35,3},{4,36},{36... | collective-permute-start | bytes 1572872 | tf_op jit(solution)/shard_map/ppermute | solution.py:678
  59.9 2.3 %collective-permute-start.7 = (bf16[1024,256]{1,0:T(8,128)(2,1)}, bf16[1024,256]{1,0:T(8,128)(2,1)S(1)}, u32[]{:S(2)}, u32[]{:S(2)}) collective-permute-start(bf16[1024,256]{1,0:T(8,128)(2,1)} %shard_map.81.piece_ref), channel_id=1, source_target_pairs={{0,32},{32,0},{1,33},{33,1},{2,34},{34,2},{3,35},{35,3},{4,36},{36... | collective-permute-start | bytes 1572872 | tf_op jit(solution)/shard_map/ppermute | solution.py:678
  65.4 34.3 %all-to-all-start = ((bf16[64,8,1280]{2,1,0:T(8,128)(2,1)}), bf16[64,8,1280]{2,1,0:T(8,128)(2,1)S(1)}, u32[]{:S(2)}, u32[]{:S(2)}) async-start(bf16[64,8,1280]{2,1,0:T(8,128)(2,1)} %bitcast.13), calls=%async_computation | async-start | bytes 2621440 | tf_op jit(solution)/shard_map/all_to_all | solution.py:683
  89.2 2.9 %collective-permute-start.9 = (bf16[2048,256]{1,0:T(8,128)(2,1)}, bf16[2048,256]{1,0:T(8,128)(2,1)S(1)}, u32[]{:S(2)}, u32[]{:S(2)}) collective-permute-start(bf16[2048,256]{1,0:T(8,128)(2,1)} %bitcast.16), channel_id=1, source_target_pairs={{0,32},{32,0},{1,33},{33,1},{2,34},{34,2},{3,35},{35,3},{4,36},{36... | collective-permute-start | bytes 3145736 | tf_op jit(solution)/shard_map/ppermute | solution.py:678
  100.8 6.6 %copy-start.12 = (f32[256,128]{1,0:T(8,128)S(1)}, f32[256,128]{1,0:T(8,128)}, u32[]{:S(2)}) copy-start(f32[256,128]{1,0:T(8,128)} %copy-done.11) | copy-start | bytes 393220
  100.8 8.9 %copy-start.5 = (bf16[1024,128]{1,0:T(8,128)(2,1)S(1)}, bf16[1024,128]{1,0:T(8,128)(2,1)}, u32[]{:S(2)}) copy-start(bf16[1024,128]{1,0:T(8,128)(2,1)} %readout_ref.5) | copy-start | bytes 786436
  100.8 36.5 %all-to-all-start.1 = ((bf16[64,8,2048]{2,1,0:T(8,128)(2,1)}), bf16[64,8,2048]{2,1,0:T(8,128)(2,1)S(1)}, u32[]{:S(2)}, u32[]{:S(2)}) async-start(bf16[64,8,2048]{2,1,0:T(8,128)(2,1)} %bitcast.14), calls=%async_computation.1 | async-start | bytes 4194304 | tf_op jit(solution)/shard_map/all_to_all | solution.py:683
  (8 other events, 30.2 us)

commit v6 on v5

--- a/solution.py
+++ b/solution.py
@@ -244,6 +244,7 @@
     hidden_ref,
     forecast_ref,
     probs,
+    inverse_ref,
     stat_rows,
     buffer,
     arrived,
@@ -257,7 +258,6 @@
             copies[place].start()
         normed_ref[:WIN] = layer_norm(left_ref[...])
         normed_ref[WIN:] = layer_norm(right_ref[...])
-        probs[...] = jnp.zeros_like(probs)
 
     fetch_one(weight_ref, buffer, arrived, WIDTH, 1024, step).wait()
     fetch_one(weight_ref, buffer, arrived, WIDTH, 1024, step + 4).wait()
@@ -287,9 +287,9 @@
                 q_head = jnp.where(low_q, query_fill, q_pair)
                 k_head = jnp.where(low_k, fill, k_pair)
             scores.append(dot_nt(k_head, q_head))
-    scales = []
+    tops = []
     for slot in range(4):
-        totals, levels = [], []
+        levels = []
         for tile in range(2):
             rows = slice(tile * 128, tile * 128 + 640)
             lanes = slice(tile * 128, tile * 128 + 128)
@@ -298,26 +298,28 @@
                 jnp.max(middle, axis=0, keepdims=True),
                 jnp.max(jnp.maximum(first, last), axis=0, keepdims=True),
             )
-            first = jnp.exp(first - top)
-            middle = jnp.exp(middle - top)
-            last = jnp.exp(last - top)
-            total = jnp.sum(middle, axis=0, keepdims=True) + jnp.sum(
-                first + last, axis=0, keepdims=True
-            )
             start = tile * 128
-            probs[slot, start : start + 128, lanes] = first.astype(BF)
-            probs[slot, start + 128 : start + 512, lanes] = middle.astype(BF)
-            probs[slot, start + 512 : start + 640, lanes] = last.astype(BF)
-            totals.append(total)
-            levels.append(top + jnp.log(total))
-        scales.append(1.0 / jnp.concatenate(totals, axis=1))
-        stat_rows[pl.ds(step * 4 + slot, 1), :] = jnp.concatenate(levels, axis=1)
+            probs[slot, start : start + 128, lanes] = jnp.exp(first - top).astype(BF)
+            probs[slot, start + 128 : start + 512, lanes] = jnp.exp(middle - top).astype(BF)
+            probs[slot, start + 512 : start + 640, lanes] = jnp.exp(last - top).astype(BF)
+            levels.append(top)
+        probs[slot, :128, 128:] = jnp.zeros((128, 128), BF)
+        probs[slot, 640:, :128] = jnp.zeros((128, 128), BF)
+        tops.append(jnp.concatenate(levels, axis=1))
+    ones = jnp.ones((16, fill.shape[0]), BF)
     for pair in range(2):
         halves = []
         for half in range(2):
             slot = pair * 2 + half
             lanes = slice(half * HEAD_WIDTH, (half + 1) * HEAD_WIDTH)
-            halves.append(dot_nn(turned[pair][lanes], probs[slot]) * scales[slot])
+            values = jnp.concatenate([turned[pair][lanes], ones], axis=0)
+            mixed = dot_nn(values, probs[slot])
+            total = mixed[HEAD_WIDTH : HEAD_WIDTH + 1]
+            inverse = 1.0 / total
+            halves.append(mixed[:HEAD_WIDTH] * inverse)
+            head = step * 4 + slot
+            inverse_ref[pl.ds(head, 1), :] = inverse
+            stat_rows[pl.ds(head, 1), :] = tops[slot] + jnp.log(total)
         start = pl.multiple_of(step * WIDTH + pair * PAIR, PAIR)
         attended_ref[:, pl.ds(start, PAIR)] = jnp.concatenate(halves, axis=0).T
 
@@ -358,6 +360,8 @@
             whole(BLOCK, 128),
             whole(BLOCK, 1024),
             whole(BLOCK, 128),
+            pl.BlockSpec((4, window, BLOCK), lambda j: (j, 0, 0)),
+            whole(HEADS, BLOCK),
         ],
         out_shape=[
             jax.ShapeDtypeStruct((2 * WIN, 1024), BF),
@@ -367,9 +371,10 @@
             jax.ShapeDtypeStruct((BLOCK, 128), F32),
             jax.ShapeDtypeStruct((BLOCK, 1024), BF),
             jax.ShapeDtypeStruct((BLOCK, 128), F32),
+            jax.ShapeDtypeStruct((HEADS, window, BLOCK), BF),
+            jax.ShapeDtypeStruct((HEADS, BLOCK), F32),
         ],
         scratch_shapes=[
-            pltpu.VMEM((4, window, BLOCK), BF),
             pltpu.VMEM((128, BLOCK), F32),
             pltpu.VMEM((8, 1024, WIDTH), BF),
             pltpu.SemaphoreType.DMA((8,)),
@@ -471,77 +476,57 @@
 
 
 def query_kernel(
-    counts_ref, q_ref, kcat_ref, vcat_ref, grad_ref, packed_ref, dq_ref, dscores
+    kcat_ref, vcat_ref, grad_ref, packed_ref, probs_ref, inverse_ref, dq_ref, dscores
 ):
     step = pl.program_id(0)
-
-    @pl.when(step == 0)
-    def _():
-        dscores[...] = jnp.zeros_like(dscores)
-
-    fill = key_fill([(counts_ref[0], WIN), (counts_ref[1], BLOCK), (counts_ref[2], WIN)])
-    value_fill = (spare_lane(fill.shape) < 3).astype(BF)
+    window = kcat_ref.shape[0]
+    value_fill = (spare_lane((window, PAIR)) < 3).astype(BF)
     low_q = iota((BLOCK, PAIR), 1) < HEAD_WIDTH
-    low_k = iota(fill.shape, 1) < HEAD_WIDTH
-    terms = packed_ref[:, 128:]
-    ones = (spare_lane((BLOCK, WIDTH)) == 3).astype(F32)
-    q_fill = (dot_nn(terms, stat_spread(step, 0)) + ones).astype(BF)
-    g_fill = dot_nn(terms, stat_spread(step, HEADS)).astype(BF)
+    low_k = iota((window, PAIR), 1) < HEAD_WIDTH
+    g_fill = dot_nn(packed_ref[:, 128:], stat_spread(step, HEADS)).astype(BF)
     turned = []
     for pair in range(2):
         columns = slice(pair * PAIR, (pair + 1) * PAIR)
-        q_pair = q_ref[:, columns] * jnp.asarray(HEAD_WIDTH ** (-0.5), BF)
         g_pair = grad_ref[:, columns]
-        k_pair = kcat_ref[:, columns]
         v_pair = vcat_ref[:, columns]
-        k_turned = k_pair.T
+        k_turned = kcat_ref[:, columns].T
         for half in range(2):
             slot = pair * 2 + half
             pick_q = low_q if half == 0 else ~low_q
             pick_k = low_k if half == 0 else ~low_k
-            q_head = jnp.where(pick_q, q_pair, q_fill[:, columns])
             g_head = jnp.where(pick_q, g_pair, g_fill[:, columns])
-            k_head = jnp.where(pick_k, k_pair, fill)
             v_head = jnp.where(pick_k, v_pair, value_fill)
-            scores = dot_nt(k_head, q_head)
             change = dot_nt(v_head, g_head)
-            for tile in range(2):
-                rows = slice(tile * 128, tile * 128 + 640)
-                lanes = slice(tile * 128, tile * 128 + 128)
-                ends = jnp.exp(scores[rows, lanes]) * change[rows, lanes]
-                first, middle, last = keep_band(ends, 0.0)
-                start = tile * 128
-                dscores[slot, start : start + 128, lanes] = first.astype(BF)
-                dscores[slot, start + 128 : start + 512, lanes] = middle.astype(BF)
-                dscores[slot, start + 512 : start + 640, lanes] = last.astype(BF)
+            dscores[slot] = (probs_ref[slot].astype(F32) * change).astype(BF)
             turned.append(k_turned[half * HEAD_WIDTH : (half + 1) * HEAD_WIDTH])
     for slot in range(4):
-        dquery = dot_nn(turned[slot], dscores[slot]) * HEAD_WIDTH ** (-0.5)
+        scale = inverse_ref[pl.ds(step * 4 + slot, 1), :] * HEAD_WIDTH ** (-0.5)
+        dquery = dot_nn(turned[slot], dscores[slot]) * scale
         dq_ref[slot * HEAD_WIDTH : (slot + 1) * HEAD_WIDTH] = dquery.astype(BF)
 
 
-def query_grads(counts, projected, kcat, vcat, grad, packed):
+def query_grads(kcat, vcat, grad, packed, probs, inverse):
     part = lambda rows, first: pl.BlockSpec((rows, WIDTH), lambda j: (0, first + j))
     window = 2 * WIN + BLOCK
     return pl.pallas_call(
         query_kernel,
         grid=(4,),
         in_specs=[
-            pl.BlockSpec(memory_space=pltpu.SMEM),
-            part(BLOCK, 0),
             part(window, 0),
             part(window, 0),
             part(BLOCK, 0),
             pl.BlockSpec((BLOCK, 256), lambda j: (0, 0)),
+            pl.BlockSpec((4, window, BLOCK), lambda j: (j, 0, 0)),
+            pl.BlockSpec((HEADS, BLOCK), lambda j: (0, 0)),
         ],
         out_specs=pl.BlockSpec((WIDTH, BLOCK), lambda j: (j, 0)),
         out_shape=jax.ShapeDtypeStruct((1024, BLOCK), BF),
         scratch_shapes=[pltpu.VMEM((4, window, BLOCK), BF)],
-        compiler_params=pltpu.CompilerParams(vmem_limit_bytes=12 * 1024 * 1024),
+        compiler_params=pltpu.CompilerParams(vmem_limit_bytes=16 * 1024 * 1024),
         cost_estimate=pl.CostEstimate(
             flops=6 << 30, bytes_accessed=5 << 20, transcendentals=3 << 20
         ),
-    )(counts, projected, kcat, vcat, grad, packed)
+    )(kcat, vcat, grad, packed, probs, inverse)
 
 
 def key_kernel(
@@ -707,7 +692,7 @@
 
     projected, turned = project(latent_own, w_qkv)
     turned_other = swap_core(turned)
-    normed_halo, kcat, vcat, attended, stats, hidden, forecast = forward(
+    normed_halo, kcat, vcat, attended, stats, hidden, forecast, probs, inverse = forward(
         scalars, from_left, from_right, latent_own, w_qkv, projected, w_out, readout_weight
     )
     near = lax.ppermute(forecast, "x_hi", SWAP)
@@ -721,7 +706,7 @@
     packed_left = lax.ppermute(packed, CELLS, up)
     packed_right = lax.ppermute(packed, CELLS, down)
 
-    dquery = query_grads(scalars, projected, kcat, vcat, grad, packed)
+    dquery = query_grads(kcat, vcat, grad, packed, probs, inverse)
     dquery, packed_left, packed_right = lax.optimization_barrier(
         (dquery, packed_left, packed_right)
     )

time: 139 us -> 139 us (level)
  local copies, waits for them, and re-layouts: 5.53 us -> 8.93 us
  Pallas kernels: 52.2 us -> 48.9 us
    unnamed x41, local copies, waits for them, and re-layouts: 4.07 us -> 7.46 us
    pallas_call x1, Pallas kernels: 7.56 us -> 4.42 us  [query_grads(): pl.pallas_call(query_kernel, grid=(4,), in_specs=[part(window, 0), part(w...]
  transfers between devices with their start and end apart: 12 -> 12, of which waited for: 7 -> 7; matrix products, arithmetic and copies ran while one was open for 3% -> 3% of each run, Pallas kernels for 26% -> 24%
where the time goes in v6:
time: 139 us; the launch traced here: 138 us
  Pallas kernels  48.9 us (35%)
  waiting for transfers between devices  41.1 us (30%)
  starting transfers between devices  33.6 us (24%)
  local copies, waits for them, and re-layouts  8.93 us (6%)
  other arithmetic  3.16 us (2%)
  between operations  2.24 us (2%)
    all_to_all x2, waiting for transfers between devices, scatter(): lax.all_to_all(partial.reshape(64, 8, columns), CHIPS, split_axis=0, conc...  31.1 us
    all_to_all x2, starting transfers between devices, scatter(): lax.all_to_all(partial.reshape(64, 8, columns), CHIPS, split_axis=0, conc...  19.1 us
    pallas_call x1, Pallas kernels, forward(): pl.pallas_call(forward_kernel, grid=(4,), in_specs=[pl.BlockSpec(memory_s...  13.3 us
    pallas_call x1, Pallas kernels, key_grads(): pl.pallas_call(key_kernel, grid=(4,), in_specs=[pl.BlockSpec(memory_space...  11.3 us
    unnamed x41, local copies, waits for them, and re-layouts  7.46 us
    pallas_call x1, Pallas kernels, project(): pl.pallas_call(project_kernel, grid=(6,), in_specs=[pl.BlockSpec((rows, w...  6.41 us
    pallas_call x2, Pallas kernels, partial_sums(): pl.pallas_call(partial_kernel if smalls else plain_partial_kernel, in_spe...  5.54 us
    ppermute x5, waiting for transfers between devices, swap_core(): return lax.ppermute(values, 'core', SWAP)  5.35 us
  transfers between devices with their start and end apart: 12, of which 7 were waited for; matrix products, arithmetic and copies ran while one was open for 3% of the time, Pallas kernels for 24%

profile of v6, /device:TPU:0, one launch (start us, length us, event | category | flops | bytes accessed | tf_op | source)
XLA Modules:
  0.0 138.2 jit_solution(3955966745156490217)
XLA Ops:
  0.6 3.9 %collective-permute-start = (bf16[256,1024]{1,0:T(8,128)(2,1)}, bf16[256,1024]{1,0:T(8,128)(2,1)S(1)}, u32[]{:S(2)}, u32[]{:S(2)}) collective-permute-start(bf16[256,1024]{1,0:T(8,128)(2,1)} %bitcast.25), channel_id=1, source_target_pairs={{0,1},{1,2},{2,3},{3,4},{4,5},{5,6},{6,7},{7,8},{8,9},{9,10},{10,1... | collective-permute-start | bytes 1572872 | tf_op jit(solution)/shard_map/ppermute | solution.py:683
  4.6 1.3 collective-permute-start.1
  5.9 1.4 fusion.2
  9.2 6.4 %shard_map.77 = (bf16[256,3072]{1,0:T(8,128)(2,1)}, bf16[1024,256]{1,0:T(8,128)(2,1)}) custom-call(bf16[256,1024]{1,0:T(8,128)(2,1)} %bitcast.27, bf16[1024,3072]{1,0:T(8,128)(2,1)} %weight_ref.5), custom_call_target="tpu_custom_call" | custom-call | flops 2147483648 | bytes 8388608 | tf_op jit(solution)/shard_map/pallas_call | solution.py:95
  16.0 4.2 %collective-permute-done.1.right_ref = bf16[256,1024]{1,0:T(8,128)(2,1)S(1)} collective-permute-done((bf16[256,1024]{1,0:T(8,128)(2,1)}, bf16[256,1024]{1,0:T(8,128)(2,1)S(1)}, u32[]{:S(2)}, u32[]{:S(2)}) %collective-permute-start.1) | collective-permute-done | bytes 524320 | tf_op jit(solution)/shard_map/ppermute | solution.py:684
  20.2 13.3 %shard_map.78 = (bf16[512,1024]{1,0:T(8,128)(2,1)S(1)}, bf16[768,1024]{1,0:T(8,128)(2,1)}, bf16[768,1024]{1,0:T(8,128)(2,1)}, f32[256,1024]{1,0:T(8,128)S(1)}, f...) custom-call(s32[3]{0:T(128)S(1)} %pad_add_fusion.counts_ref, ...), custom_call_target="tpu_custom_call" | custom-call | flops 6442450944 | bytes 12582912 | tf_op jit(solution)/shard_map/pallas_call | solution.py:340
  34.6 3.0 %collective-permute-start.2 = (f32[256,128]{1,0:T(8,128)S(1)}, f32[256,128]{1,0:T(8,128)S(1)}, u32[]{:S(2)}, u32[]{:S(2)}) collective-permute-start(f32[256,128]{1,0:T(8,128)S(1)} %get-tuple-element.27.own_ref), channel_id=1, source_target_pairs={{0,64},{64,0},{1,65},{65,1},{2,66},{66,2},{3,67},{67,3},{4,68},{68... | collective-permute-start | bytes 393224 | tf_op jit(solution)/shard_map/ppermute | solution.py:698
  37.6 4.3 %shard_map.79.qhalo_ref = bf16[512,1024]{1,0:T(8,128)(2,1)S(1)} custom-call(bf16[512,1024]{1,0:T(8,128)(2,1)} %copy-done.6, bf16[1024,3072]{1,0:T(8,128)(2,1)} %weight_ref.5), custom_call_target="tpu_custom_call" | custom-call | tf_op jit(solution)/shard_map/pallas_call | solution.py:133
  43.6 3.6 %shard_map.80 = (f32[256,128]{1,0:T(8,128)S(1)}, bf16[256,256]{1,0:T(8,128)(2,1)S(1)}, bf16[256,1024]{1,0:T(8,128)(2,1)S(1)}, bf16[1024,256]{1,0:T(8,128)(2,1)}) custom-call(s32[3]{0:T(128)S(1)} %pad_add_fusion.counts_ref, f32[256,128]{1,0:T(8,128)S(1)} %get-tuple-element.27.own_ref, f32[256,128]{1,0:T(8,128)S(1)} %collective-permute-done.2.near_ref, ...), custom_call_target="tpu_custom_call" | custom-call | tf_op jit(solution)/shard_map/pallas_call | solution.py:464
  47.9 3.6 %collective-permute-start.5 = (bf16[256,256]{1,0:T(8,128)(2,1)S(1)}, bf16[256,256]{1,0:T(8,128)(2,1)S(1)}, u32[]{:S(2)}, u32[]{:S(2)}) collective-permute-start(bf16[256,256]{1,0:T(8,128)(2,1)S(1)} %get-tuple-element.38.packed_ref.own_ref), channel_id=1, source_target_pairs={{0,1},{1,2},{2,3},{3,4},{4,5},{5,6},{6,7},{7,8},{8,9},{9,10},{10,1... | collective-permute-start | bytes 393224 | tf_op jit(solution)/shard_map/ppermute | solution.py:706
  51.5 1.3 collective-permute-start.6
  52.9 2.8 %copy-done.14 = bf16[16,768,256]{2,1,0:T(8,128)(2,1)S(1)} copy-done((bf16[16,768,256]{2,1,0:T(8,128)(2,1)S(1)}, bf16[16,768,256]{2,1,0:T(8,128)(2,1)}, u32[]{:S(2)}) %copy-start.14) | copy-done | bytes 6291480
  55.7 4.4 %shard_map.81.piece_ref = bf16[1024,256]{1,0:T(8,128)(2,1)S(1)} custom-call(bf16[768,1024]{1,0:T(8,128)(2,1)S(1)} %copy-done.15, bf16[768,1024]{1,0:T(8,128)(2,1)S(1)} %copy-done.16, bf16[256,1024]{1,0:T(8,128)(2,1)S(1)} %get-tuple-element.37.grad_ref, bf16[256,256]{1,0:T(8,128)(2,1)S(1)} %get-tuple-element.38.packed_ref.own_ref, ...), custom_call_target="tpu_custom_call" | custom-call | flops 6442450944 | bytes 5242880 | tf_op jit(solution)/shard_map/pallas_call | solution.py:511
  60.8 1.5 %collective-permute-done.7.other_ref = bf16[1024,256]{1,0:T(8,128)(2,1)S(1)} collective-permute-done((bf16[1024,256]{1,0:T(8,128)(2,1)S(1)}, bf16[1024,256]{1,0:T(8,128)(2,1)S(1)}, u32[]{:S(2)}, u32[]{:S(2)}) %collective-permute-start.7) | collective-permute-done | bytes 524320 | tf_op jit(solution)/shard_map/ppermute | solution.py:663
  62.3 2.9 %shard_map.82 = bf16[512,1280]{1,0:T(8,128)(2,1)} custom-call(s32[1]{0:T(128)} %bitcast.7.core_ref, bf16[2,2,256,256]{3,2,1,0:T(8,128)(2,1)S(1)} %bitcast.18, bf16[2,2,256,256]{3,2,1,0:T(8,128)(2,1)S(1)} %bitcast.20, bf16[1024,256]{1,0:T(8,128)(2,1)S(1)} %shard_map.81.piece_ref, bf16[1024,256]{1,0:T(8,128)(2,1)S(1)} %collective-permute-done.7.other_ref, ...), custom_call_target="tpu_custom_call" | custom-call | tf_op jit(solution)/shard_map/pallas_call | solution.py:178
  65.2 12.5 %all-to-all-start = ((bf16[64,8,1280]{2,1,0:T(8,128)(2,1)}), bf16[64,8,1280]{2,1,0:T(8,128)(2,1)S(1)}, u32[]{:S(2)}, u32[]{:S(2)}) async-start(bf16[64,8,1280]{2,1,0:T(8,128)(2,1)} %bitcast.13), calls=%async_computation | async-start | bytes 2621440 | tf_op jit(solution)/shard_map/all_to_all | solution.py:668
  77.8 11.3 %shard_map.83 = bf16[2,1024,256]{2,1,0:T(8,128)(2,1)} custom-call(s32[3]{0:T(128)} %copy-done.12, bf16[256,3072]{1,0:T(8,128)(2,1)} %get-tuple-element.26.q_ref.k_ref.v_ref, bf16[256,3072]{1,0:T(8,128)(2,1)} %get-tuple-element.26.q_ref.k_ref.v_ref, bf16[256,3072]{1,0:T(8,128)(2,1)} %get-tuple-element.26.q_ref.k_ref.v_ref, bf16[512,1024]{1,0:T(8,128)(2,1)} %copy-done.2, ...), custom_call_target="tpu_custom_call" | custom-call | tf_op jit(solution)/shard_map/pallas_call | solution.py:615
  89.1 2.8 %collective-permute-done.9.other_ref = bf16[2048,256]{1,0:T(8,128)(2,1)S(1)} collective-permute-done((bf16[2048,256]{1,0:T(8,128)(2,1)}, bf16[2048,256]{1,0:T(8,128)(2,1)S(1)}, u32[]{:S(2)}, u32[]{:S(2)}) %collective-permute-start.9) | collective-permute-done | bytes 1048608 | tf_op jit(solution)/shard_map/ppermute | solution.py:663
  91.9 1.2 copy-done.1
  93.1 2.6 %shard_map.84 = bf16[512,2048]{1,0:T(8,128)(2,1)} custom-call(s32[1]{0:T(128)} %bitcast.7.core_ref, bf16[2,2,256,256]{3,2,1,0:T(8,128)(2,1)S(1)} %bitcast.19, bf16[2,2,256,256]{3,2,1,0:T(8,128)(2,1)S(1)} %bitcast.21, bf16[2048,256]{1,0:T(8,128)(2,1)S(1)} %bitcast.17, bf16[2048,256]{1,0:T(8,128)(2,1)S(1)} %collective-permute-done.9.other_ref), custom_call_target="tpu_custom_call" | custom-call | tf_op jit(solution)/shard_map/pallas_call | solution.py:178
  95.8 3.8 %all-to-all-done = bf16[64,8,1280]{2,1,0:T(8,128)(2,1)S(1)} async-done(((bf16[64,8,1280]{2,1,0:T(8,128)(2,1)}), bf16[64,8,1280]{2,1,0:T(8,128)(2,1)S(1)}, u32[]{:S(2)}, u32[]{:S(2)}) %all-to-all-start) | async-done | bytes 1310752 | tf_op jit(solution)/shard_map/all_to_all | solution.py:668
  100.6 6.6 %all-to-all-start.1 = ((bf16[64,8,2048]{2,1,0:T(8,128)(2,1)}), bf16[64,8,2048]{2,1,0:T(8,128)(2,1)S(1)}, u32[]{:S(2)}, u32[]{:S(2)}) async-start(bf16[64,8,2048]{2,1,0:T(8,128)(2,1)} %bitcast.14), calls=%async_computation.1 | async-start | bytes 4194304 | tf_op jit(solution)/shard_map/all_to_all | solution.py:668
  108.0 1.5 %convert_reduce_fusion.1 = f32[8,1280]{1,0:T(8,128)S(1)} fusion(bf16[64,8,1280]{2,1,0:T(8,128)(2,1)} %copy-done.17), kind=kLoop, calls=%fused_computation.1 | loop fusion | flops 1300480 | bytes 1351680 | tf_op jit(solution)/shard_map/reduce_sum | solution.py:672
  109.9 27.3 %all-to-all-done.1 = bf16[64,8,2048]{2,1,0:T(8,128)(2,1)S(1)} async-done(((bf16[64,8,2048]{2,1,0:T(8,128)(2,1)}), bf16[64,8,2048]{2,1,0:T(8,128)(2,1)S(1)}, u32[]{:S(2)}, u32[]{:S(2)}) %all-to-all-start.1) | async-done | bytes 2097184 | tf_op jit(solution)/shard_map/all_to_all | solution.py:668
  (59 shorter events, 8.2 us)
Async XLA Ops:
  0.6 15.4 %collective-permute-start = (bf16[256,1024]{1,0:T(8,128)(2,1)}, bf16[256,1024]{1,0:T(8,128)(2,1)S(1)}, u32[]{:S(2)}, u32[]{:S(2)}) collective-permute-start(bf16[256,1024]{1,0:T(8,128)(2,1)} %bitcast.25), channel_id=1, source_target_pairs={{0,1},{1,2},{2,3},{3,4},{4,5},{5,6},{6,7},{7,8},{8,9},{9,10},{10,1... | collective-permute-start | bytes 1572872 | tf_op jit(solution)/shard_map/ppermute | solution.py:683
  4.6 15.6 %collective-permute-start.1 = (bf16[256,1024]{1,0:T(8,128)(2,1)}, bf16[256,1024]{1,0:T(8,128)(2,1)S(1)}, u32[]{:S(2)}, u32[]{:S(2)}) collective-permute-start(bf16[256,1024]{1,0:T(8,128)(2,1)} %bitcast.26), channel_id=1, source_target_pairs={{1,0},{2,1},{3,2},{4,3},{5,4},{6,5},{7,6},{8,7},{9,8},{10,9},{11,1... | collective-permute-start | bytes 1572872 | tf_op jit(solution)/shard_map/ppermute | solution.py:684
  9.2 34.4 %copy-start.12 = (s32[3]{0:T(128)}, s32[3]{0:T(128)S(1)}, u32[]{:S(2)}) copy-start(s32[3]{0:T(128)S(1)} %pad_add_fusion.counts_ref) | copy-start | bytes 40
  9.2 11.0 %copy-start.3 = (bf16[1024,128]{1,0:T(8,128)(2,1)S(1)}, bf16[1024,128]{1,0:T(8,128)(2,1)}, u32[]{:S(2)}) copy-start(bf16[1024,128]{1,0:T(8,128)(2,1)} %readout_ref.5) | copy-start | bytes 786436
  9.2 11.0 %copy-start.13 = (bf16[1,256,1024]{2,1,0:T(8,128)(2,1)S(1)}, bf16[1,256,1024]{2,1,0:T(8,128)(2,1)}, u32[]{:S(2)}) copy-start(bf16[1,256,1024]{2,1,0:T(8,128)(2,1)} %param.6) | copy-start | bytes 1572868
  34.6 7.4 %collective-permute-start.2 = (f32[256,128]{1,0:T(8,128)S(1)}, f32[256,128]{1,0:T(8,128)S(1)}, u32[]{:S(2)}, u32[]{:S(2)}) collective-permute-start(f32[256,128]{1,0:T(8,128)S(1)} %get-tuple-element.27.own_ref), channel_id=1, source_target_pairs={{0,64},{64,0},{1,65},{65,1},{2,66},{66,2},{3,67},{67,3},{4,68},{68... | collective-permute-start | bytes 393224 | tf_op jit(solution)/shard_map/ppermute | solution.py:698
  37.6 6.0 %copy-start = (bf16[1024,1024]{1,0:T(8,128)(2,1)S(1)}, bf16[1024,1024]{1,0:T(8,128)(2,1)}, u32[]{:S(2)}) copy-start(bf16[1024,1024]{1,0:T(8,128)(2,1)} %w_out_ref.5) | copy-start | bytes 6291460
  37.6 6.0 %copy-start.9 = (f32[256,128]{1,0:T(8,128)S(1)}, f32[256,128]{1,0:T(8,128)}, u32[]{:S(2)}) copy-start(f32[256,128]{1,0:T(8,128)} %target_ref.1) | copy-start | bytes 393220
  41.9 5.3 %copy-start.2 = (bf16[512,1024]{1,0:T(8,128)(2,1)}, bf16[512,1024]{1,0:T(8,128)(2,1)S(1)}, u32[]{:S(2)}) copy-start(bf16[512,1024]{1,0:T(8,128)(2,1)S(1)} %shard_map.79.qhalo_ref) | copy-start | bytes 3145732
  42.0 1.6 %collective-permute-start.3 = (f32[2,256,128]{2,1,0:T(8,128)S(1)}, f32[2,256,128]{2,1,0:T(8,128)S(1)}, u32[]{:S(2)}, u32[]{:S(2)}) collective-permute-start(f32[2,256,128]{2,1,0:T(8,128)S(1)} %pad_maximum_fusion), channel_id=1, source_target_pairs={{0,32},{32,0},{1,33},{33,1},{2,34},{34,2},{3,35},{35,3},{4,36},{36... | collective-permute-start | bytes 786440 | tf_op jit(solution)/shard_map/ppermute | solution.py:663
  42.1 18.7 %collective-permute-start.4 = (bf16[1024,256]{1,0:T(8,128)(2,1)S(1)}, bf16[1024,256]{1,0:T(8,128)(2,1)S(1)}, u32[]{:S(2)}, u32[]{:S(2)}) collective-permute-start(bf16[1024,256]{1,0:T(8,128)(2,1)S(1)} %copy-done.5), channel_id=1, source_target_pairs={{0,32},{32,0},{1,33},{33,1},{2,34},{34,2},{3,35},{35,3},{4,36},{36... | collective-permute-start | bytes 1572872 | tf_op jit(solution)/shard_map/ppermute | solution.py:663
  43.6 9.3 %copy-start.15 = (bf16[768,1024]{1,0:T(8,128)(2,1)S(1)}, bf16[768,1024]{1,0:T(8,128)(2,1)}, u32[]{:S(2)}) copy-start(bf16[768,1024]{1,0:T(8,128)(2,1)} %get-tuple-element.35.kcat_ref) | copy-start | bytes 4718596
  43.6 9.3 %copy-start.16 = (bf16[768,1024]{1,0:T(8,128)(2,1)S(1)}, bf16[768,1024]{1,0:T(8,128)(2,1)}, u32[]{:S(2)}) copy-start(bf16[768,1024]{1,0:T(8,128)(2,1)} %get-tuple-element.36.vcat_ref) | copy-start | bytes 4718596
  47.9 12.3 %copy-start.7 = (bf16[256,1024]{1,0:T(8,128)(2,1)}, bf16[256,1024]{1,0:T(8,128)(2,1)S(1)}, u32[]{:S(2)}) copy-start(bf16[256,1024]{1,0:T(8,128)(2,1)S(1)} %get-tuple-element.37.grad_ref) | copy-start | bytes 1572868
  47.9 12.3 %copy-start.8 = (bf16[256,256]{1,0:T(8,128)(2,1)}, bf16[256,256]{1,0:T(8,128)(2,1)S(1)}, u32[]{:S(2)}) copy-start(bf16[256,256]{1,0:T(8,128)(2,1)S(1)} %get-tuple-element.38.packed_ref.own_ref) | copy-start | bytes 393220
  47.9 12.3 %collective-permute-start.5 = (bf16[256,256]{1,0:T(8,128)(2,1)S(1)}, bf16[256,256]{1,0:T(8,128)(2,1)S(1)}, u32[]{:S(2)}, u32[]{:S(2)}) collective-permute-start(bf16[256,256]{1,0:T(8,128)(2,1)S(1)} %get-tuple-element.38.packed_ref.own_ref), channel_id=1, source_target_pairs={{0,1},{1,2},{2,3},{3,4},{4,5},{5,6},{6,7},{7,8},{8,9},{9,10},{10,1... | collective-permute-start | bytes 393224 | tf_op jit(solution)/shard_map/ppermute | solution.py:706
  51.5 8.7 %collective-permute-start.6 = (bf16[256,256]{1,0:T(8,128)(2,1)S(1)}, bf16[256,256]{1,0:T(8,128)(2,1)S(1)}, u32[]{:S(2)}, u32[]{:S(2)}) collective-permute-start(bf16[256,256]{1,0:T(8,128)(2,1)S(1)} %get-tuple-element.38.packed_ref.own_ref), channel_id=1, source_target_pairs={{1,0},{2,1},{3,2},{4,3},{5,4},{6,5},{7,6},{8,7},{9,8},{10,9},{11,1... | collective-permute-start | bytes 393224 | tf_op jit(solution)/shard_map/ppermute | solution.py:707
  52.8 8.0 %collective-permute-start.8 = (bf16[1024,256]{1,0:T(8,128)(2,1)}, bf16[1024,256]{1,0:T(8,128)(2,1)S(1)}, u32[]{:S(2)}, u32[]{:S(2)}) collective-permute-start(bf16[1024,256]{1,0:T(8,128)(2,1)} %get-tuple-element.42), channel_id=1, source_target_pairs={{0,32},{32,0},{1,33},{33,1},{2,34},{34,2},{3,35},{35,3},{4,36},{36... | collective-permute-start | bytes 1572872 | tf_op jit(solution)/shard_map/ppermute | solution.py:663
  60.2 2.1 %collective-permute-start.7 = (bf16[1024,256]{1,0:T(8,128)(2,1)S(1)}, bf16[1024,256]{1,0:T(8,128)(2,1)S(1)}, u32[]{:S(2)}, u32[]{:S(2)}) collective-permute-start(bf16[1024,256]{1,0:T(8,128)(2,1)S(1)} %shard_map.81.piece_ref), channel_id=1, source_target_pairs={{0,32},{32,0},{1,33},{33,1},{2,34},{34,2},{3,35},{35,3},{4,36},{36... | collective-permute-start | bytes 1572872 | tf_op jit(solution)/shard_map/ppermute | solution.py:663
  65.2 34.3 %all-to-all-start = ((bf16[64,8,1280]{2,1,0:T(8,128)(2,1)}), bf16[64,8,1280]{2,1,0:T(8,128)(2,1)S(1)}, u32[]{:S(2)}, u32[]{:S(2)}) async-start(bf16[64,8,1280]{2,1,0:T(8,128)(2,1)} %bitcast.13), calls=%async_computation | async-start | bytes 2621440 | tf_op jit(solution)/shard_map/all_to_all | solution.py:668
  89.0 2.9 %collective-permute-start.9 = (bf16[2048,256]{1,0:T(8,128)(2,1)}, bf16[2048,256]{1,0:T(8,128)(2,1)S(1)}, u32[]{:S(2)}, u32[]{:S(2)}) collective-permute-start(bf16[2048,256]{1,0:T(8,128)(2,1)} %bitcast.16), channel_id=1, source_target_pairs={{0,32},{32,0},{1,33},{33,1},{2,34},{34,2},{3,35},{35,3},{4,36},{36... | collective-permute-start | bytes 3145736 | tf_op jit(solution)/shard_map/ppermute | solution.py:663
  100.6 6.6 %copy-start.11 = (f32[256,128]{1,0:T(8,128)S(1)}, f32[256,128]{1,0:T(8,128)}, u32[]{:S(2)}) copy-start(f32[256,128]{1,0:T(8,128)} %copy-done.10) | copy-start | bytes 393220
  100.6 8.9 %copy-start.4 = (bf16[1024,128]{1,0:T(8,128)(2,1)S(1)}, bf16[1024,128]{1,0:T(8,128)(2,1)}, u32[]{:S(2)}) copy-start(bf16[1024,128]{1,0:T(8,128)(2,1)} %readout_ref.5) | copy-start | bytes 786436
  100.6 36.6 %all-to-all-start.1 = ((bf16[64,8,2048]{2,1,0:T(8,128)(2,1)}), bf16[64,8,2048]{2,1,0:T(8,128)(2,1)S(1)}, u32[]{:S(2)}, u32[]{:S(2)}) async-start(bf16[64,8,2048]{2,1,0:T(8,128)(2,1)} %bitcast.14), calls=%async_computation.1 | async-start | bytes 4194304 | tf_op jit(solution)/shard_map/all_to_all | solution.py:668
  (8 other events, 21.3 us)

commit v7 on v6

--- a/solution.py
+++ b/solution.py
@@ -56,6 +56,10 @@
 
 FREE = pl.CostEstimate(flops=0, bytes_accessed=0, transcendentals=0)
 HBM = pl.BlockSpec(memory_space=pltpu.HBM)
+
+
+def in_hbm(values):
+    return pltpu.with_memory_space_constraint(values, pltpu.HBM)
 
 
 def fetches(weight_ref, buffer, arrived, width, first):
@@ -109,11 +113,11 @@
             pltpu.VMEM((6, width, 512), BF),
             pltpu.SemaphoreType.DMA((6,)),
         ],
-        compiler_params=pltpu.CompilerParams(vmem_limit_bytes=56 * 1024 * 1024),
+        compiler_params=pltpu.CompilerParams(vmem_limit_bytes=16 * 1024 * 1024),
         cost_estimate=pl.CostEstimate(
             flops=2 * rows * width * width * 4, bytes_accessed=8 << 20, transcendentals=0
         ),
-    )(latent_own, w_qkv)
+    )(latent_own, in_hbm(w_qkv))
 
 
 def halo_query_kernel(normed_ref, weight_ref, out_ref, buffer, arrived):
@@ -140,9 +144,9 @@
             pltpu.VMEM((4, width, 256), BF),
             pltpu.SemaphoreType.DMA((4,)),
         ],
-        compiler_params=pltpu.CompilerParams(vmem_limit_bytes=52 * 1024 * 1024),
+        compiler_params=pltpu.CompilerParams(vmem_limit_bytes=12 * 1024 * 1024),
         cost_estimate=FREE,
-    )(normed_halo, w_qkv)
+    )(normed_halo, in_hbm(w_qkv))
 
 
 def partial_kernel(
@@ -379,7 +383,7 @@
             pltpu.VMEM((8, 1024, WIDTH), BF),
             pltpu.SemaphoreType.DMA((8,)),
         ],
-        compiler_params=pltpu.CompilerParams(vmem_limit_bytes=48 * 1024 * 1024),
+        compiler_params=pltpu.CompilerParams(vmem_limit_bytes=30 * 1024 * 1024),
         cost_estimate=pl.CostEstimate(
             flops=6 << 30, bytes_accessed=12 << 20, transcendentals=3 << 20
         ),
@@ -388,7 +392,7 @@
         left,
         right,
         latent_own,
-        w_qkv,
+        in_hbm(w_qkv),
         projected,
         projected,
         projected,
@@ -635,7 +639,7 @@
             pltpu.VMEM((4, window, BLOCK), BF),
             pltpu.VMEM((2 * WIN, 1024), BF),
         ],
-        compiler_params=pltpu.CompilerParams(vmem_limit_bytes=56 * 1024 * 1024),
+        compiler_params=pltpu.CompilerParams(vmem_limit_bytes=18 * 1024 * 1024),
         cost_estimate=FREE,
     )(
         counts,
@@ -647,7 +651,7 @@
         own,
         left,
         right,
-        w_out,
+        in_hbm(w_out),
         readout_weight,
     )
 

time: 139 us -> 137 us (0.986)
  Pallas kernels: 48.9 us -> 44.9 us
  starting transfers between devices: 33.6 us -> 36.8 us
    all_to_all x2, starting transfers between devices: 19.1 us -> 22.3 us  [scatter(): lax.all_to_all(partial.reshape(64, 8, columns), CHIPS, split_axis=0, conc...]
    pallas_call x1, Pallas kernels: 6.41 us -> 4.15 us  [project(): pl.pallas_call(project_kernel, grid=(6,), in_specs=[pl.BlockSpec((rows, w...]
    all_to_all x2, waiting for transfers between devices: 31.1 us -> 29.4 us  [scatter(): lax.all_to_all(partial.reshape(64, 8, columns), CHIPS, split_axis=0, conc...]
    pallas_call x1, Pallas kernels: 13.3 us -> 11.6 us  [forward(): pl.pallas_call(forward_kernel, grid=(4,), in_specs=[pl.BlockSpec(memory_s...]
    pallas_call x2, Pallas kernels: 5.54 us -> 7.18 us  [partial_sums(): pl.pallas_call(partial_kernel if smalls else plain_partial_kernel, in_spe...]
    unnamed x41 -> x25, local copies, waits for them, and re-layouts: 7.46 us -> 6.57 us
  transfers between devices with their start and end apart: 12 -> 12, of which waited for: 7 -> 8; matrix products, arithmetic and copies ran while one was open for 3% -> 4% of each run, Pallas kernels for 24% -> 22%
where the time goes in v7:
time: 137 us
  Pallas kernels  44.9 us (33%)
  waiting for transfers between devices  41.2 us (30%)
  starting transfers between devices  36.8 us (27%)
  local copies, waits for them, and re-layouts  8.1 us (6%)
  other arithmetic  3.26 us (2%)
  between operations  2.12 us (2%)
    all_to_all x2, waiting for transfers between devices, scatter(): lax.all_to_all(partial.reshape(64, 8, columns), CHIPS, split_axis=0, conc...  29.4 us
    all_to_all x2, starting transfers between devices, scatter(): lax.all_to_all(partial.reshape(64, 8, columns), CHIPS, split_axis=0, conc...  22.3 us
    pallas_call x1, Pallas kernels, forward(): pl.pallas_call(forward_kernel, grid=(4,), in_specs=[pl.BlockSpec(memory_s...  11.6 us
    pallas_call x1, Pallas kernels, key_grads(): pl.pallas_call(key_kernel, grid=(4,), in_specs=[pl.BlockSpec(memory_space...  10.1 us
    pallas_call x2, Pallas kernels, partial_sums(): pl.pallas_call(partial_kernel if smalls else plain_partial_kernel, in_spe...  7.18 us
    unnamed x25, local copies, waits for them, and re-layouts  6.57 us
    ppermute x5, waiting for transfers between devices, swap_core(): return lax.ppermute(values, 'core', SWAP)  5.55 us
    pallas_call x1, Pallas kernels, query_grads(): pl.pallas_call(query_kernel, grid=(4,), in_specs=[part(window, 0), part(w...  5.3 us
  transfers between devices with their start and end apart: 12, of which 8 were waited for; matrix products, arithmetic and copies ran while one was open for 4% of the time, Pallas kernels for 22%

profile of v7, /device:TPU:0, one launch (start us, length us, event | category | flops | bytes accessed | tf_op | source)
XLA Modules:
  0.0 136.7 jit_solution(15512314880039395470)
XLA Ops:
  0.6 3.9 %collective-permute-start = (bf16[256,1024]{1,0:T(8,128)(2,1)}, bf16[256,1024]{1,0:T(8,128)(2,1)S(1)}, u32[]{:S(2)}, u32[]{:S(2)}) collective-permute-start(bf16[256,1024]{1,0:T(8,128)(2,1)} %bitcast.22), channel_id=1, source_target_pairs={{0,1},{1,2},{2,3},{3,4},{4,5},{5,6},{6,7},{7,8},{8,9},{9,10},{10,1... | collective-permute-start | bytes 1572872 | tf_op jit(solution)/shard_map/ppermute | solution.py:687
  4.6 1.3 collective-permute-start.1
  5.9 1.4 %fusion.2 = (s32[1]{0:T(128)}, s32[1]{0:T(128)}, s32[1]{0:T(128)}) fusion(s32[32]{0:T(128)} %param.7, s32[]{:T(128)S(6)} %max.3, s32[]{:T(128)S(6)} %select_n.19, s32[]{:T(128)S(6)} %select_n.18), kind=kLoop, calls=%fused_computation.8 | loop fusion | bytes 36 | tf_op jit(solution)/shard_map/dynamic_slice | solution.py:691
  9.4 1.0 copy-done.11
  10.4 4.1 %shard_map.77 = (bf16[256,3072]{1,0:T(8,128)(2,1)S(1)}, bf16[1024,256]{1,0:T(8,128)(2,1)S(1)}) custom-call(bf16[256,1024]{1,0:T(8,128)(2,1)S(1)} %bitcast.24, bf16[1024,3072]{1,0:T(8,128)(2,1)} %weight_ref.5), custom_call_target="tpu_custom_call" | custom-call | flops 2147483648 | bytes 8388608 | tf_op jit(solution)/shard_map/pallas_call | solution.py:99
  14.6 1.5 %collective-permute-done.left_ref = bf16[256,1024]{1,0:T(8,128)(2,1)S(1)} collective-permute-done((bf16[256,1024]{1,0:T(8,128)(2,1)}, bf16[256,1024]{1,0:T(8,128)(2,1)S(1)}, u32[]{:S(2)}, u32[]{:S(2)}) %collective-permute-start) | collective-permute-done | bytes 524320 | tf_op jit(solution)/shard_map/ppermute | solution.py:687
  16.0 4.3 %collective-permute-done.1.right_ref = bf16[256,1024]{1,0:T(8,128)(2,1)} collective-permute-done((bf16[256,1024]{1,0:T(8,128)(2,1)}, bf16[256,1024]{1,0:T(8,128)(2,1)}, u32[]{:S(2)}, u32[]{:S(2)}) %collective-permute-start.1) | collective-permute-done | bytes 524320 | tf_op jit(solution)/shard_map/ppermute | solution.py:688
  20.3 11.6 %shard_map.78 = (bf16[512,1024]{1,0:T(8,128)(2,1)S(1)}, bf16[768,1024]{1,0:T(8,128)(2,1)S(1)}, bf16[768,1024]{1,0:T(8,128)(2,1)S(1)}, f32[256,1024]{1,0:T(8,128)...) custom-call(s32[3]{0:T(128)S(1)} %pad_add_fusion.counts_ref, ...), custom_call_target="tpu_custom_call" | custom-call | flops 6442450944 | bytes 12582912 | tf_op jit(solution)/shard_map/pallas_call | solution.py:344
  32.0 3.1 %collective-permute-start.2 = (f32[256,128]{1,0:T(8,128)S(1)}, f32[256,128]{1,0:T(8,128)S(1)}, u32[]{:S(2)}, u32[]{:S(2)}) collective-permute-start(f32[256,128]{1,0:T(8,128)S(1)} %get-tuple-element.27.own_ref), channel_id=1, source_target_pairs={{0,64},{64,0},{1,65},{65,1},{2,66},{66,2},{3,67},{67,3},{4,68},{68... | collective-permute-start | bytes 393224 | tf_op jit(solution)/shard_map/ppermute | solution.py:702
  35.1 3.0 %shard_map.79.qhalo_ref = bf16[512,1024]{1,0:T(8,128)(2,1)S(1)} custom-call(bf16[512,1024]{1,0:T(8,128)(2,1)S(1)} %get-tuple-element.28.normed_ref, bf16[1024,3072]{1,0:T(8,128)(2,1)} %weight_ref.5), custom_call_target="tpu_custom_call" | custom-call | tf_op jit(solution)/shard_map/pallas_call | solution.py:137
  40.2 3.6 %shard_map.80 = (f32[256,128]{1,0:T(8,128)S(1)}, bf16[256,256]{1,0:T(8,128)(2,1)S(1)}, bf16[256,1024]{1,0:T(8,128)(2,1)S(1)}, bf16[1024,256]{1,0:T(8,128)(2,1)}) custom-call(s32[3]{0:T(128)S(1)} %pad_add_fusion.counts_ref, f32[256,128]{1,0:T(8,128)S(1)} %get-tuple-element.27.own_ref, f32[256,128]{1,0:T(8,128)S(1)} %collective-permute-done.2.near_ref, ...), custom_call_target="tpu_custom_call" | custom-call | tf_op jit(solution)/shard_map/pallas_call | solution.py:468
  44.4 3.6 %collective-permute-start.5 = (bf16[256,256]{1,0:T(8,128)(2,1)S(1)}, bf16[256,256]{1,0:T(8,128)(2,1)S(1)}, u32[]{:S(2)}, u32[]{:S(2)}) collective-permute-start(bf16[256,256]{1,0:T(8,128)(2,1)S(1)} %get-tuple-element.38.packed_ref.own_ref), channel_id=1, source_target_pairs={{0,1},{1,2},{2,3},{3,4},{4,5},{5,6},{6,7},{7,8},{8,9},{9,10},{10,1... | collective-permute-start | bytes 393224 | tf_op jit(solution)/shard_map/ppermute | solution.py:710
  48.0 1.3 collective-permute-start.6
  49.4 5.3 %shard_map.81.piece_ref = bf16[1024,256]{1,0:T(8,128)(2,1)} custom-call(bf16[768,1024]{1,0:T(8,128)(2,1)S(1)} %get-tuple-element.35.kcat_ref, bf16[768,1024]{1,0:T(8,128)(2,1)S(1)} %get-tuple-element.36.vcat_ref, bf16[256,1024]{1,0:T(8,128)(2,1)S(1)} %get-tuple-element.37.grad_ref, bf16[256,256]{1,0:T(8,128)(2,1)S(1)} %get-tuple-element.38.packed_ref.own_ref, ...), custom_call_target="tpu_custom_call" | custom-call | flops 6442450944 | bytes 5242880 | tf_op jit(solution)/shard_map/pallas_call | solution.py:515
  56.6 1.9 %collective-permute-done.7.other_ref = bf16[1024,256]{1,0:T(8,128)(2,1)} collective-permute-done((bf16[1024,256]{1,0:T(8,128)(2,1)}, bf16[1024,256]{1,0:T(8,128)(2,1)}, u32[]{:S(2)}, u32[]{:S(2)}) %collective-permute-start.7) | collective-permute-done | bytes 524320 | tf_op jit(solution)/shard_map/ppermute | solution.py:667
  58.4 3.5 %shard_map.82 = bf16[512,1280]{1,0:T(8,128)(2,1)} custom-call(s32[1]{0:T(128)} %bitcast.7.core_ref, bf16[2,2,256,256]{3,2,1,0:T(8,128)(2,1)S(1)} %bitcast.18, bf16[2,2,256,256]{3,2,1,0:T(8,128)(2,1)} %bitcast.9.normed_other_ref, bf16[1024,256]{1,0:T(8,128)(2,1)} %shard_map.81.piece_ref, bf16[1024,256]{1,0:T(8,128)(2,1)} %collective-permute-done.7.other_ref, ...), custom_call_target="tpu_custom_call" | custom-call | tf_op jit(solution)/shard_map/pallas_call | solution.py:182
  61.9 14.0 %all-to-all-start = ((bf16[64,8,1280]{2,1,0:T(8,128)(2,1)}), bf16[64,8,1280]{2,1,0:T(8,128)(2,1)}, u32[]{:S(2)}, u32[]{:S(2)}) async-start(bf16[64,8,1280]{2,1,0:T(8,128)(2,1)} %bitcast.13), calls=%async_computation | async-start | bytes 2621440 | tf_op jit(solution)/shard_map/all_to_all | solution.py:672
  78.8 10.1 %shard_map.83 = bf16[2,1024,256]{2,1,0:T(8,128)(2,1)S(1)} custom-call(s32[3]{0:T(128)S(1)} %pad_add_fusion.counts_ref, bf16[256,3072]{1,0:T(8,128)(2,1)S(1)} %get-tuple-element.26.q_ref.k_ref.v_ref, bf16[256,3072]{1,0:T(8,128)(2,1)S(1)} %get-tuple-element.26.q_ref.k_ref.v_ref, bf16[256,3072]{1,0:T(8,128)(2,1)S(1)} %get-tuple-element.26.q_ref.k_ref.v_ref, ...), custom_call_target="tpu_custom_call" | custom-call | tf_op jit(solution)/shard_map/pallas_call | solution.py:619
  89.1 2.6 %collective-permute-done.9.other_ref = bf16[2048,256]{1,0:T(8,128)(2,1)S(1)} collective-permute-done((bf16[2048,256]{1,0:T(8,128)(2,1)S(1)}, bf16[2048,256]{1,0:T(8,128)(2,1)S(1)}, u32[]{:S(2)}, u32[]{:S(2)}) %collective-permute-start.9) | collective-permute-done | bytes 1048608 | tf_op jit(solution)/shard_map/ppermute | solution.py:667
  91.7 3.7 %shard_map.84 = bf16[512,2048]{1,0:T(8,128)(2,1)} custom-call(s32[1]{0:T(128)} %bitcast.7.core_ref, bf16[2,2,256,256]{3,2,1,0:T(8,128)(2,1)S(1)} %bitcast.19, bf16[2,2,256,256]{3,2,1,0:T(8,128)(2,1)} %bitcast.9.normed_other_ref, bf16[2048,256]{1,0:T(8,128)(2,1)S(1)} %bitcast.17, bf16[2048,256]{1,0:T(8,128)(2,1)S(1)} %collective-permute-done.9.other_ref), custom_call_target="tpu_custom_call" | custom-call | tf_op jit(solution)/shard_map/pallas_call | solution.py:182
  95.4 2.0 %all-to-all-done = bf16[64,8,1280]{2,1,0:T(8,128)(2,1)} async-done(((bf16[64,8,1280]{2,1,0:T(8,128)(2,1)}), bf16[64,8,1280]{2,1,0:T(8,128)(2,1)}, u32[]{:S(2)}, u32[]{:S(2)}) %all-to-all-start) | async-done | bytes 1310752 | tf_op jit(solution)/shard_map/all_to_all | solution.py:672
  97.4 8.3 %all-to-all-start.1 = ((bf16[64,8,2048]{2,1,0:T(8,128)(2,1)}), bf16[64,8,2048]{2,1,0:T(8,128)(2,1)S(1)}, u32[]{:S(2)}, u32[]{:S(2)}) async-start(bf16[64,8,2048]{2,1,0:T(8,128)(2,1)} %bitcast.14), calls=%async_computation.1 | async-start | bytes 4194304 | tf_op jit(solution)/shard_map/all_to_all | solution.py:672
  106.5 1.5 %convert_reduce_fusion.1 = f32[8,1280]{1,0:T(8,128)S(1)} fusion(bf16[64,8,1280]{2,1,0:T(8,128)(2,1)} %all-to-all-done), kind=kLoop, calls=%fused_computation.1 | loop fusion | flops 1300480 | bytes 1351680 | tf_op jit(solution)/shard_map/reduce_sum | solution.py:676
  108.4 27.3 %all-to-all-done.1 = bf16[64,8,2048]{2,1,0:T(8,128)(2,1)S(1)} async-done(((bf16[64,8,2048]{2,1,0:T(8,128)(2,1)}), bf16[64,8,2048]{2,1,0:T(8,128)(2,1)S(1)}, u32[]{:S(2)}, u32[]{:S(2)}) %all-to-all-start.1) | async-done | bytes 2097184 | tf_op jit(solution)/shard_map/all_to_all | solution.py:672
  (43 shorter events, 10.4 us)
Async XLA Ops:
  0.6 15.4 %collective-permute-start = (bf16[256,1024]{1,0:T(8,128)(2,1)}, bf16[256,1024]{1,0:T(8,128)(2,1)S(1)}, u32[]{:S(2)}, u32[]{:S(2)}) collective-permute-start(bf16[256,1024]{1,0:T(8,128)(2,1)} %bitcast.22), channel_id=1, source_target_pairs={{0,1},{1,2},{2,3},{3,4},{4,5},{5,6},{6,7},{7,8},{8,9},{9,10},{10,1... | collective-permute-start | bytes 1572872 | tf_op jit(solution)/shard_map/ppermute | solution.py:687
  4.6 15.8 %collective-permute-start.1 = (bf16[256,1024]{1,0:T(8,128)(2,1)}, bf16[256,1024]{1,0:T(8,128)(2,1)}, u32[]{:S(2)}, u32[]{:S(2)}) collective-permute-start(bf16[256,1024]{1,0:T(8,128)(2,1)} %bitcast.23), channel_id=1, source_target_pairs={{1,0},{2,1},{3,2},{4,3},{5,4},{6,5},{7,6},{8,7},{9,8},{10,9},{11,1... | collective-permute-start | bytes 1572872 | tf_op jit(solution)/shard_map/ppermute | solution.py:688
  9.4 1.0 copy-start.11
  10.4 9.9 %copy-start = (bf16[1024,1024]{1,0:T(8,128)(2,1)S(1)}, bf16[1024,1024]{1,0:T(8,128)(2,1)}, u32[]{:S(2)}) copy-start(bf16[1024,1024]{1,0:T(8,128)(2,1)} %w_out_ref.5) | copy-start | bytes 6291460
  10.4 9.9 %copy-start.1 = (bf16[1024,128]{1,0:T(8,128)(2,1)S(1)}, bf16[1024,128]{1,0:T(8,128)(2,1)}, u32[]{:S(2)}) copy-start(bf16[1024,128]{1,0:T(8,128)(2,1)} %readout_ref.5) | copy-start | bytes 786436
  32.0 6.6 %collective-permute-start.2 = (f32[256,128]{1,0:T(8,128)S(1)}, f32[256,128]{1,0:T(8,128)S(1)}, u32[]{:S(2)}, u32[]{:S(2)}) collective-permute-start(f32[256,128]{1,0:T(8,128)S(1)} %get-tuple-element.27.own_ref), channel_id=1, source_target_pairs={{0,64},{64,0},{1,65},{65,1},{2,66},{66,2},{3,67},{67,3},{4,68},{68... | collective-permute-start | bytes 393224 | tf_op jit(solution)/shard_map/ppermute | solution.py:702
  35.1 5.1 %copy-start.8 = (f32[256,128]{1,0:T(8,128)S(1)}, f32[256,128]{1,0:T(8,128)}, u32[]{:S(2)}) copy-start(f32[256,128]{1,0:T(8,128)} %target_ref.1) | copy-start | bytes 393220
  38.5 1.6 %collective-permute-start.3 = (f32[2,256,128]{2,1,0:T(8,128)S(1)}, f32[2,256,128]{2,1,0:T(8,128)S(1)}, u32[]{:S(2)}, u32[]{:S(2)}) collective-permute-start(f32[2,256,128]{2,1,0:T(8,128)S(1)} %pad_maximum_fusion), channel_id=1, source_target_pairs={{0,32},{32,0},{1,33},{33,1},{2,34},{34,2},{3,35},{35,3},{4,36},{36... | collective-permute-start | bytes 786440 | tf_op jit(solution)/shard_map/ppermute | solution.py:667
  38.6 17.9 %collective-permute-start.4 = (bf16[1024,256]{1,0:T(8,128)(2,1)S(1)}, bf16[1024,256]{1,0:T(8,128)(2,1)}, u32[]{:S(2)}, u32[]{:S(2)}) collective-permute-start(bf16[1024,256]{1,0:T(8,128)(2,1)S(1)} %get-tuple-element.34), channel_id=1, source_target_pairs={{0,32},{32,0},{1,33},{33,1},{2,34},{34,2},{3,35},{35,3},{4,36},{36... | collective-permute-start | bytes 1572872 | tf_op jit(solution)/shard_map/ppermute | solution.py:667
  43.7 0.7 copy-start.9
  44.4 10.3 %copy-start.2 = (bf16[256,1024]{1,0:T(8,128)(2,1)}, bf16[256,1024]{1,0:T(8,128)(2,1)S(1)}, u32[]{:S(2)}) copy-start(bf16[256,1024]{1,0:T(8,128)(2,1)S(1)} %get-tuple-element.37.grad_ref) | copy-start | bytes 1572868
  44.4 10.3 %collective-permute-start.5 = (bf16[256,256]{1,0:T(8,128)(2,1)S(1)}, bf16[256,256]{1,0:T(8,128)(2,1)S(1)}, u32[]{:S(2)}, u32[]{:S(2)}) collective-permute-start(bf16[256,256]{1,0:T(8,128)(2,1)S(1)} %get-tuple-element.38.packed_ref.own_ref), channel_id=1, source_target_pairs={{0,1},{1,2},{2,3},{3,4},{4,5},{5,6},{6,7},{7,8},{8,9},{9,10},{10,1... | collective-permute-start | bytes 393224 | tf_op jit(solution)/shard_map/ppermute | solution.py:710
  48.0 7.4 %collective-permute-start.6 = (bf16[256,256]{1,0:T(8,128)(2,1)S(1)}, bf16[256,256]{1,0:T(8,128)(2,1)S(1)}, u32[]{:S(2)}, u32[]{:S(2)}) collective-permute-start(bf16[256,256]{1,0:T(8,128)(2,1)S(1)} %get-tuple-element.38.packed_ref.own_ref), channel_id=1, source_target_pairs={{1,0},{2,1},{3,2},{4,3},{5,4},{6,5},{7,6},{8,7},{9,8},{10,9},{11,1... | collective-permute-start | bytes 393224 | tf_op jit(solution)/shard_map/ppermute | solution.py:711
  49.3 7.2 %collective-permute-start.8 = (bf16[1024,256]{1,0:T(8,128)(2,1)}, bf16[1024,256]{1,0:T(8,128)(2,1)}, u32[]{:S(2)}, u32[]{:S(2)}) collective-permute-start(bf16[1024,256]{1,0:T(8,128)(2,1)} %get-tuple-element.42), channel_id=1, source_target_pairs={{0,32},{32,0},{1,33},{33,1},{2,34},{34,2},{3,35},{35,3},{4,36},{36... | collective-permute-start | bytes 1572872 | tf_op jit(solution)/shard_map/ppermute | solution.py:667
  54.7 0.7 copy-start.4
  55.4 0.7 copy-start.6
  56.1 2.4 %collective-permute-start.7 = (bf16[1024,256]{1,0:T(8,128)(2,1)}, bf16[1024,256]{1,0:T(8,128)(2,1)}, u32[]{:S(2)}, u32[]{:S(2)}) collective-permute-start(bf16[1024,256]{1,0:T(8,128)(2,1)} %shard_map.81.piece_ref), channel_id=1, source_target_pairs={{0,32},{32,0},{1,33},{33,1},{2,34},{34,2},{3,35},{35,3},{4,36},{36... | collective-permute-start | bytes 1572872 | tf_op jit(solution)/shard_map/ppermute | solution.py:667
  61.9 35.5 %all-to-all-start = ((bf16[64,8,1280]{2,1,0:T(8,128)(2,1)}), bf16[64,8,1280]{2,1,0:T(8,128)(2,1)}, u32[]{:S(2)}, u32[]{:S(2)}) async-start(bf16[64,8,1280]{2,1,0:T(8,128)(2,1)} %bitcast.13), calls=%async_computation | async-start | bytes 2621440 | tf_op jit(solution)/shard_map/all_to_all | solution.py:672
  76.0 1.0 copy-start.3
  77.0 0.9 copy-start.5
  77.9 0.9 copy-start.7
  89.0 2.7 %collective-permute-start.9 = (bf16[2048,256]{1,0:T(8,128)(2,1)S(1)}, bf16[2048,256]{1,0:T(8,128)(2,1)S(1)}, u32[]{:S(2)}, u32[]{:S(2)}) collective-permute-start(bf16[2048,256]{1,0:T(8,128)(2,1)S(1)} %bitcast.16), channel_id=1, source_target_pairs={{0,32},{32,0},{1,33},{33,1},{2,34},{34,2},{3,35},{35,3},{4,36},{36... | collective-permute-start | bytes 3145736 | tf_op jit(solution)/shard_map/ppermute | solution.py:667
  97.4 8.3 %copy-start.10 = (f32[256,128]{1,0:T(8,128)S(1)}, f32[256,128]{1,0:T(8,128)}, u32[]{:S(2)}) copy-start(f32[256,128]{1,0:T(8,128)} %copy-done.9) | copy-start | bytes 393220
  97.4 38.3 %all-to-all-start.1 = ((bf16[64,8,2048]{2,1,0:T(8,128)(2,1)}), bf16[64,8,2048]{2,1,0:T(8,128)(2,1)S(1)}, u32[]{:S(2)}, u32[]{:S(2)}) async-start(bf16[64,8,2048]{2,1,0:T(8,128)(2,1)} %bitcast.14), calls=%async_computation.1 | async-start | bytes 4194304 | tf_op jit(solution)/shard_map/all_to_all | solution.py:672

commit v8 on v7

--- a/solution.py
+++ b/solution.py
@@ -60,6 +60,10 @@
 
 def in_hbm(values):
     return pltpu.with_memory_space_constraint(values, pltpu.HBM)
+
+
+def in_vmem(values):
+    return pltpu.with_memory_space_constraint(values, pltpu.VMEM)
 
 
 def fetches(weight_ref, buffer, arrived, width, first):
@@ -188,11 +192,11 @@
         cost_estimate=FREE,
     )(
         core.astype(jnp.int32).reshape(1),
-        by_core(turned),
-        by_core(turned_other),
-        piece,
-        other,
-        *(by_core(small) for small in smalls),
+        in_vmem(by_core(turned)),
+        in_vmem(by_core(turned_other)),
+        in_vmem(piece),
+        in_vmem(other),
+        *(in_vmem(by_core(small)) for small in smalls),
     )
 
 
@@ -375,7 +379,7 @@
             jax.ShapeDtypeStruct((BLOCK, 128), F32),
             jax.ShapeDtypeStruct((BLOCK, 1024), BF),
             jax.ShapeDtypeStruct((BLOCK, 128), F32),
-            jax.ShapeDtypeStruct((HEADS, window, BLOCK), BF),
+            pltpu.HBM((HEADS, window, BLOCK), BF),
             jax.ShapeDtypeStruct((HEADS, BLOCK), F32),
         ],
         scratch_shapes=[
@@ -471,9 +475,9 @@
         out_specs=[vmem] * 4,
         out_shape=[
             jax.ShapeDtypeStruct((BLOCK, 128), F32),
-            jax.ShapeDtypeStruct((BLOCK, 256), BF),
-            jax.ShapeDtypeStruct((BLOCK, 1024), BF),
-            jax.ShapeDtypeStruct((1024, 256), BF),
+            pltpu.VMEM((BLOCK, 256), BF),
+            pltpu.VMEM((BLOCK, 1024), BF),
+            pltpu.VMEM((1024, 256), BF),
         ],
         compiler_params=pltpu.CompilerParams(vmem_limit_bytes=12 * 1024 * 1024),
     )(counts, own, near, others, target, attended, hidden, stats, w_out, readout_weight)
@@ -524,13 +528,13 @@
             pl.BlockSpec((HEADS, BLOCK), lambda j: (0, 0)),
         ],
         out_specs=pl.BlockSpec((WIDTH, BLOCK), lambda j: (j, 0)),
-        out_shape=jax.ShapeDtypeStruct((1024, BLOCK), BF),
+        out_shape=pltpu.VMEM((1024, BLOCK), BF),
         scratch_shapes=[pltpu.VMEM((4, window, BLOCK), BF)],
         compiler_params=pltpu.CompilerParams(vmem_limit_bytes=16 * 1024 * 1024),
         cost_estimate=pl.CostEstimate(
             flops=6 << 30, bytes_accessed=5 << 20, transcendentals=3 << 20
         ),
-    )(kcat, vcat, grad, packed, probs, inverse)
+    )(kcat, vcat, grad, packed, in_hbm(probs), inverse)
 
 
 def key_kernel(
@@ -633,7 +637,7 @@
             whole(1024, 128),
         ],
         out_specs=pl.BlockSpec((2, WIDTH, BLOCK), lambda j: (0, j, 0)),
-        out_shape=jax.ShapeDtypeStruct((2, 1024, BLOCK), BF),
+        out_shape=pltpu.VMEM((2, 1024, BLOCK), BF),
         scratch_shapes=[
             pltpu.VMEM((4, window, BLOCK), BF),
             pltpu.VMEM((4, window, BLOCK), BF),
@@ -647,10 +651,10 @@
         projected,
         projected,
         qhalo,
-        grad,
+        in_vmem(grad),
         own,
-        left,
-        right,
+        in_vmem(left),
+        in_vmem(right),
         in_hbm(w_out),
         readout_weight,
     )

time: 137 us -> 140 us (1.022)
  Pallas kernels: 44.9 us -> 47.7 us
    pallas_call x1, Pallas kernels: 5.3 us -> 6.88 us  [query_grads(): pl.pallas_call(query_kernel, grid=(4,), in_specs=[part(window, 0), part(w...]
  transfers between devices with their start and end apart: 12 -> 12, of which waited for: 8 -> 8; matrix products, arithmetic and copies ran while one was open for 4% -> 3% of each run, Pallas kernels for 22% -> 23%
where the time goes in v8:
time: 140 us; the launch traced here: 139 us
  Pallas kernels  47.7 us (34%)
  waiting for transfers between devices  41.4 us (30%)
  starting transfers between devices  36.3 us (26%)
  local copies, waits for them, and re-layouts  8.03 us (6%)
  other arithmetic  3.21 us (2%)
  between operations  2.12 us (2%)
    all_to_all x2, waiting for transfers between devices, scatter(): lax.all_to_all(partial.reshape(64, 8, columns), CHIPS, split_axis=0, conc...  29.6 us
    all_to_all x2, starting transfers between devices, scatter(): lax.all_to_all(partial.reshape(64, 8, columns), CHIPS, split_axis=0, conc...  21.7 us
    pallas_call x1, Pallas kernels, forward(): pl.pallas_call(forward_kernel, grid=(4,), in_specs=[pl.BlockSpec(memory_s...  12.8 us
    pallas_call x1, Pallas kernels, key_grads(): pl.pallas_call(key_kernel, grid=(4,), in_specs=[pl.BlockSpec(memory_space...  10.2 us
    pallas_call x2, Pallas kernels, partial_sums(): pl.pallas_call(partial_kernel if smalls else plain_partial_kernel, in_spe...  7.18 us
    pallas_call x1, Pallas kernels, query_grads(): pl.pallas_call(query_kernel, grid=(4,), in_specs=[part(window, 0), part(w...  6.88 us
    unnamed x25, local copies, waits for them, and re-layouts  6.56 us
    ppermute x5, waiting for transfers between devices, swap_core(): return lax.ppermute(values, 'core', SWAP)  5.49 us
  transfers between devices with their start and end apart: 12, of which 8 were waited for; matrix products, arithmetic and copies ran while one was open for 3% of the time, Pallas kernels for 23%

profile of v8, /device:TPU:0, one launch (start us, length us, event | category | flops | bytes accessed | tf_op | source)
XLA Modules:
  0.0 139.0 jit_solution(6552480485548263661)
XLA Ops:
  0.6 3.9 %collective-permute-start = (bf16[256,1024]{1,0:T(8,128)(2,1)}, bf16[256,1024]{1,0:T(8,128)(2,1)S(1)}, u32[]{:S(2)}, u32[]{:S(2)}) collective-permute-start(bf16[256,1024]{1,0:T(8,128)(2,1)} %bitcast.22), channel_id=1, source_target_pairs={{0,1},{1,2},{2,3},{3,4},{4,5},{5,6},{6,7},{7,8},{8,9},{9,10},{10,1... | collective-permute-start | bytes 1572872 | tf_op jit(solution)/shard_map/ppermute | solution.py:691
  4.6 1.3 collective-permute-start.1
  5.9 1.4 fusion.2
  9.3 1.0 copy-done.11
  10.3 4.1 %shard_map.77 = (bf16[256,3072]{1,0:T(8,128)(2,1)S(1)}, bf16[1024,256]{1,0:T(8,128)(2,1)S(1)}) custom-call(bf16[256,1024]{1,0:T(8,128)(2,1)S(1)} %bitcast.24, bf16[1024,3072]{1,0:T(8,128)(2,1)} %weight_ref.5), custom_call_target="tpu_custom_call" | custom-call | flops 2147483648 | bytes 8388608 | tf_op jit(solution)/shard_map/pallas_call | solution.py:103
  14.5 1.6 %collective-permute-done.left_ref = bf16[256,1024]{1,0:T(8,128)(2,1)S(1)} collective-permute-done((bf16[256,1024]{1,0:T(8,128)(2,1)}, bf16[256,1024]{1,0:T(8,128)(2,1)S(1)}, u32[]{:S(2)}, u32[]{:S(2)}) %collective-permute-start) | collective-permute-done | bytes 524320 | tf_op jit(solution)/shard_map/ppermute | solution.py:691
  16.0 4.3 %collective-permute-done.1.right_ref = bf16[256,1024]{1,0:T(8,128)(2,1)} collective-permute-done((bf16[256,1024]{1,0:T(8,128)(2,1)}, bf16[256,1024]{1,0:T(8,128)(2,1)}, u32[]{:S(2)}, u32[]{:S(2)}) %collective-permute-start.1) | collective-permute-done | bytes 524320 | tf_op jit(solution)/shard_map/ppermute | solution.py:692
  20.3 12.8 %shard_map.78 = (bf16[512,1024]{1,0:T(8,128)(2,1)S(1)}, bf16[768,1024]{1,0:T(8,128)(2,1)S(1)}, bf16[768,1024]{1,0:T(8,128)(2,1)S(1)}, f32[256,1024]{1,0:T(8,128)...) custom-call(s32[3]{0:T(128)S(1)} %pad_add_fusion.counts_ref, ...), custom_call_target="tpu_custom_call" | custom-call | flops 6442450944 | bytes 12582912 | tf_op jit(solution)/shard_map/pallas_call | solution.py:348
  33.1 3.1 %collective-permute-start.2 = (f32[256,128]{1,0:T(8,128)S(1)}, f32[256,128]{1,0:T(8,128)S(1)}, u32[]{:S(2)}, u32[]{:S(2)}) collective-permute-start(f32[256,128]{1,0:T(8,128)S(1)} %get-tuple-element.27.own_ref), channel_id=1, source_target_pairs={{0,64},{64,0},{1,65},{65,1},{2,66},{66,2},{3,67},{67,3},{4,68},{68... | collective-permute-start | bytes 393224 | tf_op jit(solution)/shard_map/ppermute | solution.py:706
  36.2 3.0 %shard_map.79.qhalo_ref = bf16[512,1024]{1,0:T(8,128)(2,1)S(1)} custom-call(bf16[512,1024]{1,0:T(8,128)(2,1)S(1)} %get-tuple-element.28.normed_ref, bf16[1024,3072]{1,0:T(8,128)(2,1)} %weight_ref.5), custom_call_target="tpu_custom_call" | custom-call | tf_op jit(solution)/shard_map/pallas_call | solution.py:141
  41.3 3.6 %shard_map.80 = (f32[256,128]{1,0:T(8,128)S(1)}, bf16[256,256]{1,0:T(8,128)(2,1)S(1)}, bf16[256,1024]{1,0:T(8,128)(2,1)S(1)}, bf16[1024,256]{1,0:T(8,128)(2,1)}) custom-call(s32[3]{0:T(128)S(1)} %pad_add_fusion.counts_ref, f32[256,128]{1,0:T(8,128)S(1)} %get-tuple-element.27.own_ref, f32[256,128]{1,0:T(8,128)S(1)} %collective-permute-done.2.near_ref, ...), custom_call_target="tpu_custom_call" | custom-call | tf_op jit(solution)/shard_map/pallas_call | solution.py:472
  45.5 3.6 %collective-permute-start.5 = (bf16[256,256]{1,0:T(8,128)(2,1)S(1)}, bf16[256,256]{1,0:T(8,128)(2,1)S(1)}, u32[]{:S(2)}, u32[]{:S(2)}) collective-permute-start(bf16[256,256]{1,0:T(8,128)(2,1)S(1)} %get-tuple-element.38.packed_ref.own_ref), channel_id=1, source_target_pairs={{0,1},{1,2},{2,3},{3,4},{4,5},{5,6},{6,7},{7,8},{8,9},{9,10},{10,1... | collective-permute-start | bytes 393224 | tf_op jit(solution)/shard_map/ppermute | solution.py:714
  49.2 1.3 collective-permute-start.6
  50.6 6.9 %shard_map.81.piece_ref = bf16[1024,256]{1,0:T(8,128)(2,1)} custom-call(bf16[768,1024]{1,0:T(8,128)(2,1)S(1)} %get-tuple-element.35.kcat_ref, bf16[768,1024]{1,0:T(8,128)(2,1)S(1)} %get-tuple-element.36.vcat_ref, bf16[256,1024]{1,0:T(8,128)(2,1)S(1)} %get-tuple-element.37.grad_ref, bf16[256,256]{1,0:T(8,128)(2,1)S(1)} %get-tuple-element.38.packed_ref.own_ref, ...), custom_call_target="tpu_custom_call" | custom-call | flops 6442450944 | bytes 5242880 | tf_op jit(solution)/shard_map/pallas_call | solution.py:519
  59.3 1.9 %collective-permute-done.7.other_ref = bf16[1024,256]{1,0:T(8,128)(2,1)} collective-permute-done((bf16[1024,256]{1,0:T(8,128)(2,1)}, bf16[1024,256]{1,0:T(8,128)(2,1)}, u32[]{:S(2)}, u32[]{:S(2)}) %collective-permute-start.7) | collective-permute-done | bytes 524320 | tf_op jit(solution)/shard_map/ppermute | solution.py:671
  61.1 3.5 %shard_map.82 = bf16[512,1280]{1,0:T(8,128)(2,1)} custom-call(s32[1]{0:T(128)} %bitcast.7.core_ref, bf16[2,2,256,256]{3,2,1,0:T(8,128)(2,1)S(1)} %bitcast.18, bf16[2,2,256,256]{3,2,1,0:T(8,128)(2,1)} %bitcast.9.normed_other_ref, bf16[1024,256]{1,0:T(8,128)(2,1)} %shard_map.81.piece_ref, bf16[1024,256]{1,0:T(8,128)(2,1)} %collective-permute-done.7.other_ref, ...), custom_call_target="tpu_custom_call" | custom-call | tf_op jit(solution)/shard_map/pallas_call | solution.py:186
  64.7 13.7 %all-to-all-start = ((bf16[64,8,1280]{2,1,0:T(8,128)(2,1)}), bf16[64,8,1280]{2,1,0:T(8,128)(2,1)}, u32[]{:S(2)}, u32[]{:S(2)}) async-start(bf16[64,8,1280]{2,1,0:T(8,128)(2,1)} %bitcast.13), calls=%async_computation | async-start | bytes 2621440 | tf_op jit(solution)/shard_map/all_to_all | solution.py:676
  81.2 10.2 %shard_map.83 = bf16[2,1024,256]{2,1,0:T(8,128)(2,1)S(1)} custom-call(s32[3]{0:T(128)S(1)} %pad_add_fusion.counts_ref, bf16[256,3072]{1,0:T(8,128)(2,1)S(1)} %get-tuple-element.26.q_ref.k_ref.v_ref, bf16[256,3072]{1,0:T(8,128)(2,1)S(1)} %get-tuple-element.26.q_ref.k_ref.v_ref, bf16[256,3072]{1,0:T(8,128)(2,1)S(1)} %get-tuple-element.26.q_ref.k_ref.v_ref, ...), custom_call_target="tpu_custom_call" | custom-call | tf_op jit(solution)/shard_map/pallas_call | solution.py:623
  91.5 2.6 %collective-permute-done.9.other_ref = bf16[2048,256]{1,0:T(8,128)(2,1)S(1)} collective-permute-done((bf16[2048,256]{1,0:T(8,128)(2,1)S(1)}, bf16[2048,256]{1,0:T(8,128)(2,1)S(1)}, u32[]{:S(2)}, u32[]{:S(2)}) %collective-permute-start.9) | collective-permute-done | bytes 1048608 | tf_op jit(solution)/shard_map/ppermute | solution.py:671
  94.1 3.7 %shard_map.84 = bf16[512,2048]{1,0:T(8,128)(2,1)} custom-call(s32[1]{0:T(128)} %bitcast.7.core_ref, bf16[2,2,256,256]{3,2,1,0:T(8,128)(2,1)S(1)} %bitcast.19, bf16[2,2,256,256]{3,2,1,0:T(8,128)(2,1)} %bitcast.9.normed_other_ref, bf16[2048,256]{1,0:T(8,128)(2,1)S(1)} %bitcast.17, bf16[2048,256]{1,0:T(8,128)(2,1)S(1)} %collective-permute-done.9.other_ref), custom_call_target="tpu_custom_call" | custom-call | tf_op jit(solution)/shard_map/pallas_call | solution.py:186
  97.8 2.2 %all-to-all-done = bf16[64,8,1280]{2,1,0:T(8,128)(2,1)} async-done(((bf16[64,8,1280]{2,1,0:T(8,128)(2,1)}), bf16[64,8,1280]{2,1,0:T(8,128)(2,1)}, u32[]{:S(2)}, u32[]{:S(2)}) %all-to-all-start) | async-done | bytes 1310752 | tf_op jit(solution)/shard_map/all_to_all | solution.py:676
  100.0 8.1 %all-to-all-start.1 = ((bf16[64,8,2048]{2,1,0:T(8,128)(2,1)}), bf16[64,8,2048]{2,1,0:T(8,128)(2,1)S(1)}, u32[]{:S(2)}, u32[]{:S(2)}) async-start(bf16[64,8,2048]{2,1,0:T(8,128)(2,1)} %bitcast.14), calls=%async_computation.1 | async-start | bytes 4194304 | tf_op jit(solution)/shard_map/all_to_all | solution.py:676
  108.9 1.5 %convert_reduce_fusion.1 = f32[8,1280]{1,0:T(8,128)S(1)} fusion(bf16[64,8,1280]{2,1,0:T(8,128)(2,1)} %all-to-all-done), kind=kLoop, calls=%fused_computation.1 | loop fusion | flops 1300480 | bytes 1351680 | tf_op jit(solution)/shard_map/reduce_sum | solution.py:680
  110.7 27.3 %all-to-all-done.1 = bf16[64,8,2048]{2,1,0:T(8,128)(2,1)S(1)} async-done(((bf16[64,8,2048]{2,1,0:T(8,128)(2,1)}), bf16[64,8,2048]{2,1,0:T(8,128)(2,1)S(1)}, u32[]{:S(2)}, u32[]{:S(2)}) %all-to-all-start.1) | async-done | bytes 2097184 | tf_op jit(solution)/shard_map/all_to_all | solution.py:676
  (43 shorter events, 10.4 us)
Async XLA Ops:
  0.6 15.4 %collective-permute-start = (bf16[256,1024]{1,0:T(8,128)(2,1)}, bf16[256,1024]{1,0:T(8,128)(2,1)S(1)}, u32[]{:S(2)}, u32[]{:S(2)}) collective-permute-start(bf16[256,1024]{1,0:T(8,128)(2,1)} %bitcast.22), channel_id=1, source_target_pairs={{0,1},{1,2},{2,3},{3,4},{4,5},{5,6},{6,7},{7,8},{8,9},{9,10},{10,1... | collective-permute-start | bytes 1572872 | tf_op jit(solution)/shard_map/ppermute | solution.py:691
  4.6 15.8 %collective-permute-start.1 = (bf16[256,1024]{1,0:T(8,128)(2,1)}, bf16[256,1024]{1,0:T(8,128)(2,1)}, u32[]{:S(2)}, u32[]{:S(2)}) collective-permute-start(bf16[256,1024]{1,0:T(8,128)(2,1)} %bitcast.23), channel_id=1, source_target_pairs={{1,0},{2,1},{3,2},{4,3},{5,4},{6,5},{7,6},{8,7},{9,8},{10,9},{11,1... | collective-permute-start | bytes 1572872 | tf_op jit(solution)/shard_map/ppermute | solution.py:692
  9.3 1.0 copy-start.11
  10.3 10.0 %copy-start = (bf16[1024,1024]{1,0:T(8,128)(2,1)S(1)}, bf16[1024,1024]{1,0:T(8,128)(2,1)}, u32[]{:S(2)}) copy-start(bf16[1024,1024]{1,0:T(8,128)(2,1)} %w_out_ref.5) | copy-start | bytes 6291460
  10.3 10.0 %copy-start.1 = (bf16[1024,128]{1,0:T(8,128)(2,1)S(1)}, bf16[1024,128]{1,0:T(8,128)(2,1)}, u32[]{:S(2)}) copy-start(bf16[1024,128]{1,0:T(8,128)(2,1)} %readout_ref.5) | copy-start | bytes 786436
  33.1 6.6 %collective-permute-start.2 = (f32[256,128]{1,0:T(8,128)S(1)}, f32[256,128]{1,0:T(8,128)S(1)}, u32[]{:S(2)}, u32[]{:S(2)}) collective-permute-start(f32[256,128]{1,0:T(8,128)S(1)} %get-tuple-element.27.own_ref), channel_id=1, source_target_pairs={{0,64},{64,0},{1,65},{65,1},{2,66},{66,2},{3,67},{67,3},{4,68},{68... | collective-permute-start | bytes 393224 | tf_op jit(solution)/shard_map/ppermute | solution.py:706
  36.2 5.1 %copy-start.8 = (f32[256,128]{1,0:T(8,128)S(1)}, f32[256,128]{1,0:T(8,128)}, u32[]{:S(2)}) copy-start(f32[256,128]{1,0:T(8,128)} %target_ref.1) | copy-start | bytes 393220
  39.7 1.6 %collective-permute-start.3 = (f32[2,256,128]{2,1,0:T(8,128)S(1)}, f32[2,256,128]{2,1,0:T(8,128)S(1)}, u32[]{:S(2)}, u32[]{:S(2)}) collective-permute-start(f32[2,256,128]{2,1,0:T(8,128)S(1)} %pad_maximum_fusion), channel_id=1, source_target_pairs={{0,32},{32,0},{1,33},{33,1},{2,34},{34,2},{3,35},{35,3},{4,36},{36... | collective-permute-start | bytes 786440 | tf_op jit(solution)/shard_map/ppermute | solution.py:671
  39.8 19.5 %collective-permute-start.4 = (bf16[1024,256]{1,0:T(8,128)(2,1)S(1)}, bf16[1024,256]{1,0:T(8,128)(2,1)}, u32[]{:S(2)}, u32[]{:S(2)}) collective-permute-start(bf16[1024,256]{1,0:T(8,128)(2,1)S(1)} %get-tuple-element.34), channel_id=1, source_target_pairs={{0,32},{32,0},{1,33},{33,1},{2,34},{34,2},{3,35},{35,3},{4,36},{36... | collective-permute-start | bytes 1572872 | tf_op jit(solution)/shard_map/ppermute | solution.py:671
  44.9 0.7 copy-start.9
  45.5 11.9 %copy-start.2 = (bf16[256,1024]{1,0:T(8,128)(2,1)}, bf16[256,1024]{1,0:T(8,128)(2,1)S(1)}, u32[]{:S(2)}) copy-start(bf16[256,1024]{1,0:T(8,128)(2,1)S(1)} %get-tuple-element.37.grad_ref) | copy-start | bytes 1572868
  45.5 11.9 %collective-permute-start.5 = (bf16[256,256]{1,0:T(8,128)(2,1)S(1)}, bf16[256,256]{1,0:T(8,128)(2,1)S(1)}, u32[]{:S(2)}, u32[]{:S(2)}) collective-permute-start(bf16[256,256]{1,0:T(8,128)(2,1)S(1)} %get-tuple-element.38.packed_ref.own_ref), channel_id=1, source_target_pairs={{0,1},{1,2},{2,3},{3,4},{4,5},{5,6},{6,7},{7,8},{8,9},{9,10},{10,1... | collective-permute-start | bytes 393224 | tf_op jit(solution)/shard_map/ppermute | solution.py:714
  49.2 8.9 %collective-permute-start.6 = (bf16[256,256]{1,0:T(8,128)(2,1)S(1)}, bf16[256,256]{1,0:T(8,128)(2,1)S(1)}, u32[]{:S(2)}, u32[]{:S(2)}) collective-permute-start(bf16[256,256]{1,0:T(8,128)(2,1)S(1)} %get-tuple-element.38.packed_ref.own_ref), channel_id=1, source_target_pairs={{1,0},{2,1},{3,2},{4,3},{5,4},{6,5},{7,6},{8,7},{9,8},{10,9},{11,1... | collective-permute-start | bytes 393224 | tf_op jit(solution)/shard_map/ppermute | solution.py:715
  50.5 8.8 %collective-permute-start.8 = (bf16[1024,256]{1,0:T(8,128)(2,1)}, bf16[1024,256]{1,0:T(8,128)(2,1)}, u32[]{:S(2)}, u32[]{:S(2)}) collective-permute-start(bf16[1024,256]{1,0:T(8,128)(2,1)} %get-tuple-element.42), channel_id=1, source_target_pairs={{0,32},{32,0},{1,33},{33,1},{2,34},{34,2},{3,35},{35,3},{4,36},{36... | collective-permute-start | bytes 1572872 | tf_op jit(solution)/shard_map/ppermute | solution.py:671
  57.5 0.7 copy-start.4
  58.1 0.7 copy-start.6
  58.8 2.4 %collective-permute-start.7 = (bf16[1024,256]{1,0:T(8,128)(2,1)}, bf16[1024,256]{1,0:T(8,128)(2,1)}, u32[]{:S(2)}, u32[]{:S(2)}) collective-permute-start(bf16[1024,256]{1,0:T(8,128)(2,1)} %shard_map.81.piece_ref), channel_id=1, source_target_pairs={{0,32},{32,0},{1,33},{33,1},{2,34},{34,2},{3,35},{35,3},{4,36},{36... | collective-permute-start | bytes 1572872 | tf_op jit(solution)/shard_map/ppermute | solution.py:671
  64.7 35.3 %all-to-all-start = ((bf16[64,8,1280]{2,1,0:T(8,128)(2,1)}), bf16[64,8,1280]{2,1,0:T(8,128)(2,1)}, u32[]{:S(2)}, u32[]{:S(2)}) async-start(bf16[64,8,1280]{2,1,0:T(8,128)(2,1)} %bitcast.13), calls=%async_computation | async-start | bytes 2621440 | tf_op jit(solution)/shard_map/all_to_all | solution.py:676
  78.3 1.0 copy-start.3
  79.4 0.9 copy-start.5
  80.3 0.9 copy-start.7
  91.4 2.7 %collective-permute-start.9 = (bf16[2048,256]{1,0:T(8,128)(2,1)S(1)}, bf16[2048,256]{1,0:T(8,128)(2,1)S(1)}, u32[]{:S(2)}, u32[]{:S(2)}) collective-permute-start(bf16[2048,256]{1,0:T(8,128)(2,1)S(1)} %bitcast.16), channel_id=1, source_target_pairs={{0,32},{32,0},{1,33},{33,1},{2,34},{34,2},{3,35},{35,3},{4,36},{36... | collective-permute-start | bytes 3145736 | tf_op jit(solution)/shard_map/ppermute | solution.py:671
  100.0 8.1 %copy-start.10 = (f32[256,128]{1,0:T(8,128)S(1)}, f32[256,128]{1,0:T(8,128)}, u32[]{:S(2)}) copy-start(f32[256,128]{1,0:T(8,128)} %copy-done.9) | copy-start | bytes 393220
  100.0 38.1 %all-to-all-start.1 = ((bf16[64,8,2048]{2,1,0:T(8,128)(2,1)}), bf16[64,8,2048]{2,1,0:T(8,128)(2,1)S(1)}, u32[]{:S(2)}, u32[]{:S(2)}) async-start(bf16[64,8,2048]{2,1,0:T(8,128)(2,1)} %bitcast.14), calls=%async_computation.1 | async-start | bytes 4194304 | tf_op jit(solution)/shard_map/all_to_all | solution.py:676

commit v9 on v7

--- a/solution.py
+++ b/solution.py
@@ -150,41 +150,85 @@
 
 
 def partial_kernel(
-    core_ref, normed_ref, normed_other_ref, piece_ref, other_ref, small_ref, small_other_ref,
-    out_ref,
+    smalls, core_ref, normed_ref, normed_other_ref, piece_ref, other_ref, *refs
 ):
+    small_refs, (out_ref, rows, pieces, others, sums, staged, arrived, left) = (
+        refs[:smalls],
+        refs[smalls:],
+    )
     core = core_ref[0]
-    for top in range(2):
-        rows = slice(top * 256, (top + 1) * 256)
-        own = normed_ref[top, core]
-        near = normed_other_ref[top, core]
-        for first in range(0, piece_ref.shape[0], 512):
-            columns = slice(first, first + 512)
-            out_ref[rows, columns] = (
-                dot_nt(own, piece_ref[columns]) + dot_nt(near, other_ref[columns])
+    chunks = piece_ref.shape[0] // 512
+    sources = [
+        (normed_ref.at[:, core], rows.at[0]),
+        (normed_other_ref.at[:, core], rows.at[1]),
+    ]
+    for chunk in range(chunks):
+        part = pl.ds(chunk * 512, 512)
+        sources.append((piece_ref.at[part], pieces.at[chunk]))
+        sources.append((other_ref.at[part], others.at[chunk]))
+    for place, small_ref in enumerate(small_refs):
+        sources.append((small_ref.at[:, core], sums.at[place]))
+    copies = [
+        pltpu.make_async_copy(source, target, arrived.at[place])
+        for place, (source, target) in enumerate(sources)
+    ]
+    for copy in copies:
+        copy.start()
+    copies[0].wait()
+    copies[1].wait()
+    writes = []
+    for chunk in range(chunks):
+        copies[2 + 2 * chunk].wait()
+        copies[3 + 2 * chunk].wait()
+        for top in range(2):
+            staged[chunk, top * 256 : (top + 1) * 256] = (
+                dot_nt(rows[0, top], pieces[chunk]) + dot_nt(rows[1, top], others[chunk])
             ).astype(BF)
-        if small_ref is not None:
-            out_ref[rows, piece_ref.shape[0] :] = (
-                small_ref[top, core].astype(F32) + small_other_ref[top, core].astype(F32)
+        writes.append(
+            pltpu.make_async_copy(
+                staged.at[chunk], out_ref.at[:, pl.ds(chunk * 512, 512)], left.at[chunk]
+            )
+        )
+        writes[-1].start()
+    if smalls:
+        copies[-2].wait()
+        copies[-1].wait()
+        for top in range(2):
+            staged[chunks, top * 256 : (top + 1) * 256, :256] = (
+                sums[0, top].astype(F32) + sums[1, top].astype(F32)
             ).astype(BF)
-
-
-def plain_partial_kernel(core_ref, normed_ref, normed_other_ref, piece_ref, other_ref, out_ref):
-    partial_kernel(
-        core_ref, normed_ref, normed_other_ref, piece_ref, other_ref, None, None, out_ref
-    )
+        writes.append(
+            pltpu.make_async_copy(
+                staged.at[chunks, :, pl.ds(0, 256)],
+                out_ref.at[:, pl.ds(chunks * 512, 256)],
+                left.at[chunks],
+            )
+        )
+        writes[-1].start()
+    for write in writes:
+        write.wait()
 
 
 def partial_sums(core, turned, turned_other, piece, other, smalls=()):
     by_core = lambda values: values.reshape(2, 2, 256, 256)
-    vmem = pl.BlockSpec(memory_space=pltpu.VMEM)
+    anywhere = pl.BlockSpec(memory_space=pl.ANY)
+    chunks = piece.shape[0] // 512
     columns = piece.shape[0] + 256 * (len(smalls) // 2)
     return pl.pallas_call(
-        partial_kernel if smalls else plain_partial_kernel,
-        in_specs=[pl.BlockSpec(memory_space=pltpu.SMEM)] + [vmem] * (4 + len(smalls)),
-        out_specs=vmem,
+        functools.partial(partial_kernel, len(smalls)),
+        in_specs=[pl.BlockSpec(memory_space=pltpu.SMEM)] + [anywhere] * (4 + len(smalls)),
+        out_specs=anywhere,
         out_shape=jax.ShapeDtypeStruct((512, columns), BF),
-        compiler_params=pltpu.CompilerParams(vmem_limit_bytes=12 * 1024 * 1024),
+        scratch_shapes=[
+            pltpu.VMEM((2, 2, 256, 256), BF),
+            pltpu.VMEM((chunks, 512, 256), BF),
+            pltpu.VMEM((chunks, 512, 256), BF),
+            pltpu.VMEM((2, 2, 256, 256), BF),
+            pltpu.VMEM((chunks + 1, 512, 512), BF),
+            pltpu.SemaphoreType.DMA((2 + 2 * chunks + len(smalls),)),
+            pltpu.SemaphoreType.DMA((chunks + 1,)),
+        ],
+        compiler_params=pltpu.CompilerParams(vmem_limit_bytes=14 * 1024 * 1024),
         cost_estimate=FREE,
     )(
         core.astype(jnp.int32).reshape(1),
@@ -647,10 +691,10 @@
         projected,
         projected,
         qhalo,
-        grad,
+        in_hbm(grad),
         own,
-        left,
-        right,
+        in_hbm(left),
+        in_hbm(right),
         in_hbm(w_out),
         readout_weight,
     )

time: 137 us -> 134 us (0.978)
  local copies, waits for them, and re-layouts: 8.1 us -> 4.72 us
  waiting for transfers between devices: 41.2 us -> 44.3 us
  starting transfers between devices: 36.8 us -> 34.3 us
    unnamed x25 -> x19, local copies, waits for them, and re-layouts: 6.57 us -> 3.25 us
    all_to_all x2, waiting for transfers between devices: 29.4 us -> 31.9 us  [scatter(): lax.all_to_all(partial.reshape(64, 8, columns), CHIPS, split_axis=0, conc...]
    all_to_all x2, starting transfers between devices: 22.3 us -> 19.8 us  [scatter(): lax.all_to_all(partial.reshape(64, 8, columns), CHIPS, split_axis=0, conc...]
  transfers between devices with their start and end apart: 12 -> 12, of which waited for: 8 -> 9; matrix products, arithmetic and copies ran while one was open for 4% -> 3% of each run, Pallas kernels for 22% -> 23%
where the time goes in v9:
time: 134 us
  Pallas kernels  44.9 us (34%)
  waiting for transfers between devices  44.3 us (33%)
  starting transfers between devices  34.3 us (26%)
  local copies, waits for them, and re-layouts  4.72 us (4%)
  other arithmetic  3.15 us (2%)
  between operations  2.13 us (2%)
    all_to_all x2, waiting for transfers between devices, scatter(): lax.all_to_all(partial.reshape(64, 8, columns), CHIPS, split_axis=0, conc...  31.9 us
    all_to_all x2, starting transfers between devices, scatter(): lax.all_to_all(partial.reshape(64, 8, columns), CHIPS, split_axis=0, conc...  19.8 us
    pallas_call x1, Pallas kernels, forward(): pl.pallas_call(forward_kernel, grid=(4,), in_specs=[pl.BlockSpec(memory_s...  11.6 us
    pallas_call x1, Pallas kernels, key_grads(): pl.pallas_call(key_kernel, grid=(4,), in_specs=[pl.BlockSpec(memory_space...  10.3 us
    pallas_call x2, Pallas kernels, partial_sums(): pl.pallas_call(functools.partial(partial_kernel, len(smalls)), in_specs=[...  6.96 us
    ppermute x5, waiting for transfers between devices, swap_core(): return lax.ppermute(values, 'core', SWAP)  5.55 us
    pallas_call x1, Pallas kernels, query_grads(): pl.pallas_call(query_kernel, grid=(4,), in_specs=[part(window, 0), part(w...  5.29 us
    ppermute x1, waiting for transfers between devices, per_device(): from_right = lax.ppermute(latent_own, CELLS, down)  4.3 us
  transfers between devices with their start and end apart: 12, of which 9 were waited for; matrix products, arithmetic and copies ran while one was open for 3% of the time, Pallas kernels for 23%

profile of v9, /device:TPU:0, one launch (start us, length us, event | category | flops | bytes accessed | tf_op | source)
XLA Modules:
  0.0 133.8 jit_solution(8737754880532874096)
XLA Ops:
  0.6 3.9 %collective-permute-start = (bf16[256,1024]{1,0:T(8,128)(2,1)}, bf16[256,1024]{1,0:T(8,128)(2,1)S(1)}, u32[]{:S(2)}, u32[]{:S(2)}) collective-permute-start(bf16[256,1024]{1,0:T(8,128)(2,1)} %bitcast.22), channel_id=1, source_target_pairs={{0,1},{1,2},{2,3},{3,4},{4,5},{5,6},{6,7},{7,8},{8,9},{9,10},{10,1... | collective-permute-start | bytes 1572872 | tf_op jit(solution)/shard_map/ppermute | solution.py:731
  4.6 1.3 collective-permute-start.1
  5.9 1.4 %fusion.2 = (s32[1]{0:T(128)}, s32[1]{0:T(128)}, s32[1]{0:T(128)}) fusion(s32[32]{0:T(128)} %param.7, s32[]{:T(128)S(6)} %max.3, s32[]{:T(128)S(6)} %select_n.19, s32[]{:T(128)S(6)} %select_n.18), kind=kLoop, calls=%fused_computation.8 | loop fusion | bytes 36 | tf_op jit(solution)/shard_map/dynamic_slice | solution.py:735
  9.2 1.0 copy-done.6
  10.2 4.1 %shard_map.77 = (bf16[256,3072]{1,0:T(8,128)(2,1)S(1)}, bf16[1024,256]{1,0:T(8,128)(2,1)S(1)}) custom-call(bf16[256,1024]{1,0:T(8,128)(2,1)S(1)} %bitcast.24, bf16[1024,3072]{1,0:T(8,128)(2,1)} %weight_ref.5), custom_call_target="tpu_custom_call" | custom-call | flops 2147483648 | bytes 8388608 | tf_op jit(solution)/shard_map/pallas_call | solution.py:99
  14.4 1.6 %collective-permute-done.left_ref = bf16[256,1024]{1,0:T(8,128)(2,1)S(1)} collective-permute-done((bf16[256,1024]{1,0:T(8,128)(2,1)}, bf16[256,1024]{1,0:T(8,128)(2,1)S(1)}, u32[]{:S(2)}, u32[]{:S(2)}) %collective-permute-start) | collective-permute-done | bytes 524320 | tf_op jit(solution)/shard_map/ppermute | solution.py:731
  16.0 4.3 %collective-permute-done.1.right_ref = bf16[256,1024]{1,0:T(8,128)(2,1)} collective-permute-done((bf16[256,1024]{1,0:T(8,128)(2,1)}, bf16[256,1024]{1,0:T(8,128)(2,1)}, u32[]{:S(2)}, u32[]{:S(2)}) %collective-permute-start.1) | collective-permute-done | bytes 524320 | tf_op jit(solution)/shard_map/ppermute | solution.py:732
  20.3 11.6 %shard_map.78 = (bf16[512,1024]{1,0:T(8,128)(2,1)S(1)}, bf16[768,1024]{1,0:T(8,128)(2,1)S(1)}, bf16[768,1024]{1,0:T(8,128)(2,1)S(1)}, f32[256,1024]{1,0:T(8,128)...) custom-call(s32[3]{0:T(128)S(1)} %pad_add_fusion.counts_ref, ...), custom_call_target="tpu_custom_call" | custom-call | flops 6442450944 | bytes 12582912 | tf_op jit(solution)/shard_map/pallas_call | solution.py:388
  32.0 3.1 %collective-permute-start.2 = (f32[256,128]{1,0:T(8,128)S(1)}, f32[256,128]{1,0:T(8,128)S(1)}, u32[]{:S(2)}, u32[]{:S(2)}) collective-permute-start(f32[256,128]{1,0:T(8,128)S(1)} %get-tuple-element.27.own_ref), channel_id=1, source_target_pairs={{0,64},{64,0},{1,65},{65,1},{2,66},{66,2},{3,67},{67,3},{4,68},{68... | collective-permute-start | bytes 393224 | tf_op jit(solution)/shard_map/ppermute | solution.py:746
  35.1 3.0 %shard_map.79.qhalo_ref = bf16[512,1024]{1,0:T(8,128)(2,1)S(1)} custom-call(bf16[512,1024]{1,0:T(8,128)(2,1)S(1)} %get-tuple-element.28.normed_ref, bf16[1024,3072]{1,0:T(8,128)(2,1)} %weight_ref.5), custom_call_target="tpu_custom_call" | custom-call | tf_op jit(solution)/shard_map/pallas_call | solution.py:137
  40.2 3.6 %shard_map.80 = (f32[256,128]{1,0:T(8,128)S(1)}, bf16[256,256]{1,0:T(8,128)(2,1)S(1)}, bf16[256,1024]{1,0:T(8,128)(2,1)S(1)}, bf16[1024,256]{1,0:T(8,128)(2,1)}) custom-call(s32[3]{0:T(128)S(1)} %pad_add_fusion.counts_ref, f32[256,128]{1,0:T(8,128)S(1)} %get-tuple-element.27.own_ref, f32[256,128]{1,0:T(8,128)S(1)} %collective-permute-done.2.near_ref, ...), custom_call_target="tpu_custom_call" | custom-call | tf_op jit(solution)/shard_map/pallas_call | solution.py:512
  44.4 3.6 %collective-permute-start.5 = (bf16[256,256]{1,0:T(8,128)(2,1)S(1)}, bf16[256,256]{1,0:T(8,128)(2,1)S(1)}, u32[]{:S(2)}, u32[]{:S(2)}) collective-permute-start(bf16[256,256]{1,0:T(8,128)(2,1)S(1)} %get-tuple-element.38.packed_ref.own_ref), channel_id=1, source_target_pairs={{0,1},{1,2},{2,3},{3,4},{4,5},{5,6},{6,7},{7,8},{8,9},{9,10},{10,1... | collective-permute-start | bytes 393224 | tf_op jit(solution)/shard_map/ppermute | solution.py:754
  48.1 1.3 collective-permute-start.6
  49.4 5.3 %shard_map.81.piece_ref = bf16[1024,256]{1,0:T(8,128)(2,1)} custom-call(bf16[768,1024]{1,0:T(8,128)(2,1)S(1)} %get-tuple-element.35.kcat_ref, bf16[768,1024]{1,0:T(8,128)(2,1)S(1)} %get-tuple-element.36.vcat_ref, bf16[256,1024]{1,0:T(8,128)(2,1)S(1)} %get-tuple-element.37.grad_ref, bf16[256,256]{1,0:T(8,128)(2,1)S(1)} %get-tuple-element.38.packed_ref.own_ref, ...), custom_call_target="tpu_custom_call" | custom-call | flops 6442450944 | bytes 5242880 | tf_op jit(solution)/shard_map/pallas_call | solution.py:559
  56.5 1.9 %collective-permute-done.7.other_ref = bf16[1024,256]{1,0:T(8,128)(2,1)} collective-permute-done((bf16[1024,256]{1,0:T(8,128)(2,1)}, bf16[1024,256]{1,0:T(8,128)(2,1)}, u32[]{:S(2)}, u32[]{:S(2)}) %collective-permute-start.7) | collective-permute-done | bytes 524320 | tf_op jit(solution)/shard_map/ppermute | solution.py:711
  58.4 3.1 %shard_map.82 = bf16[512,1280]{1,0:T(8,128)(2,1)} custom-call(s32[1]{0:T(128)} %bitcast.7.core_ref, bf16[2,2,256,256]{3,2,1,0:T(8,128)(2,1)S(1)} %bitcast.18, bf16[2,2,256,256]{3,2,1,0:T(8,128)(2,1)} %bitcast.9.normed_other_ref, bf16[1024,256]{1,0:T(8,128)(2,1)} %shard_map.81.piece_ref, bf16[1024,256]{1,0:T(8,128)(2,1)} %collective-permute-done.7.other_ref, ...), custom_call_target="tpu_custom_call" | custom-call | tf_op jit(solution)/shard_map/pallas_call | solution.py:217
  61.5 14.0 %all-to-all-start = ((bf16[64,8,1280]{2,1,0:T(8,128)(2,1)}), bf16[64,8,1280]{2,1,0:T(8,128)(2,1)}, u32[]{:S(2)}, u32[]{:S(2)}) async-start(bf16[64,8,1280]{2,1,0:T(8,128)(2,1)} %bitcast.13), calls=%async_computation | async-start | bytes 2621440 | tf_op jit(solution)/shard_map/all_to_all | solution.py:716
  75.6 10.3 %shard_map.83 = bf16[2,1024,256]{2,1,0:T(8,128)(2,1)S(1)} custom-call(s32[3]{0:T(128)S(1)} %pad_add_fusion.counts_ref, bf16[256,3072]{1,0:T(8,128)(2,1)S(1)} %get-tuple-element.26.q_ref.k_ref.v_ref, bf16[256,3072]{1,0:T(8,128)(2,1)S(1)} %get-tuple-element.26.q_ref.k_ref.v_ref, bf16[256,3072]{1,0:T(8,128)(2,1)S(1)} %get-tuple-element.26.q_ref.k_ref.v_ref, ...), custom_call_target="tpu_custom_call" | custom-call | tf_op jit(solution)/shard_map/pallas_call | solution.py:663
  86.0 2.6 %collective-permute-done.9.other_ref = bf16[2048,256]{1,0:T(8,128)(2,1)S(1)} collective-permute-done((bf16[2048,256]{1,0:T(8,128)(2,1)S(1)}, bf16[2048,256]{1,0:T(8,128)(2,1)S(1)}, u32[]{:S(2)}, u32[]{:S(2)}) %collective-permute-start.9) | collective-permute-done | bytes 1048608 | tf_op jit(solution)/shard_map/ppermute | solution.py:711
  88.6 3.8 %shard_map.84 = bf16[512,2048]{1,0:T(8,128)(2,1)} custom-call(s32[1]{0:T(128)} %bitcast.7.core_ref, bf16[2,2,256,256]{3,2,1,0:T(8,128)(2,1)S(1)} %bitcast.19, bf16[2,2,256,256]{3,2,1,0:T(8,128)(2,1)} %bitcast.9.normed_other_ref, bf16[2048,256]{1,0:T(8,128)(2,1)S(1)} %bitcast.17, bf16[2048,256]{1,0:T(8,128)(2,1)S(1)} %collective-permute-done.9.other_ref), custom_call_target="tpu_custom_call" | custom-call | tf_op jit(solution)/shard_map/pallas_call | solution.py:217
  92.5 4.6 %all-to-all-done = bf16[64,8,1280]{2,1,0:T(8,128)(2,1)} async-done(((bf16[64,8,1280]{2,1,0:T(8,128)(2,1)}), bf16[64,8,1280]{2,1,0:T(8,128)(2,1)}, u32[]{:S(2)}, u32[]{:S(2)}) %all-to-all-start) | async-done | bytes 1310752 | tf_op jit(solution)/shard_map/all_to_all | solution.py:716
  97.0 5.8 %all-to-all-start.1 = ((bf16[64,8,2048]{2,1,0:T(8,128)(2,1)}), bf16[64,8,2048]{2,1,0:T(8,128)(2,1)S(1)}, u32[]{:S(2)}, u32[]{:S(2)}) async-start(bf16[64,8,2048]{2,1,0:T(8,128)(2,1)} %bitcast.14), calls=%async_computation.1 | async-start | bytes 4194304 | tf_op jit(solution)/shard_map/all_to_all | solution.py:716
  103.6 1.5 %convert_reduce_fusion.1 = f32[8,1280]{1,0:T(8,128)S(1)} fusion(bf16[64,8,1280]{2,1,0:T(8,128)(2,1)} %all-to-all-done), kind=kLoop, calls=%fused_computation.1 | loop fusion | flops 1300480 | bytes 1351680 | tf_op jit(solution)/shard_map/reduce_sum | solution.py:720
  105.5 27.3 %all-to-all-done.1 = bf16[64,8,2048]{2,1,0:T(8,128)(2,1)S(1)} async-done(((bf16[64,8,2048]{2,1,0:T(8,128)(2,1)}), bf16[64,8,2048]{2,1,0:T(8,128)(2,1)S(1)}, u32[]{:S(2)}, u32[]{:S(2)}) %all-to-all-start.1) | async-done | bytes 2097184 | tf_op jit(solution)/shard_map/all_to_all | solution.py:716
  (37 shorter events, 7.4 us)
Async XLA Ops:
  0.6 15.4 %collective-permute-start = (bf16[256,1024]{1,0:T(8,128)(2,1)}, bf16[256,1024]{1,0:T(8,128)(2,1)S(1)}, u32[]{:S(2)}, u32[]{:S(2)}) collective-permute-start(bf16[256,1024]{1,0:T(8,128)(2,1)} %bitcast.22), channel_id=1, source_target_pairs={{0,1},{1,2},{2,3},{3,4},{4,5},{5,6},{6,7},{7,8},{8,9},{9,10},{10,1... | collective-permute-start | bytes 1572872 | tf_op jit(solution)/shard_map/ppermute | solution.py:731
  4.6 15.8 %collective-permute-start.1 = (bf16[256,1024]{1,0:T(8,128)(2,1)}, bf16[256,1024]{1,0:T(8,128)(2,1)}, u32[]{:S(2)}, u32[]{:S(2)}) collective-permute-start(bf16[256,1024]{1,0:T(8,128)(2,1)} %bitcast.23), channel_id=1, source_target_pairs={{1,0},{2,1},{3,2},{4,3},{5,4},{6,5},{7,6},{8,7},{9,8},{10,9},{11,1... | collective-permute-start | bytes 1572872 | tf_op jit(solution)/shard_map/ppermute | solution.py:732
  9.2 1.0 copy-start.6
  10.2 10.1 %copy-start = (bf16[1024,1024]{1,0:T(8,128)(2,1)S(1)}, bf16[1024,1024]{1,0:T(8,128)(2,1)}, u32[]{:S(2)}) copy-start(bf16[1024,1024]{1,0:T(8,128)(2,1)} %w_out_ref.5) | copy-start | bytes 6291460
  10.2 10.1 %copy-start.1 = (bf16[1024,128]{1,0:T(8,128)(2,1)S(1)}, bf16[1024,128]{1,0:T(8,128)(2,1)}, u32[]{:S(2)}) copy-start(bf16[1024,128]{1,0:T(8,128)(2,1)} %readout_ref.5) | copy-start | bytes 786436
  32.0 6.6 %collective-permute-start.2 = (f32[256,128]{1,0:T(8,128)S(1)}, f32[256,128]{1,0:T(8,128)S(1)}, u32[]{:S(2)}, u32[]{:S(2)}) collective-permute-start(f32[256,128]{1,0:T(8,128)S(1)} %get-tuple-element.27.own_ref), channel_id=1, source_target_pairs={{0,64},{64,0},{1,65},{65,1},{2,66},{66,2},{3,67},{67,3},{4,68},{68... | collective-permute-start | bytes 393224 | tf_op jit(solution)/shard_map/ppermute | solution.py:746
  35.1 5.1 %copy-start.3 = (f32[256,128]{1,0:T(8,128)S(1)}, f32[256,128]{1,0:T(8,128)}, u32[]{:S(2)}) copy-start(f32[256,128]{1,0:T(8,128)} %target_ref.1) | copy-start | bytes 393220
  38.5 1.6 %collective-permute-start.3 = (f32[2,256,128]{2,1,0:T(8,128)S(1)}, f32[2,256,128]{2,1,0:T(8,128)S(1)}, u32[]{:S(2)}, u32[]{:S(2)}) collective-permute-start(f32[2,256,128]{2,1,0:T(8,128)S(1)} %pad_maximum_fusion), channel_id=1, source_target_pairs={{0,32},{32,0},{1,33},{33,1},{2,34},{34,2},{3,35},{35,3},{4,36},{36... | collective-permute-start | bytes 786440 | tf_op jit(solution)/shard_map/ppermute | solution.py:711
  38.6 17.9 %collective-permute-start.4 = (bf16[1024,256]{1,0:T(8,128)(2,1)S(1)}, bf16[1024,256]{1,0:T(8,128)(2,1)}, u32[]{:S(2)}, u32[]{:S(2)}) collective-permute-start(bf16[1024,256]{1,0:T(8,128)(2,1)S(1)} %get-tuple-element.34), channel_id=1, source_target_pairs={{0,32},{32,0},{1,33},{33,1},{2,34},{34,2},{3,35},{35,3},{4,36},{36... | collective-permute-start | bytes 1572872 | tf_op jit(solution)/shard_map/ppermute | solution.py:711
  43.8 0.7 copy-start.4
  44.4 10.3 %copy-start.2 = (bf16[256,1024]{1,0:T(8,128)(2,1)}, bf16[256,1024]{1,0:T(8,128)(2,1)S(1)}, u32[]{:S(2)}) copy-start(bf16[256,1024]{1,0:T(8,128)(2,1)S(1)} %get-tuple-element.37.grad_ref) | copy-start | bytes 1572868
  44.4 10.3 %collective-permute-start.5 = (bf16[256,256]{1,0:T(8,128)(2,1)S(1)}, bf16[256,256]{1,0:T(8,128)(2,1)S(1)}, u32[]{:S(2)}, u32[]{:S(2)}) collective-permute-start(bf16[256,256]{1,0:T(8,128)(2,1)S(1)} %get-tuple-element.38.packed_ref.own_ref), channel_id=1, source_target_pairs={{0,1},{1,2},{2,3},{3,4},{4,5},{5,6},{6,7},{7,8},{8,9},{9,10},{10,1... | collective-permute-start | bytes 393224 | tf_op jit(solution)/shard_map/ppermute | solution.py:754
  48.1 7.2 %collective-permute-start.6 = (bf16[256,256]{1,0:T(8,128)(2,1)S(1)}, bf16[256,256]{1,0:T(8,128)(2,1)S(1)}, u32[]{:S(2)}, u32[]{:S(2)}) collective-permute-start(bf16[256,256]{1,0:T(8,128)(2,1)S(1)} %get-tuple-element.38.packed_ref.own_ref), channel_id=1, source_target_pairs={{1,0},{2,1},{3,2},{4,3},{5,4},{6,5},{7,6},{8,7},{9,8},{10,9},{11,1... | collective-permute-start | bytes 393224 | tf_op jit(solution)/shard_map/ppermute | solution.py:755
  49.4 7.2 %collective-permute-start.8 = (bf16[1024,256]{1,0:T(8,128)(2,1)}, bf16[1024,256]{1,0:T(8,128)(2,1)}, u32[]{:S(2)}, u32[]{:S(2)}) collective-permute-start(bf16[1024,256]{1,0:T(8,128)(2,1)} %get-tuple-element.42), channel_id=1, source_target_pairs={{0,32},{32,0},{1,33},{33,1},{2,34},{34,2},{3,35},{35,3},{4,36},{36... | collective-permute-start | bytes 1572872 | tf_op jit(solution)/shard_map/ppermute | solution.py:711
  54.7 0.7 copy-start.7
  55.4 0.7 copy-start.8
  56.0 2.4 %collective-permute-start.7 = (bf16[1024,256]{1,0:T(8,128)(2,1)}, bf16[1024,256]{1,0:T(8,128)(2,1)}, u32[]{:S(2)}, u32[]{:S(2)}) collective-permute-start(bf16[1024,256]{1,0:T(8,128)(2,1)} %shard_map.81.piece_ref), channel_id=1, source_target_pairs={{0,32},{32,0},{1,33},{33,1},{2,34},{34,2},{3,35},{35,3},{4,36},{36... | collective-permute-start | bytes 1572872 | tf_op jit(solution)/shard_map/ppermute | solution.py:711
  61.5 35.5 %all-to-all-start = ((bf16[64,8,1280]{2,1,0:T(8,128)(2,1)}), bf16[64,8,1280]{2,1,0:T(8,128)(2,1)}, u32[]{:S(2)}, u32[]{:S(2)}) async-start(bf16[64,8,1280]{2,1,0:T(8,128)(2,1)} %bitcast.13), calls=%async_computation | async-start | bytes 2621440 | tf_op jit(solution)/shard_map/all_to_all | solution.py:716
  85.9 2.7 %collective-permute-start.9 = (bf16[2048,256]{1,0:T(8,128)(2,1)S(1)}, bf16[2048,256]{1,0:T(8,128)(2,1)S(1)}, u32[]{:S(2)}, u32[]{:S(2)}) collective-permute-start(bf16[2048,256]{1,0:T(8,128)(2,1)S(1)} %bitcast.16), channel_id=1, source_target_pairs={{0,32},{32,0},{1,33},{33,1},{2,34},{34,2},{3,35},{35,3},{4,36},{36... | collective-permute-start | bytes 3145736 | tf_op jit(solution)/shard_map/ppermute | solution.py:711
  97.0 5.8 %copy-start.5 = (f32[256,128]{1,0:T(8,128)S(1)}, f32[256,128]{1,0:T(8,128)}, u32[]{:S(2)}) copy-start(f32[256,128]{1,0:T(8,128)} %copy-done.4) | copy-start | bytes 393220
  97.0 35.8 %all-to-all-start.1 = ((bf16[64,8,2048]{2,1,0:T(8,128)(2,1)}), bf16[64,8,2048]{2,1,0:T(8,128)(2,1)S(1)}, u32[]{:S(2)}, u32[]{:S(2)}) async-start(bf16[64,8,2048]{2,1,0:T(8,128)(2,1)} %bitcast.14), calls=%async_computation.1 | async-start | bytes 4194304 | tf_op jit(solution)/shard_map/all_to_all | solution.py:716

commit v10 on v9

--- a/solution.py
+++ b/solution.py
@@ -514,8 +514,8 @@
         in_specs=[pl.BlockSpec(memory_space=pltpu.SMEM)] + [vmem] * 9,
         out_specs=[vmem] * 4,
         out_shape=[
-            jax.ShapeDtypeStruct((BLOCK, 128), F32),
-            jax.ShapeDtypeStruct((BLOCK, 256), BF),
+            pltpu.HBM((BLOCK, 128), F32),
+            pltpu.HBM((BLOCK, 256), BF),
             jax.ShapeDtypeStruct((BLOCK, 1024), BF),
             jax.ShapeDtypeStruct((1024, 256), BF),
         ],
@@ -574,7 +574,7 @@
         cost_estimate=pl.CostEstimate(
             flops=6 << 30, bytes_accessed=5 << 20, transcendentals=3 << 20
         ),
-    )(kcat, vcat, grad, packed, probs, inverse)
+    )(kcat, vcat, grad, in_hbm(packed), probs, inverse)
 
 
 def key_kernel(
@@ -692,7 +692,7 @@
         projected,
         qhalo,
         in_hbm(grad),
-        own,
+        in_hbm(own),
         in_hbm(left),
         in_hbm(right),
         in_hbm(w_out),
@@ -751,13 +751,10 @@
         scalars, forecast, near, others, target, attended, hidden, stats, w_out, readout_weight
     )
     crps = lax.dynamic_slice_in_dim(crps_whole, member_index * 32, 32, 1)
+    dquery = query_grads(kcat, vcat, grad, packed, probs, inverse)
+    packed, dquery = lax.optimization_barrier((packed, dquery))
     packed_left = lax.ppermute(packed, CELLS, up)
     packed_right = lax.ppermute(packed, CELLS, down)
-
-    dquery = query_grads(kcat, vcat, grad, packed, probs, inverse)
-    dquery, packed_left, packed_right = lax.optimization_barrier(
-        (dquery, packed_left, packed_right)
-    )
 
     first_part = partial_sums(
         core, turned, turned_other, dquery, swap_core(dquery), (small, swap_core(small))

time: 134 us -> 147 us (1.097)
  waiting for transfers between devices: 44.3 us -> 54.6 us
  starting transfers between devices: 34.3 us -> 36.7 us
    ppermute x1, waiting for transfers between devices: 0.01 us -> 12.5 us  [per_device(): packed_left = lax.ppermute(packed, CELLS, up)]
    all_to_all x2, waiting for transfers between devices: 31.9 us -> 27.3 us  [scatter(): lax.all_to_all(partial.reshape(64, 8, columns), CHIPS, split_axis=0, conc...]
    all_to_all x2, starting transfers between devices: 19.8 us -> 22.2 us  [scatter(): lax.all_to_all(partial.reshape(64, 8, columns), CHIPS, split_axis=0, conc...]
    ppermute x1, waiting for transfers between devices: 0.46 us -> 2.28 us  [per_device(): packed_right = lax.ppermute(packed, CELLS, down)]
  transfers between devices with their start and end apart: 12 -> 12, of which waited for: 9 -> 10; matrix products, arithmetic and copies ran while one was open for 3% -> 3% of each run, Pallas kernels for 23% -> 21%
where the time goes in v10:
time: 147 us
  waiting for transfers between devices  54.6 us (37%)
  Pallas kernels  45.7 us (31%)
  starting transfers between devices  36.7 us (25%)
  local copies, waits for them, and re-layouts  3.88 us (3%)
  other arithmetic  3.15 us (2%)
  between operations  2.14 us (1%)
    all_to_all x2, waiting for transfers between devices, scatter(): lax.all_to_all(partial.reshape(64, 8, columns), CHIPS, split_axis=0, conc...  27.3 us
    all_to_all x2, starting transfers between devices, scatter(): lax.all_to_all(partial.reshape(64, 8, columns), CHIPS, split_axis=0, conc...  22.2 us
    ppermute x1, waiting for transfers between devices, per_device(): packed_left = lax.ppermute(packed, CELLS, up)  12.5 us
    pallas_call x1, Pallas kernels, forward(): pl.pallas_call(forward_kernel, grid=(4,), in_specs=[pl.BlockSpec(memory_s...  11.6 us
    pallas_call x1, Pallas kernels, key_grads(): pl.pallas_call(key_kernel, grid=(4,), in_specs=[pl.BlockSpec(memory_space...  10.3 us
    pallas_call x2, Pallas kernels, partial_sums(): pl.pallas_call(functools.partial(partial_kernel, len(smalls)), in_specs=[...  6.96 us
    pallas_call x1, Pallas kernels, query_grads(): pl.pallas_call(query_kernel, grid=(4,), in_specs=[part(window, 0), part(w...  6.09 us
    ppermute x5, waiting for transfers between devices, swap_core(): return lax.ppermute(values, 'core', SWAP)  6.06 us
  transfers between devices with their start and end apart: 12, of which 10 were waited for; matrix products, arithmetic and copies ran while one was open for 3% of the time, Pallas kernels for 21%

profile of v10, /device:TPU:0, one launch (start us, length us, event | category | flops | bytes accessed | tf_op | source)
XLA Modules:
  0.0 146.5 jit_solution(8015755296555385876)
XLA Ops:
  0.6 3.9 %collective-permute-start = (bf16[256,1024]{1,0:T(8,128)(2,1)}, bf16[256,1024]{1,0:T(8,128)(2,1)S(1)}, u32[]{:S(2)}, u32[]{:S(2)}) collective-permute-start(bf16[256,1024]{1,0:T(8,128)(2,1)} %bitcast.22), channel_id=1, source_target_pairs={{0,1},{1,2},{2,3},{3,4},{4,5},{5,6},{6,7},{7,8},{8,9},{9,10},{10,1... | collective-permute-start | bytes 1572872 | tf_op jit(solution)/shard_map/ppermute | solution.py:731
  4.6 1.3 collective-permute-start.1
  5.9 1.4 fusion.2
  10.2 4.1 %shard_map.77 = (bf16[256,3072]{1,0:T(8,128)(2,1)S(1)}, bf16[1024,256]{1,0:T(8,128)(2,1)S(1)}) custom-call(bf16[256,1024]{1,0:T(8,128)(2,1)S(1)} %bitcast.24, bf16[1024,3072]{1,0:T(8,128)(2,1)} %weight_ref.5), custom_call_target="tpu_custom_call" | custom-call | flops 2147483648 | bytes 8388608 | tf_op jit(solution)/shard_map/pallas_call | solution.py:99
  14.4 1.6 %collective-permute-done.left_ref = bf16[256,1024]{1,0:T(8,128)(2,1)S(1)} collective-permute-done((bf16[256,1024]{1,0:T(8,128)(2,1)}, bf16[256,1024]{1,0:T(8,128)(2,1)S(1)}, u32[]{:S(2)}, u32[]{:S(2)}) %collective-permute-start) | collective-permute-done | bytes 524320 | tf_op jit(solution)/shard_map/ppermute | solution.py:731
  16.0 4.3 %collective-permute-done.1.right_ref = bf16[256,1024]{1,0:T(8,128)(2,1)} collective-permute-done((bf16[256,1024]{1,0:T(8,128)(2,1)}, bf16[256,1024]{1,0:T(8,128)(2,1)}, u32[]{:S(2)}, u32[]{:S(2)}) %collective-permute-start.1) | collective-permute-done | bytes 524320 | tf_op jit(solution)/shard_map/ppermute | solution.py:732
  20.3 11.6 %shard_map.78 = (bf16[512,1024]{1,0:T(8,128)(2,1)S(1)}, bf16[768,1024]{1,0:T(8,128)(2,1)S(1)}, bf16[768,1024]{1,0:T(8,128)(2,1)S(1)}, f32[256,1024]{1,0:T(8,128)...) custom-call(s32[3]{0:T(128)S(1)} %pad_add_fusion.counts_ref, ...), custom_call_target="tpu_custom_call" | custom-call | flops 6442450944 | bytes 12582912 | tf_op jit(solution)/shard_map/pallas_call | solution.py:388
  32.0 3.1 %collective-permute-start.2 = (f32[256,128]{1,0:T(8,128)S(1)}, f32[256,128]{1,0:T(8,128)S(1)}, u32[]{:S(2)}, u32[]{:S(2)}) collective-permute-start(f32[256,128]{1,0:T(8,128)S(1)} %get-tuple-element.26.own_ref), channel_id=1, source_target_pairs={{0,64},{64,0},{1,65},{65,1},{2,66},{66,2},{3,67},{67,3},{4,68},{68... | collective-permute-start | bytes 393224 | tf_op jit(solution)/shard_map/ppermute | solution.py:746
  35.1 3.0 %shard_map.79.qhalo_ref = bf16[512,1024]{1,0:T(8,128)(2,1)S(1)} custom-call(bf16[512,1024]{1,0:T(8,128)(2,1)S(1)} %get-tuple-element.27.normed_ref, bf16[1024,3072]{1,0:T(8,128)(2,1)} %weight_ref.5), custom_call_target="tpu_custom_call" | custom-call | tf_op jit(solution)/shard_map/pallas_call | solution.py:137
  40.2 3.6 %shard_map.80 = (f32[256,128]{1,0:T(8,128)}, bf16[256,256]{1,0:T(8,128)(2,1)}, bf16[256,1024]{1,0:T(8,128)(2,1)S(1)}, bf16[1024,256]{1,0:T(8,128)(2,1)}) custom-call(s32[3]{0:T(128)S(1)} %pad_add_fusion.counts_ref, f32[256,128]{1,0:T(8,128)S(1)} %get-tuple-element.26.own_ref, f32[256,128]{1,0:T(8,128)S(1)} %collective-permute-done.2.near_ref, ...), custom_call_target="tpu_custom_call" | custom-call | tf_op jit(solution)/shard_map/pallas_call | solution.py:512
  43.8 6.1 %shard_map.81.piece_ref = bf16[1024,256]{1,0:T(8,128)(2,1)} custom-call(bf16[768,1024]{1,0:T(8,128)(2,1)S(1)} %get-tuple-element.35.kcat_ref, bf16[768,1024]{1,0:T(8,128)(2,1)S(1)} %get-tuple-element.36.vcat_ref, bf16[256,1024]{1,0:T(8,128)(2,1)S(1)} %get-tuple-element.37.grad_ref, bf16[256,256]{1,0:T(8,128)(2,1)} %get-tuple-element.44.packed_ref.own_ref, ...), custom_call_target="tpu_custom_call" | custom-call | flops 6442450944 | bytes 5242880 | tf_op jit(solution)/shard_map/pallas_call | solution.py:559
  50.4 1.7 %collective-permute-done.5.other_ref = bf16[1024,256]{1,0:T(8,128)(2,1)} collective-permute-done((bf16[1024,256]{1,0:T(8,128)(2,1)}, bf16[1024,256]{1,0:T(8,128)(2,1)}, u32[]{:S(2)}, u32[]{:S(2)}) %collective-permute-start.5) | collective-permute-done | bytes 524320 | tf_op jit(solution)/shard_map/ppermute | solution.py:711
  52.9 3.1 %shard_map.82 = bf16[512,1280]{1,0:T(8,128)(2,1)} custom-call(s32[1]{0:T(128)} %bitcast.7.core_ref, bf16[2,2,256,256]{3,2,1,0:T(8,128)(2,1)S(1)} %bitcast.18, bf16[2,2,256,256]{3,2,1,0:T(8,128)(2,1)} %bitcast.9.normed_other_ref, bf16[1024,256]{1,0:T(8,128)(2,1)} %shard_map.81.piece_ref, bf16[1024,256]{1,0:T(8,128)(2,1)} %collective-permute-done.5.other_ref, ...), custom_call_target="tpu_custom_call" | custom-call | tf_op jit(solution)/shard_map/pallas_call | solution.py:217
  56.0 12.7 %all-to-all-start = ((bf16[64,8,1280]{2,1,0:T(8,128)(2,1)}), bf16[64,8,1280]{2,1,0:T(8,128)(2,1)}, u32[]{:S(2)}, u32[]{:S(2)}) async-start(bf16[64,8,1280]{2,1,0:T(8,128)(2,1)} %bitcast.13), calls=%async_computation | async-start | bytes 2621440 | tf_op jit(solution)/shard_map/all_to_all | solution.py:716
  68.7 3.4 %collective-permute-start.7 = (bf16[256,256]{1,0:T(8,128)(2,1)S(1)}, bf16[256,256]{1,0:T(8,128)(2,1)S(1)}, u32[]{:S(2)}, u32[]{:S(2)}) collective-permute-start(bf16[256,256]{1,0:T(8,128)(2,1)S(1)} %copy-done.5), channel_id=1, source_target_pairs={{0,1},{1,2},{2,3},{3,4},{4,5},{5,6},{6,7},{7,8},{8,9},{9,10},{10,1... | collective-permute-start | bytes 393224 | tf_op jit(solution)/shard_map/ppermute | solution.py:756
  72.2 1.5 %collective-permute-start.8 = (bf16[256,256]{1,0:T(8,128)(2,1)S(1)}, bf16[256,256]{1,0:T(8,128)(2,1)S(1)}, u32[]{:S(2)}, u32[]{:S(2)}) collective-permute-start(bf16[256,256]{1,0:T(8,128)(2,1)S(1)} %copy-done.5), channel_id=1, source_target_pairs={{1,0},{2,1},{3,2},{4,3},{5,4},{6,5},{7,6},{8,7},{9,8},{10,9},{11,1... | collective-permute-start | bytes 393224 | tf_op jit(solution)/shard_map/ppermute | solution.py:757
  73.6 12.5 %collective-permute-done.7.left_ref = bf16[256,256]{1,0:T(8,128)(2,1)S(1)} collective-permute-done((bf16[256,256]{1,0:T(8,128)(2,1)S(1)}, bf16[256,256]{1,0:T(8,128)(2,1)S(1)}, u32[]{:S(2)}, u32[]{:S(2)}) %collective-permute-start.7) | collective-permute-done | bytes 131104 | tf_op jit(solution)/shard_map/ppermute | solution.py:756
  86.2 2.3 %collective-permute-done.8.right_ref = bf16[256,256]{1,0:T(8,128)(2,1)S(1)} collective-permute-done((bf16[256,256]{1,0:T(8,128)(2,1)S(1)}, bf16[256,256]{1,0:T(8,128)(2,1)S(1)}, u32[]{:S(2)}, u32[]{:S(2)}) %collective-permute-start.8) | collective-permute-done | bytes 131104 | tf_op jit(solution)/shard_map/ppermute | solution.py:757
  89.1 10.3 %shard_map.83 = bf16[2,1024,256]{2,1,0:T(8,128)(2,1)S(1)} custom-call(s32[3]{0:T(128)S(1)} %pad_add_fusion.counts_ref, bf16[256,3072]{1,0:T(8,128)(2,1)S(1)} %get-tuple-element.25.q_ref.k_ref.v_ref, bf16[256,3072]{1,0:T(8,128)(2,1)S(1)} %get-tuple-element.25.q_ref.k_ref.v_ref, bf16[256,3072]{1,0:T(8,128)(2,1)S(1)} %get-tuple-element.25.q_ref.k_ref.v_ref, ...), custom_call_target="tpu_custom_call" | custom-call | tf_op jit(solution)/shard_map/pallas_call | solution.py:663
  99.6 2.5 %collective-permute-done.9.other_ref = bf16[2048,256]{1,0:T(8,128)(2,1)S(1)} collective-permute-done((bf16[2048,256]{1,0:T(8,128)(2,1)S(1)}, bf16[2048,256]{1,0:T(8,128)(2,1)S(1)}, u32[]{:S(2)}, u32[]{:S(2)}) %collective-permute-start.9) | collective-permute-done | bytes 1048608 | tf_op jit(solution)/shard_map/ppermute | solution.py:711
  102.2 3.8 %shard_map.84 = bf16[512,2048]{1,0:T(8,128)(2,1)} custom-call(s32[1]{0:T(128)} %bitcast.7.core_ref, bf16[2,2,256,256]{3,2,1,0:T(8,128)(2,1)S(1)} %bitcast.19, bf16[2,2,256,256]{3,2,1,0:T(8,128)(2,1)} %bitcast.9.normed_other_ref, bf16[2048,256]{1,0:T(8,128)(2,1)S(1)} %bitcast.17, bf16[2048,256]{1,0:T(8,128)(2,1)S(1)} %collective-permute-done.9.other_ref), custom_call_target="tpu_custom_call" | custom-call | tf_op jit(solution)/shard_map/pallas_call | solution.py:217
  106.1 9.5 %all-to-all-start.1 = ((bf16[64,8,2048]{2,1,0:T(8,128)(2,1)}), bf16[64,8,2048]{2,1,0:T(8,128)(2,1)S(1)}, u32[]{:S(2)}, u32[]{:S(2)}) async-start(bf16[64,8,2048]{2,1,0:T(8,128)(2,1)} %bitcast.14), calls=%async_computation.1 | async-start | bytes 4194304 | tf_op jit(solution)/shard_map/all_to_all | solution.py:716
  116.4 1.5 %convert_reduce_fusion.1 = f32[8,1280]{1,0:T(8,128)S(1)} fusion(bf16[64,8,1280]{2,1,0:T(8,128)(2,1)} %all-to-all-done), kind=kLoop, calls=%fused_computation.1 | loop fusion | flops 1300480 | bytes 1351680 | tf_op jit(solution)/shard_map/reduce_sum | solution.py:720
  118.2 27.3 %all-to-all-done.1 = bf16[64,8,2048]{2,1,0:T(8,128)(2,1)S(1)} async-done(((bf16[64,8,2048]{2,1,0:T(8,128)(2,1)}), bf16[64,8,2048]{2,1,0:T(8,128)(2,1)S(1)}, u32[]{:S(2)}, u32[]{:S(2)}) %all-to-all-start.1) | async-done | bytes 2097184 | tf_op jit(solution)/shard_map/all_to_all | solution.py:716
  (37 shorter events, 8.0 us)
Async XLA Ops:
  0.6 15.4 %collective-permute-start = (bf16[256,1024]{1,0:T(8,128)(2,1)}, bf16[256,1024]{1,0:T(8,128)(2,1)S(1)}, u32[]{:S(2)}, u32[]{:S(2)}) collective-permute-start(bf16[256,1024]{1,0:T(8,128)(2,1)} %bitcast.22), channel_id=1, source_target_pairs={{0,1},{1,2},{2,3},{3,4},{4,5},{5,6},{6,7},{7,8},{8,9},{9,10},{10,1... | collective-permute-start | bytes 1572872 | tf_op jit(solution)/shard_map/ppermute | solution.py:731
  4.6 15.8 %collective-permute-start.1 = (bf16[256,1024]{1,0:T(8,128)(2,1)}, bf16[256,1024]{1,0:T(8,128)(2,1)}, u32[]{:S(2)}, u32[]{:S(2)}) collective-permute-start(bf16[256,1024]{1,0:T(8,128)(2,1)} %bitcast.23), channel_id=1, source_target_pairs={{1,0},{2,1},{3,2},{4,3},{5,4},{6,5},{7,6},{8,7},{9,8},{10,9},{11,1... | collective-permute-start | bytes 1572872 | tf_op jit(solution)/shard_map/ppermute | solution.py:732
  9.2 1.0 copy-start.4
  10.2 10.1 %copy-start = (bf16[1024,1024]{1,0:T(8,128)(2,1)S(1)}, bf16[1024,1024]{1,0:T(8,128)(2,1)}, u32[]{:S(2)}) copy-start(bf16[1024,1024]{1,0:T(8,128)(2,1)} %w_out_ref.5) | copy-start | bytes 6291460
  10.2 10.1 %copy-start.1 = (bf16[1024,128]{1,0:T(8,128)(2,1)S(1)}, bf16[1024,128]{1,0:T(8,128)(2,1)}, u32[]{:S(2)}) copy-start(bf16[1024,128]{1,0:T(8,128)(2,1)} %readout_ref.5) | copy-start | bytes 786436
  32.0 6.6 %collective-permute-start.2 = (f32[256,128]{1,0:T(8,128)S(1)}, f32[256,128]{1,0:T(8,128)S(1)}, u32[]{:S(2)}, u32[]{:S(2)}) collective-permute-start(f32[256,128]{1,0:T(8,128)S(1)} %get-tuple-element.26.own_ref), channel_id=1, source_target_pairs={{0,64},{64,0},{1,65},{65,1},{2,66},{66,2},{3,67},{67,3},{4,68},{68... | collective-permute-start | bytes 393224 | tf_op jit(solution)/shard_map/ppermute | solution.py:746
  35.1 5.1 %copy-start.3 = (f32[256,128]{1,0:T(8,128)S(1)}, f32[256,128]{1,0:T(8,128)}, u32[]{:S(2)}) copy-start(f32[256,128]{1,0:T(8,128)} %target_ref.1) | copy-start | bytes 393220
  38.5 1.6 %collective-permute-start.3 = (f32[2,256,128]{2,1,0:T(8,128)S(1)}, f32[2,256,128]{2,1,0:T(8,128)S(1)}, u32[]{:S(2)}, u32[]{:S(2)}) collective-permute-start(f32[2,256,128]{2,1,0:T(8,128)S(1)} %pad_maximum_fusion), channel_id=1, source_target_pairs={{0,32},{32,0},{1,33},{33,1},{2,34},{34,2},{3,35},{35,3},{4,36},{36... | collective-permute-start | bytes 786440 | tf_op jit(solution)/shard_map/ppermute | solution.py:711
  38.6 11.7 %collective-permute-start.4 = (bf16[1024,256]{1,0:T(8,128)(2,1)S(1)}, bf16[1024,256]{1,0:T(8,128)(2,1)}, u32[]{:S(2)}, u32[]{:S(2)}) collective-permute-start(bf16[1024,256]{1,0:T(8,128)(2,1)S(1)} %get-tuple-element.33), channel_id=1, source_target_pairs={{0,32},{32,0},{1,33},{33,1},{2,34},{34,2},{3,35},{35,3},{4,36},{36... | collective-permute-start | bytes 1572872 | tf_op jit(solution)/shard_map/ppermute | solution.py:711
  43.8 6.1 %copy-start.2 = (bf16[256,1024]{1,0:T(8,128)(2,1)}, bf16[256,1024]{1,0:T(8,128)(2,1)S(1)}, u32[]{:S(2)}) copy-start(bf16[256,1024]{1,0:T(8,128)(2,1)S(1)} %get-tuple-element.37.grad_ref) | copy-start | bytes 1572868
  49.9 2.3 %collective-permute-start.5 = (bf16[1024,256]{1,0:T(8,128)(2,1)}, bf16[1024,256]{1,0:T(8,128)(2,1)}, u32[]{:S(2)}, u32[]{:S(2)}) collective-permute-start(bf16[1024,256]{1,0:T(8,128)(2,1)} %shard_map.81.piece_ref), channel_id=1, source_target_pairs={{0,32},{32,0},{1,33},{33,1},{2,34},{34,2},{3,35},{35,3},{4,36},{36... | collective-permute-start | bytes 1572872 | tf_op jit(solution)/shard_map/ppermute | solution.py:711
  50.0 2.9 %collective-permute-start.6 = (bf16[1024,256]{1,0:T(8,128)(2,1)}, bf16[1024,256]{1,0:T(8,128)(2,1)}, u32[]{:S(2)}, u32[]{:S(2)}) collective-permute-start(bf16[1024,256]{1,0:T(8,128)(2,1)} %get-tuple-element.41), channel_id=1, source_target_pairs={{0,32},{32,0},{1,33},{33,1},{2,34},{34,2},{3,35},{35,3},{4,36},{36... | collective-permute-start | bytes 1572872 | tf_op jit(solution)/shard_map/ppermute | solution.py:711
  56.0 12.7 %copy-start.5 = (bf16[256,256]{1,0:T(8,128)(2,1)S(1)}, bf16[256,256]{1,0:T(8,128)(2,1)}, u32[]{:S(2)}) copy-start(bf16[256,256]{1,0:T(8,128)(2,1)} %get-tuple-element.44.packed_ref.own_ref) | copy-start | bytes 393220
  56.0 50.0 %all-to-all-start = ((bf16[64,8,1280]{2,1,0:T(8,128)(2,1)}), bf16[64,8,1280]{2,1,0:T(8,128)(2,1)}, u32[]{:S(2)}, u32[]{:S(2)}) async-start(bf16[64,8,1280]{2,1,0:T(8,128)(2,1)} %bitcast.13), calls=%async_computation | async-start | bytes 2621440 | tf_op jit(solution)/shard_map/all_to_all | solution.py:716
  68.7 17.4 %collective-permute-start.7 = (bf16[256,256]{1,0:T(8,128)(2,1)S(1)}, bf16[256,256]{1,0:T(8,128)(2,1)S(1)}, u32[]{:S(2)}, u32[]{:S(2)}) collective-permute-start(bf16[256,256]{1,0:T(8,128)(2,1)S(1)} %copy-done.5), channel_id=1, source_target_pairs={{0,1},{1,2},{2,3},{3,4},{4,5},{5,6},{6,7},{7,8},{8,9},{9,10},{10,1... | collective-permute-start | bytes 393224 | tf_op jit(solution)/shard_map/ppermute | solution.py:756
  72.2 16.3 %collective-permute-start.8 = (bf16[256,256]{1,0:T(8,128)(2,1)S(1)}, bf16[256,256]{1,0:T(8,128)(2,1)S(1)}, u32[]{:S(2)}, u32[]{:S(2)}) collective-permute-start(bf16[256,256]{1,0:T(8,128)(2,1)S(1)} %copy-done.5), channel_id=1, source_target_pairs={{1,0},{2,1},{3,2},{4,3},{5,4},{6,5},{7,6},{8,7},{9,8},{10,9},{11,1... | collective-permute-start | bytes 393224 | tf_op jit(solution)/shard_map/ppermute | solution.py:757
  86.2 2.3 %copy-start.6 = (bf16[256,256]{1,0:T(8,128)(2,1)}, bf16[256,256]{1,0:T(8,128)(2,1)S(1)}, u32[]{:S(2)}) copy-start(bf16[256,256]{1,0:T(8,128)(2,1)S(1)} %collective-permute-done.7.left_ref) | copy-start | bytes 393220
  88.5 0.7 copy-start.7
  99.4 2.7 %collective-permute-start.9 = (bf16[2048,256]{1,0:T(8,128)(2,1)S(1)}, bf16[2048,256]{1,0:T(8,128)(2,1)S(1)}, u32[]{:S(2)}, u32[]{:S(2)}) collective-permute-start(bf16[2048,256]{1,0:T(8,128)(2,1)S(1)} %bitcast.16), channel_id=1, source_target_pairs={{0,32},{32,0},{1,33},{33,1},{2,34},{34,2},{3,35},{35,3},{4,36},{36... | collective-permute-start | bytes 3145736 | tf_op jit(solution)/shard_map/ppermute | solution.py:711
  106.0 9.5 %copy-start.8 = (f32[256,128]{1,0:T(8,128)S(1)}, f32[256,128]{1,0:T(8,128)}, u32[]{:S(2)}) copy-start(f32[256,128]{1,0:T(8,128)} %get-tuple-element.32) | copy-start | bytes 393220
  106.1 39.5 %all-to-all-start.1 = ((bf16[64,8,2048]{2,1,0:T(8,128)(2,1)}), bf16[64,8,2048]{2,1,0:T(8,128)(2,1)S(1)}, u32[]{:S(2)}, u32[]{:S(2)}) async-start(bf16[64,8,2048]{2,1,0:T(8,128)(2,1)} %bitcast.14), calls=%async_computation.1 | async-start | bytes 4194304 | tf_op jit(solution)/shard_map/all_to_all | solution.py:716

commit v11 on v10

--- a/solution.py
+++ b/solution.py
@@ -756,8 +756,11 @@
     packed_left = lax.ppermute(packed, CELLS, up)
     packed_right = lax.ppermute(packed, CELLS, down)
 
+    dquery_other, packed_left, packed_right = lax.optimization_barrier(
+        (swap_core(dquery), packed_left, packed_right)
+    )
     first_part = partial_sums(
-        core, turned, turned_other, dquery, swap_core(dquery), (small, swap_core(small))
+        core, turned, turned_other, dquery, dquery_other, (small, swap_core(small))
     )
     first_part, scalars = lax.optimization_barrier((first_part, scalars))
     first = scatter(first_part)

time: 147 us -> 138 us (0.939)
  waiting for transfers between devices: 54.6 us -> 47.9 us
  starting transfers between devices: 36.7 us -> 34.8 us
    ppermute x1, waiting for transfers between devices: 12.5 us -> 1.32 us  [per_device(): packed_left = lax.ppermute(packed, CELLS, up)]
    all_to_all x2, waiting for transfers between devices: 27.3 us -> 31.3 us  [scatter(): lax.all_to_all(partial.reshape(64, 8, columns), CHIPS, split_axis=0, conc...]
    ppermute x1, waiting for transfers between devices: 2.28 us -> 4.86 us  [per_device(): packed_right = lax.ppermute(packed, CELLS, down)]
    all_to_all x2, starting transfers between devices: 22.2 us -> 20.1 us  [scatter(): lax.all_to_all(partial.reshape(64, 8, columns), CHIPS, split_axis=0, conc...]
    ppermute x5, waiting for transfers between devices: 6.06 us -> 4.18 us  [swap_core(): return lax.ppermute(values, 'core', SWAP)]
  transfers between devices with their start and end apart: 12 -> 12, of which waited for: 10 -> 9; matrix products, arithmetic and copies ran while one was open for 3% -> 3% of each run, Pallas kernels for 21% -> 16%
where the time goes in v11:
time: 138 us; the launch traced here: 137 us
  waiting for transfers between devices  47.9 us (35%)
  Pallas kernels  45.8 us (33%)
  starting transfers between devices  34.8 us (25%)
  local copies, waits for them, and re-layouts  3.24 us (2%)
  other arithmetic  3.23 us (2%)
  between operations  2.12 us (2%)
    all_to_all x2, waiting for transfers between devices, scatter(): lax.all_to_all(partial.reshape(64, 8, columns), CHIPS, split_axis=0, conc...  31.3 us
    all_to_all x2, starting transfers between devices, scatter(): lax.all_to_all(partial.reshape(64, 8, columns), CHIPS, split_axis=0, conc...  20.1 us
    pallas_call x1, Pallas kernels, forward(): pl.pallas_call(forward_kernel, grid=(4,), in_specs=[pl.BlockSpec(memory_s...  11.6 us
    pallas_call x1, Pallas kernels, key_grads(): pl.pallas_call(key_kernel, grid=(4,), in_specs=[pl.BlockSpec(memory_space...  10.4 us
    pallas_call x2, Pallas kernels, partial_sums(): pl.pallas_call(functools.partial(partial_kernel, len(smalls)), in_specs=[...  6.95 us
    pallas_call x1, Pallas kernels, query_grads(): pl.pallas_call(query_kernel, grid=(4,), in_specs=[part(window, 0), part(w...  6.15 us
    ppermute x1, waiting for transfers between devices, per_device(): packed_right = lax.ppermute(packed, CELLS, down)  4.86 us
    ppermute x1, starting transfers between devices, per_device(): packed_left = lax.ppermute(packed, CELLS, up)  4.31 us
  transfers between devices with their start and end apart: 12, of which 9 were waited for; matrix products, arithmetic and copies ran while one was open for 3% of the time, Pallas kernels for 16%

profile of v11, /device:TPU:0, one launch (start us, length us, event | category | flops | bytes accessed | tf_op | source)
XLA Modules:
  0.0 137.4 jit_solution(2280846143768785574)
XLA Ops:
  0.6 3.9 %collective-permute-start = (bf16[256,1024]{1,0:T(8,128)(2,1)}, bf16[256,1024]{1,0:T(8,128)(2,1)S(1)}, u32[]{:S(2)}, u32[]{:S(2)}) collective-permute-start(bf16[256,1024]{1,0:T(8,128)(2,1)} %bitcast.22), channel_id=1, source_target_pairs={{0,1},{1,2},{2,3},{3,4},{4,5},{5,6},{6,7},{7,8},{8,9},{9,10},{10,1... | collective-permute-start | bytes 1572872 | tf_op jit(solution)/shard_map/ppermute | solution.py:731
  4.6 1.3 collective-permute-start.1
  5.9 1.4 %fusion.2 = (s32[1]{0:T(128)}, s32[1]{0:T(128)}, s32[1]{0:T(128)}) fusion(s32[32]{0:T(128)} %param.7, s32[]{:T(128)S(6)} %max.3, s32[]{:T(128)S(6)} %select_n.19, s32[]{:T(128)S(6)} %select_n.18), kind=kLoop, calls=%fused_computation.8 | loop fusion | bytes 36 | tf_op jit(solution)/shard_map/dynamic_slice | solution.py:735
  10.3 4.1 %shard_map.77 = (bf16[256,3072]{1,0:T(8,128)(2,1)S(1)}, bf16[1024,256]{1,0:T(8,128)(2,1)S(1)}) custom-call(bf16[256,1024]{1,0:T(8,128)(2,1)S(1)} %bitcast.24, bf16[1024,3072]{1,0:T(8,128)(2,1)} %weight_ref.5), custom_call_target="tpu_custom_call" | custom-call | flops 2147483648 | bytes 8388608 | tf_op jit(solution)/shard_map/pallas_call | solution.py:99
  14.5 1.5 %collective-permute-done.left_ref = bf16[256,1024]{1,0:T(8,128)(2,1)S(1)} collective-permute-done((bf16[256,1024]{1,0:T(8,128)(2,1)}, bf16[256,1024]{1,0:T(8,128)(2,1)S(1)}, u32[]{:S(2)}, u32[]{:S(2)}) %collective-permute-start) | collective-permute-done | bytes 524320 | tf_op jit(solution)/shard_map/ppermute | solution.py:731
  16.0 4.3 %collective-permute-done.1.right_ref = bf16[256,1024]{1,0:T(8,128)(2,1)} collective-permute-done((bf16[256,1024]{1,0:T(8,128)(2,1)}, bf16[256,1024]{1,0:T(8,128)(2,1)}, u32[]{:S(2)}, u32[]{:S(2)}) %collective-permute-start.1) | collective-permute-done | bytes 524320 | tf_op jit(solution)/shard_map/ppermute | solution.py:732
  20.3 11.6 %shard_map.78 = (bf16[512,1024]{1,0:T(8,128)(2,1)S(1)}, bf16[768,1024]{1,0:T(8,128)(2,1)S(1)}, bf16[768,1024]{1,0:T(8,128)(2,1)S(1)}, f32[256,1024]{1,0:T(8,128)...) custom-call(s32[3]{0:T(128)S(1)} %pad_add_fusion.counts_ref, ...), custom_call_target="tpu_custom_call" | custom-call | flops 6442450944 | bytes 12582912 | tf_op jit(solution)/shard_map/pallas_call | solution.py:388
  32.0 3.1 %collective-permute-start.2 = (f32[256,128]{1,0:T(8,128)S(1)}, f32[256,128]{1,0:T(8,128)S(1)}, u32[]{:S(2)}, u32[]{:S(2)}) collective-permute-start(f32[256,128]{1,0:T(8,128)S(1)} %get-tuple-element.29.own_ref), channel_id=1, source_target_pairs={{0,64},{64,0},{1,65},{65,1},{2,66},{66,2},{3,67},{67,3},{4,68},{68... | collective-permute-start | bytes 393224 | tf_op jit(solution)/shard_map/ppermute | solution.py:746
  35.1 3.0 %shard_map.79.qhalo_ref = bf16[512,1024]{1,0:T(8,128)(2,1)S(1)} custom-call(bf16[512,1024]{1,0:T(8,128)(2,1)S(1)} %get-tuple-element.30.normed_ref, bf16[1024,3072]{1,0:T(8,128)(2,1)} %weight_ref.5), custom_call_target="tpu_custom_call" | custom-call | tf_op jit(solution)/shard_map/pallas_call | solution.py:137
  38.6 1.5 %collective-permute-done.3.others_ref = f32[2,256,128]{2,1,0:T(8,128)S(1)} collective-permute-done((f32[2,256,128]{2,1,0:T(8,128)S(1)}, f32[2,256,128]{2,1,0:T(8,128)S(1)}, u32[]{:S(2)}, u32[]{:S(2)}) %collective-permute-start.3) | collective-permute-done | bytes 262176 | tf_op jit(solution)/shard_map/ppermute | solution.py:711
  40.2 3.6 %shard_map.80 = (f32[256,128]{1,0:T(8,128)}, bf16[256,256]{1,0:T(8,128)(2,1)}, bf16[256,1024]{1,0:T(8,128)(2,1)S(1)}, bf16[1024,256]{1,0:T(8,128)(2,1)}) custom-call(s32[3]{0:T(128)S(1)} %pad_add_fusion.counts_ref, f32[256,128]{1,0:T(8,128)S(1)} %get-tuple-element.29.own_ref, f32[256,128]{1,0:T(8,128)S(1)} %collective-permute-done.2.near_ref, ...), custom_call_target="tpu_custom_call" | custom-call | tf_op jit(solution)/shard_map/pallas_call | solution.py:512
  43.8 6.1 %shard_map.81.piece_ref = bf16[1024,256]{1,0:T(8,128)(2,1)} custom-call(bf16[768,1024]{1,0:T(8,128)(2,1)S(1)} %get-tuple-element.38.kcat_ref, bf16[768,1024]{1,0:T(8,128)(2,1)S(1)} %get-tuple-element.39.vcat_ref, bf16[256,1024]{1,0:T(8,128)(2,1)S(1)} %get-tuple-element.40.grad_ref, bf16[256,256]{1,0:T(8,128)(2,1)} %get-tuple-element.44.packed_ref.own_ref, ...), custom_call_target="tpu_custom_call" | custom-call | flops 6442450944 | bytes 5242880 | tf_op jit(solution)/shard_map/pallas_call | solution.py:559
  50.5 4.3 %collective-permute-start.6 = (bf16[256,256]{1,0:T(8,128)(2,1)S(1)}, bf16[256,256]{1,0:T(8,128)(2,1)}, u32[]{:S(2)}, u32[]{:S(2)}) collective-permute-start(bf16[256,256]{1,0:T(8,128)(2,1)S(1)} %copy-done.5), channel_id=1, source_target_pairs={{0,1},{1,2},{2,3},{3,4},{4,5},{5,6},{6,7},{7,8},{8,9},{9,10},{10,1... | collective-permute-start | bytes 393224 | tf_op jit(solution)/shard_map/ppermute | solution.py:756
  56.1 1.3 collective-permute-done.6.left_ref
  57.5 4.9 %collective-permute-done.7.right_ref = bf16[256,256]{1,0:T(8,128)(2,1)} collective-permute-done((bf16[256,256]{1,0:T(8,128)(2,1)S(1)}, bf16[256,256]{1,0:T(8,128)(2,1)}, u32[]{:S(2)}, u32[]{:S(2)}) %collective-permute-start.7) | collective-permute-done | bytes 131104 | tf_op jit(solution)/shard_map/ppermute | solution.py:757
  62.3 3.1 %shard_map.82 = bf16[512,1280]{1,0:T(8,128)(2,1)} custom-call(s32[1]{0:T(128)} %bitcast.7.core_ref, bf16[2,2,256,256]{3,2,1,0:T(8,128)(2,1)S(1)} %bitcast.18, bf16[2,2,256,256]{3,2,1,0:T(8,128)(2,1)} %bitcast.9.normed_other_ref, bf16[1024,256]{1,0:T(8,128)(2,1)} %shard_map.81.piece_ref, bf16[1024,256]{1,0:T(8,128)(2,1)} %collective-permute-done.5.other_ref, ...), custom_call_target="tpu_custom_call" | custom-call | tf_op jit(solution)/shard_map/pallas_call | solution.py:217
  65.5 13.7 %all-to-all-start = ((bf16[64,8,1280]{2,1,0:T(8,128)(2,1)}), bf16[64,8,1280]{2,1,0:T(8,128)(2,1)}, u32[]{:S(2)}, u32[]{:S(2)}) async-start(bf16[64,8,1280]{2,1,0:T(8,128)(2,1)} %bitcast.13), calls=%async_computation | async-start | bytes 2621440 | tf_op jit(solution)/shard_map/all_to_all | solution.py:716
  79.2 10.4 %shard_map.83 = bf16[2,1024,256]{2,1,0:T(8,128)(2,1)S(1)} custom-call(s32[3]{0:T(128)S(1)} %pad_add_fusion.counts_ref, bf16[256,3072]{1,0:T(8,128)(2,1)S(1)} %get-tuple-element.28.q_ref.k_ref.v_ref, bf16[256,3072]{1,0:T(8,128)(2,1)S(1)} %get-tuple-element.28.q_ref.k_ref.v_ref, bf16[256,3072]{1,0:T(8,128)(2,1)S(1)} %get-tuple-element.28.q_ref.k_ref.v_ref, ...), custom_call_target="tpu_custom_call" | custom-call | tf_op jit(solution)/shard_map/pallas_call | solution.py:663
  89.6 2.6 %collective-permute-done.9.other_ref = bf16[2048,256]{1,0:T(8,128)(2,1)S(1)} collective-permute-done((bf16[2048,256]{1,0:T(8,128)(2,1)S(1)}, bf16[2048,256]{1,0:T(8,128)(2,1)S(1)}, u32[]{:S(2)}, u32[]{:S(2)}) %collective-permute-start.9) | collective-permute-done | bytes 1048608 | tf_op jit(solution)/shard_map/ppermute | solution.py:711
  92.3 3.8 %shard_map.84 = bf16[512,2048]{1,0:T(8,128)(2,1)} custom-call(s32[1]{0:T(128)} %bitcast.7.core_ref, bf16[2,2,256,256]{3,2,1,0:T(8,128)(2,1)S(1)} %bitcast.19, bf16[2,2,256,256]{3,2,1,0:T(8,128)(2,1)} %bitcast.9.normed_other_ref, bf16[2048,256]{1,0:T(8,128)(2,1)S(1)} %bitcast.17, bf16[2048,256]{1,0:T(8,128)(2,1)S(1)} %collective-permute-done.9.other_ref), custom_call_target="tpu_custom_call" | custom-call | tf_op jit(solution)/shard_map/pallas_call | solution.py:217
  96.1 3.9 %all-to-all-done = bf16[64,8,1280]{2,1,0:T(8,128)(2,1)} async-done(((bf16[64,8,1280]{2,1,0:T(8,128)(2,1)}), bf16[64,8,1280]{2,1,0:T(8,128)(2,1)}, u32[]{:S(2)}, u32[]{:S(2)}) %all-to-all-start) | async-done | bytes 1310752 | tf_op jit(solution)/shard_map/all_to_all | solution.py:716
  100.0 6.4 %all-to-all-start.1 = ((bf16[64,8,2048]{2,1,0:T(8,128)(2,1)}), bf16[64,8,2048]{2,1,0:T(8,128)(2,1)S(1)}, u32[]{:S(2)}, u32[]{:S(2)}) async-start(bf16[64,8,2048]{2,1,0:T(8,128)(2,1)} %bitcast.14), calls=%async_computation.1 | async-start | bytes 4194304 | tf_op jit(solution)/shard_map/all_to_all | solution.py:716
  107.3 1.5 %convert_reduce_fusion.1 = f32[8,1280]{1,0:T(8,128)S(1)} fusion(bf16[64,8,1280]{2,1,0:T(8,128)(2,1)} %all-to-all-done), kind=kLoop, calls=%fused_computation.1 | loop fusion | flops 1300480 | bytes 1351680 | tf_op jit(solution)/shard_map/reduce_sum | solution.py:720
  109.1 27.3 %all-to-all-done.1 = bf16[64,8,2048]{2,1,0:T(8,128)(2,1)S(1)} async-done(((bf16[64,8,2048]{2,1,0:T(8,128)(2,1)}), bf16[64,8,2048]{2,1,0:T(8,128)(2,1)S(1)}, u32[]{:S(2)}, u32[]{:S(2)}) %all-to-all-start.1) | async-done | bytes 2097184 | tf_op jit(solution)/shard_map/all_to_all | solution.py:716
  (33 shorter events, 6.4 us)
Async XLA Ops:
  0.6 15.4 %collective-permute-start = (bf16[256,1024]{1,0:T(8,128)(2,1)}, bf16[256,1024]{1,0:T(8,128)(2,1)S(1)}, u32[]{:S(2)}, u32[]{:S(2)}) collective-permute-start(bf16[256,1024]{1,0:T(8,128)(2,1)} %bitcast.22), channel_id=1, source_target_pairs={{0,1},{1,2},{2,3},{3,4},{4,5},{5,6},{6,7},{7,8},{8,9},{9,10},{10,1... | collective-permute-start | bytes 1572872 | tf_op jit(solution)/shard_map/ppermute | solution.py:731
  4.6 15.8 %collective-permute-start.1 = (bf16[256,1024]{1,0:T(8,128)(2,1)}, bf16[256,1024]{1,0:T(8,128)(2,1)}, u32[]{:S(2)}, u32[]{:S(2)}) collective-permute-start(bf16[256,1024]{1,0:T(8,128)(2,1)} %bitcast.23), channel_id=1, source_target_pairs={{1,0},{2,1},{3,2},{4,3},{5,4},{6,5},{7,6},{8,7},{9,8},{10,9},{11,1... | collective-permute-start | bytes 1572872 | tf_op jit(solution)/shard_map/ppermute | solution.py:732
  9.3 1.0 copy-start.4
  10.3 10.0 %copy-start = (bf16[1024,1024]{1,0:T(8,128)(2,1)S(1)}, bf16[1024,1024]{1,0:T(8,128)(2,1)}, u32[]{:S(2)}) copy-start(bf16[1024,1024]{1,0:T(8,128)(2,1)} %w_out_ref.5) | copy-start | bytes 6291460
  10.3 10.0 %copy-start.1 = (bf16[1024,128]{1,0:T(8,128)(2,1)S(1)}, bf16[1024,128]{1,0:T(8,128)(2,1)}, u32[]{:S(2)}) copy-start(bf16[1024,128]{1,0:T(8,128)(2,1)} %readout_ref.5) | copy-start | bytes 786436
  32.0 6.6 %collective-permute-start.2 = (f32[256,128]{1,0:T(8,128)S(1)}, f32[256,128]{1,0:T(8,128)S(1)}, u32[]{:S(2)}, u32[]{:S(2)}) collective-permute-start(f32[256,128]{1,0:T(8,128)S(1)} %get-tuple-element.29.own_ref), channel_id=1, source_target_pairs={{0,64},{64,0},{1,65},{65,1},{2,66},{66,2},{3,67},{67,3},{4,68},{68... | collective-permute-start | bytes 393224 | tf_op jit(solution)/shard_map/ppermute | solution.py:746
  35.1 5.1 %copy-start.3 = (f32[256,128]{1,0:T(8,128)S(1)}, f32[256,128]{1,0:T(8,128)}, u32[]{:S(2)}) copy-start(f32[256,128]{1,0:T(8,128)} %target_ref.1) | copy-start | bytes 393220
  38.5 1.6 %collective-permute-start.3 = (f32[2,256,128]{2,1,0:T(8,128)S(1)}, f32[2,256,128]{2,1,0:T(8,128)S(1)}, u32[]{:S(2)}, u32[]{:S(2)}) collective-permute-start(f32[2,256,128]{2,1,0:T(8,128)S(1)} %pad_maximum_fusion), channel_id=1, source_target_pairs={{0,32},{32,0},{1,33},{33,1},{2,34},{34,2},{3,35},{35,3},{4,36},{36... | collective-permute-start | bytes 786440 | tf_op jit(solution)/shard_map/ppermute | solution.py:711
  43.8 6.2 %copy-start.2 = (bf16[256,1024]{1,0:T(8,128)(2,1)}, bf16[256,1024]{1,0:T(8,128)(2,1)S(1)}, u32[]{:S(2)}) copy-start(bf16[256,1024]{1,0:T(8,128)(2,1)S(1)} %get-tuple-element.40.grad_ref) | copy-start | bytes 1572868
  43.8 6.8 %copy-start.5 = (bf16[256,256]{1,0:T(8,128)(2,1)S(1)}, bf16[256,256]{1,0:T(8,128)(2,1)}, u32[]{:S(2)}) copy-start(bf16[256,256]{1,0:T(8,128)(2,1)} %get-tuple-element.44.packed_ref.own_ref) | copy-start | bytes 393220
  49.9 12.4 %collective-permute-start.5 = (bf16[1024,256]{1,0:T(8,128)(2,1)}, bf16[1024,256]{1,0:T(8,128)(2,1)}, u32[]{:S(2)}, u32[]{:S(2)}) collective-permute-start(bf16[1024,256]{1,0:T(8,128)(2,1)} %shard_map.81.piece_ref), channel_id=1, source_target_pairs={{0,32},{32,0},{1,33},{33,1},{2,34},{34,2},{3,35},{35,3},{4,36},{36... | collective-permute-start | bytes 1572872 | tf_op jit(solution)/shard_map/ppermute | solution.py:711
  50.0 12.3 %collective-permute-start.4 = (bf16[1024,256]{1,0:T(8,128)(2,1)S(1)}, bf16[1024,256]{1,0:T(8,128)(2,1)}, u32[]{:S(2)}, u32[]{:S(2)}) collective-permute-start(bf16[1024,256]{1,0:T(8,128)(2,1)S(1)} %get-tuple-element.36), channel_id=1, source_target_pairs={{0,32},{32,0},{1,33},{33,1},{2,34},{34,2},{3,35},{35,3},{4,36},{36... | collective-permute-start | bytes 1572872 | tf_op jit(solution)/shard_map/ppermute | solution.py:711
  50.4 11.9 %collective-permute-start.8 = (bf16[1024,256]{1,0:T(8,128)(2,1)}, bf16[1024,256]{1,0:T(8,128)(2,1)}, u32[]{:S(2)}, u32[]{:S(2)}) collective-permute-start(bf16[1024,256]{1,0:T(8,128)(2,1)} %get-tuple-element.46), channel_id=1, source_target_pairs={{0,32},{32,0},{1,33},{33,1},{2,34},{34,2},{3,35},{35,3},{4,36},{36... | collective-permute-start | bytes 1572872 | tf_op jit(solution)/shard_map/ppermute | solution.py:711
  50.5 6.9 %collective-permute-start.6 = (bf16[256,256]{1,0:T(8,128)(2,1)S(1)}, bf16[256,256]{1,0:T(8,128)(2,1)}, u32[]{:S(2)}, u32[]{:S(2)}) collective-permute-start(bf16[256,256]{1,0:T(8,128)(2,1)S(1)} %copy-done.5), channel_id=1, source_target_pairs={{0,1},{1,2},{2,3},{3,4},{4,5},{5,6},{6,7},{7,8},{8,9},{9,10},{10,1... | collective-permute-start | bytes 393224 | tf_op jit(solution)/shard_map/ppermute | solution.py:756
  54.9 7.5 %collective-permute-start.7 = (bf16[256,256]{1,0:T(8,128)(2,1)S(1)}, bf16[256,256]{1,0:T(8,128)(2,1)}, u32[]{:S(2)}, u32[]{:S(2)}) collective-permute-start(bf16[256,256]{1,0:T(8,128)(2,1)S(1)} %copy-done.5), channel_id=1, source_target_pairs={{1,0},{2,1},{3,2},{4,3},{5,4},{6,5},{7,6},{8,7},{9,8},{10,9},{11,1... | collective-permute-start | bytes 393224 | tf_op jit(solution)/shard_map/ppermute | solution.py:757
  65.5 34.6 %all-to-all-start = ((bf16[64,8,1280]{2,1,0:T(8,128)(2,1)}), bf16[64,8,1280]{2,1,0:T(8,128)(2,1)}, u32[]{:S(2)}, u32[]{:S(2)}) async-start(bf16[64,8,1280]{2,1,0:T(8,128)(2,1)} %bitcast.13), calls=%async_computation | async-start | bytes 2621440 | tf_op jit(solution)/shard_map/all_to_all | solution.py:716
  89.5 2.7 %collective-permute-start.9 = (bf16[2048,256]{1,0:T(8,128)(2,1)S(1)}, bf16[2048,256]{1,0:T(8,128)(2,1)S(1)}, u32[]{:S(2)}, u32[]{:S(2)}) collective-permute-start(bf16[2048,256]{1,0:T(8,128)(2,1)S(1)} %bitcast.16), channel_id=1, source_target_pairs={{0,32},{32,0},{1,33},{33,1},{2,34},{34,2},{3,35},{35,3},{4,36},{36... | collective-permute-start | bytes 3145736 | tf_op jit(solution)/shard_map/ppermute | solution.py:711
  100.0 6.4 %copy-start.6 = (f32[256,128]{1,0:T(8,128)S(1)}, f32[256,128]{1,0:T(8,128)}, u32[]{:S(2)}) copy-start(f32[256,128]{1,0:T(8,128)} %get-tuple-element.35) | copy-start | bytes 393220
  100.0 36.4 %all-to-all-start.1 = ((bf16[64,8,2048]{2,1,0:T(8,128)(2,1)}), bf16[64,8,2048]{2,1,0:T(8,128)(2,1)S(1)}, u32[]{:S(2)}, u32[]{:S(2)}) async-start(bf16[64,8,2048]{2,1,0:T(8,128)(2,1)} %bitcast.14), calls=%async_computation.1 | async-start | bytes 4194304 | tf_op jit(solution)/shard_map/all_to_all | solution.py:716

commit v12 on v9

--- a/solution.py
+++ b/solution.py
@@ -458,6 +458,7 @@
     readout_ref,
     crps_ref,
     packed_ref,
+    sent_ref,
     grad_ref,
     small_ref,
 ):
@@ -503,6 +504,7 @@
         terms += dot_nn(term, shift.astype(BF))
     packed_ref[:, :128] = slope
     packed_ref[:, 128:] = terms.astype(BF)
+    sent_ref[...] = packed_ref[...]
     small_ref[:, :128] = dot_tn(attended.astype(BF), slope).astype(BF)
     small_ref[:, 128:] = dot_tn(hidden_ref[...], slope).astype(BF)
 
@@ -512,10 +514,11 @@
     return pl.pallas_call(
         score_kernel,
         in_specs=[pl.BlockSpec(memory_space=pltpu.SMEM)] + [vmem] * 9,
-        out_specs=[vmem] * 4,
+        out_specs=[vmem] * 5,
         out_shape=[
-            jax.ShapeDtypeStruct((BLOCK, 128), F32),
+            pltpu.HBM((BLOCK, 128), F32),
             jax.ShapeDtypeStruct((BLOCK, 256), BF),
+            pltpu.HBM((BLOCK, 256), BF),
             jax.ShapeDtypeStruct((BLOCK, 1024), BF),
             jax.ShapeDtypeStruct((1024, 256), BF),
         ],
@@ -747,12 +750,12 @@
     qhalo = halo_queries(normed_halo, w_qkv)
     near, qhalo = lax.optimization_barrier((near, qhalo))
     others = swap_core(jnp.stack([forecast, near]))
-    crps_whole, packed, grad, small = score(
+    crps_whole, packed, sent, grad, small = score(
         scalars, forecast, near, others, target, attended, hidden, stats, w_out, readout_weight
     )
     crps = lax.dynamic_slice_in_dim(crps_whole, member_index * 32, 32, 1)
-    packed_left = lax.ppermute(packed, CELLS, up)
-    packed_right = lax.ppermute(packed, CELLS, down)
+    packed_left = lax.ppermute(sent, CELLS, up)
+    packed_right = lax.ppermute(sent, CELLS, down)
 
     dquery = query_grads(kcat, vcat, grad, packed, probs, inverse)
     dquery, packed_left, packed_right = lax.optimization_barrier(

time: 134 us -> 134 us (level)
    unnamed x19 -> x17, local copies, waits for them, and re-layouts: 3.25 us -> 3.08 us
  transfers between devices with their start and end apart: 12 -> 12, of which waited for: 9 -> 8; matrix products, arithmetic and copies ran while one was open for 3% -> 4% of each run, Pallas kernels for 23% -> 23%
where the time goes in v12:
time: 134 us; the launch traced here: 133 us
  Pallas kernels  44.9 us (34%)
  waiting for transfers between devices  43.7 us (33%)
  starting transfers between devices  34.5 us (26%)
  local copies, waits for them, and re-layouts  4.6 us (3%)
  other arithmetic  3.21 us (2%)
  between operations  2.13 us (2%)
    all_to_all x2, waiting for transfers between devices, scatter(): lax.all_to_all(partial.reshape(64, 8, columns), CHIPS, split_axis=0, conc...  31.9 us
    all_to_all x2, starting transfers between devices, scatter(): lax.all_to_all(partial.reshape(64, 8, columns), CHIPS, split_axis=0, conc...  20 us
    pallas_call x1, Pallas kernels, forward(): pl.pallas_call(forward_kernel, grid=(4,), in_specs=[pl.BlockSpec(memory_s...  11.6 us
    pallas_call x1, Pallas kernels, key_grads(): pl.pallas_call(key_kernel, grid=(4,), in_specs=[pl.BlockSpec(memory_space...  10.3 us
    pallas_call x2, Pallas kernels, partial_sums(): pl.pallas_call(functools.partial(partial_kernel, len(smalls)), in_specs=[...  6.94 us
    ppermute x5, waiting for transfers between devices, swap_core(): return lax.ppermute(values, 'core', SWAP)  5.55 us
    pallas_call x1, Pallas kernels, query_grads(): pl.pallas_call(query_kernel, grid=(4,), in_specs=[part(window, 0), part(w...  5.29 us
    ppermute x1, waiting for transfers between devices, per_device(): from_right = lax.ppermute(latent_own, CELLS, down)  4.3 us
  transfers between devices with their start and end apart: 12, of which 8 were waited for; matrix products, arithmetic and copies ran while one was open for 4% of the time, Pallas kernels for 23%

profile of v12, /device:TPU:0, one launch (start us, length us, event | category | flops | bytes accessed | tf_op | source)
XLA Modules:
  0.0 133.4 jit_solution(3860170973261635734)
XLA Ops:
  0.6 3.9 %collective-permute-start = (bf16[256,1024]{1,0:T(8,128)(2,1)}, bf16[256,1024]{1,0:T(8,128)(2,1)S(1)}, u32[]{:S(2)}, u32[]{:S(2)}) collective-permute-start(bf16[256,1024]{1,0:T(8,128)(2,1)} %bitcast.22), channel_id=1, source_target_pairs={{0,1},{1,2},{2,3},{3,4},{4,5},{5,6},{6,7},{7,8},{8,9},{9,10},{10,1... | collective-permute-start | bytes 1572872 | tf_op jit(solution)/shard_map/ppermute | solution.py:734
  4.6 1.3 collective-permute-start.1
  5.9 1.4 %fusion.2 = (s32[1]{0:T(128)}, s32[1]{0:T(128)}, s32[1]{0:T(128)}) fusion(s32[32]{0:T(128)} %param.7, s32[]{:T(128)S(6)} %max.3, s32[]{:T(128)S(6)} %select_n.19, s32[]{:T(128)S(6)} %select_n.18), kind=kLoop, calls=%fused_computation.8 | loop fusion | bytes 36 | tf_op jit(solution)/shard_map/dynamic_slice | solution.py:738
  9.3 1.0 copy-done.4
  10.4 4.1 %shard_map.77 = (bf16[256,3072]{1,0:T(8,128)(2,1)S(1)}, bf16[1024,256]{1,0:T(8,128)(2,1)S(1)}) custom-call(bf16[256,1024]{1,0:T(8,128)(2,1)S(1)} %bitcast.24, bf16[1024,3072]{1,0:T(8,128)(2,1)} %weight_ref.5), custom_call_target="tpu_custom_call" | custom-call | flops 2147483648 | bytes 8388608 | tf_op jit(solution)/shard_map/pallas_call | solution.py:99
  14.5 1.5 %collective-permute-done.left_ref = bf16[256,1024]{1,0:T(8,128)(2,1)S(1)} collective-permute-done((bf16[256,1024]{1,0:T(8,128)(2,1)}, bf16[256,1024]{1,0:T(8,128)(2,1)S(1)}, u32[]{:S(2)}, u32[]{:S(2)}) %collective-permute-start) | collective-permute-done | bytes 524320 | tf_op jit(solution)/shard_map/ppermute | solution.py:734
  16.0 4.3 %collective-permute-done.1.right_ref = bf16[256,1024]{1,0:T(8,128)(2,1)} collective-permute-done((bf16[256,1024]{1,0:T(8,128)(2,1)}, bf16[256,1024]{1,0:T(8,128)(2,1)}, u32[]{:S(2)}, u32[]{:S(2)}) %collective-permute-start.1) | collective-permute-done | bytes 524320 | tf_op jit(solution)/shard_map/ppermute | solution.py:735
  20.3 11.6 %shard_map.78 = (bf16[512,1024]{1,0:T(8,128)(2,1)S(1)}, bf16[768,1024]{1,0:T(8,128)(2,1)S(1)}, bf16[768,1024]{1,0:T(8,128)(2,1)S(1)}, f32[256,1024]{1,0:T(8,128)...) custom-call(s32[3]{0:T(128)S(1)} %pad_add_fusion.counts_ref, ...), custom_call_target="tpu_custom_call" | custom-call | flops 6442450944 | bytes 12582912 | tf_op jit(solution)/shard_map/pallas_call | solution.py:388
  32.0 3.1 %collective-permute-start.2 = (f32[256,128]{1,0:T(8,128)S(1)}, f32[256,128]{1,0:T(8,128)S(1)}, u32[]{:S(2)}, u32[]{:S(2)}) collective-permute-start(f32[256,128]{1,0:T(8,128)S(1)} %get-tuple-element.28.own_ref), channel_id=1, source_target_pairs={{0,64},{64,0},{1,65},{65,1},{2,66},{66,2},{3,67},{67,3},{4,68},{68... | collective-permute-start | bytes 393224 | tf_op jit(solution)/shard_map/ppermute | solution.py:749
  35.1 3.0 %shard_map.79.qhalo_ref = bf16[512,1024]{1,0:T(8,128)(2,1)S(1)} custom-call(bf16[512,1024]{1,0:T(8,128)(2,1)S(1)} %get-tuple-element.29.normed_ref, bf16[1024,3072]{1,0:T(8,128)(2,1)} %weight_ref.5), custom_call_target="tpu_custom_call" | custom-call | tf_op jit(solution)/shard_map/pallas_call | solution.py:137
  40.2 3.6 %shard_map.80 = (f32[256,128]{1,0:T(8,128)}, bf16[256,256]{1,0:T(8,128)(2,1)S(1)}, bf16[256,256]{1,0:T(8,128)(2,1)}, bf16[256,1024]{1,0:T(8,128)(2,1)S(1)}, bf16[1024,256]{1,0:T(8,128)(2,1)}) custom-call(s32[3]{0:T(128)S(1)} %pad_add_fusion.counts_ref, f32[256,128]{1,0:T(8,128)S(1)} %get-tuple-element.28.own_ref, ...), custom_call_target="tpu_custom_call" | custom-call | tf_op jit(solution)/shard_map/pallas_call | solution.py:514
  43.8 3.6 %collective-permute-start.5 = (bf16[256,256]{1,0:T(8,128)(2,1)}, bf16[256,256]{1,0:T(8,128)(2,1)S(1)}, u32[]{:S(2)}, u32[]{:S(2)}) collective-permute-start(bf16[256,256]{1,0:T(8,128)(2,1)} %get-tuple-element.42), channel_id=1, source_target_pairs={{0,1},{1,2},{2,3},{3,4},{4,5},{5,6},{6,7},{7,8},{8,9},{9,10},{10,1... | collective-permute-start | bytes 393224 | tf_op jit(solution)/shard_map/ppermute | solution.py:757
  47.4 1.3 collective-permute-start.6
  48.8 5.3 %shard_map.81.piece_ref = bf16[1024,256]{1,0:T(8,128)(2,1)} custom-call(bf16[768,1024]{1,0:T(8,128)(2,1)S(1)} %get-tuple-element.36.kcat_ref, bf16[768,1024]{1,0:T(8,128)(2,1)S(1)} %get-tuple-element.37.vcat_ref, bf16[256,1024]{1,0:T(8,128)(2,1)S(1)} %get-tuple-element.38.grad_ref, bf16[256,256]{1,0:T(8,128)(2,1)S(1)} %get-tuple-element.39.packed_ref.own_ref, ...), custom_call_target="tpu_custom_call" | custom-call | flops 6442450944 | bytes 5242880 | tf_op jit(solution)/shard_map/pallas_call | solution.py:562
  55.9 1.9 %collective-permute-done.7.other_ref = bf16[1024,256]{1,0:T(8,128)(2,1)} collective-permute-done((bf16[1024,256]{1,0:T(8,128)(2,1)}, bf16[1024,256]{1,0:T(8,128)(2,1)}, u32[]{:S(2)}, u32[]{:S(2)}) %collective-permute-start.7) | collective-permute-done | bytes 524320 | tf_op jit(solution)/shard_map/ppermute | solution.py:714
  57.8 3.1 %shard_map.82 = bf16[512,1280]{1,0:T(8,128)(2,1)} custom-call(s32[1]{0:T(128)} %bitcast.7.core_ref, bf16[2,2,256,256]{3,2,1,0:T(8,128)(2,1)S(1)} %bitcast.18, bf16[2,2,256,256]{3,2,1,0:T(8,128)(2,1)} %bitcast.9.normed_other_ref, bf16[1024,256]{1,0:T(8,128)(2,1)} %shard_map.81.piece_ref, bf16[1024,256]{1,0:T(8,128)(2,1)} %collective-permute-done.7.other_ref, ...), custom_call_target="tpu_custom_call" | custom-call | tf_op jit(solution)/shard_map/pallas_call | solution.py:217
  60.9 14.2 %all-to-all-start = ((bf16[64,8,1280]{2,1,0:T(8,128)(2,1)}), bf16[64,8,1280]{2,1,0:T(8,128)(2,1)}, u32[]{:S(2)}, u32[]{:S(2)}) async-start(bf16[64,8,1280]{2,1,0:T(8,128)(2,1)} %bitcast.13), calls=%async_computation | async-start | bytes 2621440 | tf_op jit(solution)/shard_map/all_to_all | solution.py:719
  75.2 10.3 %shard_map.83 = bf16[2,1024,256]{2,1,0:T(8,128)(2,1)S(1)} custom-call(s32[3]{0:T(128)S(1)} %pad_add_fusion.counts_ref, bf16[256,3072]{1,0:T(8,128)(2,1)S(1)} %get-tuple-element.27.q_ref.k_ref.v_ref, bf16[256,3072]{1,0:T(8,128)(2,1)S(1)} %get-tuple-element.27.q_ref.k_ref.v_ref, bf16[256,3072]{1,0:T(8,128)(2,1)S(1)} %get-tuple-element.27.q_ref.k_ref.v_ref, ...), custom_call_target="tpu_custom_call" | custom-call | tf_op jit(solution)/shard_map/pallas_call | solution.py:666
  85.6 2.6 %collective-permute-done.9.other_ref = bf16[2048,256]{1,0:T(8,128)(2,1)S(1)} collective-permute-done((bf16[2048,256]{1,0:T(8,128)(2,1)S(1)}, bf16[2048,256]{1,0:T(8,128)(2,1)S(1)}, u32[]{:S(2)}, u32[]{:S(2)}) %collective-permute-start.9) | collective-permute-done | bytes 1048608 | tf_op jit(solution)/shard_map/ppermute | solution.py:714
  88.2 3.8 %shard_map.84 = bf16[512,2048]{1,0:T(8,128)(2,1)} custom-call(s32[1]{0:T(128)} %bitcast.7.core_ref, bf16[2,2,256,256]{3,2,1,0:T(8,128)(2,1)S(1)} %bitcast.19, bf16[2,2,256,256]{3,2,1,0:T(8,128)(2,1)} %bitcast.9.normed_other_ref, bf16[2048,256]{1,0:T(8,128)(2,1)S(1)} %bitcast.17, bf16[2048,256]{1,0:T(8,128)(2,1)S(1)} %collective-permute-done.9.other_ref), custom_call_target="tpu_custom_call" | custom-call | tf_op jit(solution)/shard_map/pallas_call | solution.py:217
  92.1 4.6 %all-to-all-done = bf16[64,8,1280]{2,1,0:T(8,128)(2,1)} async-done(((bf16[64,8,1280]{2,1,0:T(8,128)(2,1)}), bf16[64,8,1280]{2,1,0:T(8,128)(2,1)}, u32[]{:S(2)}, u32[]{:S(2)}) %all-to-all-start) | async-done | bytes 1310752 | tf_op jit(solution)/shard_map/all_to_all | solution.py:719
  96.6 5.8 %all-to-all-start.1 = ((bf16[64,8,2048]{2,1,0:T(8,128)(2,1)}), bf16[64,8,2048]{2,1,0:T(8,128)(2,1)S(1)}, u32[]{:S(2)}, u32[]{:S(2)}) async-start(bf16[64,8,2048]{2,1,0:T(8,128)(2,1)} %bitcast.14), calls=%async_computation.1 | async-start | bytes 4194304 | tf_op jit(solution)/shard_map/all_to_all | solution.py:719
  103.2 1.5 %convert_reduce_fusion.1 = f32[8,1280]{1,0:T(8,128)S(1)} fusion(bf16[64,8,1280]{2,1,0:T(8,128)(2,1)} %all-to-all-done), kind=kLoop, calls=%fused_computation.1 | loop fusion | flops 1300480 | bytes 1351680 | tf_op jit(solution)/shard_map/reduce_sum | solution.py:723
  105.0 27.3 %all-to-all-done.1 = bf16[64,8,2048]{2,1,0:T(8,128)(2,1)S(1)} async-done(((bf16[64,8,2048]{2,1,0:T(8,128)(2,1)}), bf16[64,8,2048]{2,1,0:T(8,128)(2,1)S(1)}, u32[]{:S(2)}, u32[]{:S(2)}) %all-to-all-start.1) | async-done | bytes 2097184 | tf_op jit(solution)/shard_map/all_to_all | solution.py:719
  (35 shorter events, 6.9 us)
Async XLA Ops:
  0.6 15.4 %collective-permute-start = (bf16[256,1024]{1,0:T(8,128)(2,1)}, bf16[256,1024]{1,0:T(8,128)(2,1)S(1)}, u32[]{:S(2)}, u32[]{:S(2)}) collective-permute-start(bf16[256,1024]{1,0:T(8,128)(2,1)} %bitcast.22), channel_id=1, source_target_pairs={{0,1},{1,2},{2,3},{3,4},{4,5},{5,6},{6,7},{7,8},{8,9},{9,10},{10,1... | collective-permute-start | bytes 1572872 | tf_op jit(solution)/shard_map/ppermute | solution.py:734
  4.6 15.8 %collective-permute-start.1 = (bf16[256,1024]{1,0:T(8,128)(2,1)}, bf16[256,1024]{1,0:T(8,128)(2,1)}, u32[]{:S(2)}, u32[]{:S(2)}) collective-permute-start(bf16[256,1024]{1,0:T(8,128)(2,1)} %bitcast.23), channel_id=1, source_target_pairs={{1,0},{2,1},{3,2},{4,3},{5,4},{6,5},{7,6},{8,7},{9,8},{10,9},{11,1... | collective-permute-start | bytes 1572872 | tf_op jit(solution)/shard_map/ppermute | solution.py:735
  9.3 1.0 copy-start.4
  10.3 10.0 %copy-start = (bf16[1024,1024]{1,0:T(8,128)(2,1)S(1)}, bf16[1024,1024]{1,0:T(8,128)(2,1)}, u32[]{:S(2)}) copy-start(bf16[1024,1024]{1,0:T(8,128)(2,1)} %w_out_ref.5) | copy-start | bytes 6291460
  10.4 10.0 %copy-start.1 = (bf16[1024,128]{1,0:T(8,128)(2,1)S(1)}, bf16[1024,128]{1,0:T(8,128)(2,1)}, u32[]{:S(2)}) copy-start(bf16[1024,128]{1,0:T(8,128)(2,1)} %readout_ref.5) | copy-start | bytes 786436
  32.0 6.6 %collective-permute-start.2 = (f32[256,128]{1,0:T(8,128)S(1)}, f32[256,128]{1,0:T(8,128)S(1)}, u32[]{:S(2)}, u32[]{:S(2)}) collective-permute-start(f32[256,128]{1,0:T(8,128)S(1)} %get-tuple-element.28.own_ref), channel_id=1, source_target_pairs={{0,64},{64,0},{1,65},{65,1},{2,66},{66,2},{3,67},{67,3},{4,68},{68... | collective-permute-start | bytes 393224 | tf_op jit(solution)/shard_map/ppermute | solution.py:749
  35.1 5.1 %copy-start.3 = (f32[256,128]{1,0:T(8,128)S(1)}, f32[256,128]{1,0:T(8,128)}, u32[]{:S(2)}) copy-start(f32[256,128]{1,0:T(8,128)} %target_ref.1) | copy-start | bytes 393220
  38.5 1.6 %collective-permute-start.3 = (f32[2,256,128]{2,1,0:T(8,128)S(1)}, f32[2,256,128]{2,1,0:T(8,128)S(1)}, u32[]{:S(2)}, u32[]{:S(2)}) collective-permute-start(f32[2,256,128]{2,1,0:T(8,128)S(1)} %pad_maximum_fusion), channel_id=1, source_target_pairs={{0,32},{32,0},{1,33},{33,1},{2,34},{34,2},{3,35},{35,3},{4,36},{36... | collective-permute-start | bytes 786440 | tf_op jit(solution)/shard_map/ppermute | solution.py:714
  38.6 17.3 %collective-permute-start.4 = (bf16[1024,256]{1,0:T(8,128)(2,1)S(1)}, bf16[1024,256]{1,0:T(8,128)(2,1)}, u32[]{:S(2)}, u32[]{:S(2)}) collective-permute-start(bf16[1024,256]{1,0:T(8,128)(2,1)S(1)} %get-tuple-element.35), channel_id=1, source_target_pairs={{0,32},{32,0},{1,33},{33,1},{2,34},{34,2},{3,35},{35,3},{4,36},{36... | collective-permute-start | bytes 1572872 | tf_op jit(solution)/shard_map/ppermute | solution.py:714
  43.8 10.3 %copy-start.2 = (bf16[256,1024]{1,0:T(8,128)(2,1)}, bf16[256,1024]{1,0:T(8,128)(2,1)S(1)}, u32[]{:S(2)}) copy-start(bf16[256,1024]{1,0:T(8,128)(2,1)S(1)} %get-tuple-element.38.grad_ref) | copy-start | bytes 1572868
  43.8 10.3 %collective-permute-start.5 = (bf16[256,256]{1,0:T(8,128)(2,1)}, bf16[256,256]{1,0:T(8,128)(2,1)S(1)}, u32[]{:S(2)}, u32[]{:S(2)}) collective-permute-start(bf16[256,256]{1,0:T(8,128)(2,1)} %get-tuple-element.42), channel_id=1, source_target_pairs={{0,1},{1,2},{2,3},{3,4},{4,5},{5,6},{6,7},{7,8},{8,9},{9,10},{10,1... | collective-permute-start | bytes 393224 | tf_op jit(solution)/shard_map/ppermute | solution.py:757
  47.4 7.4 %collective-permute-start.6 = (bf16[256,256]{1,0:T(8,128)(2,1)}, bf16[256,256]{1,0:T(8,128)(2,1)S(1)}, u32[]{:S(2)}, u32[]{:S(2)}) collective-permute-start(bf16[256,256]{1,0:T(8,128)(2,1)} %get-tuple-element.42), channel_id=1, source_target_pairs={{1,0},{2,1},{3,2},{4,3},{5,4},{6,5},{7,6},{8,7},{9,8},{10,9},{11,1... | collective-permute-start | bytes 393224 | tf_op jit(solution)/shard_map/ppermute | solution.py:758
  48.7 7.2 %collective-permute-start.8 = (bf16[1024,256]{1,0:T(8,128)(2,1)}, bf16[1024,256]{1,0:T(8,128)(2,1)}, u32[]{:S(2)}, u32[]{:S(2)}) collective-permute-start(bf16[1024,256]{1,0:T(8,128)(2,1)} %get-tuple-element.44), channel_id=1, source_target_pairs={{0,32},{32,0},{1,33},{33,1},{2,34},{34,2},{3,35},{35,3},{4,36},{36... | collective-permute-start | bytes 1572872 | tf_op jit(solution)/shard_map/ppermute | solution.py:714
  54.1 0.7 copy-start.5
  54.8 0.7 copy-start.6
  55.4 2.3 %collective-permute-start.7 = (bf16[1024,256]{1,0:T(8,128)(2,1)}, bf16[1024,256]{1,0:T(8,128)(2,1)}, u32[]{:S(2)}, u32[]{:S(2)}) collective-permute-start(bf16[1024,256]{1,0:T(8,128)(2,1)} %shard_map.81.piece_ref), channel_id=1, source_target_pairs={{0,32},{32,0},{1,33},{33,1},{2,34},{34,2},{3,35},{35,3},{4,36},{36... | collective-permute-start | bytes 1572872 | tf_op jit(solution)/shard_map/ppermute | solution.py:714
  60.9 35.7 %all-to-all-start = ((bf16[64,8,1280]{2,1,0:T(8,128)(2,1)}), bf16[64,8,1280]{2,1,0:T(8,128)(2,1)}, u32[]{:S(2)}, u32[]{:S(2)}) async-start(bf16[64,8,1280]{2,1,0:T(8,128)(2,1)} %bitcast.13), calls=%async_computation | async-start | bytes 2621440 | tf_op jit(solution)/shard_map/all_to_all | solution.py:719
  85.5 2.7 %collective-permute-start.9 = (bf16[2048,256]{1,0:T(8,128)(2,1)S(1)}, bf16[2048,256]{1,0:T(8,128)(2,1)S(1)}, u32[]{:S(2)}, u32[]{:S(2)}) collective-permute-start(bf16[2048,256]{1,0:T(8,128)(2,1)S(1)} %bitcast.16), channel_id=1, source_target_pairs={{0,32},{32,0},{1,33},{33,1},{2,34},{34,2},{3,35},{35,3},{4,36},{36... | collective-permute-start | bytes 3145736 | tf_op jit(solution)/shard_map/ppermute | solution.py:714
  96.6 5.8 %copy-start.7 = (f32[256,128]{1,0:T(8,128)S(1)}, f32[256,128]{1,0:T(8,128)}, u32[]{:S(2)}) copy-start(f32[256,128]{1,0:T(8,128)} %get-tuple-element.34) | copy-start | bytes 393220
  96.6 35.8 %all-to-all-start.1 = ((bf16[64,8,2048]{2,1,0:T(8,128)(2,1)}), bf16[64,8,2048]{2,1,0:T(8,128)(2,1)S(1)}, u32[]{:S(2)}, u32[]{:S(2)}) async-start(bf16[64,8,2048]{2,1,0:T(8,128)(2,1)} %bitcast.14), calls=%async_computation.1 | async-start | bytes 4194304 | tf_op jit(solution)/shard_map/all_to_all | solution.py:719

commit v13 on v12

--- a/solution.py
+++ b/solution.py
@@ -445,18 +445,47 @@
     )
 
 
+def crps_kernel(counts_ref, own_ref, near_ref, third_ref, fourth_ref, target_ref, crps_ref):
+    members = 4
+    fair_eps = (1.0 - alpha_fair) / members
+    coefficient = (1.0 - fair_eps) / (members * (members - 1))
+    valid = (iota((BLOCK, 1), 0) < counts_ref[1]).astype(F32)
+    forecasts = [own_ref[...], near_ref[...], third_ref[...], fourth_ref[...]]
+    target = target_ref[...]
+    error = jnp.zeros_like(target)
+    for forecast in forecasts:
+        error += smooth_abs(forecast - target)
+    spread = jnp.full_like(target, members * smooth_width**0.5)
+    for first in range(members):
+        for second in range(first + 1, members):
+            spread += 2.0 * smooth_abs(forecasts[first] - forecasts[second])
+    crps_ref[...] = valid * (error / members - 0.5 * coefficient * spread)
+
+
+def crps_of(counts, own, near, third, fourth, target):
+    vmem = pl.BlockSpec(memory_space=pltpu.VMEM)
+    return pl.pallas_call(
+        crps_kernel,
+        in_specs=[pl.BlockSpec(memory_space=pltpu.SMEM)] + [vmem] * 5,
+        out_specs=vmem,
+        out_shape=jax.ShapeDtypeStruct((BLOCK, 128), F32),
+        compiler_params=pltpu.CompilerParams(vmem_limit_bytes=8 * 1024 * 1024),
+        cost_estimate=FREE,
+    )(counts, own, near, third, fourth, target)
+
+
 def score_kernel(
     counts_ref,
     own_ref,
     near_ref,
-    others_ref,
+    third_ref,
+    fourth_ref,
     target_ref,
     attended_ref,
     hidden_ref,
     stats_ref,
     w_out_ref,
     readout_ref,
-    crps_ref,
     packed_ref,
     sent_ref,
     grad_ref,
@@ -467,18 +496,9 @@
     coefficient = (1.0 - fair_eps) / (members * (members - 1))
     valid = (iota((BLOCK, 1), 0) < counts_ref[1]).astype(F32)
     own = own_ref[...]
-    forecasts = [own, near_ref[...], others_ref[0], others_ref[1]]
     target = target_ref[...]
-    error = jnp.zeros_like(target)
-    for forecast in forecasts:
-        error += smooth_abs(forecast - target)
-    spread = jnp.full_like(target, members * smooth_width**0.5)
-    for first in range(members):
-        for second in range(first + 1, members):
-            spread += 2.0 * smooth_abs(forecasts[first] - forecasts[second])
-    crps_ref[...] = valid * (error / members - 0.5 * coefficient * spread)
     pull = jnp.zeros_like(target)
-    for other in forecasts[1:]:
+    for other in (near_ref[...], third_ref[...], fourth_ref[...]):
         pull += smooth_sign(own - other)
     slope = (
         valid / 128 * (smooth_sign(own - target) / members - coefficient * pull)
@@ -509,21 +529,34 @@
     small_ref[:, 128:] = dot_tn(hidden_ref[...], slope).astype(BF)
 
 
-def score(counts, own, near, others, target, attended, hidden, stats, w_out, readout_weight):
+def score(
+    counts, own, near, third, fourth, target, attended, hidden, stats, w_out, readout_weight
+):
     vmem = pl.BlockSpec(memory_space=pltpu.VMEM)
     return pl.pallas_call(
         score_kernel,
-        in_specs=[pl.BlockSpec(memory_space=pltpu.SMEM)] + [vmem] * 9,
-        out_specs=[vmem] * 5,
+        in_specs=[pl.BlockSpec(memory_space=pltpu.SMEM)] + [vmem] * 10,
+        out_specs=[vmem] * 4,
         out_shape=[
-            pltpu.HBM((BLOCK, 128), F32),
             jax.ShapeDtypeStruct((BLOCK, 256), BF),
             pltpu.HBM((BLOCK, 256), BF),
             jax.ShapeDtypeStruct((BLOCK, 1024), BF),
             jax.ShapeDtypeStruct((1024, 256), BF),
         ],
         compiler_params=pltpu.CompilerParams(vmem_limit_bytes=12 * 1024 * 1024),
-    )(counts, own, near, others, target, attended, hidden, stats, w_out, readout_weight)
+    )(
+        counts,
+        own,
+        near,
+        third,
+        fourth,
+        target,
+        attended,
+        hidden,
+        stats,
+        w_out,
+        readout_weight,
+    )
 
 
 def query_kernel(
@@ -747,13 +780,23 @@
         scalars, from_left, from_right, latent_own, w_qkv, projected, w_out, readout_weight
     )
     near = lax.ppermute(forecast, "x_hi", SWAP)
+    third = swap_core(forecast)
     qhalo = halo_queries(normed_halo, w_qkv)
-    near, qhalo = lax.optimization_barrier((near, qhalo))
-    others = swap_core(jnp.stack([forecast, near]))
-    crps_whole, packed, sent, grad, small = score(
-        scalars, forecast, near, others, target, attended, hidden, stats, w_out, readout_weight
-    )
-    crps = lax.dynamic_slice_in_dim(crps_whole, member_index * 32, 32, 1)
+    near, third, qhalo = lax.optimization_barrier((near, third, qhalo))
+    fourth = swap_core(near)
+    packed, sent, grad, small = score(
+        scalars,
+        forecast,
+        near,
+        third,
+        fourth,
+        target,
+        attended,
+        hidden,
+        stats,
+        w_out,
+        readout_weight,
+    )
     packed_left = lax.ppermute(sent, CELLS, up)
     packed_right = lax.ppermute(sent, CELLS, down)
 
@@ -781,7 +824,10 @@
     pairs = pairs.reshape(2048, BLOCK)
     second_part = partial_sums(core, turned, turned_other, pairs, swap_core(pairs))
     second_part, first = lax.optimization_barrier((second_part, first))
+    second_part, late_near = lax.optimization_barrier((second_part, near))
     second = add_up(scatter(second_part))
+    crps_whole = crps_of(scalars, forecast, late_near, third, fourth, target)
+    crps = lax.dynamic_slice_in_dim(crps_whole, member_index * 32, 32, 1)
     first = add_up(first)
     grad_out = lax.dot_general(
         first[:, 1024:1152],

time: 134 us -> 134 us (level)
  waiting for transfers between devices: 43.7 us -> 41.5 us
    all_to_all x2, waiting for transfers between devices: 31.9 us -> 29.9 us  [scatter(): lax.all_to_all(partial.reshape(64, 8, columns), CHIPS, split_axis=0, conc...]
    unnamed x17 -> x35, local copies, waits for them, and re-layouts: 3.08 us -> 3.98 us
    ppermute x5 -> x6, waiting for transfers between devices: 5.55 us -> 5.36 us  [swap_core(): return lax.ppermute(values, 'core', SWAP)]
  transfers between devices with their start and end apart: 12 -> 13, of which waited for: 8 -> 8; matrix products, arithmetic and copies ran while one was open for 4% -> 4% of each run, Pallas kernels for 23% -> 23%
where the time goes in v13:
time: 134 us
  Pallas kernels  45.5 us (34%)
  waiting for transfers between devices  41.5 us (31%)
  starting transfers between devices  35.4 us (26%)
  local copies, waits for them, and re-layouts  5.52 us (4%)
  other arithmetic  3.26 us (2%)
  between operations  2.2 us (2%)
    all_to_all x2, waiting for transfers between devices, scatter(): lax.all_to_all(partial.reshape(64, 8, columns), CHIPS, split_axis=0, conc...  29.9 us
    all_to_all x2, starting transfers between devices, scatter(): lax.all_to_all(partial.reshape(64, 8, columns), CHIPS, split_axis=0, conc...  20.9 us
    pallas_call x1, Pallas kernels, forward(): pl.pallas_call(forward_kernel, grid=(4,), in_specs=[pl.BlockSpec(memory_s...  11.6 us
    pallas_call x1, Pallas kernels, key_grads(): pl.pallas_call(key_kernel, grid=(4,), in_specs=[pl.BlockSpec(memory_space...  10.3 us
    pallas_call x2, Pallas kernels, partial_sums(): pl.pallas_call(functools.partial(partial_kernel, len(smalls)), in_specs=[...  6.96 us
    ppermute x6, waiting for transfers between devices, swap_core(): return lax.ppermute(values, 'core', SWAP)  5.36 us
    pallas_call x1, Pallas kernels, query_grads(): pl.pallas_call(query_kernel, grid=(4,), in_specs=[part(window, 0), part(w...  5.28 us
    ppermute x1, waiting for transfers between devices, per_device(): from_right = lax.ppermute(latent_own, CELLS, down)  4.3 us
  transfers between devices with their start and end apart: 13, of which 8 were waited for; matrix products, arithmetic and copies ran while one was open for 4% of the time, Pallas kernels for 23%

profile of v13, /device:TPU:0, one launch (start us, length us, event | category | flops | bytes accessed | tf_op | source)
XLA Modules:
  0.0 133.7 jit_solution(2089079223286849550)
XLA Ops:
  0.6 3.9 %collective-permute-start.1 = (bf16[256,1024]{1,0:T(8,128)(2,1)}, bf16[256,1024]{1,0:T(8,128)(2,1)S(1)}, u32[]{:S(2)}, u32[]{:S(2)}) collective-permute-start(bf16[256,1024]{1,0:T(8,128)(2,1)} %bitcast.18), channel_id=1, source_target_pairs={{0,1},{1,2},{2,3},{3,4},{4,5},{5,6},{6,7},{7,8},{8,9},{9,10},{10,1... | collective-permute-start | bytes 1572872 | tf_op jit(solution)/shard_map/ppermute | solution.py:767
  4.6 1.3 collective-permute-start.2
  5.9 1.4 %fusion.2 = (s32[1]{0:T(128)}, s32[1]{0:T(128)}, s32[1]{0:T(128)}) fusion(s32[32]{0:T(128)} %param.7, s32[]{:T(128)S(6)} %max.3, s32[]{:T(128)S(6)} %select_n.19, s32[]{:T(128)S(6)} %select_n.18), kind=kLoop, calls=%fused_computation.7 | loop fusion | bytes 36 | tf_op jit(solution)/shard_map/dynamic_slice | solution.py:771
  10.4 4.1 %shard_map.77 = (bf16[256,3072]{1,0:T(8,128)(2,1)S(1)}, bf16[1024,256]{1,0:T(8,128)(2,1)S(1)}) custom-call(bf16[256,1024]{1,0:T(8,128)(2,1)S(1)} %bitcast.20, bf16[1024,3072]{1,0:T(8,128)(2,1)} %weight_ref.5), custom_call_target="tpu_custom_call" | custom-call | flops 2147483648 | bytes 8388608 | tf_op jit(solution)/shard_map/pallas_call | solution.py:99
  14.6 1.4 %collective-permute-done.1.left_ref = bf16[256,1024]{1,0:T(8,128)(2,1)S(1)} collective-permute-done((bf16[256,1024]{1,0:T(8,128)(2,1)}, bf16[256,1024]{1,0:T(8,128)(2,1)S(1)}, u32[]{:S(2)}, u32[]{:S(2)}) %collective-permute-start.1) | collective-permute-done | bytes 524320 | tf_op jit(solution)/shard_map/ppermute | solution.py:767
  16.0 4.3 %collective-permute-done.2.right_ref = bf16[256,1024]{1,0:T(8,128)(2,1)} collective-permute-done((bf16[256,1024]{1,0:T(8,128)(2,1)}, bf16[256,1024]{1,0:T(8,128)(2,1)}, u32[]{:S(2)}, u32[]{:S(2)}) %collective-permute-start.2) | collective-permute-done | bytes 524320 | tf_op jit(solution)/shard_map/ppermute | solution.py:768
  20.3 11.6 %shard_map.78 = (bf16[512,1024]{1,0:T(8,128)(2,1)S(1)}, bf16[768,1024]{1,0:T(8,128)(2,1)S(1)}, bf16[768,1024]{1,0:T(8,128)(2,1)S(1)}, f32[256,1024]{1,0:T(8,128)...) custom-call(s32[3]{0:T(128)S(1)} %pad_add_fusion.counts_ref, ...), custom_call_target="tpu_custom_call" | custom-call | flops 6442450944 | bytes 12582912 | tf_op jit(solution)/shard_map/pallas_call | solution.py:388
  32.0 3.1 %collective-permute-start.3 = (f32[256,128]{1,0:T(8,128)S(1)}, f32[256,128]{1,0:T(8,128)S(1)}, u32[]{:S(2)}, u32[]{:S(2)}) collective-permute-start(f32[256,128]{1,0:T(8,128)S(1)} %get-tuple-element.33.own_ref), channel_id=1, source_target_pairs={{0,64},{64,0},{1,65},{65,1},{2,66},{66,2},{3,67},{67,3},{4,68},{68... | collective-permute-start | bytes 393224 | tf_op jit(solution)/shard_map/ppermute | solution.py:782
  35.1 3.0 %shard_map.79.qhalo_ref = bf16[512,1024]{1,0:T(8,128)(2,1)S(1)} custom-call(bf16[512,1024]{1,0:T(8,128)(2,1)S(1)} %get-tuple-element.34.normed_ref, bf16[1024,3072]{1,0:T(8,128)(2,1)} %weight_ref.5), custom_call_target="tpu_custom_call" | custom-call | tf_op jit(solution)/shard_map/pallas_call | solution.py:137
  40.0 3.2 %shard_map.80 = (bf16[256,256]{1,0:T(8,128)(2,1)S(1)}, bf16[256,256]{1,0:T(8,128)(2,1)}, bf16[256,1024]{1,0:T(8,128)(2,1)S(1)}, bf16[1024,256]{1,0:T(8,128)(2,1)}) custom-call(s32[3]{0:T(128)S(1)} %pad_add_fusion.counts_ref, f32[256,128]{1,0:T(8,128)S(1)} %get-tuple-element.33.own_ref, f32[256,128]{1,0:T(8,128)S(1)} %collective-permute-done.3.near_ref, ...), custom_call_target="tpu_custom_call" | custom-call | tf_op jit(solution)/shard_map/pallas_call | solution.py:536
  43.2 3.6 %collective-permute-start.6 = (bf16[256,256]{1,0:T(8,128)(2,1)}, bf16[256,256]{1,0:T(8,128)(2,1)S(1)}, u32[]{:S(2)}, u32[]{:S(2)}) collective-permute-start(bf16[256,256]{1,0:T(8,128)(2,1)} %get-tuple-element.44), channel_id=1, source_target_pairs={{0,1},{1,2},{2,3},{3,4},{4,5},{5,6},{6,7},{7,8},{8,9},{9,10},{10,1... | collective-permute-start | bytes 393224 | tf_op jit(solution)/shard_map/ppermute | solution.py:800
  46.8 1.3 collective-permute-start.7
  48.2 5.3 %shard_map.81.piece_ref = bf16[1024,256]{1,0:T(8,128)(2,1)} custom-call(bf16[768,1024]{1,0:T(8,128)(2,1)S(1)} %get-tuple-element.31.kcat_ref, bf16[768,1024]{1,0:T(8,128)(2,1)S(1)} %get-tuple-element.32.vcat_ref, bf16[256,1024]{1,0:T(8,128)(2,1)S(1)} %get-tuple-element.40.grad_ref, bf16[256,256]{1,0:T(8,128)(2,1)S(1)} %get-tuple-element.41.packed_ref.own_ref, ...), custom_call_target="tpu_custom_call" | custom-call | flops 6442450944 | bytes 5242880 | tf_op jit(solution)/shard_map/pallas_call | solution.py:595
  55.3 1.9 %collective-permute-done.8.other_ref = bf16[1024,256]{1,0:T(8,128)(2,1)} collective-permute-done((bf16[1024,256]{1,0:T(8,128)(2,1)}, bf16[1024,256]{1,0:T(8,128)(2,1)}, u32[]{:S(2)}, u32[]{:S(2)}) %collective-permute-start.8) | collective-permute-done | bytes 524320 | tf_op jit(solution)/shard_map/ppermute | solution.py:747
  57.2 3.1 %shard_map.82 = bf16[512,1280]{1,0:T(8,128)(2,1)} custom-call(s32[1]{0:T(128)} %bitcast.core_ref, bf16[2,2,256,256]{3,2,1,0:T(8,128)(2,1)S(1)} %bitcast.16, bf16[2,2,256,256]{3,2,1,0:T(8,128)(2,1)} %bitcast.3.normed_other_ref, bf16[1024,256]{1,0:T(8,128)(2,1)} %shard_map.81.piece_ref, bf16[1024,256]{1,0:T(8,128)(2,1)} %collective-permute-done.8.other_ref, ...), custom_call_target="tpu_custom_call" | custom-call | tf_op jit(solution)/shard_map/pallas_call | solution.py:217
  60.3 14.3 %all-to-all-start = ((bf16[64,8,1280]{2,1,0:T(8,128)(2,1)}), bf16[64,8,1280]{2,1,0:T(8,128)(2,1)}, u32[]{:S(2)}, u32[]{:S(2)}) async-start(bf16[64,8,1280]{2,1,0:T(8,128)(2,1)} %bitcast.11), calls=%async_computation | async-start | bytes 2621440 | tf_op jit(solution)/shard_map/all_to_all | solution.py:752
  75.5 10.3 %shard_map.83 = bf16[2,1024,256]{2,1,0:T(8,128)(2,1)S(1)} custom-call(s32[3]{0:T(128)S(1)} %pad_add_fusion.counts_ref, bf16[256,3072]{1,0:T(8,128)(2,1)S(1)} %get-tuple-element.30.q_ref.k_ref.v_ref, bf16[256,3072]{1,0:T(8,128)(2,1)S(1)} %get-tuple-element.30.q_ref.k_ref.v_ref, bf16[256,3072]{1,0:T(8,128)(2,1)S(1)} %get-tuple-element.30.q_ref.k_ref.v_ref, ...), custom_call_target="tpu_custom_call" | custom-call | tf_op jit(solution)/shard_map/pallas_call | solution.py:699
  85.9 2.6 %collective-permute-done.10.other_ref = bf16[2048,256]{1,0:T(8,128)(2,1)S(1)} collective-permute-done((bf16[2048,256]{1,0:T(8,128)(2,1)S(1)}, bf16[2048,256]{1,0:T(8,128)(2,1)S(1)}, u32[]{:S(2)}, u32[]{:S(2)}) %collective-permute-start.10) | collective-permute-done | bytes 1048608 | tf_op jit(solution)/shard_map/ppermute | solution.py:747
  88.5 3.8 %shard_map.84 = bf16[512,2048]{1,0:T(8,128)(2,1)} custom-call(s32[1]{0:T(128)} %bitcast.core_ref, bf16[2,2,256,256]{3,2,1,0:T(8,128)(2,1)S(1)} %bitcast.17, bf16[2,2,256,256]{3,2,1,0:T(8,128)(2,1)} %bitcast.3.normed_other_ref, bf16[2048,256]{1,0:T(8,128)(2,1)S(1)} %bitcast.15, bf16[2048,256]{1,0:T(8,128)(2,1)S(1)} %collective-permute-done.10.other_ref), custom_call_target="tpu_custom_call" | custom-call | tf_op jit(solution)/shard_map/pallas_call | solution.py:217
  92.4 3.7 %all-to-all-done = bf16[64,8,1280]{2,1,0:T(8,128)(2,1)} async-done(((bf16[64,8,1280]{2,1,0:T(8,128)(2,1)}), bf16[64,8,1280]{2,1,0:T(8,128)(2,1)}, u32[]{:S(2)}, u32[]{:S(2)}) %all-to-all-start) | async-done | bytes 1310752 | tf_op jit(solution)/shard_map/all_to_all | solution.py:752
  96.0 6.7 %all-to-all-start.1 = ((bf16[64,8,2048]{2,1,0:T(8,128)(2,1)}), bf16[64,8,2048]{2,1,0:T(8,128)(2,1)S(1)}, u32[]{:S(2)}, u32[]{:S(2)}) async-start(bf16[64,8,2048]{2,1,0:T(8,128)(2,1)} %bitcast.12), calls=%async_computation.1 | async-start | bytes 4194304 | tf_op jit(solution)/shard_map/all_to_all | solution.py:752
  102.7 1.5 %convert_reduce_fusion.1 = f32[8,1280]{1,0:T(8,128)S(1)} fusion(bf16[64,8,1280]{2,1,0:T(8,128)(2,1)} %all-to-all-done), kind=kLoop, calls=%fused_computation.1 | loop fusion | flops 1300480 | bytes 1351680 | tf_op jit(solution)/shard_map/reduce_sum | solution.py:756
  104.3 1.1 shard_map.85
  106.5 26.2 %all-to-all-done.1 = bf16[64,8,2048]{2,1,0:T(8,128)(2,1)S(1)} async-done(((bf16[64,8,2048]{2,1,0:T(8,128)(2,1)}), bf16[64,8,2048]{2,1,0:T(8,128)(2,1)S(1)}, u32[]{:S(2)}, u32[]{:S(2)}) %all-to-all-start.1) | async-done | bytes 2097184 | tf_op jit(solution)/shard_map/all_to_all | solution.py:752
  (55 shorter events, 8.7 us)
Async XLA Ops:
  0.6 15.4 %collective-permute-start.1 = (bf16[256,1024]{1,0:T(8,128)(2,1)}, bf16[256,1024]{1,0:T(8,128)(2,1)S(1)}, u32[]{:S(2)}, u32[]{:S(2)}) collective-permute-start(bf16[256,1024]{1,0:T(8,128)(2,1)} %bitcast.18), channel_id=1, source_target_pairs={{0,1},{1,2},{2,3},{3,4},{4,5},{5,6},{6,7},{7,8},{8,9},{9,10},{10,1... | collective-permute-start | bytes 1572872 | tf_op jit(solution)/shard_map/ppermute | solution.py:767
  4.6 15.8 %collective-permute-start.2 = (bf16[256,1024]{1,0:T(8,128)(2,1)}, bf16[256,1024]{1,0:T(8,128)(2,1)}, u32[]{:S(2)}, u32[]{:S(2)}) collective-permute-start(bf16[256,1024]{1,0:T(8,128)(2,1)} %bitcast.19), channel_id=1, source_target_pairs={{1,0},{2,1},{3,2},{4,3},{5,4},{6,5},{7,6},{8,7},{9,8},{10,9},{11,1... | collective-permute-start | bytes 1572872 | tf_op jit(solution)/shard_map/ppermute | solution.py:768
  10.4 9.9 %copy-start = (bf16[1024,1024]{1,0:T(8,128)(2,1)S(1)}, bf16[1024,1024]{1,0:T(8,128)(2,1)}, u32[]{:S(2)}) copy-start(bf16[1024,1024]{1,0:T(8,128)(2,1)} %w_out_ref.5) | copy-start | bytes 6291460
  10.4 9.9 %copy-start.1 = (bf16[1024,128]{1,0:T(8,128)(2,1)S(1)}, bf16[1024,128]{1,0:T(8,128)(2,1)}, u32[]{:S(2)}) copy-start(bf16[1024,128]{1,0:T(8,128)(2,1)} %readout_ref.5) | copy-start | bytes 786436
  32.0 8.0 %copy-start.4 = (f32[256,128]{1,0:T(8,128)}, f32[256,128]{1,0:T(8,128)S(1)}, u32[]{:S(2)}) copy-start(f32[256,128]{1,0:T(8,128)S(1)} %get-tuple-element.33.own_ref) | copy-start | bytes 393220
  32.0 6.6 %collective-permute-start.3 = (f32[256,128]{1,0:T(8,128)S(1)}, f32[256,128]{1,0:T(8,128)S(1)}, u32[]{:S(2)}, u32[]{:S(2)}) collective-permute-start(f32[256,128]{1,0:T(8,128)S(1)} %get-tuple-element.33.own_ref), channel_id=1, source_target_pairs={{0,64},{64,0},{1,65},{65,1},{2,66},{66,2},{3,67},{67,3},{4,68},{68... | collective-permute-start | bytes 393224 | tf_op jit(solution)/shard_map/ppermute | solution.py:782
  35.1 3.5 %collective-permute-start.4 = (f32[256,128]{1,0:T(8,128)S(1)}, f32[256,128]{1,0:T(8,128)S(1)}, u32[]{:S(2)}, u32[]{:S(2)}) collective-permute-start(f32[256,128]{1,0:T(8,128)S(1)} %get-tuple-element.33.own_ref), channel_id=1, source_target_pairs={{0,32},{32,0},{1,33},{33,1},{2,34},{34,2},{3,35},{35,3},{4,36},{36... | collective-permute-start | bytes 393224 | tf_op jit(solution)/shard_map/ppermute | solution.py:747
  35.1 4.9 %copy-start.3 = (f32[256,128]{1,0:T(8,128)S(1)}, f32[256,128]{1,0:T(8,128)}, u32[]{:S(2)}) copy-start(f32[256,128]{1,0:T(8,128)} %target_ref.3) | copy-start | bytes 393220
  38.5 4.6 %copy-start.6 = (f32[256,128]{1,0:T(8,128)}, f32[256,128]{1,0:T(8,128)S(1)}, u32[]{:S(2)}) copy-start(f32[256,128]{1,0:T(8,128)S(1)} %collective-permute-done.3.near_ref) | copy-start | bytes 393220
  38.5 1.4 %collective-permute-start.5 = (f32[256,128]{1,0:T(8,128)S(1)}, f32[256,128]{1,0:T(8,128)S(1)}, u32[]{:S(2)}, u32[]{:S(2)}) collective-permute-start(f32[256,128]{1,0:T(8,128)S(1)} %collective-permute-done.3.near_ref), channel_id=1, source_target_pairs={{0,32},{32,0},{1,33},{33,1},{2,34},{34,2},{3,35},{35,3},{4,36},{36... | collective-permute-start | bytes 393224 | tf_op jit(solution)/shard_map/ppermute | solution.py:747
  38.7 16.6 %collective-permute-start = (bf16[1024,256]{1,0:T(8,128)(2,1)S(1)}, bf16[1024,256]{1,0:T(8,128)(2,1)}, u32[]{:S(2)}, u32[]{:S(2)}) collective-permute-start(bf16[1024,256]{1,0:T(8,128)(2,1)S(1)} %get-tuple-element.29), channel_id=1, source_target_pairs={{0,32},{32,0},{1,33},{33,1},{2,34},{34,2},{3,35},{35,3},{4,36},{36... | collective-permute-start | bytes 1572872 | tf_op jit(solution)/shard_map/ppermute | solution.py:747
  43.2 10.3 %copy-start.2 = (bf16[256,1024]{1,0:T(8,128)(2,1)}, bf16[256,1024]{1,0:T(8,128)(2,1)S(1)}, u32[]{:S(2)}) copy-start(bf16[256,1024]{1,0:T(8,128)(2,1)S(1)} %get-tuple-element.40.grad_ref) | copy-start | bytes 1572868
  43.2 10.3 %copy-start.12 = (bf16[256,256]{1,0:T(8,128)(2,1)}, bf16[256,256]{1,0:T(8,128)(2,1)S(1)}, u32[]{:S(2)}) copy-start(bf16[256,256]{1,0:T(8,128)(2,1)S(1)} %get-tuple-element.41.packed_ref.own_ref) | copy-start | bytes 393220
  43.2 10.3 %collective-permute-start.6 = (bf16[256,256]{1,0:T(8,128)(2,1)}, bf16[256,256]{1,0:T(8,128)(2,1)S(1)}, u32[]{:S(2)}, u32[]{:S(2)}) collective-permute-start(bf16[256,256]{1,0:T(8,128)(2,1)} %get-tuple-element.44), channel_id=1, source_target_pairs={{0,1},{1,2},{2,3},{3,4},{4,5},{5,6},{6,7},{7,8},{8,9},{9,10},{10,1... | collective-permute-start | bytes 393224 | tf_op jit(solution)/shard_map/ppermute | solution.py:800
  46.8 7.4 %collective-permute-start.7 = (bf16[256,256]{1,0:T(8,128)(2,1)}, bf16[256,256]{1,0:T(8,128)(2,1)S(1)}, u32[]{:S(2)}, u32[]{:S(2)}) collective-permute-start(bf16[256,256]{1,0:T(8,128)(2,1)} %get-tuple-element.44), channel_id=1, source_target_pairs={{1,0},{2,1},{3,2},{4,3},{5,4},{6,5},{7,6},{8,7},{9,8},{10,9},{11,1... | collective-permute-start | bytes 393224 | tf_op jit(solution)/shard_map/ppermute | solution.py:801
  48.1 7.2 %collective-permute-start.9 = (bf16[1024,256]{1,0:T(8,128)(2,1)}, bf16[1024,256]{1,0:T(8,128)(2,1)}, u32[]{:S(2)}, u32[]{:S(2)}) collective-permute-start(bf16[1024,256]{1,0:T(8,128)(2,1)} %get-tuple-element.46), channel_id=1, source_target_pairs={{0,32},{32,0},{1,33},{33,1},{2,34},{34,2},{3,35},{35,3},{4,36},{36... | collective-permute-start | bytes 1572872 | tf_op jit(solution)/shard_map/ppermute | solution.py:747
  54.9 2.3 %collective-permute-start.8 = (bf16[1024,256]{1,0:T(8,128)(2,1)}, bf16[1024,256]{1,0:T(8,128)(2,1)}, u32[]{:S(2)}, u32[]{:S(2)}) collective-permute-start(bf16[1024,256]{1,0:T(8,128)(2,1)} %shard_map.81.piece_ref), channel_id=1, source_target_pairs={{0,32},{32,0},{1,33},{33,1},{2,34},{34,2},{3,35},{35,3},{4,36},{36... | collective-permute-start | bytes 1572872 | tf_op jit(solution)/shard_map/ppermute | solution.py:747
  60.3 35.7 %all-to-all-start = ((bf16[64,8,1280]{2,1,0:T(8,128)(2,1)}), bf16[64,8,1280]{2,1,0:T(8,128)(2,1)}, u32[]{:S(2)}, u32[]{:S(2)}) async-start(bf16[64,8,1280]{2,1,0:T(8,128)(2,1)} %bitcast.11), calls=%async_computation | async-start | bytes 2621440 | tf_op jit(solution)/shard_map/all_to_all | solution.py:752
  85.8 2.7 %collective-permute-start.10 = (bf16[2048,256]{1,0:T(8,128)(2,1)S(1)}, bf16[2048,256]{1,0:T(8,128)(2,1)S(1)}, u32[]{:S(2)}, u32[]{:S(2)}) collective-permute-start(bf16[2048,256]{1,0:T(8,128)(2,1)S(1)} %bitcast.14), channel_id=1, source_target_pairs={{0,32},{32,0},{1,33},{33,1},{2,34},{34,2},{3,35},{35,3},{4,36},{36... | collective-permute-start | bytes 3145736 | tf_op jit(solution)/shard_map/ppermute | solution.py:747
  96.0 8.2 %copy-start.5 = (f32[256,128]{1,0:T(8,128)S(1)}, f32[256,128]{1,0:T(8,128)}, u32[]{:S(2)}) copy-start(f32[256,128]{1,0:T(8,128)} %copy-done.4) | copy-start | bytes 393220
  96.0 8.2 %copy-start.7 = (f32[256,128]{1,0:T(8,128)S(1)}, f32[256,128]{1,0:T(8,128)}, u32[]{:S(2)}) copy-start(f32[256,128]{1,0:T(8,128)} %copy-done.6) | copy-start | bytes 393220
  96.0 8.3 %copy-start.9 = (f32[256,128]{1,0:T(8,128)S(1)}, f32[256,128]{1,0:T(8,128)}, u32[]{:S(2)}) copy-start(f32[256,128]{1,0:T(8,128)} %copy-done.8) | copy-start | bytes 393220
  96.0 8.3 %copy-start.11 = (f32[256,128]{1,0:T(8,128)S(1)}, f32[256,128]{1,0:T(8,128)}, u32[]{:S(2)}) copy-start(f32[256,128]{1,0:T(8,128)} %copy-done.10) | copy-start | bytes 393220
  96.0 36.7 %all-to-all-start.1 = ((bf16[64,8,2048]{2,1,0:T(8,128)(2,1)}), bf16[64,8,2048]{2,1,0:T(8,128)(2,1)S(1)}, u32[]{:S(2)}, u32[]{:S(2)}) async-start(bf16[64,8,2048]{2,1,0:T(8,128)(2,1)} %bitcast.12), calls=%async_computation.1 | async-start | bytes 4194304 | tf_op jit(solution)/shard_map/all_to_all | solution.py:752
  (6 other events, 11.0 us)

commit v14 on v12

--- a/solution.py
+++ b/solution.py
@@ -596,19 +596,31 @@
     probs,
     dscores,
     dhidden,
+    sides,
+    arrived,
 ):
     step = pl.program_id(0)
 
     @pl.when(step == 0)
     def _():
-        probs[...] = jnp.zeros_like(probs)
-        dscores[...] = jnp.zeros_like(dscores)
-        dhidden[:WIN] = dot_nt(left_ref[:, :128], readout_ref[...]).astype(BF)
-        dhidden[WIN:] = dot_nt(right_ref[:, :128], readout_ref[...]).astype(BF)
+        copies = [
+            pltpu.make_async_copy(side_ref, sides.at[place], arrived.at[place])
+            for place, side_ref in enumerate((left_ref, right_ref))
+        ]
+        for copy in copies:
+            copy.start()
+        for slot in range(4):
+            for held in (probs, dscores):
+                held[slot, :128, 128:] = jnp.zeros((128, 128), BF)
+                held[slot, 640:, :128] = jnp.zeros((128, 128), BF)
+        for place, copy in enumerate(copies):
+            copy.wait()
+            rows = slice(place * WIN, (place + 1) * WIN)
+            dhidden[rows] = dot_nt(sides[place, :, :128], readout_ref[...]).astype(BF)
 
     ghalo = dot_nt(dhidden[...], w_out_ref[...]).astype(BF)
     terms = jnp.concatenate(
-        [left_ref[:, 128:], own_ref[:, 128:], right_ref[:, 128:]], axis=0
+        [sides[0, :, 128:], own_ref[:, 128:], sides[1, :, 128:]], axis=0
     )
     window = terms.shape[0]
     fill = key_fill([(counts_ref[1], BLOCK)])
@@ -674,8 +686,8 @@
             part(2 * WIN, 0),
             part(BLOCK, 0),
             whole(BLOCK, 256),
-            whole(BLOCK, 256),
-            whole(BLOCK, 256),
+            pl.BlockSpec(memory_space=pl.ANY),
+            pl.BlockSpec(memory_space=pl.ANY),
             pl.BlockSpec((WIDTH, 1024), lambda j: (j, 0)),
             whole(1024, 128),
         ],
@@ -685,6 +697,8 @@
             pltpu.VMEM((4, window, BLOCK), BF),
             pltpu.VMEM((4, window, BLOCK), BF),
             pltpu.VMEM((2 * WIN, 1024), BF),
+            pltpu.VMEM((2, WIN, 256), BF),
+            pltpu.SemaphoreType.DMA((2,)),
         ],
         compiler_params=pltpu.CompilerParams(vmem_limit_bytes=18 * 1024 * 1024),
         cost_estimate=FREE,
@@ -696,8 +710,8 @@
         qhalo,
         in_hbm(grad),
         own,
-        in_hbm(left),
-        in_hbm(right),
+        left,
+        right,
         in_hbm(w_out),
         readout_weight,
     )

time: 134 us -> 136 us (1.015)
  starting transfers between devices: 34.5 us -> 36.6 us
  waiting for transfers between devices: 43.7 us -> 41.6 us
  local copies, waits for them, and re-layouts: 4.6 us -> 6.42 us
    all_to_all x2, waiting for transfers between devices: 31.9 us -> 29.8 us  [scatter(): lax.all_to_all(partial.reshape(64, 8, columns), CHIPS, split_axis=0, conc...]
    all_to_all x2, starting transfers between devices: 20 us -> 22.1 us  [scatter(): lax.all_to_all(partial.reshape(64, 8, columns), CHIPS, split_axis=0, conc...]
    unnamed x17 -> x21, local copies, waits for them, and re-layouts: 3.08 us -> 4.89 us
  transfers between devices with their start and end apart: 12 -> 12, of which waited for: 8 -> 8; matrix products, arithmetic and copies ran while one was open for 4% -> 4% of each run, Pallas kernels for 23% -> 22%
where the time goes in v14:
time: 136 us; the launch traced here: 135 us
  Pallas kernels  45.2 us (33%)
  waiting for transfers between devices  41.6 us (31%)
  starting transfers between devices  36.6 us (27%)
  local copies, waits for them, and re-layouts  6.42 us (5%)
  other arithmetic  3.26 us (2%)
  between operations  2.14 us (2%)
    all_to_all x2, waiting for transfers between devices, scatter(): lax.all_to_all(partial.reshape(64, 8, columns), CHIPS, split_axis=0, conc...  29.8 us
    all_to_all x2, starting transfers between devices, scatter(): lax.all_to_all(partial.reshape(64, 8, columns), CHIPS, split_axis=0, conc...  22.1 us
    pallas_call x1, Pallas kernels, forward(): pl.pallas_call(forward_kernel, grid=(4,), in_specs=[pl.BlockSpec(memory_s...  11.6 us
    pallas_call x1, Pallas kernels, key_grads(): pl.pallas_call(key_kernel, grid=(4,), in_specs=[pl.BlockSpec(memory_space...  10.6 us
    pallas_call x2, Pallas kernels, partial_sums(): pl.pallas_call(functools.partial(partial_kernel, len(smalls)), in_specs=[...  6.93 us
    ppermute x5, waiting for transfers between devices, swap_core(): return lax.ppermute(values, 'core', SWAP)  5.55 us
    pallas_call x1, Pallas kernels, query_grads(): pl.pallas_call(query_kernel, grid=(4,), in_specs=[part(window, 0), part(w...  5.29 us
    unnamed x21, local copies, waits for them, and re-layouts  4.89 us
  transfers between devices with their start and end apart: 12, of which 8 were waited for; matrix products, arithmetic and copies ran while one was open for 4% of the time, Pallas kernels for 22%

profile of v14, /device:TPU:0, one launch (start us, length us, event | category | flops | bytes accessed | tf_op | source)
XLA Modules:
  0.0 135.5 jit_solution(2827795091208749142)
XLA Ops:
  0.6 3.9 %collective-permute-start = (bf16[256,1024]{1,0:T(8,128)(2,1)}, bf16[256,1024]{1,0:T(8,128)(2,1)S(1)}, u32[]{:S(2)}, u32[]{:S(2)}) collective-permute-start(bf16[256,1024]{1,0:T(8,128)(2,1)} %bitcast.22), channel_id=1, source_target_pairs={{0,1},{1,2},{2,3},{3,4},{4,5},{5,6},{6,7},{7,8},{8,9},{9,10},{10,1... | collective-permute-start | bytes 1572872 | tf_op jit(solution)/shard_map/ppermute | solution.py:748
  4.6 1.3 collective-permute-start.1
  5.9 1.4 %fusion.2 = (s32[1]{0:T(128)}, s32[1]{0:T(128)}, s32[1]{0:T(128)}) fusion(s32[32]{0:T(128)} %param.7, s32[]{:T(128)S(6)} %max.3, s32[]{:T(128)S(6)} %select_n.19, s32[]{:T(128)S(6)} %select_n.18), kind=kLoop, calls=%fused_computation.8 | loop fusion | bytes 36 | tf_op jit(solution)/shard_map/dynamic_slice | solution.py:752
  9.4 1.0 copy-done.8
  10.4 4.1 %shard_map.77 = (bf16[256,3072]{1,0:T(8,128)(2,1)S(1)}, bf16[1024,256]{1,0:T(8,128)(2,1)S(1)}) custom-call(bf16[256,1024]{1,0:T(8,128)(2,1)S(1)} %bitcast.24, bf16[1024,3072]{1,0:T(8,128)(2,1)} %weight_ref.5), custom_call_target="tpu_custom_call" | custom-call | flops 2147483648 | bytes 8388608 | tf_op jit(solution)/shard_map/pallas_call | solution.py:99
  14.6 1.5 %collective-permute-done.left_ref = bf16[256,1024]{1,0:T(8,128)(2,1)S(1)} collective-permute-done((bf16[256,1024]{1,0:T(8,128)(2,1)}, bf16[256,1024]{1,0:T(8,128)(2,1)S(1)}, u32[]{:S(2)}, u32[]{:S(2)}) %collective-permute-start) | collective-permute-done | bytes 524320 | tf_op jit(solution)/shard_map/ppermute | solution.py:748
  16.0 4.3 %collective-permute-done.1.right_ref = bf16[256,1024]{1,0:T(8,128)(2,1)} collective-permute-done((bf16[256,1024]{1,0:T(8,128)(2,1)}, bf16[256,1024]{1,0:T(8,128)(2,1)}, u32[]{:S(2)}, u32[]{:S(2)}) %collective-permute-start.1) | collective-permute-done | bytes 524320 | tf_op jit(solution)/shard_map/ppermute | solution.py:749
  20.3 11.6 %shard_map.78 = (bf16[512,1024]{1,0:T(8,128)(2,1)S(1)}, bf16[768,1024]{1,0:T(8,128)(2,1)S(1)}, bf16[768,1024]{1,0:T(8,128)(2,1)S(1)}, f32[256,1024]{1,0:T(8,128)...) custom-call(s32[3]{0:T(128)S(1)} %pad_add_fusion.counts_ref, ...), custom_call_target="tpu_custom_call" | custom-call | flops 6442450944 | bytes 12582912 | tf_op jit(solution)/shard_map/pallas_call | solution.py:388
  32.0 3.1 %collective-permute-start.2 = (f32[256,128]{1,0:T(8,128)S(1)}, f32[256,128]{1,0:T(8,128)S(1)}, u32[]{:S(2)}, u32[]{:S(2)}) collective-permute-start(f32[256,128]{1,0:T(8,128)S(1)} %get-tuple-element.28.own_ref), channel_id=1, source_target_pairs={{0,64},{64,0},{1,65},{65,1},{2,66},{66,2},{3,67},{67,3},{4,68},{68... | collective-permute-start | bytes 393224 | tf_op jit(solution)/shard_map/ppermute | solution.py:763
  35.1 3.0 %shard_map.79.qhalo_ref = bf16[512,1024]{1,0:T(8,128)(2,1)S(1)} custom-call(bf16[512,1024]{1,0:T(8,128)(2,1)S(1)} %get-tuple-element.29.normed_ref, bf16[1024,3072]{1,0:T(8,128)(2,1)} %weight_ref.5), custom_call_target="tpu_custom_call" | custom-call | tf_op jit(solution)/shard_map/pallas_call | solution.py:137
  40.2 3.6 %shard_map.80 = (f32[256,128]{1,0:T(8,128)}, bf16[256,256]{1,0:T(8,128)(2,1)S(1)}, bf16[256,256]{1,0:T(8,128)(2,1)}, bf16[256,1024]{1,0:T(8,128)(2,1)S(1)}, bf16[1024,256]{1,0:T(8,128)(2,1)}) custom-call(s32[3]{0:T(128)S(1)} %pad_add_fusion.counts_ref, f32[256,128]{1,0:T(8,128)S(1)} %get-tuple-element.28.own_ref, ...), custom_call_target="tpu_custom_call" | custom-call | tf_op jit(solution)/shard_map/pallas_call | solution.py:514
  43.8 3.6 %collective-permute-start.5 = (bf16[256,256]{1,0:T(8,128)(2,1)}, bf16[256,256]{1,0:T(8,128)(2,1)S(1)}, u32[]{:S(2)}, u32[]{:S(2)}) collective-permute-start(bf16[256,256]{1,0:T(8,128)(2,1)} %get-tuple-element.42), channel_id=1, source_target_pairs={{0,1},{1,2},{2,3},{3,4},{4,5},{5,6},{6,7},{7,8},{8,9},{9,10},{10,1... | collective-permute-start | bytes 393224 | tf_op jit(solution)/shard_map/ppermute | solution.py:771
  47.4 1.3 collective-permute-start.6
  48.8 5.3 %shard_map.81.piece_ref = bf16[1024,256]{1,0:T(8,128)(2,1)} custom-call(bf16[768,1024]{1,0:T(8,128)(2,1)S(1)} %get-tuple-element.36.kcat_ref, bf16[768,1024]{1,0:T(8,128)(2,1)S(1)} %get-tuple-element.37.vcat_ref, bf16[256,1024]{1,0:T(8,128)(2,1)S(1)} %get-tuple-element.38.grad_ref, bf16[256,256]{1,0:T(8,128)(2,1)S(1)} %get-tuple-element.39.packed_ref.own_ref, ...), custom_call_target="tpu_custom_call" | custom-call | flops 6442450944 | bytes 5242880 | tf_op jit(solution)/shard_map/pallas_call | solution.py:562
  55.9 1.9 %collective-permute-done.7.other_ref = bf16[1024,256]{1,0:T(8,128)(2,1)} collective-permute-done((bf16[1024,256]{1,0:T(8,128)(2,1)}, bf16[1024,256]{1,0:T(8,128)(2,1)}, u32[]{:S(2)}, u32[]{:S(2)}) %collective-permute-start.7) | collective-permute-done | bytes 524320 | tf_op jit(solution)/shard_map/ppermute | solution.py:728
  57.8 3.1 %shard_map.82 = bf16[512,1280]{1,0:T(8,128)(2,1)} custom-call(s32[1]{0:T(128)} %bitcast.7.core_ref, bf16[2,2,256,256]{3,2,1,0:T(8,128)(2,1)S(1)} %bitcast.18, bf16[2,2,256,256]{3,2,1,0:T(8,128)(2,1)} %bitcast.9.normed_other_ref, bf16[1024,256]{1,0:T(8,128)(2,1)} %shard_map.81.piece_ref, bf16[1024,256]{1,0:T(8,128)(2,1)} %collective-permute-done.7.other_ref, ...), custom_call_target="tpu_custom_call" | custom-call | tf_op jit(solution)/shard_map/pallas_call | solution.py:217
  60.9 14.2 %all-to-all-start = ((bf16[64,8,1280]{2,1,0:T(8,128)(2,1)}), bf16[64,8,1280]{2,1,0:T(8,128)(2,1)}, u32[]{:S(2)}, u32[]{:S(2)}) async-start(bf16[64,8,1280]{2,1,0:T(8,128)(2,1)} %bitcast.13), calls=%async_computation | async-start | bytes 2621440 | tf_op jit(solution)/shard_map/all_to_all | solution.py:733
  77.0 10.6 %shard_map.83 = bf16[2,1024,256]{2,1,0:T(8,128)(2,1)S(1)} custom-call(s32[3]{0:T(128)S(1)} %pad_add_fusion.counts_ref, bf16[256,3072]{1,0:T(8,128)(2,1)S(1)} %get-tuple-element.27.q_ref.k_ref.v_ref, bf16[256,3072]{1,0:T(8,128)(2,1)S(1)} %get-tuple-element.27.q_ref.k_ref.v_ref, bf16[256,3072]{1,0:T(8,128)(2,1)S(1)} %get-tuple-element.27.q_ref.k_ref.v_ref, ...), custom_call_target="tpu_custom_call" | custom-call | tf_op jit(solution)/shard_map/pallas_call | solution.py:678
  87.7 2.6 %collective-permute-done.9.other_ref = bf16[2048,256]{1,0:T(8,128)(2,1)S(1)} collective-permute-done((bf16[2048,256]{1,0:T(8,128)(2,1)S(1)}, bf16[2048,256]{1,0:T(8,128)(2,1)S(1)}, u32[]{:S(2)}, u32[]{:S(2)}) %collective-permute-start.9) | collective-permute-done | bytes 1048608 | tf_op jit(solution)/shard_map/ppermute | solution.py:728
  90.3 3.8 %shard_map.84 = bf16[512,2048]{1,0:T(8,128)(2,1)} custom-call(s32[1]{0:T(128)} %bitcast.7.core_ref, bf16[2,2,256,256]{3,2,1,0:T(8,128)(2,1)S(1)} %bitcast.19, bf16[2,2,256,256]{3,2,1,0:T(8,128)(2,1)} %bitcast.9.normed_other_ref, bf16[2048,256]{1,0:T(8,128)(2,1)S(1)} %bitcast.17, bf16[2048,256]{1,0:T(8,128)(2,1)S(1)} %collective-permute-done.9.other_ref), custom_call_target="tpu_custom_call" | custom-call | tf_op jit(solution)/shard_map/pallas_call | solution.py:217
  94.2 2.4 %all-to-all-done = bf16[64,8,1280]{2,1,0:T(8,128)(2,1)} async-done(((bf16[64,8,1280]{2,1,0:T(8,128)(2,1)}), bf16[64,8,1280]{2,1,0:T(8,128)(2,1)}, u32[]{:S(2)}, u32[]{:S(2)}) %all-to-all-start) | async-done | bytes 1310752 | tf_op jit(solution)/shard_map/all_to_all | solution.py:733
  96.6 7.9 %all-to-all-start.1 = ((bf16[64,8,2048]{2,1,0:T(8,128)(2,1)}), bf16[64,8,2048]{2,1,0:T(8,128)(2,1)S(1)}, u32[]{:S(2)}, u32[]{:S(2)}) async-start(bf16[64,8,2048]{2,1,0:T(8,128)(2,1)} %bitcast.14), calls=%async_computation.1 | async-start | bytes 4194304 | tf_op jit(solution)/shard_map/all_to_all | solution.py:733
  105.3 1.5 %convert_reduce_fusion.1 = f32[8,1280]{1,0:T(8,128)S(1)} fusion(bf16[64,8,1280]{2,1,0:T(8,128)(2,1)} %all-to-all-done), kind=kLoop, calls=%fused_computation.1 | loop fusion | flops 1300480 | bytes 1351680 | tf_op jit(solution)/shard_map/reduce_sum | solution.py:737
  107.2 27.3 %all-to-all-done.1 = bf16[64,8,2048]{2,1,0:T(8,128)(2,1)S(1)} async-done(((bf16[64,8,2048]{2,1,0:T(8,128)(2,1)}), bf16[64,8,2048]{2,1,0:T(8,128)(2,1)S(1)}, u32[]{:S(2)}, u32[]{:S(2)}) %all-to-all-start.1) | async-done | bytes 2097184 | tf_op jit(solution)/shard_map/all_to_all | solution.py:733
  (39 shorter events, 8.7 us)
Async XLA Ops:
  0.6 15.4 %collective-permute-start = (bf16[256,1024]{1,0:T(8,128)(2,1)}, bf16[256,1024]{1,0:T(8,128)(2,1)S(1)}, u32[]{:S(2)}, u32[]{:S(2)}) collective-permute-start(bf16[256,1024]{1,0:T(8,128)(2,1)} %bitcast.22), channel_id=1, source_target_pairs={{0,1},{1,2},{2,3},{3,4},{4,5},{5,6},{6,7},{7,8},{8,9},{9,10},{10,1... | collective-permute-start | bytes 1572872 | tf_op jit(solution)/shard_map/ppermute | solution.py:748
  4.6 15.8 %collective-permute-start.1 = (bf16[256,1024]{1,0:T(8,128)(2,1)}, bf16[256,1024]{1,0:T(8,128)(2,1)}, u32[]{:S(2)}, u32[]{:S(2)}) collective-permute-start(bf16[256,1024]{1,0:T(8,128)(2,1)} %bitcast.23), channel_id=1, source_target_pairs={{1,0},{2,1},{3,2},{4,3},{5,4},{6,5},{7,6},{8,7},{9,8},{10,9},{11,1... | collective-permute-start | bytes 1572872 | tf_op jit(solution)/shard_map/ppermute | solution.py:749
  9.4 1.0 copy-start.8
  10.4 9.9 %copy-start = (bf16[1024,1024]{1,0:T(8,128)(2,1)S(1)}, bf16[1024,1024]{1,0:T(8,128)(2,1)}, u32[]{:S(2)}) copy-start(bf16[1024,1024]{1,0:T(8,128)(2,1)} %w_out_ref.5) | copy-start | bytes 6291460
  10.4 9.9 %copy-start.1 = (bf16[1024,128]{1,0:T(8,128)(2,1)S(1)}, bf16[1024,128]{1,0:T(8,128)(2,1)}, u32[]{:S(2)}) copy-start(bf16[1024,128]{1,0:T(8,128)(2,1)} %readout_ref.5) | copy-start | bytes 786436
  32.0 6.6 %collective-permute-start.2 = (f32[256,128]{1,0:T(8,128)S(1)}, f32[256,128]{1,0:T(8,128)S(1)}, u32[]{:S(2)}, u32[]{:S(2)}) collective-permute-start(f32[256,128]{1,0:T(8,128)S(1)} %get-tuple-element.28.own_ref), channel_id=1, source_target_pairs={{0,64},{64,0},{1,65},{65,1},{2,66},{66,2},{3,67},{67,3},{4,68},{68... | collective-permute-start | bytes 393224 | tf_op jit(solution)/shard_map/ppermute | solution.py:763
  35.1 5.1 %copy-start.7 = (f32[256,128]{1,0:T(8,128)S(1)}, f32[256,128]{1,0:T(8,128)}, u32[]{:S(2)}) copy-start(f32[256,128]{1,0:T(8,128)} %target_ref.1) | copy-start | bytes 393220
  38.5 1.6 %collective-permute-start.3 = (f32[2,256,128]{2,1,0:T(8,128)S(1)}, f32[2,256,128]{2,1,0:T(8,128)S(1)}, u32[]{:S(2)}, u32[]{:S(2)}) collective-permute-start(f32[2,256,128]{2,1,0:T(8,128)S(1)} %pad_maximum_fusion), channel_id=1, source_target_pairs={{0,32},{32,0},{1,33},{33,1},{2,34},{34,2},{3,35},{35,3},{4,36},{36... | collective-permute-start | bytes 786440 | tf_op jit(solution)/shard_map/ppermute | solution.py:728
  38.6 17.3 %collective-permute-start.4 = (bf16[1024,256]{1,0:T(8,128)(2,1)S(1)}, bf16[1024,256]{1,0:T(8,128)(2,1)}, u32[]{:S(2)}, u32[]{:S(2)}) collective-permute-start(bf16[1024,256]{1,0:T(8,128)(2,1)S(1)} %get-tuple-element.35), channel_id=1, source_target_pairs={{0,32},{32,0},{1,33},{33,1},{2,34},{34,2},{3,35},{35,3},{4,36},{36... | collective-permute-start | bytes 1572872 | tf_op jit(solution)/shard_map/ppermute | solution.py:728
  43.8 10.3 %copy-start.2 = (bf16[256,1024]{1,0:T(8,128)(2,1)}, bf16[256,1024]{1,0:T(8,128)(2,1)S(1)}, u32[]{:S(2)}) copy-start(bf16[256,1024]{1,0:T(8,128)(2,1)S(1)} %get-tuple-element.38.grad_ref) | copy-start | bytes 1572868
  43.8 10.3 %collective-permute-start.5 = (bf16[256,256]{1,0:T(8,128)(2,1)}, bf16[256,256]{1,0:T(8,128)(2,1)S(1)}, u32[]{:S(2)}, u32[]{:S(2)}) collective-permute-start(bf16[256,256]{1,0:T(8,128)(2,1)} %get-tuple-element.42), channel_id=1, source_target_pairs={{0,1},{1,2},{2,3},{3,4},{4,5},{5,6},{6,7},{7,8},{8,9},{9,10},{10,1... | collective-permute-start | bytes 393224 | tf_op jit(solution)/shard_map/ppermute | solution.py:771
  47.4 7.4 %collective-permute-start.6 = (bf16[256,256]{1,0:T(8,128)(2,1)}, bf16[256,256]{1,0:T(8,128)(2,1)S(1)}, u32[]{:S(2)}, u32[]{:S(2)}) collective-permute-start(bf16[256,256]{1,0:T(8,128)(2,1)} %get-tuple-element.42), channel_id=1, source_target_pairs={{1,0},{2,1},{3,2},{4,3},{5,4},{6,5},{7,6},{8,7},{9,8},{10,9},{11,1... | collective-permute-start | bytes 393224 | tf_op jit(solution)/shard_map/ppermute | solution.py:772
  48.7 7.2 %collective-permute-start.8 = (bf16[1024,256]{1,0:T(8,128)(2,1)}, bf16[1024,256]{1,0:T(8,128)(2,1)}, u32[]{:S(2)}, u32[]{:S(2)}) collective-permute-start(bf16[1024,256]{1,0:T(8,128)(2,1)} %get-tuple-element.44), channel_id=1, source_target_pairs={{0,32},{32,0},{1,33},{33,1},{2,34},{34,2},{3,35},{35,3},{4,36},{36... | collective-permute-start | bytes 1572872 | tf_op jit(solution)/shard_map/ppermute | solution.py:728
  54.1 0.7 copy-start.3
  54.8 0.7 copy-start.5
  55.4 2.4 %collective-permute-start.7 = (bf16[1024,256]{1,0:T(8,128)(2,1)}, bf16[1024,256]{1,0:T(8,128)(2,1)}, u32[]{:S(2)}, u32[]{:S(2)}) collective-permute-start(bf16[1024,256]{1,0:T(8,128)(2,1)} %shard_map.81.piece_ref), channel_id=1, source_target_pairs={{0,32},{32,0},{1,33},{33,1},{2,34},{34,2},{3,35},{35,3},{4,36},{36... | collective-permute-start | bytes 1572872 | tf_op jit(solution)/shard_map/ppermute | solution.py:728
  60.9 35.7 %all-to-all-start = ((bf16[64,8,1280]{2,1,0:T(8,128)(2,1)}), bf16[64,8,1280]{2,1,0:T(8,128)(2,1)}, u32[]{:S(2)}, u32[]{:S(2)}) async-start(bf16[64,8,1280]{2,1,0:T(8,128)(2,1)} %bitcast.13), calls=%async_computation | async-start | bytes 2621440 | tf_op jit(solution)/shard_map/all_to_all | solution.py:733
  75.2 0.9 copy-start.4
  76.1 0.9 copy-start.6
  87.6 2.7 %collective-permute-start.9 = (bf16[2048,256]{1,0:T(8,128)(2,1)S(1)}, bf16[2048,256]{1,0:T(8,128)(2,1)S(1)}, u32[]{:S(2)}, u32[]{:S(2)}) collective-permute-start(bf16[2048,256]{1,0:T(8,128)(2,1)S(1)} %bitcast.16), channel_id=1, source_target_pairs={{0,32},{32,0},{1,33},{33,1},{2,34},{34,2},{3,35},{35,3},{4,36},{36... | collective-permute-start | bytes 3145736 | tf_op jit(solution)/shard_map/ppermute | solution.py:728
  96.6 7.9 %copy-start.9 = (f32[256,128]{1,0:T(8,128)S(1)}, f32[256,128]{1,0:T(8,128)}, u32[]{:S(2)}) copy-start(f32[256,128]{1,0:T(8,128)} %get-tuple-element.34) | copy-start | bytes 393220
  96.6 37.9 %all-to-all-start.1 = ((bf16[64,8,2048]{2,1,0:T(8,128)(2,1)}), bf16[64,8,2048]{2,1,0:T(8,128)(2,1)S(1)}, u32[]{:S(2)}, u32[]{:S(2)}) async-start(bf16[64,8,2048]{2,1,0:T(8,128)(2,1)} %bitcast.14), calls=%async_computation.1 | async-start | bytes 4194304 | tf_op jit(solution)/shard_map/all_to_all | solution.py:733

commit v15 on v12

--- a/solution.py
+++ b/solution.py
@@ -150,12 +150,14 @@
 
 
 def partial_kernel(
-    smalls, core_ref, normed_ref, normed_other_ref, piece_ref, other_ref, *refs
+    smalls, passed, core_ref, normed_ref, normed_other_ref, piece_ref, other_ref, *refs
 ):
-    small_refs, (out_ref, rows, pieces, others, sums, staged, arrived, left) = (
-        refs[:smalls],
-        refs[smalls:],
-    )
+    small_refs, side_refs, out_ref = refs[:smalls], refs[smalls : smalls + passed], None
+    refs = refs[smalls + passed :]
+    if passed:
+        out_ref, sides_ref, rows, pieces, others, sums, staged, arrived, left, moved = refs
+    else:
+        out_ref, rows, pieces, others, sums, staged, arrived, left, moved = refs
     core = core_ref[0]
     chunks = piece_ref.shape[0] // 512
     sources = [
@@ -174,9 +176,12 @@
     ]
     for copy in copies:
         copy.start()
+    writes = []
+    for place, side_ref in enumerate(side_refs):
+        writes.append(pltpu.make_async_copy(side_ref, sides_ref.at[place], moved.at[place]))
+        writes[-1].start()
     copies[0].wait()
     copies[1].wait()
-    writes = []
     for chunk in range(chunks):
         copies[2 + 2 * chunk].wait()
         copies[3 + 2 * chunk].wait()
@@ -209,16 +214,21 @@
         write.wait()
 
 
-def partial_sums(core, turned, turned_other, piece, other, smalls=()):
+def partial_sums(core, turned, turned_other, piece, other, smalls=(), sides=()):
     by_core = lambda values: values.reshape(2, 2, 256, 256)
     anywhere = pl.BlockSpec(memory_space=pl.ANY)
     chunks = piece.shape[0] // 512
     columns = piece.shape[0] + 256 * (len(smalls) // 2)
     return pl.pallas_call(
-        functools.partial(partial_kernel, len(smalls)),
-        in_specs=[pl.BlockSpec(memory_space=pltpu.SMEM)] + [anywhere] * (4 + len(smalls)),
-        out_specs=anywhere,
-        out_shape=jax.ShapeDtypeStruct((512, columns), BF),
+        functools.partial(partial_kernel, len(smalls), len(sides)),
+        in_specs=[pl.BlockSpec(memory_space=pltpu.SMEM)]
+        + [anywhere] * (4 + len(smalls) + len(sides)),
+        out_specs=[anywhere, HBM] if sides else anywhere,
+        out_shape=(
+            [jax.ShapeDtypeStruct((512, columns), BF), pltpu.HBM((2, WIN, 256), BF)]
+            if sides
+            else jax.ShapeDtypeStruct((512, columns), BF)
+        ),
         scratch_shapes=[
             pltpu.VMEM((2, 2, 256, 256), BF),
             pltpu.VMEM((chunks, 512, 256), BF),
@@ -227,6 +237,7 @@
             pltpu.VMEM((chunks + 1, 512, 512), BF),
             pltpu.SemaphoreType.DMA((2 + 2 * chunks + len(smalls),)),
             pltpu.SemaphoreType.DMA((chunks + 1,)),
+            pltpu.SemaphoreType.DMA((2,)),
         ],
         compiler_params=pltpu.CompilerParams(vmem_limit_bytes=14 * 1024 * 1024),
         cost_estimate=FREE,
@@ -237,6 +248,7 @@
         piece,
         other,
         *(by_core(small) for small in smalls),
+        *sides,
     )
 
 
@@ -588,8 +600,7 @@
     qhalo_ref,
     grad_ref,
     own_ref,
-    left_ref,
-    right_ref,
+    sides_ref,
     w_out_ref,
     readout_ref,
     out_ref,
@@ -601,14 +612,16 @@
 
     @pl.when(step == 0)
     def _():
-        probs[...] = jnp.zeros_like(probs)
-        dscores[...] = jnp.zeros_like(dscores)
-        dhidden[:WIN] = dot_nt(left_ref[:, :128], readout_ref[...]).astype(BF)
-        dhidden[WIN:] = dot_nt(right_ref[:, :128], readout_ref[...]).astype(BF)
+        for slot in range(4):
+            for held in (probs, dscores):
+                held[slot, :128, 128:] = jnp.zeros((128, 128), BF)
+                held[slot, 640:, :128] = jnp.zeros((128, 128), BF)
+        dhidden[:WIN] = dot_nt(sides_ref[0, :, :128], readout_ref[...]).astype(BF)
+        dhidden[WIN:] = dot_nt(sides_ref[1, :, :128], readout_ref[...]).astype(BF)
 
     ghalo = dot_nt(dhidden[...], w_out_ref[...]).astype(BF)
     terms = jnp.concatenate(
-        [left_ref[:, 128:], own_ref[:, 128:], right_ref[:, 128:]], axis=0
+        [sides_ref[0, :, 128:], own_ref[:, 128:], sides_ref[1, :, 128:]], axis=0
     )
     window = terms.shape[0]
     fill = key_fill([(counts_ref[1], BLOCK)])
@@ -659,7 +672,7 @@
         out_ref[1, place] = dot_nn(turned[slot][1], probs[slot]).astype(BF)
 
 
-def key_grads(counts, projected, qhalo, grad, own, left, right, w_out, readout_weight):
+def key_grads(counts, projected, qhalo, grad, own, sides, w_out, readout_weight):
     part = lambda rows, first: pl.BlockSpec((rows, WIDTH), lambda j: (0, first + j))
     whole = lambda *shape: pl.BlockSpec(shape, lambda j: (0, 0))
     window = 2 * WIN + BLOCK
@@ -674,8 +687,7 @@
             part(2 * WIN, 0),
             part(BLOCK, 0),
             whole(BLOCK, 256),
-            whole(BLOCK, 256),
-            whole(BLOCK, 256),
+            pl.BlockSpec((2, WIN, 256), lambda j: (0, 0, 0)),
             pl.BlockSpec((WIDTH, 1024), lambda j: (j, 0)),
             whole(1024, 128),
         ],
@@ -696,8 +708,7 @@
         qhalo,
         in_hbm(grad),
         own,
-        in_hbm(left),
-        in_hbm(right),
+        in_hbm(sides),
         in_hbm(w_out),
         readout_weight,
     )
@@ -762,8 +773,14 @@
         (dquery, packed_left, packed_right)
     )
 
-    first_part = partial_sums(
-        core, turned, turned_other, dquery, swap_core(dquery), (small, swap_core(small))
+    first_part, sides = partial_sums(
+        core,
+        turned,
+        turned_other,
+        dquery,
+        swap_core(dquery),
+        (small, swap_core(small)),
+        (packed_left, packed_right),
     )
     first_part, scalars = lax.optimization_barrier((first_part, scalars))
     first = scatter(first_part)
@@ -773,8 +790,7 @@
         qhalo,
         grad,
         packed,
-        packed_left,
-        packed_right,
+        sides,
         w_out,
         readout_weight,
     )

time: 134 us -> 136 us (1.015)
  local copies, waits for them, and re-layouts: 4.6 us -> 7.48 us
    unnamed x17 -> x23, local copies, waits for them, and re-layouts: 3.08 us -> 5.95 us
  transfers between devices with their start and end apart: 12 -> 12, of which waited for: 8 -> 9; matrix products, arithmetic and copies ran while one was open for 4% -> 4% of each run, Pallas kernels for 23% -> 22%
where the time goes in v15:
time: 136 us; the launch traced here: 135 us
  waiting for transfers between devices  44 us (32%)
  Pallas kernels  43.8 us (32%)
  starting transfers between devices  34.3 us (25%)
  local copies, waits for them, and re-layouts  7.48 us (6%)
  other arithmetic  3.26 us (2%)
  between operations  2.14 us (2%)
    all_to_all x2, waiting for transfers between devices, scatter(): lax.all_to_all(partial.reshape(64, 8, columns), CHIPS, split_axis=0, conc...  32 us
    all_to_all x2, starting transfers between devices, scatter(): lax.all_to_all(partial.reshape(64, 8, columns), CHIPS, split_axis=0, conc...  20 us
    pallas_call x1, Pallas kernels, forward(): pl.pallas_call(forward_kernel, grid=(4,), in_specs=[pl.BlockSpec(memory_s...  11.5 us
    pallas_call x1, Pallas kernels, key_grads(): pl.pallas_call(key_kernel, grid=(4,), in_specs=[pl.BlockSpec(memory_space...  10.2 us
    pallas_call x2, Pallas kernels, partial_sums(): pl.pallas_call(functools.partial(partial_kernel, len(smalls), len(sides))...  6.28 us
    unnamed x23, local copies, waits for them, and re-layouts  5.95 us
    ppermute x5, waiting for transfers between devices, swap_core(): return lax.ppermute(values, 'core', SWAP)  5.59 us
    pallas_call x1, Pallas kernels, query_grads(): pl.pallas_call(query_kernel, grid=(4,), in_specs=[part(window, 0), part(w...  5.13 us
  transfers between devices with their start and end apart: 12, of which 9 were waited for; matrix products, arithmetic and copies ran while one was open for 4% of the time, Pallas kernels for 22%

profile of v15, /device:TPU:0, one launch (start us, length us, event | category | flops | bytes accessed | tf_op | source)
XLA Modules:
  0.0 135.3 jit_solution(11566089345967655914)
XLA Ops:
  0.6 3.9 %collective-permute-start = (bf16[256,1024]{1,0:T(8,128)(2,1)}, bf16[256,1024]{1,0:T(8,128)(2,1)S(1)}, u32[]{:S(2)}, u32[]{:S(2)}) collective-permute-start(bf16[256,1024]{1,0:T(8,128)(2,1)} %bitcast.23), channel_id=1, source_target_pairs={{0,1},{1,2},{2,3},{3,4},{4,5},{5,6},{6,7},{7,8},{8,9},{9,10},{10,1... | collective-permute-start | bytes 1572872 | tf_op jit(solution)/shard_map/ppermute | solution.py:745
  4.6 1.3 collective-permute-start.1
  5.9 1.4 %fusion.2 = (s32[1]{0:T(128)}, s32[1]{0:T(128)}, s32[1]{0:T(128)}) fusion(s32[32]{0:T(128)} %param.7, s32[]{:T(128)S(6)} %max.3, s32[]{:T(128)S(6)} %select_n.19, s32[]{:T(128)S(6)} %select_n.18), kind=kLoop, calls=%fused_computation.8 | loop fusion | bytes 36 | tf_op jit(solution)/shard_map/dynamic_slice | solution.py:749
  10.4 4.1 %shard_map.77 = (bf16[256,3072]{1,0:T(8,128)(2,1)S(1)}, bf16[1024,256]{1,0:T(8,128)(2,1)S(1)}) custom-call(bf16[256,1024]{1,0:T(8,128)(2,1)S(1)} %bitcast.25, bf16[1024,3072]{1,0:T(8,128)(2,1)} %weight_ref.5), custom_call_target="tpu_custom_call" | custom-call | flops 2147483648 | bytes 8388608 | tf_op jit(solution)/shard_map/pallas_call | solution.py:99
  14.6 1.5 %collective-permute-done.left_ref = bf16[256,1024]{1,0:T(8,128)(2,1)S(1)} collective-permute-done((bf16[256,1024]{1,0:T(8,128)(2,1)}, bf16[256,1024]{1,0:T(8,128)(2,1)S(1)}, u32[]{:S(2)}, u32[]{:S(2)}) %collective-permute-start) | collective-permute-done | bytes 524320 | tf_op jit(solution)/shard_map/ppermute | solution.py:745
  16.0 4.3 %collective-permute-done.1.right_ref = bf16[256,1024]{1,0:T(8,128)(2,1)} collective-permute-done((bf16[256,1024]{1,0:T(8,128)(2,1)}, bf16[256,1024]{1,0:T(8,128)(2,1)}, u32[]{:S(2)}, u32[]{:S(2)}) %collective-permute-start.1) | collective-permute-done | bytes 524320 | tf_op jit(solution)/shard_map/ppermute | solution.py:746
  20.3 11.5 %shard_map.78 = (bf16[512,1024]{1,0:T(8,128)(2,1)S(1)}, bf16[768,1024]{1,0:T(8,128)(2,1)S(1)}, bf16[768,1024]{1,0:T(8,128)(2,1)S(1)}, f32[256,1024]{1,0:T(8,128)...) custom-call(s32[3]{0:T(128)S(1)} %pad_add_fusion.counts_ref, ...), custom_call_target="tpu_custom_call" | custom-call | flops 6442450944 | bytes 12582912 | tf_op jit(solution)/shard_map/pallas_call | solution.py:400
  31.9 3.1 %collective-permute-start.2 = (f32[256,128]{1,0:T(8,128)S(1)}, f32[256,128]{1,0:T(8,128)S(1)}, u32[]{:S(2)}, u32[]{:S(2)}) collective-permute-start(f32[256,128]{1,0:T(8,128)S(1)} %get-tuple-element.30.own_ref), channel_id=1, source_target_pairs={{0,64},{64,0},{1,65},{65,1},{2,66},{66,2},{3,67},{67,3},{4,68},{68... | collective-permute-start | bytes 393224 | tf_op jit(solution)/shard_map/ppermute | solution.py:760
  35.0 3.0 %shard_map.79.qhalo_ref = bf16[512,1024]{1,0:T(8,128)(2,1)S(1)} custom-call(bf16[512,1024]{1,0:T(8,128)(2,1)S(1)} %get-tuple-element.31.normed_ref, bf16[1024,3072]{1,0:T(8,128)(2,1)} %weight_ref.5), custom_call_target="tpu_custom_call" | custom-call | tf_op jit(solution)/shard_map/pallas_call | solution.py:137
  40.1 3.6 %shard_map.80 = (f32[256,128]{1,0:T(8,128)}, bf16[256,256]{1,0:T(8,128)(2,1)S(1)}, bf16[256,256]{1,0:T(8,128)(2,1)}, bf16[256,1024]{1,0:T(8,128)(2,1)S(1)}, bf16[1024,256]{1,0:T(8,128)(2,1)}) custom-call(s32[3]{0:T(128)S(1)} %pad_add_fusion.counts_ref, f32[256,128]{1,0:T(8,128)S(1)} %get-tuple-element.30.own_ref, ...), custom_call_target="tpu_custom_call" | custom-call | tf_op jit(solution)/shard_map/pallas_call | solution.py:526
  43.7 3.6 %collective-permute-start.5 = (bf16[256,256]{1,0:T(8,128)(2,1)}, bf16[256,256]{1,0:T(8,128)(2,1)S(1)}, u32[]{:S(2)}, u32[]{:S(2)}) collective-permute-start(bf16[256,256]{1,0:T(8,128)(2,1)} %get-tuple-element.44), channel_id=1, source_target_pairs={{0,1},{1,2},{2,3},{3,4},{4,5},{5,6},{6,7},{7,8},{8,9},{9,10},{10,1... | collective-permute-start | bytes 393224 | tf_op jit(solution)/shard_map/ppermute | solution.py:768
  47.3 1.3 collective-permute-start.6
  48.7 5.1 %shard_map.81.piece_ref = bf16[1024,256]{1,0:T(8,128)(2,1)} custom-call(bf16[768,1024]{1,0:T(8,128)(2,1)S(1)} %get-tuple-element.38.kcat_ref, bf16[768,1024]{1,0:T(8,128)(2,1)S(1)} %get-tuple-element.39.vcat_ref, bf16[256,1024]{1,0:T(8,128)(2,1)S(1)} %get-tuple-element.40.grad_ref, bf16[256,256]{1,0:T(8,128)(2,1)S(1)} %get-tuple-element.41.packed_ref.own_ref, ...), custom_call_target="tpu_custom_call" | custom-call | flops 6442450944 | bytes 5242880 | tf_op jit(solution)/shard_map/pallas_call | solution.py:574
  55.6 1.9 %collective-permute-done.7.other_ref = bf16[1024,256]{1,0:T(8,128)(2,1)} collective-permute-done((bf16[1024,256]{1,0:T(8,128)(2,1)}, bf16[1024,256]{1,0:T(8,128)(2,1)}, u32[]{:S(2)}, u32[]{:S(2)}) %collective-permute-start.7) | collective-permute-done | bytes 524320 | tf_op jit(solution)/shard_map/ppermute | solution.py:725
  59.4 2.4 %shard_map.82 = (bf16[512,1280]{1,0:T(8,128)(2,1)S(1)}, bf16[2,256,256]{2,1,0:T(8,128)(2,1)}) custom-call(s32[1]{0:T(128)} %bitcast.7.core_ref, bf16[2,2,256,256]{3,2,1,0:T(8,128)(2,1)S(1)} %bitcast.18, bf16[2,2,256,256]{3,2,1,0:T(8,128)(2,1)} %bitcast.9.normed_other_ref, bf16[1024,256]{1,0:T(8,128)(2,1)} %shard_map.81.piece_ref, ...), custom_call_target="tpu_custom_call" | custom-call | tf_op jit(solution)/shard_map/pallas_call | solution.py:222
  61.8 1.1 copy-done.2
  62.9 14.3 %all-to-all-start = ((bf16[64,8,1280]{2,1,0:T(8,128)(2,1)}), bf16[64,8,1280]{2,1,0:T(8,128)(2,1)}, u32[]{:S(2)}, u32[]{:S(2)}) async-start(bf16[64,8,1280]{2,1,0:T(8,128)(2,1)} %bitcast.20), calls=%async_computation | async-start | bytes 2621440 | tf_op jit(solution)/shard_map/all_to_all | solution.py:730
  77.2 10.2 %shard_map.83 = bf16[2,1024,256]{2,1,0:T(8,128)(2,1)S(1)} custom-call(s32[3]{0:T(128)S(1)} %pad_add_fusion.counts_ref, bf16[256,3072]{1,0:T(8,128)(2,1)S(1)} %get-tuple-element.29.q_ref.k_ref.v_ref, bf16[256,3072]{1,0:T(8,128)(2,1)S(1)} %get-tuple-element.29.q_ref.k_ref.v_ref, bf16[256,3072]{1,0:T(8,128)(2,1)S(1)} %get-tuple-element.29.q_ref.k_ref.v_ref, ...), custom_call_target="tpu_custom_call" | custom-call | tf_op jit(solution)/shard_map/pallas_call | solution.py:679
  87.5 2.6 %collective-permute-done.9.other_ref = bf16[2048,256]{1,0:T(8,128)(2,1)S(1)} collective-permute-done((bf16[2048,256]{1,0:T(8,128)(2,1)S(1)}, bf16[2048,256]{1,0:T(8,128)(2,1)S(1)}, u32[]{:S(2)}, u32[]{:S(2)}) %collective-permute-start.9) | collective-permute-done | bytes 1048608 | tf_op jit(solution)/shard_map/ppermute | solution.py:725
  90.1 3.8 %shard_map.84 = bf16[512,2048]{1,0:T(8,128)(2,1)} custom-call(s32[1]{0:T(128)} %bitcast.7.core_ref, bf16[2,2,256,256]{3,2,1,0:T(8,128)(2,1)S(1)} %bitcast.19, bf16[2,2,256,256]{3,2,1,0:T(8,128)(2,1)} %bitcast.9.normed_other_ref, bf16[2048,256]{1,0:T(8,128)(2,1)S(1)} %bitcast.17, bf16[2048,256]{1,0:T(8,128)(2,1)S(1)} %collective-permute-done.9.other_ref), custom_call_target="tpu_custom_call" | custom-call | tf_op jit(solution)/shard_map/pallas_call | solution.py:222
  94.0 4.7 %all-to-all-done = bf16[64,8,1280]{2,1,0:T(8,128)(2,1)} async-done(((bf16[64,8,1280]{2,1,0:T(8,128)(2,1)}), bf16[64,8,1280]{2,1,0:T(8,128)(2,1)}, u32[]{:S(2)}, u32[]{:S(2)}) %all-to-all-start) | async-done | bytes 1310752 | tf_op jit(solution)/shard_map/all_to_all | solution.py:730
  98.7 5.6 %all-to-all-start.1 = ((bf16[64,8,2048]{2,1,0:T(8,128)(2,1)}), bf16[64,8,2048]{2,1,0:T(8,128)(2,1)S(1)}, u32[]{:S(2)}, u32[]{:S(2)}) async-start(bf16[64,8,2048]{2,1,0:T(8,128)(2,1)} %bitcast.14), calls=%async_computation.1 | async-start | bytes 4194304 | tf_op jit(solution)/shard_map/all_to_all | solution.py:730
  105.1 1.5 %convert_reduce_fusion.1 = f32[8,1280]{1,0:T(8,128)S(1)} fusion(bf16[64,8,1280]{2,1,0:T(8,128)(2,1)} %all-to-all-done), kind=kLoop, calls=%fused_computation.1 | loop fusion | flops 1300480 | bytes 1351680 | tf_op jit(solution)/shard_map/reduce_sum | solution.py:734
  107.0 27.3 %all-to-all-done.1 = bf16[64,8,2048]{2,1,0:T(8,128)(2,1)S(1)} async-done(((bf16[64,8,2048]{2,1,0:T(8,128)(2,1)}), bf16[64,8,2048]{2,1,0:T(8,128)(2,1)S(1)}, u32[]{:S(2)}, u32[]{:S(2)}) %all-to-all-start.1) | async-done | bytes 2097184 | tf_op jit(solution)/shard_map/all_to_all | solution.py:730
  (41 shorter events, 9.8 us)
Async XLA Ops:
  0.6 15.4 %collective-permute-start = (bf16[256,1024]{1,0:T(8,128)(2,1)}, bf16[256,1024]{1,0:T(8,128)(2,1)S(1)}, u32[]{:S(2)}, u32[]{:S(2)}) collective-permute-start(bf16[256,1024]{1,0:T(8,128)(2,1)} %bitcast.23), channel_id=1, source_target_pairs={{0,1},{1,2},{2,3},{3,4},{4,5},{5,6},{6,7},{7,8},{8,9},{9,10},{10,1... | collective-permute-start | bytes 1572872 | tf_op jit(solution)/shard_map/ppermute | solution.py:745
  4.6 15.8 %collective-permute-start.1 = (bf16[256,1024]{1,0:T(8,128)(2,1)}, bf16[256,1024]{1,0:T(8,128)(2,1)}, u32[]{:S(2)}, u32[]{:S(2)}) collective-permute-start(bf16[256,1024]{1,0:T(8,128)(2,1)} %bitcast.24), channel_id=1, source_target_pairs={{1,0},{2,1},{3,2},{4,3},{5,4},{6,5},{7,6},{8,7},{9,8},{10,9},{11,1... | collective-permute-start | bytes 1572872 | tf_op jit(solution)/shard_map/ppermute | solution.py:746
  9.4 1.0 copy-start.9
  10.4 9.9 %copy-start = (bf16[1024,1024]{1,0:T(8,128)(2,1)S(1)}, bf16[1024,1024]{1,0:T(8,128)(2,1)}, u32[]{:S(2)}) copy-start(bf16[1024,1024]{1,0:T(8,128)(2,1)} %w_out_ref.5) | copy-start | bytes 6291460
  10.4 9.9 %copy-start.1 = (bf16[1024,128]{1,0:T(8,128)(2,1)S(1)}, bf16[1024,128]{1,0:T(8,128)(2,1)}, u32[]{:S(2)}) copy-start(bf16[1024,128]{1,0:T(8,128)(2,1)} %readout_ref.5) | copy-start | bytes 786436
  31.9 6.6 %collective-permute-start.2 = (f32[256,128]{1,0:T(8,128)S(1)}, f32[256,128]{1,0:T(8,128)S(1)}, u32[]{:S(2)}, u32[]{:S(2)}) collective-permute-start(f32[256,128]{1,0:T(8,128)S(1)} %get-tuple-element.30.own_ref), channel_id=1, source_target_pairs={{0,64},{64,0},{1,65},{65,1},{2,66},{66,2},{3,67},{67,3},{4,68},{68... | collective-permute-start | bytes 393224 | tf_op jit(solution)/shard_map/ppermute | solution.py:760
  35.0 5.1 %copy-start.4 = (f32[256,128]{1,0:T(8,128)S(1)}, f32[256,128]{1,0:T(8,128)}, u32[]{:S(2)}) copy-start(f32[256,128]{1,0:T(8,128)} %target_ref.1) | copy-start | bytes 393220
  38.4 1.6 %collective-permute-start.3 = (f32[2,256,128]{2,1,0:T(8,128)S(1)}, f32[2,256,128]{2,1,0:T(8,128)S(1)}, u32[]{:S(2)}, u32[]{:S(2)}) collective-permute-start(f32[2,256,128]{2,1,0:T(8,128)S(1)} %pad_maximum_fusion), channel_id=1, source_target_pairs={{0,32},{32,0},{1,33},{33,1},{2,34},{34,2},{3,35},{35,3},{4,36},{36... | collective-permute-start | bytes 786440 | tf_op jit(solution)/shard_map/ppermute | solution.py:725
  38.5 17.1 %collective-permute-start.4 = (bf16[1024,256]{1,0:T(8,128)(2,1)S(1)}, bf16[1024,256]{1,0:T(8,128)(2,1)}, u32[]{:S(2)}, u32[]{:S(2)}) collective-permute-start(bf16[1024,256]{1,0:T(8,128)(2,1)S(1)} %get-tuple-element.37), channel_id=1, source_target_pairs={{0,32},{32,0},{1,33},{33,1},{2,34},{34,2},{3,35},{35,3},{4,36},{36... | collective-permute-start | bytes 1572872 | tf_op jit(solution)/shard_map/ppermute | solution.py:725
  43.7 10.2 %copy-start.3 = (bf16[256,1024]{1,0:T(8,128)(2,1)}, bf16[256,1024]{1,0:T(8,128)(2,1)S(1)}, u32[]{:S(2)}) copy-start(bf16[256,1024]{1,0:T(8,128)(2,1)S(1)} %get-tuple-element.40.grad_ref) | copy-start | bytes 1572868
  43.7 10.2 %collective-permute-start.5 = (bf16[256,256]{1,0:T(8,128)(2,1)}, bf16[256,256]{1,0:T(8,128)(2,1)S(1)}, u32[]{:S(2)}, u32[]{:S(2)}) collective-permute-start(bf16[256,256]{1,0:T(8,128)(2,1)} %get-tuple-element.44), channel_id=1, source_target_pairs={{0,1},{1,2},{2,3},{3,4},{4,5},{5,6},{6,7},{7,8},{8,9},{9,10},{10,1... | collective-permute-start | bytes 393224 | tf_op jit(solution)/shard_map/ppermute | solution.py:768
  47.3 7.4 %collective-permute-start.6 = (bf16[256,256]{1,0:T(8,128)(2,1)}, bf16[256,256]{1,0:T(8,128)(2,1)S(1)}, u32[]{:S(2)}, u32[]{:S(2)}) collective-permute-start(bf16[256,256]{1,0:T(8,128)(2,1)} %get-tuple-element.44), channel_id=1, source_target_pairs={{1,0},{2,1},{3,2},{4,3},{5,4},{6,5},{7,6},{8,7},{9,8},{10,9},{11,1... | collective-permute-start | bytes 393224 | tf_op jit(solution)/shard_map/ppermute | solution.py:769
  48.6 7.0 %collective-permute-start.8 = (bf16[1024,256]{1,0:T(8,128)(2,1)}, bf16[1024,256]{1,0:T(8,128)(2,1)}, u32[]{:S(2)}, u32[]{:S(2)}) collective-permute-start(bf16[1024,256]{1,0:T(8,128)(2,1)} %get-tuple-element.46), channel_id=1, source_target_pairs={{0,32},{32,0},{1,33},{33,1},{2,34},{34,2},{3,35},{35,3},{4,36},{36... | collective-permute-start | bytes 1572872 | tf_op jit(solution)/shard_map/ppermute | solution.py:725
  53.8 0.7 copy-start.5
  54.7 0.6 copy-start.7
  55.3 2.3 %collective-permute-start.7 = (bf16[1024,256]{1,0:T(8,128)(2,1)}, bf16[1024,256]{1,0:T(8,128)(2,1)}, u32[]{:S(2)}, u32[]{:S(2)}) collective-permute-start(bf16[1024,256]{1,0:T(8,128)(2,1)} %shard_map.81.piece_ref), channel_id=1, source_target_pairs={{0,32},{32,0},{1,33},{33,1},{2,34},{34,2},{3,35},{35,3},{4,36},{36... | collective-permute-start | bytes 1572872 | tf_op jit(solution)/shard_map/ppermute | solution.py:725
  57.6 0.9 copy-start.6
  58.5 0.9 copy-start.8
  61.8 1.1 copy-start.2
  62.9 35.8 %all-to-all-start = ((bf16[64,8,1280]{2,1,0:T(8,128)(2,1)}), bf16[64,8,1280]{2,1,0:T(8,128)(2,1)}, u32[]{:S(2)}, u32[]{:S(2)}) async-start(bf16[64,8,1280]{2,1,0:T(8,128)(2,1)} %bitcast.20), calls=%async_computation | async-start | bytes 2621440 | tf_op jit(solution)/shard_map/all_to_all | solution.py:730
  87.4 2.7 %collective-permute-start.9 = (bf16[2048,256]{1,0:T(8,128)(2,1)S(1)}, bf16[2048,256]{1,0:T(8,128)(2,1)S(1)}, u32[]{:S(2)}, u32[]{:S(2)}) collective-permute-start(bf16[2048,256]{1,0:T(8,128)(2,1)S(1)} %bitcast.16), channel_id=1, source_target_pairs={{0,32},{32,0},{1,33},{33,1},{2,34},{34,2},{3,35},{35,3},{4,36},{36... | collective-permute-start | bytes 3145736 | tf_op jit(solution)/shard_map/ppermute | solution.py:725
  98.7 5.6 %copy-start.10 = (f32[256,128]{1,0:T(8,128)S(1)}, f32[256,128]{1,0:T(8,128)}, u32[]{:S(2)}) copy-start(f32[256,128]{1,0:T(8,128)} %get-tuple-element.36) | copy-start | bytes 393220
  98.7 35.6 %all-to-all-start.1 = ((bf16[64,8,2048]{2,1,0:T(8,128)(2,1)}), bf16[64,8,2048]{2,1,0:T(8,128)(2,1)S(1)}, u32[]{:S(2)}, u32[]{:S(2)}) async-start(bf16[64,8,2048]{2,1,0:T(8,128)(2,1)} %bitcast.14), calls=%async_computation.1 | async-start | bytes 4194304 | tf_op jit(solution)/shard_map/all_to_all | solution.py:730

commit v16 on v12

--- a/solution.py
+++ b/solution.py
@@ -269,8 +269,68 @@
     shape = (128, 128)
     apart = iota(shape, 0) - iota(shape, 1)
     first = jnp.where(apart >= 0, window[:128], fill)
-    last = jnp.where(apart <= 0, window[512:], fill)
-    return first, window[128:512], last
+    last = jnp.where(apart <= 0, window[-128:], fill)
+    return first, window[128:-128], last
+
+
+def own_kernel(counts_ref, q_ref, k_ref, v_ref, probs, mixed_ref, top_ref, total_ref):
+    step = pl.program_id(0)
+    fill = key_fill([(counts_ref[1], BLOCK)])
+    low = iota((BLOCK, PAIR), 1) < HEAD_WIDTH
+    query_fill = (spare_lane((BLOCK, PAIR)) == 3).astype(BF)
+    ones = jnp.ones((16, BLOCK), BF)
+    scores, turned = [], []
+    for pair in range(2):
+        columns = slice(pair * PAIR, (pair + 1) * PAIR)
+        q_pair = q_ref[:, columns] * jnp.asarray(HEAD_WIDTH ** (-0.5), BF)
+        k_pair = k_ref[:, columns]
+        turned.append(v_ref[:, columns].T)
+        for half in range(2):
+            pick = low if half == 0 else ~low
+            scores.append(
+                dot_nt(jnp.where(pick, k_pair, fill), jnp.where(pick, q_pair, query_fill))
+            )
+    for slot in range(4):
+        top = jnp.max(scores[slot], axis=0, keepdims=True)
+        probs[slot] = jnp.exp(scores[slot] - top).astype(BF)
+        top_ref[pl.ds(step * 4 + slot, 1), :] = top
+    for slot in range(4):
+        lanes = slice(slot % 2 * HEAD_WIDTH, (slot % 2 + 1) * HEAD_WIDTH)
+        values = jnp.concatenate([turned[slot // 2][lanes], ones], axis=0)
+        mixed = dot_nn(values, probs[slot])
+        mixed_ref[slot * HEAD_WIDTH : (slot + 1) * HEAD_WIDTH] = mixed[:HEAD_WIDTH]
+        total_ref[pl.ds(step * 4 + slot, 1), :] = mixed[HEAD_WIDTH : HEAD_WIDTH + 1]
+
+
+def own_part(counts, projected):
+    part = lambda rows, first: pl.BlockSpec((rows, WIDTH), lambda j: (0, first + j))
+    whole = pl.BlockSpec((HEADS, BLOCK), lambda j: (0, 0))
+    return pl.pallas_call(
+        own_kernel,
+        grid=(4,),
+        in_specs=[
+            pl.BlockSpec(memory_space=pltpu.SMEM),
+            part(BLOCK, 0),
+            part(BLOCK, 4),
+            part(BLOCK, 8),
+        ],
+        out_specs=[
+            pl.BlockSpec((4, BLOCK, BLOCK), lambda j: (j, 0, 0)),
+            pl.BlockSpec((WIDTH, BLOCK), lambda j: (j, 0)),
+            whole,
+            whole,
+        ],
+        out_shape=[
+            jax.ShapeDtypeStruct((HEADS, BLOCK, BLOCK), BF),
+            jax.ShapeDtypeStruct((1024, BLOCK), F32),
+            jax.ShapeDtypeStruct((HEADS, BLOCK), F32),
+            jax.ShapeDtypeStruct((HEADS, BLOCK), F32),
+        ],
+        compiler_params=pltpu.CompilerParams(vmem_limit_bytes=14 * 1024 * 1024),
+        cost_estimate=pl.CostEstimate(
+            flops=1 << 30, bytes_accessed=4 << 20, transcendentals=1 << 20
+        ),
+    )(counts, projected, projected, projected)
 
 
 def forward_kernel(
@@ -280,19 +340,21 @@
     latent_ref,
     weight_ref,
     q_ref,
-    k_ref,
-    v_ref,
+    own_mixed_ref,
+    own_top_ref,
+    own_total_ref,
     w_out_ref,
     readout_ref,
     normed_ref,
-    kcat_ref,
-    vcat_ref,
+    khalo_ref,
+    vhalo_ref,
     attended_ref,
     stats_ref,
     hidden_ref,
     forecast_ref,
     probs,
     inverse_ref,
+    own_inverse_ref,
     stat_rows,
     buffer,
     arrived,
@@ -309,15 +371,9 @@
 
     fetch_one(weight_ref, buffer, arrived, WIDTH, 1024, step).wait()
     fetch_one(weight_ref, buffer, arrived, WIDTH, 1024, step + 4).wait()
-    khalo = dot_nn(normed_ref[...], buffer[step]).astype(BF)
-    kcat_ref[:WIN] = khalo[:WIN]
-    kcat_ref[WIN : WIN + BLOCK] = k_ref[...]
-    kcat_ref[WIN + BLOCK :] = khalo[WIN:]
-    vhalo = dot_nn(normed_ref[...], buffer[step + 4]).astype(BF)
-    vcat_ref[:WIN] = vhalo[:WIN]
-    vcat_ref[WIN : WIN + BLOCK] = v_ref[...]
-    vcat_ref[WIN + BLOCK :] = vhalo[WIN:]
-    fill = key_fill([(counts_ref[0], WIN), (counts_ref[1], BLOCK), (counts_ref[2], WIN)])
+    khalo_ref[...] = dot_nn(normed_ref[...], buffer[step]).astype(BF)
+    vhalo_ref[...] = dot_nn(normed_ref[...], buffer[step + 4]).astype(BF)
+    fill = key_fill([(counts_ref[0], WIN), (counts_ref[2], WIN)])
     low_q = iota((BLOCK, PAIR), 1) < HEAD_WIDTH
     low_k = iota(fill.shape, 1) < HEAD_WIDTH
     query_fill = (spare_lane((BLOCK, PAIR)) == 3).astype(BF)
@@ -325,8 +381,8 @@
     for pair in range(2):
         columns = slice(pair * PAIR, (pair + 1) * PAIR)
         q_pair = q_ref[:, columns] * jnp.asarray(HEAD_WIDTH ** (-0.5), BF)
-        k_pair = kcat_ref[:, columns]
-        turned.append(vcat_ref[:, columns].T)
+        k_pair = khalo_ref[:, columns]
+        turned.append(vhalo_ref[:, columns].T)
         for half in range(2):
             if half == 0:
                 q_head = jnp.where(low_q, q_pair, query_fill)
@@ -339,20 +395,21 @@
     for slot in range(4):
         levels = []
         for tile in range(2):
-            rows = slice(tile * 128, tile * 128 + 640)
+            rows = slice(tile * 128, tile * 128 + 384)
             lanes = slice(tile * 128, tile * 128 + 128)
             first, middle, last = keep_band(scores[slot][rows, lanes], NEVER)
             top = jnp.maximum(
                 jnp.max(middle, axis=0, keepdims=True),
                 jnp.max(jnp.maximum(first, last), axis=0, keepdims=True),
             )
+            top = jnp.maximum(top, own_top_ref[pl.ds(step * 4 + slot, 1), :][:, lanes])
             start = tile * 128
             probs[slot, start : start + 128, lanes] = jnp.exp(first - top).astype(BF)
-            probs[slot, start + 128 : start + 512, lanes] = jnp.exp(middle - top).astype(BF)
-            probs[slot, start + 512 : start + 640, lanes] = jnp.exp(last - top).astype(BF)
+            probs[slot, start + 128 : start + 256, lanes] = jnp.exp(middle - top).astype(BF)
+            probs[slot, start + 256 : start + 384, lanes] = jnp.exp(last - top).astype(BF)
             levels.append(top)
         probs[slot, :128, 128:] = jnp.zeros((128, 128), BF)
-        probs[slot, 640:, :128] = jnp.zeros((128, 128), BF)
+        probs[slot, 384:, :128] = jnp.zeros((128, 128), BF)
         tops.append(jnp.concatenate(levels, axis=1))
     ones = jnp.ones((16, fill.shape[0]), BF)
     for pair in range(2):
@@ -362,10 +419,15 @@
             lanes = slice(half * HEAD_WIDTH, (half + 1) * HEAD_WIDTH)
             values = jnp.concatenate([turned[pair][lanes], ones], axis=0)
             mixed = dot_nn(values, probs[slot])
+            head = step * 4 + slot
+            fade = jnp.exp(own_top_ref[pl.ds(head, 1), :] - tops[slot])
             total = mixed[HEAD_WIDTH : HEAD_WIDTH + 1]
+            total += own_total_ref[pl.ds(head, 1), :] * fade
             inverse = 1.0 / total
-            halves.append(mixed[:HEAD_WIDTH] * inverse)
-            head = step * 4 + slot
+            own_inverse = fade * inverse
+            own_mixed = own_mixed_ref[slot * HEAD_WIDTH : (slot + 1) * HEAD_WIDTH]
+            halves.append(mixed[:HEAD_WIDTH] * inverse + own_mixed * own_inverse)
+            own_inverse_ref[pl.ds(head, 1), :] = own_inverse
             inverse_ref[pl.ds(head, 1), :] = inverse
             stat_rows[pl.ds(head, 1), :] = tops[slot] + jnp.log(total)
         start = pl.multiple_of(step * WIDTH + pair * PAIR, PAIR)
@@ -381,7 +443,7 @@
         stats_ref[...] = stat_rows[...].T
 
 
-def forward(counts, left, right, latent_own, w_qkv, projected, w_out, readout_weight):
+def forward(counts, left, right, latent_own, w_qkv, projected, own, w_out, readout_weight):
     whole = lambda *shape: pl.BlockSpec(shape, lambda j: (0, 0))
     part = lambda rows, first: pl.BlockSpec((rows, WIDTH), lambda j: (0, first + j))
     window = 2 * WIN + BLOCK
@@ -395,31 +457,34 @@
             whole(BLOCK, 1024),
             HBM,
             part(BLOCK, 0),
-            part(BLOCK, 4),
-            part(BLOCK, 8),
+            pl.BlockSpec((WIDTH, BLOCK), lambda j: (j, 0)),
+            whole(HEADS, BLOCK),
+            whole(HEADS, BLOCK),
             whole(1024, 1024),
             whole(1024, 128),
         ],
         out_specs=[
             whole(2 * WIN, 1024),
-            part(window, 0),
-            part(window, 0),
+            part(2 * WIN, 0),
+            part(2 * WIN, 0),
             whole(BLOCK, 1024),
             whole(BLOCK, 128),
             whole(BLOCK, 1024),
             whole(BLOCK, 128),
-            pl.BlockSpec((4, window, BLOCK), lambda j: (j, 0, 0)),
+            pl.BlockSpec((4, 2 * WIN, BLOCK), lambda j: (j, 0, 0)),
+            whole(HEADS, BLOCK),
             whole(HEADS, BLOCK),
         ],
         out_shape=[
             jax.ShapeDtypeStruct((2 * WIN, 1024), BF),
-            jax.ShapeDtypeStruct((window, 1024), BF),
-            jax.ShapeDtypeStruct((window, 1024), BF),
+            jax.ShapeDtypeStruct((2 * WIN, 1024), BF),
+            jax.ShapeDtypeStruct((2 * WIN, 1024), BF),
             jax.ShapeDtypeStruct((BLOCK, 1024), F32),
             jax.ShapeDtypeStruct((BLOCK, 128), F32),
             jax.ShapeDtypeStruct((BLOCK, 1024), BF),
             jax.ShapeDtypeStruct((BLOCK, 128), F32),
-            jax.ShapeDtypeStruct((HEADS, window, BLOCK), BF),
+            jax.ShapeDtypeStruct((HEADS, 2 * WIN, BLOCK), BF),
+            jax.ShapeDtypeStruct((HEADS, BLOCK), F32),
             jax.ShapeDtypeStruct((HEADS, BLOCK), F32),
         ],
         scratch_shapes=[
@@ -438,8 +503,7 @@
         latent_own,
         in_hbm(w_qkv),
         projected,
-        projected,
-        projected,
+        *own,
         w_out,
         readout_weight,
     )
@@ -527,57 +591,93 @@
 
 
 def query_kernel(
-    kcat_ref, vcat_ref, grad_ref, packed_ref, probs_ref, inverse_ref, dq_ref, dscores
+    k_ref,
+    v_ref,
+    khalo_ref,
+    vhalo_ref,
+    grad_ref,
+    packed_ref,
+    probs_ref,
+    own_probs_ref,
+    inverse_ref,
+    own_inverse_ref,
+    dq_ref,
+    dscores,
+    own_dscores,
 ):
     step = pl.program_id(0)
-    window = kcat_ref.shape[0]
-    value_fill = (spare_lane((window, PAIR)) < 3).astype(BF)
     low_q = iota((BLOCK, PAIR), 1) < HEAD_WIDTH
-    low_k = iota((window, PAIR), 1) < HEAD_WIDTH
+    low_k = iota((2 * WIN, PAIR), 1) < HEAD_WIDTH
+    own_fill = (spare_lane((BLOCK, PAIR)) < 3).astype(BF)
+    halo_fill = (spare_lane((2 * WIN, PAIR)) < 3).astype(BF)
     g_fill = dot_nn(packed_ref[:, 128:], stat_spread(step, HEADS)).astype(BF)
     turned = []
     for pair in range(2):
         columns = slice(pair * PAIR, (pair + 1) * PAIR)
         g_pair = grad_ref[:, columns]
-        v_pair = vcat_ref[:, columns]
-        k_turned = kcat_ref[:, columns].T
+        own_turned = k_ref[:, columns].T
+        halo_turned = khalo_ref[:, columns].T
         for half in range(2):
             slot = pair * 2 + half
             pick_q = low_q if half == 0 else ~low_q
             pick_k = low_k if half == 0 else ~low_k
             g_head = jnp.where(pick_q, g_pair, g_fill[:, columns])
-            v_head = jnp.where(pick_k, v_pair, value_fill)
-            change = dot_nt(v_head, g_head)
+            own_change = dot_nt(jnp.where(pick_q, v_ref[:, columns], own_fill), g_head)
+            own_dscores[slot] = (own_probs_ref[slot].astype(F32) * own_change).astype(BF)
+            change = dot_nt(jnp.where(pick_k, vhalo_ref[:, columns], halo_fill), g_head)
             dscores[slot] = (probs_ref[slot].astype(F32) * change).astype(BF)
-            turned.append(k_turned[half * HEAD_WIDTH : (half + 1) * HEAD_WIDTH])
+            lanes = slice(half * HEAD_WIDTH, (half + 1) * HEAD_WIDTH)
+            turned.append((own_turned[lanes], halo_turned[lanes]))
     for slot in range(4):
-        scale = inverse_ref[pl.ds(step * 4 + slot, 1), :] * HEAD_WIDTH ** (-0.5)
-        dquery = dot_nn(turned[slot], dscores[slot]) * scale
-        dq_ref[slot * HEAD_WIDTH : (slot + 1) * HEAD_WIDTH] = dquery.astype(BF)
-
-
-def query_grads(kcat, vcat, grad, packed, probs, inverse):
+        row = pl.ds(step * 4 + slot, 1)
+        dquery = dot_nn(turned[slot][0], own_dscores[slot]) * own_inverse_ref[row, :]
+        dquery += dot_nn(turned[slot][1], dscores[slot]) * inverse_ref[row, :]
+        dq_ref[slot * HEAD_WIDTH : (slot + 1) * HEAD_WIDTH] = (
+            dquery * HEAD_WIDTH ** (-0.5)
+        ).astype(BF)
+
+
+def query_grads(projected, khalo, vhalo, grad, packed, probs, own_probs, inverse, own_inverse):
     part = lambda rows, first: pl.BlockSpec((rows, WIDTH), lambda j: (0, first + j))
-    window = 2 * WIN + BLOCK
+    heads = lambda rows: pl.BlockSpec((4, rows, BLOCK), lambda j: (j, 0, 0))
+    whole = pl.BlockSpec((HEADS, BLOCK), lambda j: (0, 0))
     return pl.pallas_call(
         query_kernel,
         grid=(4,),
         in_specs=[
-            part(window, 0),
-            part(window, 0),
+            part(BLOCK, 4),
+            part(BLOCK, 8),
+            part(2 * WIN, 0),
+            part(2 * WIN, 0),
             part(BLOCK, 0),
             pl.BlockSpec((BLOCK, 256), lambda j: (0, 0)),
-            pl.BlockSpec((4, window, BLOCK), lambda j: (j, 0, 0)),
-            pl.BlockSpec((HEADS, BLOCK), lambda j: (0, 0)),
+            heads(2 * WIN),
+            heads(BLOCK),
+            whole,
+            whole,
         ],
         out_specs=pl.BlockSpec((WIDTH, BLOCK), lambda j: (j, 0)),
         out_shape=jax.ShapeDtypeStruct((1024, BLOCK), BF),
-        scratch_shapes=[pltpu.VMEM((4, window, BLOCK), BF)],
+        scratch_shapes=[
+            pltpu.VMEM((4, 2 * WIN, BLOCK), BF),
+            pltpu.VMEM((4, BLOCK, BLOCK), BF),
+        ],
         compiler_params=pltpu.CompilerParams(vmem_limit_bytes=16 * 1024 * 1024),
         cost_estimate=pl.CostEstimate(
             flops=6 << 30, bytes_accessed=5 << 20, transcendentals=3 << 20
         ),
-    )(kcat, vcat, grad, packed, probs, inverse)
+    )(
+        projected,
+        projected,
+        khalo,
+        vhalo,
+        grad,
+        packed,
+        probs,
+        own_probs,
+        inverse,
+        own_inverse,
+    )
 
 
 def key_kernel(
@@ -743,8 +843,20 @@
 
     projected, turned = project(latent_own, w_qkv)
     turned_other = swap_core(turned)
-    normed_halo, kcat, vcat, attended, stats, hidden, forecast, probs, inverse = forward(
-        scalars, from_left, from_right, latent_own, w_qkv, projected, w_out, readout_weight
+    own_probs, *own = own_part(scalars, projected)
+    (
+        normed_halo,
+        khalo,
+        vhalo,
+        attended,
+        stats,
+        hidden,
+        forecast,
+        probs,
+        inverse,
+        own_inverse,
+    ) = forward(
+        scalars, from_left, from_right, latent_own, w_qkv, projected, own, w_out, readout_weight
     )
     near = lax.ppermute(forecast, "x_hi", SWAP)
     qhalo = halo_queries(normed_halo, w_qkv)
@@ -757,7 +869,9 @@
     packed_left = lax.ppermute(sent, CELLS, up)
     packed_right = lax.ppermute(sent, CELLS, down)
 
-    dquery = query_grads(kcat, vcat, grad, packed, probs, inverse)
+    dquery = query_grads(
+        projected, khalo, vhalo, grad, packed, probs, own_probs, inverse, own_inverse
+    )
     dquery, packed_left, packed_right = lax.optimization_barrier(
         (dquery, packed_left, packed_right)
     )

time: 134 us -> 132 us (0.985)
  waiting for transfers between devices: 43.7 us -> 40.3 us
  Pallas kernels: 44.9 us -> 46.6 us
    pallas_call x1 -> x2, Pallas kernels: 5.29 us -> 8.73 us  [the longest x1 5.42 us: query_grads(): pl.pallas_call(query_kernel, grid=(4,), in_specs=[part(BLOCK, 4), part(BL...]
    ppermute x1, waiting for transfers between devices: 4.3 us -> 2.39 us  [per_device(): from_right = lax.ppermute(latent_own, CELLS, down)]
    pallas_call x1, Pallas kernels: 11.6 us -> 10 us  [forward(): pl.pallas_call(forward_kernel, grid=(4,), in_specs=[pl.BlockSpec(memory_s...]
    ppermute x1, waiting for transfers between devices: 1.52 us -> 0.01 us  [per_device(): from_left = lax.ppermute(latent_own, CELLS, up)]
    unnamed x17 -> x19, local copies, waits for them, and re-layouts: 3.08 us -> 3.1 us
  transfers between devices with their start and end apart: 12 -> 12, of which waited for: 8 -> 7; matrix products, arithmetic and copies ran while one was open for 4% -> 4% of each run, Pallas kernels for 23% -> 25%
where the time goes in v16:
time: 132 us
  Pallas kernels  46.6 us (35%)
  waiting for transfers between devices  40.3 us (31%)
  starting transfers between devices  34.5 us (26%)
  local copies, waits for them, and re-layouts  4.63 us (4%)
  other arithmetic  3.26 us (2%)
  between operations  2.16 us (2%)
    all_to_all x2, waiting for transfers between devices, scatter(): lax.all_to_all(partial.reshape(64, 8, columns), CHIPS, split_axis=0, conc...  31.9 us
    all_to_all x2, starting transfers between devices, scatter(): lax.all_to_all(partial.reshape(64, 8, columns), CHIPS, split_axis=0, conc...  19.9 us
    pallas_call x1, Pallas kernels, key_grads(): pl.pallas_call(key_kernel, grid=(4,), in_specs=[pl.BlockSpec(memory_space...  10.3 us
    pallas_call x1, Pallas kernels, forward(): pl.pallas_call(forward_kernel, grid=(4,), in_specs=[pl.BlockSpec(memory_s...  10 us
    pallas_call x2, Pallas kernels, partial_sums(): pl.pallas_call(functools.partial(partial_kernel, len(smalls)), in_specs=[...  6.93 us
    ppermute x5, waiting for transfers between devices, swap_core(): return lax.ppermute(values, 'core', SWAP)  5.55 us
    pallas_call x1, Pallas kernels, query_grads(): pl.pallas_call(query_kernel, grid=(4,), in_specs=[part(BLOCK, 4), part(BL...  5.42 us
    ppermute x1, starting transfers between devices, per_device(): from_left = lax.ppermute(latent_own, CELLS, up)  4.72 us
  transfers between devices with their start and end apart: 12, of which 7 were waited for; matrix products, arithmetic and copies ran while one was open for 4% of the time, Pallas kernels for 25%

profile of v16, /device:TPU:0, one launch (start us, length us, event | category | flops | bytes accessed | tf_op | source)
XLA Modules:
  0.0 131.7 jit_solution(11908939465637503828)
XLA Ops:
  0.6 4.7 %collective-permute-start = (bf16[256,1024]{1,0:T(8,128)(2,1)}, bf16[256,1024]{1,0:T(8,128)(2,1)}, u32[]{:S(2)}, u32[]{:S(2)}) collective-permute-start(bf16[256,1024]{1,0:T(8,128)(2,1)} %bitcast.22), channel_id=1, source_target_pairs={{0,1},{1,2},{2,3},{3,4},{4,5},{5,6},{6,7},{7,8},{8,9},{9,10},{10,1... | collective-permute-start | bytes 1572872 | tf_op jit(solution)/shard_map/ppermute | solution.py:834
  5.4 1.3 collective-permute-start.1
  6.7 1.4 %fusion.2 = (s32[1]{0:T(128)}, s32[1]{0:T(128)}, s32[1]{0:T(128)}) fusion(s32[32]{0:T(128)} %param.7, s32[]{:T(128)S(6)} %max.3, s32[]{:T(128)S(6)} %select_n.19, s32[]{:T(128)S(6)} %select_n.18), kind=kLoop, calls=%fused_computation.8 | loop fusion | bytes 36 | tf_op jit(solution)/shard_map/dynamic_slice | solution.py:838
  10.1 1.0 copy-done.4
  11.2 4.0 %shard_map.77 = (bf16[256,3072]{1,0:T(8,128)(2,1)S(1)}, bf16[1024,256]{1,0:T(8,128)(2,1)S(1)}) custom-call(bf16[256,1024]{1,0:T(8,128)(2,1)S(1)} %bitcast.24, bf16[1024,3072]{1,0:T(8,128)(2,1)} %weight_ref.5), custom_call_target="tpu_custom_call" | custom-call | flops 2147483648 | bytes 8388608 | tf_op jit(solution)/shard_map/pallas_call | solution.py:99
  15.2 3.3 %shard_map.78 = (bf16[16,256,256]{2,1,0:T(8,128)(2,1)S(1)}, f32[1024,256]{1,0:T(8,128)S(1)}, f32[16,256]{1,0:T(8,128)S(1)}, f32[16,256]{1,0:T(8,128)S(1)}) custom-call(s32[3]{0:T(128)S(1)} %pad_add_fusion.counts_ref, bf16[256,3072]{1,0:T(8,128)(2,1)S(1)} %get-tuple-element.32.q_ref.k_ref.v_ref, bf16[256,3072]{1,0:T(8,128)(2,1)S(1)} %get-tuple-element.32.q_ref.k_ref.v_ref, ...), custom_call_target="tpu_custom_call" | custom-call | flops 1073741824 | bytes 4194304 | tf_op jit(solution)/shard_map/pallas_call | solution.py:308
  18.5 2.4 %collective-permute-done.1.right_ref = bf16[256,1024]{1,0:T(8,128)(2,1)} collective-permute-done((bf16[256,1024]{1,0:T(8,128)(2,1)}, bf16[256,1024]{1,0:T(8,128)(2,1)}, u32[]{:S(2)}, u32[]{:S(2)}) %collective-permute-start.1) | collective-permute-done | bytes 524320 | tf_op jit(solution)/shard_map/ppermute | solution.py:835
  20.9 10.0 %shard_map.79 = (bf16[512,1024]{1,0:T(8,128)(2,1)S(1)}, bf16[512,1024]{1,0:T(8,128)(2,1)S(1)}, bf16[512,1024]{1,0:T(8,128)(2,1)S(1)}, f32[256,1024]{1,0:T(8,128)...) custom-call(s32[3]{0:T(128)S(1)} %pad_add_fusion.counts_ref, ...), custom_call_target="tpu_custom_call" | custom-call | flops 6442450944 | bytes 12582912 | tf_op jit(solution)/shard_map/pallas_call | solution.py:450
  31.0 3.1 %collective-permute-start.2 = (f32[256,128]{1,0:T(8,128)S(1)}, f32[256,128]{1,0:T(8,128)S(1)}, u32[]{:S(2)}, u32[]{:S(2)}) collective-permute-start(f32[256,128]{1,0:T(8,128)S(1)} %get-tuple-element.36.own_ref), channel_id=1, source_target_pairs={{0,64},{64,0},{1,65},{65,1},{2,66},{66,2},{3,67},{67,3},{4,68},{68... | collective-permute-start | bytes 393224 | tf_op jit(solution)/shard_map/ppermute | solution.py:861
  34.1 3.0 %shard_map.80.qhalo_ref = bf16[512,1024]{1,0:T(8,128)(2,1)S(1)} custom-call(bf16[512,1024]{1,0:T(8,128)(2,1)S(1)} %get-tuple-element.37.normed_ref, bf16[1024,3072]{1,0:T(8,128)(2,1)} %weight_ref.5), custom_call_target="tpu_custom_call" | custom-call | tf_op jit(solution)/shard_map/pallas_call | solution.py:137
  39.2 3.6 %shard_map.81 = (f32[256,128]{1,0:T(8,128)}, bf16[256,256]{1,0:T(8,128)(2,1)S(1)}, bf16[256,256]{1,0:T(8,128)(2,1)}, bf16[256,1024]{1,0:T(8,128)(2,1)S(1)}, bf16[1024,256]{1,0:T(8,128)(2,1)}) custom-call(s32[3]{0:T(128)S(1)} %pad_add_fusion.counts_ref, f32[256,128]{1,0:T(8,128)S(1)} %get-tuple-element.36.own_ref, ...), custom_call_target="tpu_custom_call" | custom-call | tf_op jit(solution)/shard_map/pallas_call | solution.py:578
  42.8 3.0 %collective-permute-start.5 = (bf16[256,256]{1,0:T(8,128)(2,1)}, bf16[256,256]{1,0:T(8,128)(2,1)S(1)}, u32[]{:S(2)}, u32[]{:S(2)}) collective-permute-start(bf16[256,256]{1,0:T(8,128)(2,1)} %get-tuple-element.52), channel_id=1, source_target_pairs={{0,1},{1,2},{2,3},{3,4},{4,5},{5,6},{6,7},{7,8},{8,9},{9,10},{10,1... | collective-permute-start | bytes 393224 | tf_op jit(solution)/shard_map/ppermute | solution.py:869
  45.8 1.3 collective-permute-start.6
  47.2 5.4 %shard_map.82.piece_ref = bf16[1024,256]{1,0:T(8,128)(2,1)} custom-call(bf16[256,3072]{1,0:T(8,128)(2,1)S(1)} %get-tuple-element.32.q_ref.k_ref.v_ref, bf16[256,3072]{1,0:T(8,128)(2,1)S(1)} %get-tuple-element.32.q_ref.k_ref.v_ref, bf16[512,1024]{1,0:T(8,128)(2,1)S(1)} %get-tuple-element.44.khalo_ref, bf16[512,1024]{1,0:T(8,128)(2,1)S(1)} %get-tuple-element.45.vhalo_ref, ...), custom_call_target="tpu_custom_call" | custom-call | flops 6442450944 | bytes 5242880 | tf_op jit(solution)/shard_map/pallas_call | solution.py:644
  54.4 1.9 %collective-permute-done.7.other_ref = bf16[1024,256]{1,0:T(8,128)(2,1)} collective-permute-done((bf16[1024,256]{1,0:T(8,128)(2,1)}, bf16[1024,256]{1,0:T(8,128)(2,1)}, u32[]{:S(2)}, u32[]{:S(2)}) %collective-permute-start.7) | collective-permute-done | bytes 524320 | tf_op jit(solution)/shard_map/ppermute | solution.py:814
  56.3 3.1 %shard_map.83 = bf16[512,1280]{1,0:T(8,128)(2,1)} custom-call(s32[1]{0:T(128)} %bitcast.7.core_ref, bf16[2,2,256,256]{3,2,1,0:T(8,128)(2,1)S(1)} %bitcast.18, bf16[2,2,256,256]{3,2,1,0:T(8,128)(2,1)} %bitcast.9.normed_other_ref, bf16[1024,256]{1,0:T(8,128)(2,1)} %shard_map.82.piece_ref, bf16[1024,256]{1,0:T(8,128)(2,1)} %collective-permute-done.7.other_ref, ...), custom_call_target="tpu_custom_call" | custom-call | tf_op jit(solution)/shard_map/pallas_call | solution.py:217
  59.4 14.1 %all-to-all-start = ((bf16[64,8,1280]{2,1,0:T(8,128)(2,1)}), bf16[64,8,1280]{2,1,0:T(8,128)(2,1)}, u32[]{:S(2)}, u32[]{:S(2)}) async-start(bf16[64,8,1280]{2,1,0:T(8,128)(2,1)} %bitcast.13), calls=%async_computation | async-start | bytes 2621440 | tf_op jit(solution)/shard_map/all_to_all | solution.py:819
  73.5 10.3 %shard_map.84 = bf16[2,1024,256]{2,1,0:T(8,128)(2,1)S(1)} custom-call(s32[3]{0:T(128)S(1)} %pad_add_fusion.counts_ref, bf16[256,3072]{1,0:T(8,128)(2,1)S(1)} %get-tuple-element.32.q_ref.k_ref.v_ref, bf16[256,3072]{1,0:T(8,128)(2,1)S(1)} %get-tuple-element.32.q_ref.k_ref.v_ref, bf16[256,3072]{1,0:T(8,128)(2,1)S(1)} %get-tuple-element.32.q_ref.k_ref.v_ref, ...), custom_call_target="tpu_custom_call" | custom-call | tf_op jit(solution)/shard_map/pallas_call | solution.py:766
  84.0 2.6 %collective-permute-done.9.other_ref = bf16[2048,256]{1,0:T(8,128)(2,1)S(1)} collective-permute-done((bf16[2048,256]{1,0:T(8,128)(2,1)S(1)}, bf16[2048,256]{1,0:T(8,128)(2,1)S(1)}, u32[]{:S(2)}, u32[]{:S(2)}) %collective-permute-start.9) | collective-permute-done | bytes 1048608 | tf_op jit(solution)/shard_map/ppermute | solution.py:814
  86.6 3.8 %shard_map.85 = bf16[512,2048]{1,0:T(8,128)(2,1)} custom-call(s32[1]{0:T(128)} %bitcast.7.core_ref, bf16[2,2,256,256]{3,2,1,0:T(8,128)(2,1)S(1)} %bitcast.19, bf16[2,2,256,256]{3,2,1,0:T(8,128)(2,1)} %bitcast.9.normed_other_ref, bf16[2048,256]{1,0:T(8,128)(2,1)S(1)} %bitcast.17, bf16[2048,256]{1,0:T(8,128)(2,1)S(1)} %collective-permute-done.9.other_ref), custom_call_target="tpu_custom_call" | custom-call | tf_op jit(solution)/shard_map/pallas_call | solution.py:217
  90.4 4.6 %all-to-all-done = bf16[64,8,1280]{2,1,0:T(8,128)(2,1)} async-done(((bf16[64,8,1280]{2,1,0:T(8,128)(2,1)}), bf16[64,8,1280]{2,1,0:T(8,128)(2,1)}, u32[]{:S(2)}, u32[]{:S(2)}) %all-to-all-start) | async-done | bytes 1310752 | tf_op jit(solution)/shard_map/all_to_all | solution.py:819
  95.0 5.8 %all-to-all-start.1 = ((bf16[64,8,2048]{2,1,0:T(8,128)(2,1)}), bf16[64,8,2048]{2,1,0:T(8,128)(2,1)S(1)}, u32[]{:S(2)}, u32[]{:S(2)}) async-start(bf16[64,8,2048]{2,1,0:T(8,128)(2,1)} %bitcast.14), calls=%async_computation.1 | async-start | bytes 4194304 | tf_op jit(solution)/shard_map/all_to_all | solution.py:819
  101.6 1.5 %convert_reduce_fusion.1 = f32[8,1280]{1,0:T(8,128)S(1)} fusion(bf16[64,8,1280]{2,1,0:T(8,128)(2,1)} %all-to-all-done), kind=kLoop, calls=%fused_computation.1 | loop fusion | flops 1300480 | bytes 1351680 | tf_op jit(solution)/shard_map/reduce_sum | solution.py:823
  103.4 27.3 %all-to-all-done.1 = bf16[64,8,2048]{2,1,0:T(8,128)(2,1)S(1)} async-done(((bf16[64,8,2048]{2,1,0:T(8,128)(2,1)}), bf16[64,8,2048]{2,1,0:T(8,128)(2,1)S(1)}, u32[]{:S(2)}, u32[]{:S(2)}) %all-to-all-start.1) | async-done | bytes 2097184 | tf_op jit(solution)/shard_map/all_to_all | solution.py:819
  (38 shorter events, 6.9 us)
Async XLA Ops:
  0.6 17.9 %collective-permute-start = (bf16[256,1024]{1,0:T(8,128)(2,1)}, bf16[256,1024]{1,0:T(8,128)(2,1)}, u32[]{:S(2)}, u32[]{:S(2)}) collective-permute-start(bf16[256,1024]{1,0:T(8,128)(2,1)} %bitcast.22), channel_id=1, source_target_pairs={{0,1},{1,2},{2,3},{3,4},{4,5},{5,6},{6,7},{7,8},{8,9},{9,10},{10,1... | collective-permute-start | bytes 1572872 | tf_op jit(solution)/shard_map/ppermute | solution.py:834
  5.4 15.6 %collective-permute-start.1 = (bf16[256,1024]{1,0:T(8,128)(2,1)}, bf16[256,1024]{1,0:T(8,128)(2,1)}, u32[]{:S(2)}, u32[]{:S(2)}) collective-permute-start(bf16[256,1024]{1,0:T(8,128)(2,1)} %bitcast.23), channel_id=1, source_target_pairs={{1,0},{2,1},{3,2},{4,3},{5,4},{6,5},{7,6},{8,7},{9,8},{10,9},{11,1... | collective-permute-start | bytes 1572872 | tf_op jit(solution)/shard_map/ppermute | solution.py:835
  10.1 1.0 copy-start.4
  15.2 5.8 %copy-start = (bf16[1024,1024]{1,0:T(8,128)(2,1)S(1)}, bf16[1024,1024]{1,0:T(8,128)(2,1)}, u32[]{:S(2)}) copy-start(bf16[1024,1024]{1,0:T(8,128)(2,1)} %w_out_ref.5) | copy-start | bytes 6291460
  15.2 5.8 %copy-start.1 = (bf16[1024,128]{1,0:T(8,128)(2,1)S(1)}, bf16[1024,128]{1,0:T(8,128)(2,1)}, u32[]{:S(2)}) copy-start(bf16[1024,128]{1,0:T(8,128)(2,1)} %readout_ref.5) | copy-start | bytes 786436
  15.2 5.7 %copy-start.5 = (bf16[1,256,1024]{2,1,0:T(8,128)(2,1)S(1)}, bf16[1,256,1024]{2,1,0:T(8,128)(2,1)}, u32[]{:S(2)}) copy-start(bf16[1,256,1024]{2,1,0:T(8,128)(2,1)} %param.6) | copy-start | bytes 1572868
  31.0 6.6 %collective-permute-start.2 = (f32[256,128]{1,0:T(8,128)S(1)}, f32[256,128]{1,0:T(8,128)S(1)}, u32[]{:S(2)}, u32[]{:S(2)}) collective-permute-start(f32[256,128]{1,0:T(8,128)S(1)} %get-tuple-element.36.own_ref), channel_id=1, source_target_pairs={{0,64},{64,0},{1,65},{65,1},{2,66},{66,2},{3,67},{67,3},{4,68},{68... | collective-permute-start | bytes 393224 | tf_op jit(solution)/shard_map/ppermute | solution.py:861
  34.1 5.1 %copy-start.3 = (f32[256,128]{1,0:T(8,128)S(1)}, f32[256,128]{1,0:T(8,128)}, u32[]{:S(2)}) copy-start(f32[256,128]{1,0:T(8,128)} %target_ref.1) | copy-start | bytes 393220
  37.5 1.6 %collective-permute-start.3 = (f32[2,256,128]{2,1,0:T(8,128)S(1)}, f32[2,256,128]{2,1,0:T(8,128)S(1)}, u32[]{:S(2)}, u32[]{:S(2)}) collective-permute-start(f32[2,256,128]{2,1,0:T(8,128)S(1)} %pad_maximum_fusion), channel_id=1, source_target_pairs={{0,32},{32,0},{1,33},{33,1},{2,34},{34,2},{3,35},{35,3},{4,36},{36... | collective-permute-start | bytes 786440 | tf_op jit(solution)/shard_map/ppermute | solution.py:814
  37.6 16.8 %collective-permute-start.4 = (bf16[1024,256]{1,0:T(8,128)(2,1)S(1)}, bf16[1024,256]{1,0:T(8,128)(2,1)}, u32[]{:S(2)}, u32[]{:S(2)}) collective-permute-start(bf16[1024,256]{1,0:T(8,128)(2,1)S(1)} %get-tuple-element.43), channel_id=1, source_target_pairs={{0,32},{32,0},{1,33},{33,1},{2,34},{34,2},{3,35},{35,3},{4,36},{36... | collective-permute-start | bytes 1572872 | tf_op jit(solution)/shard_map/ppermute | solution.py:814
  42.8 9.8 %copy-start.2 = (bf16[256,1024]{1,0:T(8,128)(2,1)}, bf16[256,1024]{1,0:T(8,128)(2,1)S(1)}, u32[]{:S(2)}) copy-start(bf16[256,1024]{1,0:T(8,128)(2,1)S(1)} %get-tuple-element.46.grad_ref) | copy-start | bytes 1572868
  42.8 9.8 %collective-permute-start.5 = (bf16[256,256]{1,0:T(8,128)(2,1)}, bf16[256,256]{1,0:T(8,128)(2,1)S(1)}, u32[]{:S(2)}, u32[]{:S(2)}) collective-permute-start(bf16[256,256]{1,0:T(8,128)(2,1)} %get-tuple-element.52), channel_id=1, source_target_pairs={{0,1},{1,2},{2,3},{3,4},{4,5},{5,6},{6,7},{7,8},{8,9},{9,10},{10,1... | collective-permute-start | bytes 393224 | tf_op jit(solution)/shard_map/ppermute | solution.py:869
  45.8 7.5 %collective-permute-start.6 = (bf16[256,256]{1,0:T(8,128)(2,1)}, bf16[256,256]{1,0:T(8,128)(2,1)S(1)}, u32[]{:S(2)}, u32[]{:S(2)}) collective-permute-start(bf16[256,256]{1,0:T(8,128)(2,1)} %get-tuple-element.52), channel_id=1, source_target_pairs={{1,0},{2,1},{3,2},{4,3},{5,4},{6,5},{7,6},{8,7},{9,8},{10,9},{11,1... | collective-permute-start | bytes 393224 | tf_op jit(solution)/shard_map/ppermute | solution.py:870
  47.1 7.3 %collective-permute-start.8 = (bf16[1024,256]{1,0:T(8,128)(2,1)}, bf16[1024,256]{1,0:T(8,128)(2,1)}, u32[]{:S(2)}, u32[]{:S(2)}) collective-permute-start(bf16[1024,256]{1,0:T(8,128)(2,1)} %get-tuple-element.54), channel_id=1, source_target_pairs={{0,32},{32,0},{1,33},{33,1},{2,34},{34,2},{3,35},{35,3},{4,36},{36... | collective-permute-start | bytes 1572872 | tf_op jit(solution)/shard_map/ppermute | solution.py:814
  52.6 0.7 copy-start.6
  53.3 0.7 copy-start.7
  54.0 2.3 %collective-permute-start.7 = (bf16[1024,256]{1,0:T(8,128)(2,1)}, bf16[1024,256]{1,0:T(8,128)(2,1)}, u32[]{:S(2)}, u32[]{:S(2)}) collective-permute-start(bf16[1024,256]{1,0:T(8,128)(2,1)} %shard_map.82.piece_ref), channel_id=1, source_target_pairs={{0,32},{32,0},{1,33},{33,1},{2,34},{34,2},{3,35},{35,3},{4,36},{36... | collective-permute-start | bytes 1572872 | tf_op jit(solution)/shard_map/ppermute | solution.py:814
  59.4 35.6 %all-to-all-start = ((bf16[64,8,1280]{2,1,0:T(8,128)(2,1)}), bf16[64,8,1280]{2,1,0:T(8,128)(2,1)}, u32[]{:S(2)}, u32[]{:S(2)}) async-start(bf16[64,8,1280]{2,1,0:T(8,128)(2,1)} %bitcast.13), calls=%async_computation | async-start | bytes 2621440 | tf_op jit(solution)/shard_map/all_to_all | solution.py:819
  83.9 2.7 %collective-permute-start.9 = (bf16[2048,256]{1,0:T(8,128)(2,1)S(1)}, bf16[2048,256]{1,0:T(8,128)(2,1)S(1)}, u32[]{:S(2)}, u32[]{:S(2)}) collective-permute-start(bf16[2048,256]{1,0:T(8,128)(2,1)S(1)} %bitcast.16), channel_id=1, source_target_pairs={{0,32},{32,0},{1,33},{33,1},{2,34},{34,2},{3,35},{35,3},{4,36},{36... | collective-permute-start | bytes 3145736 | tf_op jit(solution)/shard_map/ppermute | solution.py:814
  95.0 5.8 %copy-start.8 = (f32[256,128]{1,0:T(8,128)S(1)}, f32[256,128]{1,0:T(8,128)}, u32[]{:S(2)}) copy-start(f32[256,128]{1,0:T(8,128)} %get-tuple-element.42) | copy-start | bytes 393220
  95.0 35.8 %all-to-all-start.1 = ((bf16[64,8,2048]{2,1,0:T(8,128)(2,1)}), bf16[64,8,2048]{2,1,0:T(8,128)(2,1)S(1)}, u32[]{:S(2)}, u32[]{:S(2)}) async-start(bf16[64,8,2048]{2,1,0:T(8,128)(2,1)} %bitcast.14), calls=%async_computation.1 | async-start | bytes 4194304 | tf_op jit(solution)/shard_map/all_to_all | solution.py:819

commit v17 on v16

--- a/solution.py
+++ b/solution.py
@@ -509,6 +509,35 @@
     )
 
 
+def crps_kernel(counts_ref, own_ref, near_ref, others_ref, target_ref, crps_ref):
+    members = 4
+    fair_eps = (1.0 - alpha_fair) / members
+    coefficient = (1.0 - fair_eps) / (members * (members - 1))
+    valid = (iota((BLOCK, 1), 0) < counts_ref[1]).astype(F32)
+    forecasts = [own_ref[...], near_ref[...], others_ref[0], others_ref[1]]
+    target = target_ref[...]
+    error = jnp.zeros_like(target)
+    for forecast in forecasts:
+        error += smooth_abs(forecast - target)
+    spread = jnp.full_like(target, members * smooth_width**0.5)
+    for first in range(members):
+        for second in range(first + 1, members):
+            spread += 2.0 * smooth_abs(forecasts[first] - forecasts[second])
+    crps_ref[...] = valid * (error / members - 0.5 * coefficient * spread)
+
+
+def crps_of(counts, own, near, others, target):
+    vmem = pl.BlockSpec(memory_space=pltpu.VMEM)
+    return pl.pallas_call(
+        crps_kernel,
+        in_specs=[pl.BlockSpec(memory_space=pltpu.SMEM)] + [vmem] * 4,
+        out_specs=vmem,
+        out_shape=jax.ShapeDtypeStruct((BLOCK, 128), F32),
+        compiler_params=pltpu.CompilerParams(vmem_limit_bytes=8 * 1024 * 1024),
+        cost_estimate=FREE,
+    )(counts, own, near, others, in_hbm(target))
+
+
 def score_kernel(
     counts_ref,
     own_ref,
@@ -520,7 +549,6 @@
     stats_ref,
     w_out_ref,
     readout_ref,
-    crps_ref,
     packed_ref,
     sent_ref,
     grad_ref,
@@ -531,18 +559,9 @@
     coefficient = (1.0 - fair_eps) / (members * (members - 1))
     valid = (iota((BLOCK, 1), 0) < counts_ref[1]).astype(F32)
     own = own_ref[...]
-    forecasts = [own, near_ref[...], others_ref[0], others_ref[1]]
     target = target_ref[...]
-    error = jnp.zeros_like(target)
-    for forecast in forecasts:
-        error += smooth_abs(forecast - target)
-    spread = jnp.full_like(target, members * smooth_width**0.5)
-    for first in range(members):
-        for second in range(first + 1, members):
-            spread += 2.0 * smooth_abs(forecasts[first] - forecasts[second])
-    crps_ref[...] = valid * (error / members - 0.5 * coefficient * spread)
     pull = jnp.zeros_like(target)
-    for other in forecasts[1:]:
+    for other in (near_ref[...], others_ref[0], others_ref[1]):
         pull += smooth_sign(own - other)
     slope = (
         valid / 128 * (smooth_sign(own - target) / members - coefficient * pull)
@@ -578,9 +597,8 @@
     return pl.pallas_call(
         score_kernel,
         in_specs=[pl.BlockSpec(memory_space=pltpu.SMEM)] + [vmem] * 9,
-        out_specs=[vmem] * 5,
+        out_specs=[vmem] * 4,
         out_shape=[
-            pltpu.HBM((BLOCK, 128), F32),
             jax.ShapeDtypeStruct((BLOCK, 256), BF),
             pltpu.HBM((BLOCK, 256), BF),
             jax.ShapeDtypeStruct((BLOCK, 1024), BF),
@@ -701,8 +719,10 @@
 
     @pl.when(step == 0)
     def _():
-        probs[...] = jnp.zeros_like(probs)
-        dscores[...] = jnp.zeros_like(dscores)
+        for slot in range(4):
+            for held in (probs, dscores):
+                held[slot, :128, 128:] = jnp.zeros((128, 128), BF)
+                held[slot, 640:, :128] = jnp.zeros((128, 128), BF)
         dhidden[:WIN] = dot_nt(left_ref[:, :128], readout_ref[...]).astype(BF)
         dhidden[WIN:] = dot_nt(right_ref[:, :128], readout_ref[...]).astype(BF)
 
@@ -795,7 +815,7 @@
         projected,
         qhalo,
         in_hbm(grad),
-        own,
+        in_hbm(own),
         in_hbm(left),
         in_hbm(right),
         in_hbm(w_out),
@@ -862,10 +882,9 @@
     qhalo = halo_queries(normed_halo, w_qkv)
     near, qhalo = lax.optimization_barrier((near, qhalo))
     others = swap_core(jnp.stack([forecast, near]))
-    crps_whole, packed, sent, grad, small = score(
+    packed, sent, grad, small = score(
         scalars, forecast, near, others, target, attended, hidden, stats, w_out, readout_weight
     )
-    crps = lax.dynamic_slice_in_dim(crps_whole, member_index * 32, 32, 1)
     packed_left = lax.ppermute(sent, CELLS, up)
     packed_right = lax.ppermute(sent, CELLS, down)
 
@@ -886,7 +905,7 @@
         projected,
         qhalo,
         grad,
-        packed,
+        sent,
         packed_left,
         packed_right,
         w_out,
@@ -895,7 +914,10 @@
     pairs = pairs.reshape(2048, BLOCK)
     second_part = partial_sums(core, turned, turned_other, pairs, swap_core(pairs))
     second_part, first = lax.optimization_barrier((second_part, first))
+    second_part, late_near = lax.optimization_barrier((second_part, near))
     second = add_up(scatter(second_part))
+    crps_whole = crps_of(scalars, forecast, late_near, others, target)
+    crps = lax.dynamic_slice_in_dim(crps_whole, member_index * 32, 32, 1)
     first = add_up(first)
     grad_out = lax.dot_general(
         first[:, 1024:1152],

time: 132 us -> 132 us (level)
    pallas_call x0 -> x1, Pallas kernels: none -> 1.44 us  [crps_of(): pl.pallas_call(crps_kernel, in_specs=[pl.BlockSpec(memory_space=pltpu.SME...]
    all_to_all x2, waiting for transfers between devices: 31.9 us -> 30.5 us  [scatter(): lax.all_to_all(partial.reshape(64, 8, columns), CHIPS, split_axis=0, conc...]
    unnamed x19 -> x25, local copies, waits for them, and re-layouts: 3.1 us -> 3.09 us
  transfers between devices with their start and end apart: 12 -> 12, of which waited for: 7 -> 7; matrix products, arithmetic and copies ran while one was open for 4% -> 4% of each run, Pallas kernels for 25% -> 26%
where the time goes in v17:
time: 132 us; the launch traced here: 131 us
  Pallas kernels  47.5 us (36%)
  waiting for transfers between devices  39 us (30%)
  starting transfers between devices  34.5 us (26%)
  local copies, waits for them, and re-layouts  4.57 us (3%)
  other arithmetic  3.23 us (2%)
  between operations  2.18 us (2%)
    all_to_all x2, waiting for transfers between devices, scatter(): lax.all_to_all(partial.reshape(64, 8, columns), CHIPS, split_axis=0, conc...  30.5 us
    all_to_all x2, starting transfers between devices, scatter(): lax.all_to_all(partial.reshape(64, 8, columns), CHIPS, split_axis=0, conc...  19.8 us
    pallas_call x1, Pallas kernels, key_grads(): pl.pallas_call(key_kernel, grid=(4,), in_specs=[pl.BlockSpec(memory_space...  10.2 us
    pallas_call x1, Pallas kernels, forward(): pl.pallas_call(forward_kernel, grid=(4,), in_specs=[pl.BlockSpec(memory_s...  10 us
    pallas_call x2, Pallas kernels, partial_sums(): pl.pallas_call(functools.partial(partial_kernel, len(smalls)), in_specs=[...  6.99 us
    ppermute x5, waiting for transfers between devices, swap_core(): return lax.ppermute(values, 'core', SWAP)  5.55 us
    pallas_call x1, Pallas kernels, query_grads(): pl.pallas_call(query_kernel, grid=(4,), in_specs=[part(BLOCK, 4), part(BL...  5.4 us
    ppermute x1, starting transfers between devices, per_device(): from_left = lax.ppermute(latent_own, CELLS, up)  4.72 us
  transfers between devices with their start and end apart: 12, of which 7 were waited for; matrix products, arithmetic and copies ran while one was open for 4% of the time, Pallas kernels for 26%

profile of v17, /device:TPU:0, one launch (start us, length us, event | category | flops | bytes accessed | tf_op | source)
XLA Modules:
  0.0 131.3 jit_solution(4807145388901408154)
XLA Ops:
  0.6 4.7 %collective-permute-start.1 = (bf16[256,1024]{1,0:T(8,128)(2,1)}, bf16[256,1024]{1,0:T(8,128)(2,1)}, u32[]{:S(2)}, u32[]{:S(2)}) collective-permute-start(bf16[256,1024]{1,0:T(8,128)(2,1)} %bitcast.22), channel_id=1, source_target_pairs={{0,1},{1,2},{2,3},{3,4},{4,5},{5,6},{6,7},{7,8},{8,9},{9,10},{10,1... | collective-permute-start | bytes 1572872 | tf_op jit(solution)/shard_map/ppermute | solution.py:854
  5.3 1.3 collective-permute-start.2
  6.7 1.4 %fusion.2 = (s32[1]{0:T(128)}, s32[1]{0:T(128)}, s32[1]{0:T(128)}) fusion(s32[32]{0:T(128)} %param.7, s32[]{:T(128)S(6)} %max.3, s32[]{:T(128)S(6)} %select_n.19, s32[]{:T(128)S(6)} %select_n.18), kind=kLoop, calls=%fused_computation.8 | loop fusion | bytes 36 | tf_op jit(solution)/shard_map/dynamic_slice | solution.py:858
  11.1 4.0 %shard_map.77 = (bf16[256,3072]{1,0:T(8,128)(2,1)S(1)}, bf16[1024,256]{1,0:T(8,128)(2,1)S(1)}) custom-call(bf16[256,1024]{1,0:T(8,128)(2,1)S(1)} %bitcast.24, bf16[1024,3072]{1,0:T(8,128)(2,1)} %weight_ref.5), custom_call_target="tpu_custom_call" | custom-call | flops 2147483648 | bytes 8388608 | tf_op jit(solution)/shard_map/pallas_call | solution.py:99
  15.1 3.3 %shard_map.78 = (bf16[16,256,256]{2,1,0:T(8,128)(2,1)S(1)}, f32[1024,256]{1,0:T(8,128)S(1)}, f32[16,256]{1,0:T(8,128)S(1)}, f32[16,256]{1,0:T(8,128)S(1)}) custom-call(s32[3]{0:T(128)S(1)} %pad_add_fusion.counts_ref, bf16[256,3072]{1,0:T(8,128)(2,1)S(1)} %get-tuple-element.34.q_ref.k_ref.v_ref, bf16[256,3072]{1,0:T(8,128)(2,1)S(1)} %get-tuple-element.34.q_ref.k_ref.v_ref, ...), custom_call_target="tpu_custom_call" | custom-call | flops 1073741824 | bytes 4194304 | tf_op jit(solution)/shard_map/pallas_call | solution.py:308
  18.4 2.5 %collective-permute-done.2.right_ref = bf16[256,1024]{1,0:T(8,128)(2,1)} collective-permute-done((bf16[256,1024]{1,0:T(8,128)(2,1)}, bf16[256,1024]{1,0:T(8,128)(2,1)}, u32[]{:S(2)}, u32[]{:S(2)}) %collective-permute-start.2) | collective-permute-done | bytes 524320 | tf_op jit(solution)/shard_map/ppermute | solution.py:855
  20.9 10.0 %shard_map.79 = (bf16[512,1024]{1,0:T(8,128)(2,1)S(1)}, bf16[512,1024]{1,0:T(8,128)(2,1)S(1)}, bf16[512,1024]{1,0:T(8,128)(2,1)S(1)}, f32[256,1024]{1,0:T(8,128)...) custom-call(s32[3]{0:T(128)S(1)} %pad_add_fusion.counts_ref, ...), custom_call_target="tpu_custom_call" | custom-call | flops 6442450944 | bytes 12582912 | tf_op jit(solution)/shard_map/pallas_call | solution.py:450
  31.0 3.1 %collective-permute-start.3 = (f32[256,128]{1,0:T(8,128)S(1)}, f32[256,128]{1,0:T(8,128)S(1)}, u32[]{:S(2)}, u32[]{:S(2)}) collective-permute-start(f32[256,128]{1,0:T(8,128)S(1)} %get-tuple-element.40.own_ref), channel_id=1, source_target_pairs={{0,64},{64,0},{1,65},{65,1},{2,66},{66,2},{3,67},{67,3},{4,68},{68... | collective-permute-start | bytes 393224 | tf_op jit(solution)/shard_map/ppermute | solution.py:881
  34.1 3.0 %shard_map.80.qhalo_ref = bf16[512,1024]{1,0:T(8,128)(2,1)S(1)} custom-call(bf16[512,1024]{1,0:T(8,128)(2,1)S(1)} %get-tuple-element.41.normed_ref, bf16[1024,3072]{1,0:T(8,128)(2,1)} %weight_ref.5), custom_call_target="tpu_custom_call" | custom-call | tf_op jit(solution)/shard_map/pallas_call | solution.py:137
  39.2 3.2 %shard_map.81 = (bf16[256,256]{1,0:T(8,128)(2,1)S(1)}, bf16[256,256]{1,0:T(8,128)(2,1)}, bf16[256,1024]{1,0:T(8,128)(2,1)S(1)}, bf16[1024,256]{1,0:T(8,128)(2,1)}) custom-call(s32[3]{0:T(128)S(1)} %pad_add_fusion.counts_ref, f32[256,128]{1,0:T(8,128)S(1)} %get-tuple-element.40.own_ref, f32[256,128]{1,0:T(8,128)S(1)} %collective-permute-done.3.near_ref, ...), custom_call_target="tpu_custom_call" | custom-call | tf_op jit(solution)/shard_map/pallas_call | solution.py:597
  42.3 3.0 %collective-permute-start.5 = (bf16[256,256]{1,0:T(8,128)(2,1)}, bf16[256,256]{1,0:T(8,128)(2,1)S(1)}, u32[]{:S(2)}, u32[]{:S(2)}) collective-permute-start(bf16[256,256]{1,0:T(8,128)(2,1)} %get-tuple-element.52.own_ref), channel_id=1, source_target_pairs={{0,1},{1,2},{2,3},{3,4},{4,5},{5,6},{6,7},{7,8},{8,9},{9,10},{10,1... | collective-permute-start | bytes 393224 | tf_op jit(solution)/shard_map/ppermute | solution.py:888
  45.4 1.3 collective-permute-start.6
  46.8 5.4 %shard_map.82.piece_ref = bf16[1024,256]{1,0:T(8,128)(2,1)} custom-call(bf16[256,3072]{1,0:T(8,128)(2,1)S(1)} %get-tuple-element.34.q_ref.k_ref.v_ref, bf16[256,3072]{1,0:T(8,128)(2,1)S(1)} %get-tuple-element.34.q_ref.k_ref.v_ref, bf16[512,1024]{1,0:T(8,128)(2,1)S(1)} %get-tuple-element.38.khalo_ref, bf16[512,1024]{1,0:T(8,128)(2,1)S(1)} %get-tuple-element.39.vhalo_ref, ...), custom_call_target="tpu_custom_call" | custom-call | flops 6442450944 | bytes 5242880 | tf_op jit(solution)/shard_map/pallas_call | solution.py:662
  54.0 1.9 %collective-permute-done.7.other_ref = bf16[1024,256]{1,0:T(8,128)(2,1)} collective-permute-done((bf16[1024,256]{1,0:T(8,128)(2,1)}, bf16[1024,256]{1,0:T(8,128)(2,1)}, u32[]{:S(2)}, u32[]{:S(2)}) %collective-permute-start.7) | collective-permute-done | bytes 524320 | tf_op jit(solution)/shard_map/ppermute | solution.py:834
  55.9 3.1 %shard_map.83 = bf16[512,1280]{1,0:T(8,128)(2,1)} custom-call(s32[1]{0:T(128)} %bitcast.core_ref, bf16[2,2,256,256]{3,2,1,0:T(8,128)(2,1)S(1)} %bitcast.18, bf16[2,2,256,256]{3,2,1,0:T(8,128)(2,1)} %bitcast.3.normed_other_ref, bf16[1024,256]{1,0:T(8,128)(2,1)} %shard_map.82.piece_ref, bf16[1024,256]{1,0:T(8,128)(2,1)} %collective-permute-done.7.other_ref, ...), custom_call_target="tpu_custom_call" | custom-call | tf_op jit(solution)/shard_map/pallas_call | solution.py:217
  59.0 14.1 %all-to-all-start = ((bf16[64,8,1280]{2,1,0:T(8,128)(2,1)}), bf16[64,8,1280]{2,1,0:T(8,128)(2,1)}, u32[]{:S(2)}, u32[]{:S(2)}) async-start(bf16[64,8,1280]{2,1,0:T(8,128)(2,1)} %bitcast.13), calls=%async_computation | async-start | bytes 2621440 | tf_op jit(solution)/shard_map/all_to_all | solution.py:839
  73.1 10.2 %shard_map.84 = bf16[2,1024,256]{2,1,0:T(8,128)(2,1)S(1)} custom-call(s32[3]{0:T(128)S(1)} %pad_add_fusion.counts_ref, bf16[256,3072]{1,0:T(8,128)(2,1)S(1)} %get-tuple-element.34.q_ref.k_ref.v_ref, bf16[256,3072]{1,0:T(8,128)(2,1)S(1)} %get-tuple-element.34.q_ref.k_ref.v_ref, bf16[256,3072]{1,0:T(8,128)(2,1)S(1)} %get-tuple-element.34.q_ref.k_ref.v_ref, ...), custom_call_target="tpu_custom_call" | custom-call | tf_op jit(solution)/shard_map/pallas_call | solution.py:786
  83.5 2.6 %collective-permute-done.9.other_ref = bf16[2048,256]{1,0:T(8,128)(2,1)S(1)} collective-permute-done((bf16[2048,256]{1,0:T(8,128)(2,1)S(1)}, bf16[2048,256]{1,0:T(8,128)(2,1)S(1)}, u32[]{:S(2)}, u32[]{:S(2)}) %collective-permute-start.9) | collective-permute-done | bytes 1048608 | tf_op jit(solution)/shard_map/ppermute | solution.py:834
  86.1 3.9 %shard_map.85 = bf16[512,2048]{1,0:T(8,128)(2,1)} custom-call(s32[1]{0:T(128)} %bitcast.core_ref, bf16[2,2,256,256]{3,2,1,0:T(8,128)(2,1)S(1)} %bitcast.19, bf16[2,2,256,256]{3,2,1,0:T(8,128)(2,1)} %bitcast.3.normed_other_ref, bf16[2048,256]{1,0:T(8,128)(2,1)S(1)} %bitcast.17, bf16[2048,256]{1,0:T(8,128)(2,1)S(1)} %collective-permute-done.9.other_ref), custom_call_target="tpu_custom_call" | custom-call | tf_op jit(solution)/shard_map/pallas_call | solution.py:217
  90.0 4.6 %all-to-all-done = bf16[64,8,1280]{2,1,0:T(8,128)(2,1)} async-done(((bf16[64,8,1280]{2,1,0:T(8,128)(2,1)}), bf16[64,8,1280]{2,1,0:T(8,128)(2,1)}, u32[]{:S(2)}, u32[]{:S(2)}) %all-to-all-start) | async-done | bytes 1310752 | tf_op jit(solution)/shard_map/all_to_all | solution.py:839
  94.6 5.7 %all-to-all-start.1 = ((bf16[64,8,2048]{2,1,0:T(8,128)(2,1)}), bf16[64,8,2048]{2,1,0:T(8,128)(2,1)S(1)}, u32[]{:S(2)}, u32[]{:S(2)}) async-start(bf16[64,8,2048]{2,1,0:T(8,128)(2,1)} %bitcast.14), calls=%async_computation.1 | async-start | bytes 4194304 | tf_op jit(solution)/shard_map/all_to_all | solution.py:839
  100.3 1.5 %convert_reduce_fusion.1 = f32[8,1280]{1,0:T(8,128)S(1)} fusion(bf16[64,8,1280]{2,1,0:T(8,128)(2,1)} %all-to-all-done), kind=kLoop, calls=%fused_computation.1 | loop fusion | flops 1300480 | bytes 1351680 | tf_op jit(solution)/shard_map/reduce_sum | solution.py:843
  101.9 1.4 %shard_map.86 = f32[256,128]{1,0:T(8,128)S(1)} custom-call(s32[3]{0:T(128)S(1)} %pad_add_fusion.counts_ref, f32[256,128]{1,0:T(8,128)S(1)} %get-tuple-element.40.own_ref, f32[256,128]{1,0:T(8,128)S(1)} %copy-done.3, f32[2,256,128]{2,1,0:T(8,128)S(1)} %copy-done.5, f32[256,128]{1,0:T(8,128)} %target_ref.3), custom_call_target="tpu_custom_call" | custom-call | tf_op jit(solution)/shard_map/pallas_call | solution.py:531
  104.4 25.9 %all-to-all-done.1 = bf16[64,8,2048]{2,1,0:T(8,128)(2,1)S(1)} async-done(((bf16[64,8,2048]{2,1,0:T(8,128)(2,1)}), bf16[64,8,2048]{2,1,0:T(8,128)(2,1)S(1)}, u32[]{:S(2)}, u32[]{:S(2)}) %all-to-all-start.1) | async-done | bytes 2097184 | tf_op jit(solution)/shard_map/all_to_all | solution.py:839
  (45 shorter events, 7.9 us)
Async XLA Ops:
  0.6 17.8 %collective-permute-start.1 = (bf16[256,1024]{1,0:T(8,128)(2,1)}, bf16[256,1024]{1,0:T(8,128)(2,1)}, u32[]{:S(2)}, u32[]{:S(2)}) collective-permute-start(bf16[256,1024]{1,0:T(8,128)(2,1)} %bitcast.22), channel_id=1, source_target_pairs={{0,1},{1,2},{2,3},{3,4},{4,5},{5,6},{6,7},{7,8},{8,9},{9,10},{10,1... | collective-permute-start | bytes 1572872 | tf_op jit(solution)/shard_map/ppermute | solution.py:854
  5.3 15.6 %collective-permute-start.2 = (bf16[256,1024]{1,0:T(8,128)(2,1)}, bf16[256,1024]{1,0:T(8,128)(2,1)}, u32[]{:S(2)}, u32[]{:S(2)}) collective-permute-start(bf16[256,1024]{1,0:T(8,128)(2,1)} %bitcast.23), channel_id=1, source_target_pairs={{1,0},{2,1},{3,2},{4,3},{5,4},{6,5},{7,6},{8,7},{9,8},{10,9},{11,1... | collective-permute-start | bytes 1572872 | tf_op jit(solution)/shard_map/ppermute | solution.py:855
  10.0 1.0 copy-start.8
  15.1 5.9 %copy-start = (bf16[1024,1024]{1,0:T(8,128)(2,1)S(1)}, bf16[1024,1024]{1,0:T(8,128)(2,1)}, u32[]{:S(2)}) copy-start(bf16[1024,1024]{1,0:T(8,128)(2,1)} %w_out_ref.5) | copy-start | bytes 6291460
  15.1 5.9 %copy-start.1 = (bf16[1024,128]{1,0:T(8,128)(2,1)S(1)}, bf16[1024,128]{1,0:T(8,128)(2,1)}, u32[]{:S(2)}) copy-start(bf16[1024,128]{1,0:T(8,128)(2,1)} %readout_ref.5) | copy-start | bytes 786436
  15.1 5.8 %copy-start.9 = (bf16[1,256,1024]{2,1,0:T(8,128)(2,1)S(1)}, bf16[1,256,1024]{2,1,0:T(8,128)(2,1)}, u32[]{:S(2)}) copy-start(bf16[1,256,1024]{2,1,0:T(8,128)(2,1)} %param.6) | copy-start | bytes 1572868
  31.0 6.6 %collective-permute-start.3 = (f32[256,128]{1,0:T(8,128)S(1)}, f32[256,128]{1,0:T(8,128)S(1)}, u32[]{:S(2)}, u32[]{:S(2)}) collective-permute-start(f32[256,128]{1,0:T(8,128)S(1)} %get-tuple-element.40.own_ref), channel_id=1, source_target_pairs={{0,64},{64,0},{1,65},{65,1},{2,66},{66,2},{3,67},{67,3},{4,68},{68... | collective-permute-start | bytes 393224 | tf_op jit(solution)/shard_map/ppermute | solution.py:881
  34.1 5.1 %copy-start.7 = (f32[256,128]{1,0:T(8,128)S(1)}, f32[256,128]{1,0:T(8,128)}, u32[]{:S(2)}) copy-start(f32[256,128]{1,0:T(8,128)} %target_ref.3) | copy-start | bytes 393220
  37.5 4.8 %copy-start.2 = (f32[256,128]{1,0:T(8,128)}, f32[256,128]{1,0:T(8,128)S(1)}, u32[]{:S(2)}) copy-start(f32[256,128]{1,0:T(8,128)S(1)} %collective-permute-done.3.near_ref) | copy-start | bytes 393220
  37.6 1.6 %collective-permute-start.4 = (f32[2,256,128]{2,1,0:T(8,128)S(1)}, f32[2,256,128]{2,1,0:T(8,128)S(1)}, u32[]{:S(2)}, u32[]{:S(2)}) collective-permute-start(f32[2,256,128]{2,1,0:T(8,128)S(1)} %pad_maximum_fusion), channel_id=1, source_target_pairs={{0,32},{32,0},{1,33},{33,1},{2,34},{34,2},{3,35},{35,3},{4,36},{36... | collective-permute-start | bytes 786440 | tf_op jit(solution)/shard_map/ppermute | solution.py:834
  37.6 16.4 %collective-permute-start = (bf16[1024,256]{1,0:T(8,128)(2,1)S(1)}, bf16[1024,256]{1,0:T(8,128)(2,1)}, u32[]{:S(2)}, u32[]{:S(2)}) collective-permute-start(bf16[1024,256]{1,0:T(8,128)(2,1)S(1)} %get-tuple-element.33), channel_id=1, source_target_pairs={{0,32},{32,0},{1,33},{33,1},{2,34},{34,2},{3,35},{35,3},{4,36},{36... | collective-permute-start | bytes 1572872 | tf_op jit(solution)/shard_map/ppermute | solution.py:834
  39.2 3.2 %copy-start.4 = (f32[2,256,128]{2,1,0:T(8,128)}, f32[2,256,128]{2,1,0:T(8,128)S(1)}, u32[]{:S(2)}) copy-start(f32[2,256,128]{2,1,0:T(8,128)S(1)} %collective-permute-done.4.others_ref) | copy-start | bytes 786436
  42.3 9.9 %copy-start.6 = (bf16[256,1024]{1,0:T(8,128)(2,1)}, bf16[256,1024]{1,0:T(8,128)(2,1)S(1)}, u32[]{:S(2)}) copy-start(bf16[256,1024]{1,0:T(8,128)(2,1)S(1)} %get-tuple-element.46.grad_ref) | copy-start | bytes 1572868
  42.3 9.8 %collective-permute-start.5 = (bf16[256,256]{1,0:T(8,128)(2,1)}, bf16[256,256]{1,0:T(8,128)(2,1)S(1)}, u32[]{:S(2)}, u32[]{:S(2)}) collective-permute-start(bf16[256,256]{1,0:T(8,128)(2,1)} %get-tuple-element.52.own_ref), channel_id=1, source_target_pairs={{0,1},{1,2},{2,3},{3,4},{4,5},{5,6},{6,7},{7,8},{8,9},{9,10},{10,1... | collective-permute-start | bytes 393224 | tf_op jit(solution)/shard_map/ppermute | solution.py:888
  45.4 7.5 %collective-permute-start.6 = (bf16[256,256]{1,0:T(8,128)(2,1)}, bf16[256,256]{1,0:T(8,128)(2,1)S(1)}, u32[]{:S(2)}, u32[]{:S(2)}) collective-permute-start(bf16[256,256]{1,0:T(8,128)(2,1)} %get-tuple-element.52.own_ref), channel_id=1, source_target_pairs={{1,0},{2,1},{3,2},{4,3},{5,4},{6,5},{7,6},{8,7},{9,8},{10,9},{11,1... | collective-permute-start | bytes 393224 | tf_op jit(solution)/shard_map/ppermute | solution.py:889
  46.7 7.3 %collective-permute-start.8 = (bf16[1024,256]{1,0:T(8,128)(2,1)}, bf16[1024,256]{1,0:T(8,128)(2,1)}, u32[]{:S(2)}, u32[]{:S(2)}) collective-permute-start(bf16[1024,256]{1,0:T(8,128)(2,1)} %get-tuple-element.54), channel_id=1, source_target_pairs={{0,32},{32,0},{1,33},{33,1},{2,34},{34,2},{3,35},{35,3},{4,36},{36... | collective-permute-start | bytes 1572872 | tf_op jit(solution)/shard_map/ppermute | solution.py:834
  52.2 0.7 copy-start.10
  52.9 0.7 copy-start.11
  53.5 2.4 %collective-permute-start.7 = (bf16[1024,256]{1,0:T(8,128)(2,1)}, bf16[1024,256]{1,0:T(8,128)(2,1)}, u32[]{:S(2)}, u32[]{:S(2)}) collective-permute-start(bf16[1024,256]{1,0:T(8,128)(2,1)} %shard_map.82.piece_ref), channel_id=1, source_target_pairs={{0,32},{32,0},{1,33},{33,1},{2,34},{34,2},{3,35},{35,3},{4,36},{36... | collective-permute-start | bytes 1572872 | tf_op jit(solution)/shard_map/ppermute | solution.py:834
  59.0 35.6 %all-to-all-start = ((bf16[64,8,1280]{2,1,0:T(8,128)(2,1)}), bf16[64,8,1280]{2,1,0:T(8,128)(2,1)}, u32[]{:S(2)}, u32[]{:S(2)}) async-start(bf16[64,8,1280]{2,1,0:T(8,128)(2,1)} %bitcast.13), calls=%async_computation | async-start | bytes 2621440 | tf_op jit(solution)/shard_map/all_to_all | solution.py:839
  83.4 2.7 %collective-permute-start.9 = (bf16[2048,256]{1,0:T(8,128)(2,1)S(1)}, bf16[2048,256]{1,0:T(8,128)(2,1)S(1)}, u32[]{:S(2)}, u32[]{:S(2)}) collective-permute-start(bf16[2048,256]{1,0:T(8,128)(2,1)S(1)} %bitcast.16), channel_id=1, source_target_pairs={{0,32},{32,0},{1,33},{33,1},{2,34},{34,2},{3,35},{35,3},{4,36},{36... | collective-permute-start | bytes 3145736 | tf_op jit(solution)/shard_map/ppermute | solution.py:834
  94.6 7.3 %copy-start.3 = (f32[256,128]{1,0:T(8,128)S(1)}, f32[256,128]{1,0:T(8,128)}, u32[]{:S(2)}) copy-start(f32[256,128]{1,0:T(8,128)} %copy-done.2) | copy-start | bytes 393220
  94.6 7.3 %copy-start.5 = (f32[2,256,128]{2,1,0:T(8,128)S(1)}, f32[2,256,128]{2,1,0:T(8,128)}, u32[]{:S(2)}) copy-start(f32[2,256,128]{2,1,0:T(8,128)} %copy-done.4) | copy-start | bytes 786436
  94.6 35.7 %all-to-all-start.1 = ((bf16[64,8,2048]{2,1,0:T(8,128)(2,1)}), bf16[64,8,2048]{2,1,0:T(8,128)(2,1)S(1)}, u32[]{:S(2)}, u32[]{:S(2)}) async-start(bf16[64,8,2048]{2,1,0:T(8,128)(2,1)} %bitcast.14), calls=%async_computation.1 | async-start | bytes 4194304 | tf_op jit(solution)/shard_map/all_to_all | solution.py:839

commit v18 on v17

--- a/solution.py
+++ b/solution.py
@@ -706,8 +706,7 @@
     qhalo_ref,
     grad_ref,
     own_ref,
-    left_ref,
-    right_ref,
+    sides_ref,
     w_out_ref,
     readout_ref,
     out_ref,
@@ -723,12 +722,12 @@
             for held in (probs, dscores):
                 held[slot, :128, 128:] = jnp.zeros((128, 128), BF)
                 held[slot, 640:, :128] = jnp.zeros((128, 128), BF)
-        dhidden[:WIN] = dot_nt(left_ref[:, :128], readout_ref[...]).astype(BF)
-        dhidden[WIN:] = dot_nt(right_ref[:, :128], readout_ref[...]).astype(BF)
+        dhidden[:WIN] = dot_nt(sides_ref[0, :, :128], readout_ref[...]).astype(BF)
+        dhidden[WIN:] = dot_nt(sides_ref[1, :, :128], readout_ref[...]).astype(BF)
 
     ghalo = dot_nt(dhidden[...], w_out_ref[...]).astype(BF)
     terms = jnp.concatenate(
-        [left_ref[:, 128:], own_ref[:, 128:], right_ref[:, 128:]], axis=0
+        [sides_ref[0, :, 128:], own_ref[:, 128:], sides_ref[1, :, 128:]], axis=0
     )
     window = terms.shape[0]
     fill = key_fill([(counts_ref[1], BLOCK)])
@@ -779,7 +778,7 @@
         out_ref[1, place] = dot_nn(turned[slot][1], probs[slot]).astype(BF)
 
 
-def key_grads(counts, projected, qhalo, grad, own, left, right, w_out, readout_weight):
+def key_grads(counts, projected, qhalo, grad, own, sides, w_out, readout_weight):
     part = lambda rows, first: pl.BlockSpec((rows, WIDTH), lambda j: (0, first + j))
     whole = lambda *shape: pl.BlockSpec(shape, lambda j: (0, 0))
     window = 2 * WIN + BLOCK
@@ -794,8 +793,7 @@
             part(2 * WIN, 0),
             part(BLOCK, 0),
             whole(BLOCK, 256),
-            whole(BLOCK, 256),
-            whole(BLOCK, 256),
+            pl.BlockSpec((2, WIN, 256), lambda j: (0, 0, 0)),
             pl.BlockSpec((WIDTH, 1024), lambda j: (j, 0)),
             whole(1024, 128),
         ],
@@ -816,8 +814,7 @@
         qhalo,
         in_hbm(grad),
         in_hbm(own),
-        in_hbm(left),
-        in_hbm(right),
+        in_hbm(sides),
         in_hbm(w_out),
         readout_weight,
     )
@@ -894,6 +891,7 @@
     dquery, packed_left, packed_right = lax.optimization_barrier(
         (dquery, packed_left, packed_right)
     )
+    sides = jnp.stack([packed_left, packed_right])
 
     first_part = partial_sums(
         core, turned, turned_other, dquery, swap_core(dquery), (small, swap_core(small))
@@ -906,8 +904,7 @@
         qhalo,
         grad,
         sent,
-        packed_left,
-        packed_right,
+        sides,
         w_out,
         readout_weight,
     )

time: 132 us -> 134 us (1.015)
  starting transfers between devices: 34.5 us -> 36.2 us
  waiting for transfers between devices: 39 us -> 37.3 us
  other arithmetic: 3.23 us -> 4.9 us
    another operation x0 -> x1, other arithmetic: none -> 1.69 us  [per_device(): sides = jnp.stack([packed_left, packed_right])]
    all_to_all x2, starting transfers between devices: 19.8 us -> 21.5 us  [scatter(): lax.all_to_all(partial.reshape(64, 8, columns), CHIPS, split_axis=0, conc...]
    all_to_all x2, waiting for transfers between devices: 30.5 us -> 28.9 us  [scatter(): lax.all_to_all(partial.reshape(64, 8, columns), CHIPS, split_axis=0, conc...]
  transfers between devices with their start and end apart: 12 -> 12, of which waited for: 7 -> 7; matrix products, arithmetic and copies ran while one was open for 4% -> 5% of each run, Pallas kernels for 26% -> 26%
where the time goes in v18:
time: 134 us; the launch traced here: 133 us
  Pallas kernels  47.5 us (35%)
  waiting for transfers between devices  37.3 us (28%)
  starting transfers between devices  36.2 us (27%)
  other arithmetic  4.9 us (4%)
  local copies, waits for them, and re-layouts  4.57 us (3%)
  between operations  2.18 us (2%)
    all_to_all x2, waiting for transfers between devices, scatter(): lax.all_to_all(partial.reshape(64, 8, columns), CHIPS, split_axis=0, conc...  28.9 us
    all_to_all x2, starting transfers between devices, scatter(): lax.all_to_all(partial.reshape(64, 8, columns), CHIPS, split_axis=0, conc...  21.5 us
    pallas_call x1, Pallas kernels, key_grads(): pl.pallas_call(key_kernel, grid=(4,), in_specs=[pl.BlockSpec(memory_space...  10.2 us
    pallas_call x1, Pallas kernels, forward(): pl.pallas_call(forward_kernel, grid=(4,), in_specs=[pl.BlockSpec(memory_s...  10 us
    pallas_call x2, Pallas kernels, partial_sums(): pl.pallas_call(functools.partial(partial_kernel, len(smalls)), in_specs=[...  6.99 us
    ppermute x5, waiting for transfers between devices, swap_core(): return lax.ppermute(values, 'core', SWAP)  5.55 us
    pallas_call x1, Pallas kernels, query_grads(): pl.pallas_call(query_kernel, grid=(4,), in_specs=[part(BLOCK, 4), part(BL...  5.41 us
    ppermute x1, starting transfers between devices, per_device(): from_left = lax.ppermute(latent_own, CELLS, up)  4.72 us
  transfers between devices with their start and end apart: 12, of which 7 were waited for; matrix products, arithmetic and copies ran while one was open for 5% of the time, Pallas kernels for 26%

profile of v18, /device:TPU:0, one launch (start us, length us, event | category | flops | bytes accessed | tf_op | source)
XLA Modules:
  0.0 132.9 jit_solution(12933764259291834718)
XLA Ops:
  0.6 4.7 %collective-permute-start.1 = (bf16[256,1024]{1,0:T(8,128)(2,1)}, bf16[256,1024]{1,0:T(8,128)(2,1)}, u32[]{:S(2)}, u32[]{:S(2)}) collective-permute-start(bf16[256,1024]{1,0:T(8,128)(2,1)} %bitcast.24), channel_id=1, source_target_pairs={{0,1},{1,2},{2,3},{3,4},{4,5},{5,6},{6,7},{7,8},{8,9},{9,10},{10,1... | collective-permute-start | bytes 1572872 | tf_op jit(solution)/shard_map/ppermute | solution.py:851
  6.7 1.4 %fusion.2 = (s32[1]{0:T(128)}, s32[1]{0:T(128)}, s32[1]{0:T(128)}) fusion(s32[32]{0:T(128)} %param.7, s32[]{:T(128)S(6)} %max.3, s32[]{:T(128)S(6)} %select_n.19, s32[]{:T(128)S(6)} %select_n.18), kind=kLoop, calls=%fused_computation.9 | loop fusion | bytes 36 | tf_op jit(solution)/shard_map/dynamic_slice | solution.py:855
  11.1 4.0 %shard_map.77 = (bf16[256,3072]{1,0:T(8,128)(2,1)S(1)}, bf16[1024,256]{1,0:T(8,128)(2,1)S(1)}) custom-call(bf16[256,1024]{1,0:T(8,128)(2,1)S(1)} %bitcast.26, bf16[1024,3072]{1,0:T(8,128)(2,1)} %weight_ref.5), custom_call_target="tpu_custom_call" | custom-call | flops 2147483648 | bytes 8388608 | tf_op jit(solution)/shard_map/pallas_call | solution.py:99
  15.2 3.3 %shard_map.78 = (bf16[16,256,256]{2,1,0:T(8,128)(2,1)S(1)}, f32[1024,256]{1,0:T(8,128)S(1)}, f32[16,256]{1,0:T(8,128)S(1)}, f32[16,256]{1,0:T(8,128)S(1)}) custom-call(s32[3]{0:T(128)S(1)} %pad_add_fusion.counts_ref, bf16[256,3072]{1,0:T(8,128)(2,1)S(1)} %get-tuple-element.34.q_ref.k_ref.v_ref, bf16[256,3072]{1,0:T(8,128)(2,1)S(1)} %get-tuple-element.34.q_ref.k_ref.v_ref, ...), custom_call_target="tpu_custom_call" | custom-call | flops 1073741824 | bytes 4194304 | tf_op jit(solution)/shard_map/pallas_call | solution.py:308
  18.5 2.5 %collective-permute-done.2.right_ref = bf16[256,1024]{1,0:T(8,128)(2,1)} collective-permute-done((bf16[256,1024]{1,0:T(8,128)(2,1)}, bf16[256,1024]{1,0:T(8,128)(2,1)}, u32[]{:S(2)}, u32[]{:S(2)}) %collective-permute-start.2) | collective-permute-done | bytes 524320 | tf_op jit(solution)/shard_map/ppermute | solution.py:852
  20.9 10.0 %shard_map.79 = (bf16[512,1024]{1,0:T(8,128)(2,1)S(1)}, bf16[512,1024]{1,0:T(8,128)(2,1)S(1)}, bf16[512,1024]{1,0:T(8,128)(2,1)S(1)}, f32[256,1024]{1,0:T(8,128)...) custom-call(s32[3]{0:T(128)S(1)} %pad_add_fusion.counts_ref, ...), custom_call_target="tpu_custom_call" | custom-call | flops 6442450944 | bytes 12582912 | tf_op jit(solution)/shard_map/pallas_call | solution.py:450
  31.0 3.1 %collective-permute-start.3 = (f32[256,128]{1,0:T(8,128)S(1)}, f32[256,128]{1,0:T(8,128)S(1)}, u32[]{:S(2)}, u32[]{:S(2)}) collective-permute-start(f32[256,128]{1,0:T(8,128)S(1)} %get-tuple-element.40.own_ref), channel_id=1, source_target_pairs={{0,64},{64,0},{1,65},{65,1},{2,66},{66,2},{3,67},{67,3},{4,68},{68... | collective-permute-start | bytes 393224 | tf_op jit(solution)/shard_map/ppermute | solution.py:878
  34.1 3.0 %shard_map.80.qhalo_ref = bf16[512,1024]{1,0:T(8,128)(2,1)S(1)} custom-call(bf16[512,1024]{1,0:T(8,128)(2,1)S(1)} %get-tuple-element.41.normed_ref, bf16[1024,3072]{1,0:T(8,128)(2,1)} %weight_ref.5), custom_call_target="tpu_custom_call" | custom-call | tf_op jit(solution)/shard_map/pallas_call | solution.py:137
  39.2 3.2 %shard_map.81 = (bf16[256,256]{1,0:T(8,128)(2,1)S(1)}, bf16[256,256]{1,0:T(8,128)(2,1)}, bf16[256,1024]{1,0:T(8,128)(2,1)S(1)}, bf16[1024,256]{1,0:T(8,128)(2,1)}) custom-call(s32[3]{0:T(128)S(1)} %pad_add_fusion.counts_ref, f32[256,128]{1,0:T(8,128)S(1)} %get-tuple-element.40.own_ref, f32[256,128]{1,0:T(8,128)S(1)} %collective-permute-done.3.near_ref, ...), custom_call_target="tpu_custom_call" | custom-call | tf_op jit(solution)/shard_map/pallas_call | solution.py:597
  42.3 3.0 %collective-permute-start.5 = (bf16[256,256]{1,0:T(8,128)(2,1)}, bf16[256,256]{1,0:T(8,128)(2,1)S(1)}, u32[]{:S(2)}, u32[]{:S(2)}) collective-permute-start(bf16[256,256]{1,0:T(8,128)(2,1)} %get-tuple-element.52.own_ref), channel_id=1, source_target_pairs={{0,1},{1,2},{2,3},{3,4},{4,5},{5,6},{6,7},{7,8},{8,9},{9,10},{10,1... | collective-permute-start | bytes 393224 | tf_op jit(solution)/shard_map/ppermute | solution.py:885
  45.4 1.3 collective-permute-start.6
  46.8 5.4 %shard_map.82.piece_ref = bf16[1024,256]{1,0:T(8,128)(2,1)} custom-call(bf16[256,3072]{1,0:T(8,128)(2,1)S(1)} %get-tuple-element.34.q_ref.k_ref.v_ref, bf16[256,3072]{1,0:T(8,128)(2,1)S(1)} %get-tuple-element.34.q_ref.k_ref.v_ref, bf16[512,1024]{1,0:T(8,128)(2,1)S(1)} %get-tuple-element.38.khalo_ref, bf16[512,1024]{1,0:T(8,128)(2,1)S(1)} %get-tuple-element.39.vhalo_ref, ...), custom_call_target="tpu_custom_call" | custom-call | flops 6442450944 | bytes 5242880 | tf_op jit(solution)/shard_map/pallas_call | solution.py:662
  54.0 1.9 %collective-permute-done.7.other_ref = bf16[1024,256]{1,0:T(8,128)(2,1)} collective-permute-done((bf16[1024,256]{1,0:T(8,128)(2,1)}, bf16[1024,256]{1,0:T(8,128)(2,1)}, u32[]{:S(2)}, u32[]{:S(2)}) %collective-permute-start.7) | collective-permute-done | bytes 524320 | tf_op jit(solution)/shard_map/ppermute | solution.py:831
  55.8 3.1 %shard_map.83 = bf16[512,1280]{1,0:T(8,128)(2,1)} custom-call(s32[1]{0:T(128)} %bitcast.core_ref, bf16[2,2,256,256]{3,2,1,0:T(8,128)(2,1)S(1)} %bitcast.20, bf16[2,2,256,256]{3,2,1,0:T(8,128)(2,1)} %bitcast.3.normed_other_ref, bf16[1024,256]{1,0:T(8,128)(2,1)} %shard_map.82.piece_ref, bf16[1024,256]{1,0:T(8,128)(2,1)} %collective-permute-done.7.other_ref, ...), custom_call_target="tpu_custom_call" | custom-call | tf_op jit(solution)/shard_map/pallas_call | solution.py:217
  59.0 14.1 %all-to-all-start = ((bf16[64,8,1280]{2,1,0:T(8,128)(2,1)}), bf16[64,8,1280]{2,1,0:T(8,128)(2,1)}, u32[]{:S(2)}, u32[]{:S(2)}) async-start(bf16[64,8,1280]{2,1,0:T(8,128)(2,1)} %bitcast.15), calls=%async_computation | async-start | bytes 2621440 | tf_op jit(solution)/shard_map/all_to_all | solution.py:836
  73.1 1.7 %pad_maximum_fusion.1.sides_ref = bf16[2,256,256]{2,1,0:T(8,128)(2,1)} fusion(bf16[1,256,256]{2,1,0:T(8,128)(2,1)} %bitcast.29, bf16[1,256,256]{2,1,0:T(8,128)(2,1)} %bitcast.28), kind=kLoop, calls=%fused_computation.3 | loop fusion | flops 131072 | bytes 524288 | tf_op jit(solution)/shard_map/stack | solution.py:894
  74.8 10.2 %shard_map.84 = bf16[2,1024,256]{2,1,0:T(8,128)(2,1)S(1)} custom-call(s32[3]{0:T(128)S(1)} %pad_add_fusion.counts_ref, bf16[256,3072]{1,0:T(8,128)(2,1)S(1)} %get-tuple-element.34.q_ref.k_ref.v_ref, bf16[256,3072]{1,0:T(8,128)(2,1)S(1)} %get-tuple-element.34.q_ref.k_ref.v_ref, bf16[256,3072]{1,0:T(8,128)(2,1)S(1)} %get-tuple-element.34.q_ref.k_ref.v_ref, ...), custom_call_target="tpu_custom_call" | custom-call | tf_op jit(solution)/shard_map/pallas_call | solution.py:785
  85.1 2.6 %collective-permute-done.9.other_ref = bf16[2048,256]{1,0:T(8,128)(2,1)S(1)} collective-permute-done((bf16[2048,256]{1,0:T(8,128)(2,1)S(1)}, bf16[2048,256]{1,0:T(8,128)(2,1)S(1)}, u32[]{:S(2)}, u32[]{:S(2)}) %collective-permute-start.9) | collective-permute-done | bytes 1048608 | tf_op jit(solution)/shard_map/ppermute | solution.py:831
  87.7 3.9 %shard_map.85 = bf16[512,2048]{1,0:T(8,128)(2,1)} custom-call(s32[1]{0:T(128)} %bitcast.core_ref, bf16[2,2,256,256]{3,2,1,0:T(8,128)(2,1)S(1)} %bitcast.21, bf16[2,2,256,256]{3,2,1,0:T(8,128)(2,1)} %bitcast.3.normed_other_ref, bf16[2048,256]{1,0:T(8,128)(2,1)S(1)} %bitcast.19, bf16[2048,256]{1,0:T(8,128)(2,1)S(1)} %collective-permute-done.9.other_ref), custom_call_target="tpu_custom_call" | custom-call | tf_op jit(solution)/shard_map/pallas_call | solution.py:217
  91.6 3.0 %all-to-all-done = bf16[64,8,1280]{2,1,0:T(8,128)(2,1)} async-done(((bf16[64,8,1280]{2,1,0:T(8,128)(2,1)}), bf16[64,8,1280]{2,1,0:T(8,128)(2,1)}, u32[]{:S(2)}, u32[]{:S(2)}) %all-to-all-start) | async-done | bytes 1310752 | tf_op jit(solution)/shard_map/all_to_all | solution.py:836
  94.6 7.4 %all-to-all-start.1 = ((bf16[64,8,2048]{2,1,0:T(8,128)(2,1)}), bf16[64,8,2048]{2,1,0:T(8,128)(2,1)S(1)}, u32[]{:S(2)}, u32[]{:S(2)}) async-start(bf16[64,8,2048]{2,1,0:T(8,128)(2,1)} %bitcast.16), calls=%async_computation.1 | async-start | bytes 4194304 | tf_op jit(solution)/shard_map/all_to_all | solution.py:836
  102.0 1.5 %convert_reduce_fusion.1 = f32[8,1280]{1,0:T(8,128)S(1)} fusion(bf16[64,8,1280]{2,1,0:T(8,128)(2,1)} %all-to-all-done), kind=kLoop, calls=%fused_computation.1 | loop fusion | flops 1300480 | bytes 1351680 | tf_op jit(solution)/shard_map/reduce_sum | solution.py:840
  103.5 1.4 %shard_map.86 = f32[256,128]{1,0:T(8,128)S(1)} custom-call(s32[3]{0:T(128)S(1)} %pad_add_fusion.counts_ref, f32[256,128]{1,0:T(8,128)S(1)} %get-tuple-element.40.own_ref, f32[256,128]{1,0:T(8,128)S(1)} %copy-done.3, f32[2,256,128]{2,1,0:T(8,128)S(1)} %copy-done.5, f32[256,128]{1,0:T(8,128)} %target_ref.3), custom_call_target="tpu_custom_call" | custom-call | tf_op jit(solution)/shard_map/pallas_call | solution.py:531
  106.1 25.9 %all-to-all-done.1 = bf16[64,8,2048]{2,1,0:T(8,128)(2,1)S(1)} async-done(((bf16[64,8,2048]{2,1,0:T(8,128)(2,1)}), bf16[64,8,2048]{2,1,0:T(8,128)(2,1)S(1)}, u32[]{:S(2)}, u32[]{:S(2)}) %all-to-all-start.1) | async-done | bytes 2097184 | tf_op jit(solution)/shard_map/all_to_all | solution.py:836
  (46 shorter events, 9.2 us)
Async XLA Ops:
  0.6 17.8 %collective-permute-start.1 = (bf16[256,1024]{1,0:T(8,128)(2,1)}, bf16[256,1024]{1,0:T(8,128)(2,1)}, u32[]{:S(2)}, u32[]{:S(2)}) collective-permute-start(bf16[256,1024]{1,0:T(8,128)(2,1)} %bitcast.24), channel_id=1, source_target_pairs={{0,1},{1,2},{2,3},{3,4},{4,5},{5,6},{6,7},{7,8},{8,9},{9,10},{10,1... | collective-permute-start | bytes 1572872 | tf_op jit(solution)/shard_map/ppermute | solution.py:851
  5.3 15.6 %collective-permute-start.2 = (bf16[256,1024]{1,0:T(8,128)(2,1)}, bf16[256,1024]{1,0:T(8,128)(2,1)}, u32[]{:S(2)}, u32[]{:S(2)}) collective-permute-start(bf16[256,1024]{1,0:T(8,128)(2,1)} %bitcast.25), channel_id=1, source_target_pairs={{1,0},{2,1},{3,2},{4,3},{5,4},{6,5},{7,6},{8,7},{9,8},{10,9},{11,1... | collective-permute-start | bytes 1572872 | tf_op jit(solution)/shard_map/ppermute | solution.py:852
  10.0 1.0 copy-start.8
  15.1 5.8 %copy-start = (bf16[1024,1024]{1,0:T(8,128)(2,1)S(1)}, bf16[1024,1024]{1,0:T(8,128)(2,1)}, u32[]{:S(2)}) copy-start(bf16[1024,1024]{1,0:T(8,128)(2,1)} %w_out_ref.5) | copy-start | bytes 6291460
  15.1 5.8 %copy-start.1 = (bf16[1024,128]{1,0:T(8,128)(2,1)S(1)}, bf16[1024,128]{1,0:T(8,128)(2,1)}, u32[]{:S(2)}) copy-start(bf16[1024,128]{1,0:T(8,128)(2,1)} %readout_ref.5) | copy-start | bytes 786436
  15.1 5.8 %copy-start.9 = (bf16[1,256,1024]{2,1,0:T(8,128)(2,1)S(1)}, bf16[1,256,1024]{2,1,0:T(8,128)(2,1)}, u32[]{:S(2)}) copy-start(bf16[1,256,1024]{2,1,0:T(8,128)(2,1)} %param.6) | copy-start | bytes 1572868
  31.0 6.6 %collective-permute-start.3 = (f32[256,128]{1,0:T(8,128)S(1)}, f32[256,128]{1,0:T(8,128)S(1)}, u32[]{:S(2)}, u32[]{:S(2)}) collective-permute-start(f32[256,128]{1,0:T(8,128)S(1)} %get-tuple-element.40.own_ref), channel_id=1, source_target_pairs={{0,64},{64,0},{1,65},{65,1},{2,66},{66,2},{3,67},{67,3},{4,68},{68... | collective-permute-start | bytes 393224 | tf_op jit(solution)/shard_map/ppermute | solution.py:878
  34.1 5.1 %copy-start.7 = (f32[256,128]{1,0:T(8,128)S(1)}, f32[256,128]{1,0:T(8,128)}, u32[]{:S(2)}) copy-start(f32[256,128]{1,0:T(8,128)} %target_ref.3) | copy-start | bytes 393220
  37.5 4.8 %copy-start.2 = (f32[256,128]{1,0:T(8,128)}, f32[256,128]{1,0:T(8,128)S(1)}, u32[]{:S(2)}) copy-start(f32[256,128]{1,0:T(8,128)S(1)} %collective-permute-done.3.near_ref) | copy-start | bytes 393220
  37.5 1.6 %collective-permute-start.4 = (f32[2,256,128]{2,1,0:T(8,128)S(1)}, f32[2,256,128]{2,1,0:T(8,128)S(1)}, u32[]{:S(2)}, u32[]{:S(2)}) collective-permute-start(f32[2,256,128]{2,1,0:T(8,128)S(1)} %pad_maximum_fusion), channel_id=1, source_target_pairs={{0,32},{32,0},{1,33},{33,1},{2,34},{34,2},{3,35},{35,3},{4,36},{36... | collective-permute-start | bytes 786440 | tf_op jit(solution)/shard_map/ppermute | solution.py:831
  37.6 16.3 %collective-permute-start = (bf16[1024,256]{1,0:T(8,128)(2,1)S(1)}, bf16[1024,256]{1,0:T(8,128)(2,1)}, u32[]{:S(2)}, u32[]{:S(2)}) collective-permute-start(bf16[1024,256]{1,0:T(8,128)(2,1)S(1)} %get-tuple-element.33), channel_id=1, source_target_pairs={{0,32},{32,0},{1,33},{33,1},{2,34},{34,2},{3,35},{35,3},{4,36},{36... | collective-permute-start | bytes 1572872 | tf_op jit(solution)/shard_map/ppermute | solution.py:831
  39.1 3.2 %copy-start.4 = (f32[2,256,128]{2,1,0:T(8,128)}, f32[2,256,128]{2,1,0:T(8,128)S(1)}, u32[]{:S(2)}) copy-start(f32[2,256,128]{2,1,0:T(8,128)S(1)} %collective-permute-done.4.others_ref) | copy-start | bytes 786436
  42.3 9.9 %copy-start.6 = (bf16[256,1024]{1,0:T(8,128)(2,1)}, bf16[256,1024]{1,0:T(8,128)(2,1)S(1)}, u32[]{:S(2)}) copy-start(bf16[256,1024]{1,0:T(8,128)(2,1)S(1)} %get-tuple-element.46.grad_ref) | copy-start | bytes 1572868
  42.3 9.9 %collective-permute-start.5 = (bf16[256,256]{1,0:T(8,128)(2,1)}, bf16[256,256]{1,0:T(8,128)(2,1)S(1)}, u32[]{:S(2)}, u32[]{:S(2)}) collective-permute-start(bf16[256,256]{1,0:T(8,128)(2,1)} %get-tuple-element.52.own_ref), channel_id=1, source_target_pairs={{0,1},{1,2},{2,3},{3,4},{4,5},{5,6},{6,7},{7,8},{8,9},{9,10},{10,1... | collective-permute-start | bytes 393224 | tf_op jit(solution)/shard_map/ppermute | solution.py:885
  45.4 7.5 %collective-permute-start.6 = (bf16[256,256]{1,0:T(8,128)(2,1)}, bf16[256,256]{1,0:T(8,128)(2,1)S(1)}, u32[]{:S(2)}, u32[]{:S(2)}) collective-permute-start(bf16[256,256]{1,0:T(8,128)(2,1)} %get-tuple-element.52.own_ref), channel_id=1, source_target_pairs={{1,0},{2,1},{3,2},{4,3},{5,4},{6,5},{7,6},{8,7},{9,8},{10,9},{11,1... | collective-permute-start | bytes 393224 | tf_op jit(solution)/shard_map/ppermute | solution.py:886
  46.7 7.3 %collective-permute-start.8 = (bf16[1024,256]{1,0:T(8,128)(2,1)}, bf16[1024,256]{1,0:T(8,128)(2,1)}, u32[]{:S(2)}, u32[]{:S(2)}) collective-permute-start(bf16[1024,256]{1,0:T(8,128)(2,1)} %get-tuple-element.54), channel_id=1, source_target_pairs={{0,32},{32,0},{1,33},{33,1},{2,34},{34,2},{3,35},{35,3},{4,36},{36... | collective-permute-start | bytes 1572872 | tf_op jit(solution)/shard_map/ppermute | solution.py:831
  52.2 0.7 copy-start.10
  52.8 0.7 copy-start.11
  53.5 2.3 %collective-permute-start.7 = (bf16[1024,256]{1,0:T(8,128)(2,1)}, bf16[1024,256]{1,0:T(8,128)(2,1)}, u32[]{:S(2)}, u32[]{:S(2)}) collective-permute-start(bf16[1024,256]{1,0:T(8,128)(2,1)} %shard_map.82.piece_ref), channel_id=1, source_target_pairs={{0,32},{32,0},{1,33},{33,1},{2,34},{34,2},{3,35},{35,3},{4,36},{36... | collective-permute-start | bytes 1572872 | tf_op jit(solution)/shard_map/ppermute | solution.py:831
  59.0 35.6 %all-to-all-start = ((bf16[64,8,1280]{2,1,0:T(8,128)(2,1)}), bf16[64,8,1280]{2,1,0:T(8,128)(2,1)}, u32[]{:S(2)}, u32[]{:S(2)}) async-start(bf16[64,8,1280]{2,1,0:T(8,128)(2,1)} %bitcast.15), calls=%async_computation | async-start | bytes 2621440 | tf_op jit(solution)/shard_map/all_to_all | solution.py:836
  85.0 2.7 %collective-permute-start.9 = (bf16[2048,256]{1,0:T(8,128)(2,1)S(1)}, bf16[2048,256]{1,0:T(8,128)(2,1)S(1)}, u32[]{:S(2)}, u32[]{:S(2)}) collective-permute-start(bf16[2048,256]{1,0:T(8,128)(2,1)S(1)} %bitcast.18), channel_id=1, source_target_pairs={{0,32},{32,0},{1,33},{33,1},{2,34},{34,2},{3,35},{35,3},{4,36},{36... | collective-permute-start | bytes 3145736 | tf_op jit(solution)/shard_map/ppermute | solution.py:831
  94.6 8.9 %copy-start.3 = (f32[256,128]{1,0:T(8,128)S(1)}, f32[256,128]{1,0:T(8,128)}, u32[]{:S(2)}) copy-start(f32[256,128]{1,0:T(8,128)} %copy-done.2) | copy-start | bytes 393220
  94.6 8.9 %copy-start.5 = (f32[2,256,128]{2,1,0:T(8,128)S(1)}, f32[2,256,128]{2,1,0:T(8,128)}, u32[]{:S(2)}) copy-start(f32[2,256,128]{2,1,0:T(8,128)} %copy-done.4) | copy-start | bytes 786436
  94.6 37.4 %all-to-all-start.1 = ((bf16[64,8,2048]{2,1,0:T(8,128)(2,1)}), bf16[64,8,2048]{2,1,0:T(8,128)(2,1)S(1)}, u32[]{:S(2)}, u32[]{:S(2)}) async-start(bf16[64,8,2048]{2,1,0:T(8,128)(2,1)} %bitcast.16), calls=%async_computation.1 | async-start | bytes 4194304 | tf_op jit(solution)/shard_map/all_to_all | solution.py:836

commit v19 on v17

--- a/solution.py
+++ b/solution.py
@@ -641,9 +641,9 @@
             pick_k = low_k if half == 0 else ~low_k
             g_head = jnp.where(pick_q, g_pair, g_fill[:, columns])
             own_change = dot_nt(jnp.where(pick_q, v_ref[:, columns], own_fill), g_head)
-            own_dscores[slot] = (own_probs_ref[slot].astype(F32) * own_change).astype(BF)
+            own_dscores[slot] = (own_probs_ref[step * 4 + slot].astype(F32) * own_change).astype(BF)
             change = dot_nt(jnp.where(pick_k, vhalo_ref[:, columns], halo_fill), g_head)
-            dscores[slot] = (probs_ref[slot].astype(F32) * change).astype(BF)
+            dscores[slot] = (probs_ref[step * 4 + slot].astype(F32) * change).astype(BF)
             lanes = slice(half * HEAD_WIDTH, (half + 1) * HEAD_WIDTH)
             turned.append((own_turned[lanes], halo_turned[lanes]))
     for slot in range(4):
@@ -657,7 +657,6 @@
 
 def query_grads(projected, khalo, vhalo, grad, packed, probs, own_probs, inverse, own_inverse):
     part = lambda rows, first: pl.BlockSpec((rows, WIDTH), lambda j: (0, first + j))
-    heads = lambda rows: pl.BlockSpec((4, rows, BLOCK), lambda j: (j, 0, 0))
     whole = pl.BlockSpec((HEADS, BLOCK), lambda j: (0, 0))
     return pl.pallas_call(
         query_kernel,
@@ -669,8 +668,8 @@
             part(2 * WIN, 0),
             part(BLOCK, 0),
             pl.BlockSpec((BLOCK, 256), lambda j: (0, 0)),
-            heads(2 * WIN),
-            heads(BLOCK),
+            pl.BlockSpec(memory_space=pltpu.VMEM),
+            pl.BlockSpec(memory_space=pltpu.VMEM),
             whole,
             whole,
         ],

time: 132 us -> 132 us (level)
  no operation moved by 1% of the time
where the time goes in v19:
time: 132 us; the launch traced here: 131 us
  Pallas kernels  47.5 us (36%)
  waiting for transfers between devices  39 us (30%)
  starting transfers between devices  34.5 us (26%)
  local copies, waits for them, and re-layouts  4.57 us (3%)
  other arithmetic  3.23 us (2%)
  between operations  2.18 us (2%)
    all_to_all x2, waiting for transfers between devices, scatter(): lax.all_to_all(partial.reshape(64, 8, columns), CHIPS, split_axis=0, conc...  30.5 us
    all_to_all x2, starting transfers between devices, scatter(): lax.all_to_all(partial.reshape(64, 8, columns), CHIPS, split_axis=0, conc...  19.8 us
    pallas_call x1, Pallas kernels, key_grads(): pl.pallas_call(key_kernel, grid=(4,), in_specs=[pl.BlockSpec(memory_space...  10.2 us
    pallas_call x1, Pallas kernels, forward(): pl.pallas_call(forward_kernel, grid=(4,), in_specs=[pl.BlockSpec(memory_s...  10 us
    pallas_call x2, Pallas kernels, partial_sums(): pl.pallas_call(functools.partial(partial_kernel, len(smalls)), in_specs=[...  6.99 us
    ppermute x5, waiting for transfers between devices, swap_core(): return lax.ppermute(values, 'core', SWAP)  5.55 us
    pallas_call x1, Pallas kernels, query_grads(): pl.pallas_call(query_kernel, grid=(4,), in_specs=[part(BLOCK, 4), part(BL...  5.4 us
    ppermute x1, starting transfers between devices, per_device(): from_left = lax.ppermute(latent_own, CELLS, up)  4.72 us
  transfers between devices with their start and end apart: 12, of which 7 were waited for; matrix products, arithmetic and copies ran while one was open for 4% of the time, Pallas kernels for 26%

profile of v19, /device:TPU:0, one launch (start us, length us, event | category | flops | bytes accessed | tf_op | source)
XLA Modules:
  0.0 131.3 jit_solution(121341136062685917)
XLA Ops:
  0.6 4.7 %collective-permute-start.1 = (bf16[256,1024]{1,0:T(8,128)(2,1)}, bf16[256,1024]{1,0:T(8,128)(2,1)}, u32[]{:S(2)}, u32[]{:S(2)}) collective-permute-start(bf16[256,1024]{1,0:T(8,128)(2,1)} %bitcast.22), channel_id=1, source_target_pairs={{0,1},{1,2},{2,3},{3,4},{4,5},{5,6},{6,7},{7,8},{8,9},{9,10},{10,1... | collective-permute-start | bytes 1572872 | tf_op jit(solution)/shard_map/ppermute | solution.py:853
  5.3 1.3 collective-permute-start.2
  6.7 1.4 %fusion.2 = (s32[1]{0:T(128)}, s32[1]{0:T(128)}, s32[1]{0:T(128)}) fusion(s32[32]{0:T(128)} %param.7, s32[]{:T(128)S(6)} %max.3, s32[]{:T(128)S(6)} %select_n.19, s32[]{:T(128)S(6)} %select_n.18), kind=kLoop, calls=%fused_computation.8 | loop fusion | bytes 36 | tf_op jit(solution)/shard_map/dynamic_slice | solution.py:857
  11.1 4.0 %shard_map.77 = (bf16[256,3072]{1,0:T(8,128)(2,1)S(1)}, bf16[1024,256]{1,0:T(8,128)(2,1)S(1)}) custom-call(bf16[256,1024]{1,0:T(8,128)(2,1)S(1)} %bitcast.24, bf16[1024,3072]{1,0:T(8,128)(2,1)} %weight_ref.5), custom_call_target="tpu_custom_call" | custom-call | flops 2147483648 | bytes 8388608 | tf_op jit(solution)/shard_map/pallas_call | solution.py:99
  15.1 3.3 %shard_map.78 = (bf16[16,256,256]{2,1,0:T(8,128)(2,1)S(1)}, f32[1024,256]{1,0:T(8,128)S(1)}, f32[16,256]{1,0:T(8,128)S(1)}, f32[16,256]{1,0:T(8,128)S(1)}) custom-call(s32[3]{0:T(128)S(1)} %pad_add_fusion.counts_ref, bf16[256,3072]{1,0:T(8,128)(2,1)S(1)} %get-tuple-element.34.q_ref.k_ref.v_ref, bf16[256,3072]{1,0:T(8,128)(2,1)S(1)} %get-tuple-element.34.q_ref.k_ref.v_ref, ...), custom_call_target="tpu_custom_call" | custom-call | flops 1073741824 | bytes 4194304 | tf_op jit(solution)/shard_map/pallas_call | solution.py:308
  18.4 2.5 %collective-permute-done.2.right_ref = bf16[256,1024]{1,0:T(8,128)(2,1)} collective-permute-done((bf16[256,1024]{1,0:T(8,128)(2,1)}, bf16[256,1024]{1,0:T(8,128)(2,1)}, u32[]{:S(2)}, u32[]{:S(2)}) %collective-permute-start.2) | collective-permute-done | bytes 524320 | tf_op jit(solution)/shard_map/ppermute | solution.py:854
  20.9 10.0 %shard_map.79 = (bf16[512,1024]{1,0:T(8,128)(2,1)S(1)}, bf16[512,1024]{1,0:T(8,128)(2,1)S(1)}, bf16[512,1024]{1,0:T(8,128)(2,1)S(1)}, f32[256,1024]{1,0:T(8,128)...) custom-call(s32[3]{0:T(128)S(1)} %pad_add_fusion.counts_ref, ...), custom_call_target="tpu_custom_call" | custom-call | flops 6442450944 | bytes 12582912 | tf_op jit(solution)/shard_map/pallas_call | solution.py:450
  31.0 3.1 %collective-permute-start.3 = (f32[256,128]{1,0:T(8,128)S(1)}, f32[256,128]{1,0:T(8,128)S(1)}, u32[]{:S(2)}, u32[]{:S(2)}) collective-permute-start(f32[256,128]{1,0:T(8,128)S(1)} %get-tuple-element.40.own_ref), channel_id=1, source_target_pairs={{0,64},{64,0},{1,65},{65,1},{2,66},{66,2},{3,67},{67,3},{4,68},{68... | collective-permute-start | bytes 393224 | tf_op jit(solution)/shard_map/ppermute | solution.py:880
  34.1 3.0 %shard_map.80.qhalo_ref = bf16[512,1024]{1,0:T(8,128)(2,1)S(1)} custom-call(bf16[512,1024]{1,0:T(8,128)(2,1)S(1)} %get-tuple-element.41.normed_ref, bf16[1024,3072]{1,0:T(8,128)(2,1)} %weight_ref.5), custom_call_target="tpu_custom_call" | custom-call | tf_op jit(solution)/shard_map/pallas_call | solution.py:137
  39.2 3.2 %shard_map.81 = (bf16[256,256]{1,0:T(8,128)(2,1)S(1)}, bf16[256,256]{1,0:T(8,128)(2,1)}, bf16[256,1024]{1,0:T(8,128)(2,1)S(1)}, bf16[1024,256]{1,0:T(8,128)(2,1)}) custom-call(s32[3]{0:T(128)S(1)} %pad_add_fusion.counts_ref, f32[256,128]{1,0:T(8,128)S(1)} %get-tuple-element.40.own_ref, f32[256,128]{1,0:T(8,128)S(1)} %collective-permute-done.3.near_ref, ...), custom_call_target="tpu_custom_call" | custom-call | tf_op jit(solution)/shard_map/pallas_call | solution.py:597
  42.3 3.0 %collective-permute-start.5 = (bf16[256,256]{1,0:T(8,128)(2,1)}, bf16[256,256]{1,0:T(8,128)(2,1)S(1)}, u32[]{:S(2)}, u32[]{:S(2)}) collective-permute-start(bf16[256,256]{1,0:T(8,128)(2,1)} %get-tuple-element.52.own_ref), channel_id=1, source_target_pairs={{0,1},{1,2},{2,3},{3,4},{4,5},{5,6},{6,7},{7,8},{8,9},{9,10},{10,1... | collective-permute-start | bytes 393224 | tf_op jit(solution)/shard_map/ppermute | solution.py:887
  45.4 1.3 collective-permute-start.6
  46.8 5.4 %shard_map.82.piece_ref = bf16[1024,256]{1,0:T(8,128)(2,1)} custom-call(bf16[256,3072]{1,0:T(8,128)(2,1)S(1)} %get-tuple-element.34.q_ref.k_ref.v_ref, bf16[256,3072]{1,0:T(8,128)(2,1)S(1)} %get-tuple-element.34.q_ref.k_ref.v_ref, bf16[512,1024]{1,0:T(8,128)(2,1)S(1)} %get-tuple-element.38.khalo_ref, bf16[512,1024]{1,0:T(8,128)(2,1)S(1)} %get-tuple-element.39.vhalo_ref, ...), custom_call_target="tpu_custom_call" | custom-call | flops 6442450944 | bytes 5242880 | tf_op jit(solution)/shard_map/pallas_call | solution.py:661
  54.0 1.9 %collective-permute-done.7.other_ref = bf16[1024,256]{1,0:T(8,128)(2,1)} collective-permute-done((bf16[1024,256]{1,0:T(8,128)(2,1)}, bf16[1024,256]{1,0:T(8,128)(2,1)}, u32[]{:S(2)}, u32[]{:S(2)}) %collective-permute-start.7) | collective-permute-done | bytes 524320 | tf_op jit(solution)/shard_map/ppermute | solution.py:833
  55.9 3.1 %shard_map.83 = bf16[512,1280]{1,0:T(8,128)(2,1)} custom-call(s32[1]{0:T(128)} %bitcast.core_ref, bf16[2,2,256,256]{3,2,1,0:T(8,128)(2,1)S(1)} %bitcast.18, bf16[2,2,256,256]{3,2,1,0:T(8,128)(2,1)} %bitcast.3.normed_other_ref, bf16[1024,256]{1,0:T(8,128)(2,1)} %shard_map.82.piece_ref, bf16[1024,256]{1,0:T(8,128)(2,1)} %collective-permute-done.7.other_ref, ...), custom_call_target="tpu_custom_call" | custom-call | tf_op jit(solution)/shard_map/pallas_call | solution.py:217
  59.0 14.1 %all-to-all-start = ((bf16[64,8,1280]{2,1,0:T(8,128)(2,1)}), bf16[64,8,1280]{2,1,0:T(8,128)(2,1)}, u32[]{:S(2)}, u32[]{:S(2)}) async-start(bf16[64,8,1280]{2,1,0:T(8,128)(2,1)} %bitcast.13), calls=%async_computation | async-start | bytes 2621440 | tf_op jit(solution)/shard_map/all_to_all | solution.py:838
  73.1 10.2 %shard_map.84 = bf16[2,1024,256]{2,1,0:T(8,128)(2,1)S(1)} custom-call(s32[3]{0:T(128)S(1)} %pad_add_fusion.counts_ref, bf16[256,3072]{1,0:T(8,128)(2,1)S(1)} %get-tuple-element.34.q_ref.k_ref.v_ref, bf16[256,3072]{1,0:T(8,128)(2,1)S(1)} %get-tuple-element.34.q_ref.k_ref.v_ref, bf16[256,3072]{1,0:T(8,128)(2,1)S(1)} %get-tuple-element.34.q_ref.k_ref.v_ref, ...), custom_call_target="tpu_custom_call" | custom-call | tf_op jit(solution)/shard_map/pallas_call | solution.py:785
  83.5 2.6 %collective-permute-done.9.other_ref = bf16[2048,256]{1,0:T(8,128)(2,1)S(1)} collective-permute-done((bf16[2048,256]{1,0:T(8,128)(2,1)S(1)}, bf16[2048,256]{1,0:T(8,128)(2,1)S(1)}, u32[]{:S(2)}, u32[]{:S(2)}) %collective-permute-start.9) | collective-permute-done | bytes 1048608 | tf_op jit(solution)/shard_map/ppermute | solution.py:833
  86.1 3.9 %shard_map.85 = bf16[512,2048]{1,0:T(8,128)(2,1)} custom-call(s32[1]{0:T(128)} %bitcast.core_ref, bf16[2,2,256,256]{3,2,1,0:T(8,128)(2,1)S(1)} %bitcast.19, bf16[2,2,256,256]{3,2,1,0:T(8,128)(2,1)} %bitcast.3.normed_other_ref, bf16[2048,256]{1,0:T(8,128)(2,1)S(1)} %bitcast.17, bf16[2048,256]{1,0:T(8,128)(2,1)S(1)} %collective-permute-done.9.other_ref), custom_call_target="tpu_custom_call" | custom-call | tf_op jit(solution)/shard_map/pallas_call | solution.py:217
  90.0 4.6 %all-to-all-done = bf16[64,8,1280]{2,1,0:T(8,128)(2,1)} async-done(((bf16[64,8,1280]{2,1,0:T(8,128)(2,1)}), bf16[64,8,1280]{2,1,0:T(8,128)(2,1)}, u32[]{:S(2)}, u32[]{:S(2)}) %all-to-all-start) | async-done | bytes 1310752 | tf_op jit(solution)/shard_map/all_to_all | solution.py:838
  94.6 5.7 %all-to-all-start.1 = ((bf16[64,8,2048]{2,1,0:T(8,128)(2,1)}), bf16[64,8,2048]{2,1,0:T(8,128)(2,1)S(1)}, u32[]{:S(2)}, u32[]{:S(2)}) async-start(bf16[64,8,2048]{2,1,0:T(8,128)(2,1)} %bitcast.14), calls=%async_computation.1 | async-start | bytes 4194304 | tf_op jit(solution)/shard_map/all_to_all | solution.py:838
  100.3 1.5 %convert_reduce_fusion.1 = f32[8,1280]{1,0:T(8,128)S(1)} fusion(bf16[64,8,1280]{2,1,0:T(8,128)(2,1)} %all-to-all-done), kind=kLoop, calls=%fused_computation.1 | loop fusion | flops 1300480 | bytes 1351680 | tf_op jit(solution)/shard_map/reduce_sum | solution.py:842
  101.9 1.4 %shard_map.86 = f32[256,128]{1,0:T(8,128)S(1)} custom-call(s32[3]{0:T(128)S(1)} %pad_add_fusion.counts_ref, f32[256,128]{1,0:T(8,128)S(1)} %get-tuple-element.40.own_ref, f32[256,128]{1,0:T(8,128)S(1)} %copy-done.3, f32[2,256,128]{2,1,0:T(8,128)S(1)} %copy-done.5, f32[256,128]{1,0:T(8,128)} %target_ref.3), custom_call_target="tpu_custom_call" | custom-call | tf_op jit(solution)/shard_map/pallas_call | solution.py:531
  104.4 25.9 %all-to-all-done.1 = bf16[64,8,2048]{2,1,0:T(8,128)(2,1)S(1)} async-done(((bf16[64,8,2048]{2,1,0:T(8,128)(2,1)}), bf16[64,8,2048]{2,1,0:T(8,128)(2,1)S(1)}, u32[]{:S(2)}, u32[]{:S(2)}) %all-to-all-start.1) | async-done | bytes 2097184 | tf_op jit(solution)/shard_map/all_to_all | solution.py:838
  (45 shorter events, 7.9 us)
Async XLA Ops:
  0.6 17.8 %collective-permute-start.1 = (bf16[256,1024]{1,0:T(8,128)(2,1)}, bf16[256,1024]{1,0:T(8,128)(2,1)}, u32[]{:S(2)}, u32[]{:S(2)}) collective-permute-start(bf16[256,1024]{1,0:T(8,128)(2,1)} %bitcast.22), channel_id=1, source_target_pairs={{0,1},{1,2},{2,3},{3,4},{4,5},{5,6},{6,7},{7,8},{8,9},{9,10},{10,1... | collective-permute-start | bytes 1572872 | tf_op jit(solution)/shard_map/ppermute | solution.py:853
  5.3 15.6 %collective-permute-start.2 = (bf16[256,1024]{1,0:T(8,128)(2,1)}, bf16[256,1024]{1,0:T(8,128)(2,1)}, u32[]{:S(2)}, u32[]{:S(2)}) collective-permute-start(bf16[256,1024]{1,0:T(8,128)(2,1)} %bitcast.23), channel_id=1, source_target_pairs={{1,0},{2,1},{3,2},{4,3},{5,4},{6,5},{7,6},{8,7},{9,8},{10,9},{11,1... | collective-permute-start | bytes 1572872 | tf_op jit(solution)/shard_map/ppermute | solution.py:854
  10.0 1.0 copy-start.8
  15.1 5.9 %copy-start = (bf16[1024,1024]{1,0:T(8,128)(2,1)S(1)}, bf16[1024,1024]{1,0:T(8,128)(2,1)}, u32[]{:S(2)}) copy-start(bf16[1024,1024]{1,0:T(8,128)(2,1)} %w_out_ref.5) | copy-start | bytes 6291460
  15.1 5.9 %copy-start.1 = (bf16[1024,128]{1,0:T(8,128)(2,1)S(1)}, bf16[1024,128]{1,0:T(8,128)(2,1)}, u32[]{:S(2)}) copy-start(bf16[1024,128]{1,0:T(8,128)(2,1)} %readout_ref.5) | copy-start | bytes 786436
  15.1 5.8 %copy-start.9 = (bf16[1,256,1024]{2,1,0:T(8,128)(2,1)S(1)}, bf16[1,256,1024]{2,1,0:T(8,128)(2,1)}, u32[]{:S(2)}) copy-start(bf16[1,256,1024]{2,1,0:T(8,128)(2,1)} %param.6) | copy-start | bytes 1572868
  31.0 6.6 %collective-permute-start.3 = (f32[256,128]{1,0:T(8,128)S(1)}, f32[256,128]{1,0:T(8,128)S(1)}, u32[]{:S(2)}, u32[]{:S(2)}) collective-permute-start(f32[256,128]{1,0:T(8,128)S(1)} %get-tuple-element.40.own_ref), channel_id=1, source_target_pairs={{0,64},{64,0},{1,65},{65,1},{2,66},{66,2},{3,67},{67,3},{4,68},{68... | collective-permute-start | bytes 393224 | tf_op jit(solution)/shard_map/ppermute | solution.py:880
  34.1 5.1 %copy-start.7 = (f32[256,128]{1,0:T(8,128)S(1)}, f32[256,128]{1,0:T(8,128)}, u32[]{:S(2)}) copy-start(f32[256,128]{1,0:T(8,128)} %target_ref.3) | copy-start | bytes 393220
  37.5 4.8 %copy-start.2 = (f32[256,128]{1,0:T(8,128)}, f32[256,128]{1,0:T(8,128)S(1)}, u32[]{:S(2)}) copy-start(f32[256,128]{1,0:T(8,128)S(1)} %collective-permute-done.3.near_ref) | copy-start | bytes 393220
  37.6 1.6 %collective-permute-start.4 = (f32[2,256,128]{2,1,0:T(8,128)S(1)}, f32[2,256,128]{2,1,0:T(8,128)S(1)}, u32[]{:S(2)}, u32[]{:S(2)}) collective-permute-start(f32[2,256,128]{2,1,0:T(8,128)S(1)} %pad_maximum_fusion), channel_id=1, source_target_pairs={{0,32},{32,0},{1,33},{33,1},{2,34},{34,2},{3,35},{35,3},{4,36},{36... | collective-permute-start | bytes 786440 | tf_op jit(solution)/shard_map/ppermute | solution.py:833
  37.6 16.4 %collective-permute-start = (bf16[1024,256]{1,0:T(8,128)(2,1)S(1)}, bf16[1024,256]{1,0:T(8,128)(2,1)}, u32[]{:S(2)}, u32[]{:S(2)}) collective-permute-start(bf16[1024,256]{1,0:T(8,128)(2,1)S(1)} %get-tuple-element.33), channel_id=1, source_target_pairs={{0,32},{32,0},{1,33},{33,1},{2,34},{34,2},{3,35},{35,3},{4,36},{36... | collective-permute-start | bytes 1572872 | tf_op jit(solution)/shard_map/ppermute | solution.py:833
  39.2 3.2 %copy-start.4 = (f32[2,256,128]{2,1,0:T(8,128)}, f32[2,256,128]{2,1,0:T(8,128)S(1)}, u32[]{:S(2)}) copy-start(f32[2,256,128]{2,1,0:T(8,128)S(1)} %collective-permute-done.4.others_ref) | copy-start | bytes 786436
  42.3 9.9 %copy-start.6 = (bf16[256,1024]{1,0:T(8,128)(2,1)}, bf16[256,1024]{1,0:T(8,128)(2,1)S(1)}, u32[]{:S(2)}) copy-start(bf16[256,1024]{1,0:T(8,128)(2,1)S(1)} %get-tuple-element.46.grad_ref) | copy-start | bytes 1572868
  42.3 9.8 %collective-permute-start.5 = (bf16[256,256]{1,0:T(8,128)(2,1)}, bf16[256,256]{1,0:T(8,128)(2,1)S(1)}, u32[]{:S(2)}, u32[]{:S(2)}) collective-permute-start(bf16[256,256]{1,0:T(8,128)(2,1)} %get-tuple-element.52.own_ref), channel_id=1, source_target_pairs={{0,1},{1,2},{2,3},{3,4},{4,5},{5,6},{6,7},{7,8},{8,9},{9,10},{10,1... | collective-permute-start | bytes 393224 | tf_op jit(solution)/shard_map/ppermute | solution.py:887
  45.4 7.5 %collective-permute-start.6 = (bf16[256,256]{1,0:T(8,128)(2,1)}, bf16[256,256]{1,0:T(8,128)(2,1)S(1)}, u32[]{:S(2)}, u32[]{:S(2)}) collective-permute-start(bf16[256,256]{1,0:T(8,128)(2,1)} %get-tuple-element.52.own_ref), channel_id=1, source_target_pairs={{1,0},{2,1},{3,2},{4,3},{5,4},{6,5},{7,6},{8,7},{9,8},{10,9},{11,1... | collective-permute-start | bytes 393224 | tf_op jit(solution)/shard_map/ppermute | solution.py:888
  46.7 7.3 %collective-permute-start.8 = (bf16[1024,256]{1,0:T(8,128)(2,1)}, bf16[1024,256]{1,0:T(8,128)(2,1)}, u32[]{:S(2)}, u32[]{:S(2)}) collective-permute-start(bf16[1024,256]{1,0:T(8,128)(2,1)} %get-tuple-element.54), channel_id=1, source_target_pairs={{0,32},{32,0},{1,33},{33,1},{2,34},{34,2},{3,35},{35,3},{4,36},{36... | collective-permute-start | bytes 1572872 | tf_op jit(solution)/shard_map/ppermute | solution.py:833
  52.2 0.7 copy-start.10
  52.9 0.7 copy-start.11
  53.5 2.4 %collective-permute-start.7 = (bf16[1024,256]{1,0:T(8,128)(2,1)}, bf16[1024,256]{1,0:T(8,128)(2,1)}, u32[]{:S(2)}, u32[]{:S(2)}) collective-permute-start(bf16[1024,256]{1,0:T(8,128)(2,1)} %shard_map.82.piece_ref), channel_id=1, source_target_pairs={{0,32},{32,0},{1,33},{33,1},{2,34},{34,2},{3,35},{35,3},{4,36},{36... | collective-permute-start | bytes 1572872 | tf_op jit(solution)/shard_map/ppermute | solution.py:833
  59.0 35.6 %all-to-all-start = ((bf16[64,8,1280]{2,1,0:T(8,128)(2,1)}), bf16[64,8,1280]{2,1,0:T(8,128)(2,1)}, u32[]{:S(2)}, u32[]{:S(2)}) async-start(bf16[64,8,1280]{2,1,0:T(8,128)(2,1)} %bitcast.13), calls=%async_computation | async-start | bytes 2621440 | tf_op jit(solution)/shard_map/all_to_all | solution.py:838
  83.4 2.7 %collective-permute-start.9 = (bf16[2048,256]{1,0:T(8,128)(2,1)S(1)}, bf16[2048,256]{1,0:T(8,128)(2,1)S(1)}, u32[]{:S(2)}, u32[]{:S(2)}) collective-permute-start(bf16[2048,256]{1,0:T(8,128)(2,1)S(1)} %bitcast.16), channel_id=1, source_target_pairs={{0,32},{32,0},{1,33},{33,1},{2,34},{34,2},{3,35},{35,3},{4,36},{36... | collective-permute-start | bytes 3145736 | tf_op jit(solution)/shard_map/ppermute | solution.py:833
  94.6 7.3 %copy-start.3 = (f32[256,128]{1,0:T(8,128)S(1)}, f32[256,128]{1,0:T(8,128)}, u32[]{:S(2)}) copy-start(f32[256,128]{1,0:T(8,128)} %copy-done.2) | copy-start | bytes 393220
  94.6 7.3 %copy-start.5 = (f32[2,256,128]{2,1,0:T(8,128)S(1)}, f32[2,256,128]{2,1,0:T(8,128)}, u32[]{:S(2)}) copy-start(f32[2,256,128]{2,1,0:T(8,128)} %copy-done.4) | copy-start | bytes 786436
  94.6 35.7 %all-to-all-start.1 = ((bf16[64,8,2048]{2,1,0:T(8,128)(2,1)}), bf16[64,8,2048]{2,1,0:T(8,128)(2,1)S(1)}, u32[]{:S(2)}, u32[]{:S(2)}) async-start(bf16[64,8,2048]{2,1,0:T(8,128)(2,1)} %bitcast.14), calls=%async_computation.1 | async-start | bytes 4194304 | tf_op jit(solution)/shard_map/all_to_all | solution.py:838
